TPU v7x, 32 devices: a whole 2x2x4 slice. The times are simulated.
32 devices in a mesh: ctx: 8 (over z, x), ch: 4 (over y, core).
Axes of the slice: x: 2, y: 2, z: 4, core: 2. Of those that a mesh axis runs over, the one named last changes fastest.
Arguments:
- inputs: bfloat16 [1536, 16384], P('ch', 'ctx'), may hold values from -6 to 6
- conv_weight: bfloat16 [3, 1536, 96], replicated, may hold values from -0.375 to 0.375
- pw_weight: bfloat16 [1536, 1536], replicated, may hold values from -0.15625 to 0.15625
- cotangent: bfloat16 [1536, 16384], P(None, ('ctx', 'ch')), may hold values from -6 to 6
Outputs:
- mixed: bfloat16 [1536, 16384], P(None, ('ctx', 'ch'))
- grad_inputs: bfloat16 [1536, 16384], P('ch', 'ctx')
All inputs are finite; a program needn't handle non-finite values.
Results may differ from a plain program's by a relative error of at most 0.012.
Values may be sent and summed in bfloat16 or wider, within the bound.
No kernel may reach another device: no remote copies, remote signals or barrier semaphores. Data moves between devices by JAX's collectives and lax.ppermute only.
A program may use at most 64 MiB of HBM per device.

v0:
```python
import jax
import jax.numpy as jnp
from jax import lax
from jax.sharding import PartitionSpec as P

DILATION_STEP = 512


def shifted(block, axis, distance):
    devices = range(lax.axis_size(axis))
    route = [(i - distance, i) for i in devices if i - distance in devices]
    return lax.ppermute(block, axis, route)


def gelu_slope(values):
    return jax.vjp(jax.nn.gelu, values)[1](jnp.ones_like(values))[0]


def group_conv(kernel_taps, weight_part):
    channels, length = kernel_taps[0].shape
    width = weight_part.shape[2]
    groups = channels // width
    total = jnp.zeros((groups, width, length), jnp.float32)
    for position_offset in range(3):
        kernel = weight_part[position_offset].reshape(groups, width, width)
        signal = kernel_taps[position_offset].reshape(groups, width, length)
        total = total + jnp.einsum(
            "gji,gip->gjp", kernel, signal, preferred_element_type=jnp.float32
        )
    return total.reshape(channels, length)


def group_conv_back(kernel_taps, weight_part):
    channels, length = kernel_taps[0].shape
    width = weight_part.shape[2]
    groups = channels // width
    total = jnp.zeros((groups, width, length), jnp.float32)
    for position_offset in range(3):
        kernel = weight_part[position_offset].reshape(groups, width, width)
        signal = kernel_taps[position_offset].reshape(groups, width, length)
        total = total + jnp.einsum(
            "gji,gjp->gip", kernel, signal, preferred_element_type=jnp.float32
        )
    return total.reshape(channels, length)


def upstream_grad(pw_weight, cotangent):
    return lax.dot_general(
        pw_weight, cotangent, (((0,), (0,)), ((), ())), preferred_element_type=jnp.float32
    ).astype(jnp.bfloat16)


def shift_rows(values, steps):
    return shifted(values, ("ctx", "ch"), steps)


def shift_grads(values, steps):
    return shifted(values, ("ctx", "ch"), steps)


def body(inputs, conv_weight, pw_weight, cotangent):
    track_rows = lax.all_to_all(inputs, "ch", split_axis=1, concat_axis=0, tiled=True)
    position_stride = DILATION_STEP // track_rows.shape[1]
    kernel_taps = [
        shift_rows(track_rows, position_stride),
        track_rows,
        shift_rows(track_rows, -position_stride),
    ]
    conv_out = group_conv(kernel_taps, conv_weight)
    active = jax.nn.gelu(conv_out).astype(jnp.bfloat16)
    mixed = jnp.dot(pw_weight, active, preferred_element_type=jnp.float32).astype(jnp.bfloat16)
    grad_active = upstream_grad(pw_weight, cotangent)
    convolved_gradient = (grad_active.astype(jnp.float32) * gelu_slope(conv_out)).astype(
        jnp.bfloat16
    )
    back_taps = [
        shift_grads(convolved_gradient, -position_stride),
        convolved_gradient,
        shift_grads(convolved_gradient, position_stride),
    ]
    grad_rows = group_conv_back(back_taps, conv_weight).astype(jnp.bfloat16)
    grad_inputs = lax.all_to_all(grad_rows, "ch", split_axis=0, concat_axis=1, tiled=True)
    return (mixed, grad_inputs)


def solution(mesh):
    placed = (P("ch", "ctx"), P(), P(), P(None, ("ctx", "ch")))
    return jax.shard_map(
        body,
        mesh=mesh,
        in_specs=placed,
        out_specs=(P(None, ("ctx", "ch")), P("ch", "ctx")),
        check_vma=False,
    )
```

profile of v0, /device:TPU:24, one launch (start us, length us, event | category | flops | bytes accessed | tf_op | source)
XLA Modules:
  0.0 137.1 jit_solution(3559311727145144728)
XLA Ops:
  0.6 0.0 copy-start
  0.7 1.7 %copy.21 = bf16[48,4,8,512]{3,2,0,1:T(8,128)(2,1)S(1)} copy(bf16[48,4,8,512]{3,2,1,0:T(8,128)(2,1)} %bitcast.67) | data formatting | bytes 3145728 | tf_op jit(solution)/shard_map/all_to_all | solution.py:62
  2.3 22.7 %all_to_all.35 = bf16[384,4,512]{2,0,1:T(8,128)(2,1)S(1)} all-to-all(bf16[384,4,512]{2,0,1:T(8,128)(2,1)S(1)} %bitcast.56), channel_id=1, replica_groups=mesh['ctx'=8,'ch'=4] {'ch'}, dimensions={1} | all-to-all | bytes 3145728 | tf_op jit(solution)/shard_map/all_to_all | solution.py:62
  25.0 1.9 %collective-permute-start = (bf16[1536,512]{1,0:T(8,128)(2,1)S(1)}, bf16[1536,512]{1,0:T(8,128)(2,1)}, u32[]{:S(2)}, u32[]{:S(2)}) collective-permute-start(bf16[1536,512]{1,0:T(8,128)(2,1)S(1)} %bitcast.57), channel_id=1, source_target_pairs={{0,1},{1,2},{2,3},{3,4},{4,5},{5,6},{6,7},{7,8},{8,9},{9,10},{10,1... | collective-permute-start | bytes 4718600 | tf_op jit(solution)/shard_map/ppermute | solution.py:12
  26.9 5.4 %collective-permute-start.1 = (bf16[1536,512]{1,0:T(8,128)(2,1)S(1)}, bf16[1536,512]{1,0:T(8,128)(2,1)}, u32[]{:S(2)}, u32[]{:S(2)}) collective-permute-start(bf16[1536,512]{1,0:T(8,128)(2,1)S(1)} %bitcast.58), channel_id=1, source_target_pairs={{1,0},{2,1},{3,2},{4,3},{5,4},{6,5},{7,6},{8,7},{9,8},{10,9},{11,1... | collective-permute-start | bytes 4718600 | tf_op jit(solution)/shard_map/ppermute | solution.py:12
  32.4 0.9 fusion.11
  33.3 1.9 %copy.6 = bf16[1,1536,96]{2,1,0:T(8,128)(2,1)} copy(bf16[1,1536,96]{1,2,0:T(8,128)(2,1)} %get-tuple-element.7) | data formatting | bytes 589824 | tf_op jit(solution)/shard_map/slice | solution.py:25
  35.1 0.9 copy.8
  36.1 1.2 copy.9
  37.2 0.0 copy-start.1
  37.3 1.6 %fusion.13 = f32[16,96,512]{2,1,0:T(8,128)S(1)} fusion(bf16[16,96,96]{2,1,0:T(8,128)(2,1)} %bitcast.64, bf16[16,96,512]{2,1,0:T(8,128)(2,1)S(1)} %bitcast.59), kind=kOutput, calls=%fused_computation.22 | convolution fusion | flops 150994944 | bytes 5013504 | tf_op jit(solution)/shard_map/gji,gip->gjp/dot_general | solution.py:27
  38.9 9.9 %collective-permute-done = bf16[1536,512]{1,0:T(8,128)(2,1)} collective-permute-done((bf16[1536,512]{1,0:T(8,128)(2,1)S(1)}, bf16[1536,512]{1,0:T(8,128)(2,1)}, u32[]{:S(2)}, u32[]{:S(2)}) %collective-permute-start) | collective-permute-done | bytes 1572896 | tf_op jit(solution)/shard_map/ppermute | solution.py:12
  48.7 2.1 %fusion.12 = f32[16,96,512]{2,1,0:T(8,128)S(1)} fusion(bf16[16,96,96]{2,1,0:T(8,128)(2,1)S(1)} %bitcast.62, bf16[16,96,512]{2,1,0:T(8,128)(2,1)} %bitcast.3), kind=kOutput, calls=%fused_computation.21 | convolution fusion | flops 150994944 | bytes 5013504 | tf_op jit(solution)/shard_map/gji,gip->gjp/dot_general | solution.py:27
  50.9 0.0 collective-permute-done.1
  50.9 0.0 slice-start.1
  50.9 2.0 %add_add_fusion = f32[16,96,512]{2,1,0:T(8,128)S(1)} fusion(f32[16,96,512]{2,1,0:T(8,128)S(1)} %fusion.12, f32[16,96,512]{2,1,0:T(8,128)S(1)} %fusion.13, bf16[16,96,96]{2,1,0:T(8,128)(2,1)S(1)} %bitcast.60, bf16[16,96,512]{2,1,0:T(8,128)(2,1)} %bitcast.8), kind=kOutput, calls=%fused_computation.15 | convolution fusion | flops 152567808 | bytes 11304960 | tf_op jit(solution)/shard_map/gji,gip->gjp/dot_general | solution.py:27
  52.9 2.1 %fusion.3 = (f32[1536,512]{1,0:T(8,128)S(1)}, bf16[1536,512]{1,0:T(8,128)(2,1)}) fusion(f32[16,96,512]{2,1,0:T(8,128)S(1)} %add_add_fusion), kind=kLoop, calls=%fused_computation.5 | loop fusion | flops 7077888 | bytes 7864320 | tf_op jit(solution)/shard_map/tanh | solution.py:70
  55.1 0.0 slice-done
  55.1 0.0 copy-start.2
  55.1 3.8 %fusion.7 = bf16[1536,512]{1,0:T(8,128)(2,1)S(1)} fusion(f32[16,96,512]{2,1,0:T(8,128)S(1)} %add_add_fusion, f32[1536,512]{1,0:T(8,128)S(1)} %get-tuple-element.4, bf16[1536,1536]{1,0:T(8,128)(2,1)S(1)} %bitcast.72, bf16[1536,512]{1,0:T(8,128)(2,1)S(1)} %copy-done), kind=kOutput, calls=%fused_computation.9 | convolution fusion | flops 2429288448 | bytes 14155776 | tf_op jit(solution)/shard_map/dot_general | solution.py:48
  58.9 5.2 %collective-permute-start.2 = (bf16[1536,512]{1,0:T(8,128)(2,1)S(1)}, bf16[1536,512]{1,0:T(8,128)(2,1)S(1)}, u32[]{:S(2)}, u32[]{:S(2)}) collective-permute-start(bf16[1536,512]{1,0:T(8,128)(2,1)S(1)} %fusion.7), channel_id=1, source_target_pairs={{1,0},{2,1},{3,2},{4,3},{5,4},{6,5},{7,6},{8,7},{9,8},{10,9},{11,1... | collective-permute-start | bytes 4718600 | tf_op jit(solution)/shard_map/ppermute | solution.py:12
  64.1 13.0 %collective-permute-start.3 = (bf16[1536,512]{1,0:T(8,128)(2,1)S(1)}, bf16[1536,512]{1,0:T(8,128)(2,1)S(1)}, u32[]{:S(2)}, u32[]{:S(2)}) collective-permute-start(bf16[1536,512]{1,0:T(8,128)(2,1)S(1)} %fusion.7), channel_id=1, source_target_pairs={{0,1},{1,2},{2,3},{3,4},{4,5},{5,6},{6,7},{7,8},{8,9},{9,10},{10,1... | collective-permute-start | bytes 4718600 | tf_op jit(solution)/shard_map/ppermute | solution.py:12
  77.2 0.6 fusion.15
  77.8 4.2 %collective-permute-done.2 = bf16[1536,512]{1,0:T(8,128)(2,1)S(1)} collective-permute-done((bf16[1536,512]{1,0:T(8,128)(2,1)S(1)}, bf16[1536,512]{1,0:T(8,128)(2,1)S(1)}, u32[]{:S(2)}, u32[]{:S(2)}) %collective-permute-start.2) | collective-permute-done | bytes 1572896 | tf_op jit(solution)/shard_map/ppermute | solution.py:12
  82.1 0.6 fusion.14
  82.7 14.5 %collective-permute-done.3 = bf16[1536,512]{1,0:T(8,128)(2,1)S(1)} collective-permute-done((bf16[1536,512]{1,0:T(8,128)(2,1)S(1)}, bf16[1536,512]{1,0:T(8,128)(2,1)S(1)}, u32[]{:S(2)}, u32[]{:S(2)}) %collective-permute-start.3) | collective-permute-done | bytes 1572896 | tf_op jit(solution)/shard_map/ppermute | solution.py:12
  97.2 1.8 %add_convert_fusion = bf16[16,512,96]{1,2,0:T(8,128)(2,1)} fusion(f32[16,512,96]{1,2,0:T(8,128)S(1)} %fusion.14, f32[16,512,96]{1,2,0:T(8,128)S(1)} %fusion.15, bf16[16,96,512]{2,1,0:T(8,128)(2,1)S(1)} %bitcast.66, bf16[16,96,96]{2,1,0:T(8,128)(2,1)S(1)} %bitcast.61), kind=kOutput, calls=%fused_computation.14 | convolution fusion | flops 153354240 | bytes 9732096 | tf_op jit(solution)/shard_map/gji,gjp->gip/dot_general | solution.py:41
  99.0 16.7 %all-to-all-start.1 = ((bf16[4,384,512]{2,1,0:T(8,128)(2,1)}), bf16[4,384,512]{2,1,0:T(8,128)(2,1)S(1)}, u32[]{:S(2)}, u32[]{:S(2)}) async-start(bf16[4,384,512]{2,1,0:T(8,128)(2,1)} %bitcast.55), calls=%async_computation.1 | async-start | bytes 3145728 | tf_op jit(solution)/shard_map/all_to_all | solution.py:82
  115.6 6.6 %fusion.10 = bf16[1536,512]{0,1:T(8,128)(2,1)} fusion(bf16[1536,512]{1,0:T(8,128)(2,1)} %get-tuple-element.5, bf16[1536,1536]{1,0:T(8,128)(2,1)} %param.6), kind=kOutput, calls=%fused_computation.18 | convolution fusion | flops 2416705536 | bytes 7864320 | tf_op jit(solution)/shard_map/dot_general | solution.py:71
  122.2 2.6 %copy.14 = bf16[1536,512]{1,0:T(8,128)(2,1)} copy(bf16[1536,512]{0,1:T(8,128)(2,1)} %fusion.10) | data formatting | bytes 3145728
  124.8 10.9 %all-to-all-done.1 = bf16[4,384,512]{2,1,0:T(8,128)(2,1)S(1)} async-done(((bf16[4,384,512]{2,1,0:T(8,128)(2,1)}), bf16[4,384,512]{2,1,0:T(8,128)(2,1)S(1)}, u32[]{:S(2)}, u32[]{:S(2)}) %all-to-all-start.1) | async-done | bytes 1572896 | tf_op jit(solution)/shard_map/all_to_all | solution.py:82
  135.7 1.4 copy.19
  (8 shorter events, 0.0 us)
Async XLA Ops:
  0.6 54.4 %copy-start = (bf16[1536,512]{1,0:T(8,128)(2,1)S(1)}, bf16[1536,512]{1,0:T(8,128)(2,1)}, u32[]{:S(2)}) copy-start(bf16[1536,512]{1,0:T(8,128)(2,1)} %param.7) | copy-start | bytes 4718596
  0.6 31.7 %copy-start.3 = (bf16[3,1536,96]{1,2,0:T(8,128)(2,1)S(1)}, bf16[3,1536,96]{1,2,0:T(8,128)(2,1)}, u32[]{:S(2)}) copy-start(bf16[3,1536,96]{1,2,0:T(8,128)(2,1)} %param.5) | copy-start | bytes 2654212
  25.0 23.7 %collective-permute-start = (bf16[1536,512]{1,0:T(8,128)(2,1)S(1)}, bf16[1536,512]{1,0:T(8,128)(2,1)}, u32[]{:S(2)}, u32[]{:S(2)}) collective-permute-start(bf16[1536,512]{1,0:T(8,128)(2,1)S(1)} %bitcast.57), channel_id=1, source_target_pairs={{0,1},{1,2},{2,3},{3,4},{4,5},{5,6},{6,7},{7,8},{8,9},{9,10},{10,1... | collective-permute-start | bytes 4718600 | tf_op jit(solution)/shard_map/ppermute | solution.py:12
  26.9 23.9 %collective-permute-start.1 = (bf16[1536,512]{1,0:T(8,128)(2,1)S(1)}, bf16[1536,512]{1,0:T(8,128)(2,1)}, u32[]{:S(2)}, u32[]{:S(2)}) collective-permute-start(bf16[1536,512]{1,0:T(8,128)(2,1)S(1)} %bitcast.58), channel_id=1, source_target_pairs={{1,0},{2,1},{3,2},{4,3},{5,4},{6,5},{7,6},{8,7},{9,8},{10,9},{11,1... | collective-permute-start | bytes 4718600 | tf_op jit(solution)/shard_map/ppermute | solution.py:12
  37.2 11.5 %copy-start.1 = (bf16[1,1536,96]{2,1,0:T(8,128)(2,1)S(1)}, bf16[1,1536,96]{2,1,0:T(8,128)(2,1)}, u32[]{:S(2)}) copy-start(bf16[1,1536,96]{2,1,0:T(8,128)(2,1)} %copy.6) | copy-start | bytes 884740
  48.7 6.3 %slice-start = ((s8[4718592]{0:T(1024)(128)(4,1)}), s8[4194304]{0:T(1024)(128)(4,1)S(1)}, s32[]{:S(2)}) async-start(s8[4718592]{0:T(1024)(128)(4,1)} %bitcast.71), calls=%async_computation.2 | async-start | bytes 8388608
  50.9 4.2 %slice-start.1 = ((s8[4718592]{0:T(1024)(128)(4,1)}), s8[524288]{0:T(1024)(128)(4,1)S(1)}, s32[]{:S(2)}) async-start(s8[4718592]{0:T(1024)(128)(4,1)} %bitcast.71), calls=%async_computation.3 | async-start | bytes 1048576
  55.1 22.1 %copy-start.2 = (bf16[1,1536,96]{2,1,0:T(8,128)(2,1)S(1)}, bf16[1,1536,96]{2,1,0:T(8,128)(2,1)}, u32[]{:S(2)}) copy-start(bf16[1,1536,96]{2,1,0:T(8,128)(2,1)} %copy.8) | copy-start | bytes 884740
  58.9 23.1 %collective-permute-start.2 = (bf16[1536,512]{1,0:T(8,128)(2,1)S(1)}, bf16[1536,512]{1,0:T(8,128)(2,1)S(1)}, u32[]{:S(2)}, u32[]{:S(2)}) collective-permute-start(bf16[1536,512]{1,0:T(8,128)(2,1)S(1)} %fusion.7), channel_id=1, source_target_pairs={{1,0},{2,1},{3,2},{4,3},{5,4},{6,5},{7,6},{8,7},{9,8},{10,9},{11,1... | collective-permute-start | bytes 4718600 | tf_op jit(solution)/shard_map/ppermute | solution.py:12
  64.1 33.0 %collective-permute-start.3 = (bf16[1536,512]{1,0:T(8,128)(2,1)S(1)}, bf16[1536,512]{1,0:T(8,128)(2,1)S(1)}, u32[]{:S(2)}, u32[]{:S(2)}) collective-permute-start(bf16[1536,512]{1,0:T(8,128)(2,1)S(1)} %fusion.7), channel_id=1, source_target_pairs={{0,1},{1,2},{2,3},{3,4},{4,5},{5,6},{6,7},{7,8},{8,9},{9,10},{10,1... | collective-permute-start | bytes 4718600 | tf_op jit(solution)/shard_map/ppermute | solution.py:12
  99.0 36.7 %all-to-all-start.1 = ((bf16[4,384,512]{2,1,0:T(8,128)(2,1)}), bf16[4,384,512]{2,1,0:T(8,128)(2,1)S(1)}, u32[]{:S(2)}, u32[]{:S(2)}) async-start(bf16[4,384,512]{2,1,0:T(8,128)(2,1)} %bitcast.55), calls=%async_computation.1 | async-start | bytes 3145728 | tf_op jit(solution)/shard_map/all_to_all | solution.py:82
where the time goes:
time: 138 us; the launch traced here: 137 us
  starting transfers between devices  42.3 us (31%)
  waiting for transfers between devices  39.5 us (29%)
  blocking collectives  22.7 us (16%)
  matrix products  19.2 us (14%)
  local copies, waits for them, and re-layouts  10.5 us (8%)
  other arithmetic  2.13 us (2%)
    ppermute x4, waiting for transfers between devices, shifted(): return lax.ppermute(block, axis, route)  28.6 us
    ppermute x4, starting transfers between devices, shifted(): return lax.ppermute(block, axis, route)  25.6 us
    all_to_all x1, blocking collectives, body(): lax.all_to_all(inputs, 'ch', split_axis=1, concat_axis=0, tiled=True)  22.7 us
    all_to_all x1, starting transfers between devices, body(): lax.all_to_all(grad_rows, 'ch', split_axis=0, concat_axis=1, tiled=True)  16.7 us
    all_to_all x1, waiting for transfers between devices, body(): lax.all_to_all(grad_rows, 'ch', split_axis=0, concat_axis=1, tiled=True)  10.9 us
    dot_general x1, matrix products, body(): jnp.dot(pw_weight, active, preferred_element_type=jnp.float32)  6.61 us
    dot_general x3, matrix products, group_conv(): jnp.einsum('gji,gip->gjp', kernel, signal, preferred_element_type=jnp.flo...  5.76 us
    slice x4, local copies, waits for them, and re-layouts, group_conv(): kernel = weight_part[position_offset].reshape(groups, width, width)  4.85 us
  transfers between devices with their start and end apart: 5, of which 4 were waited for; matrix products, arithmetic and copies ran while one was open for 14% of the time, Pallas kernels for 0%

commit v1 on v0

v1 whole, which is shorter than its diff:
```python
import functools

import jax
import jax.numpy as jnp
from jax import lax
from jax.experimental import pallas as pl
from jax.experimental.pallas import tpu as pltpu
from jax.sharding import PartitionSpec as P

DILATION_STEP = 512
VMEM = pltpu.VMEM
MIB = 1 << 20


def params(mib):
    return pltpu.CompilerParams(vmem_limit_bytes=mib * MIB)


def gelu_and_slope(v):
    square = v * v
    inner = v * (0.7978845608 + (0.7978845608 * 0.044715) * square)
    th = jnp.tanh(inner)
    half = 0.5 + 0.5 * th
    active = v * half
    inner_slope = 0.7978845608 + (3.0 * 0.7978845608 * 0.044715) * square
    slope = half + (0.5 * v) * (1.0 - th * th) * inner_slope
    return active, slope


def full(shape):
    return pl.BlockSpec(memory_space=VMEM)


def upstream_kernel(order, ch_ref, pw_ref, cot_ref, *piece_refs):
    step = pl.program_id(0)
    result = lax.dot_general(
        pw_ref[...], cot_ref[...], (((0,), (0,)), ((), ())), preferred_element_type=jnp.float32
    ).astype(jnp.bfloat16)
    for place in range(len(order)):
        @pl.when(step == place)
        def _(place=place):
            piece_refs[place][...] = result


def upstream(ch, pw_weight, cotangent, chunk, width, channels, order):
    total = pw_weight.shape[0]
    if channels % 128 != 0 or width % 128 != 0:
        whole = lax.dot_general(
            pw_weight, cotangent[:, chunk * width:(chunk + 1) * width], (((0,), (0,)), ((), ())),
            preferred_element_type=jnp.float32,
        ).astype(jnp.bfloat16)
        return [lax.dynamic_slice_in_dim(whole, (ch[0] ^ k) * channels, channels, 0) for k in order]

    def pw_index(step, ch_ref):
        k = order[0]
        for place in range(1, len(order)):
            k = jnp.where(step == place, order[place], k)
        return 0, ch_ref[0] ^ k

    return pl.pallas_call(
        functools.partial(upstream_kernel, order),
        grid_spec=pltpu.PrefetchScalarGridSpec(
            num_scalar_prefetch=1,
            grid=(len(order),),
            in_specs=[
                pl.BlockSpec((total, channels), pw_index),
                pl.BlockSpec((total, width), lambda step, ch_ref: (0, chunk)),
            ],
            out_specs=[pl.BlockSpec((channels, width), lambda step, ch_ref: (0, 0))] * len(order),
        ),
        out_shape=[jax.ShapeDtypeStruct((channels, width), jnp.bfloat16)] * len(order),
        compiler_params=params(24),
        name="upstream",
    )(ch, pw_weight, cotangent)


def forward_kernel(chunk, n, halo, group, ch_ref, x_ref, left_ref, right_ref, w_ref, *rest):
    active_refs, slope_ref, wide = rest[:n], rest[n], rest[n + 1]
    channels, width = active_refs[0].shape
    block = x_ref.shape[1] // n
    wide[:, :halo * width] = left_ref[...]
    for b in range(n):
        start = b * block + chunk * width
        wide[:, (halo + b) * width:(halo + b + 1) * width] = x_ref[:, start:start + width]
    wide[:, (halo + n) * width:] = right_ref[...]
    for k in range(n):
        b = ch_ref[0] ^ k
        for g in range(channels // group):
            rows = slice(g * group, (g + 1) * group)
            taps = [
                wide[rows, pl.ds(pl.multiple_of((b + t * halo) * width, width), width)]
                for t in range(3)
            ]
            conv_out = jnp.dot(
                w_ref[rows, :], jnp.concatenate(taps, axis=0), preferred_element_type=jnp.float32
            )
            active, slope = gelu_and_slope(conv_out)
            active_refs[k][rows, :] = active.astype(jnp.bfloat16)
            slope_ref[k, rows, :] = slope


def forward(ch, inputs, left, right, weight, chunk, n, halo, width, group):
    channels = inputs.shape[0]
    outs = pl.pallas_call(
        functools.partial(forward_kernel, chunk, n, halo, group),
        in_specs=[pl.BlockSpec(memory_space=pltpu.SMEM)] + [pl.BlockSpec(memory_space=VMEM)] * 4,
        out_specs=[pl.BlockSpec(memory_space=VMEM)] * (n + 1),
        out_shape=[jax.ShapeDtypeStruct((channels, width), jnp.bfloat16)] * n
        + [jax.ShapeDtypeStruct((n, channels, width), jnp.float32)],
        scratch_shapes=[VMEM((channels, (n + 2 * halo) * width), jnp.bfloat16)],
        compiler_params=params(24),
        name="forward",
    )(ch, inputs, left, right, weight)
    return outs[:n], outs[n]


def slope_kernel(n, halo, ch_ref, slope_ref, *rest):
    piece_refs, (grad_ref, first_ref, last_ref) = rest[:n], rest[n:]
    width = piece_refs[0].shape[1]
    for k in range(n):
        b = ch_ref[0] ^ k
        product = (piece_refs[k][...].astype(jnp.float32) * slope_ref[k]).astype(jnp.bfloat16)
        grad_ref[:, pl.ds(pl.multiple_of(b * width, width), width)] = product
    first_ref[...] = grad_ref[:, :halo * width]
    last_ref[...] = grad_ref[:, (n - halo) * width:]


def grad_conv(ch, slope, pieces, halo):
    n, (channels, width) = len(pieces), pieces[0].shape
    shapes = [(channels, n * width), (channels, halo * width), (channels, halo * width)]
    return pl.pallas_call(
        functools.partial(slope_kernel, n, halo),
        in_specs=[pl.BlockSpec(memory_space=pltpu.SMEM)] + [pl.BlockSpec(memory_space=VMEM)] * (n + 1),
        out_specs=[pl.BlockSpec(memory_space=VMEM)] * 3,
        out_shape=[jax.ShapeDtypeStruct(s, jnp.bfloat16) for s in shapes],
        compiler_params=params(24),
        name="grad_conv",
    )(ch, slope, *pieces)


def back_kernel(n, halo, group, grad_ref, left_ref, right_ref, w_ref, *rest):
    out_ref, wide = rest[-2:]
    channels, width = out_ref.shape
    step = pl.program_id(0)

    @pl.when(step == 0)
    def _():
        wide[:, :halo * width] = left_ref[...]
        wide[:, halo * width:(halo + n) * width] = grad_ref[...]
        wide[:, (halo + n) * width:] = right_ref[...]

    for g in range(channels // group):
        rows = slice(g * group, (g + 1) * group)
        taps = [
            wide[rows, pl.ds(pl.multiple_of((step + t * halo) * width, width), width)]
            for t in range(3)
        ]
        out_ref[rows, :] = jnp.dot(
            w_ref[rows, :], jnp.concatenate(taps, axis=0), preferred_element_type=jnp.float32
        ).astype(jnp.bfloat16)


def backward(grad, left, right, weight, before, chunk, chunks, n, halo, group):
    channels, length = grad.shape
    width = length // n
    operands = [grad, left, right, weight]
    specs = [pl.BlockSpec(o.shape, lambda b: (0, 0)) for o in operands]
    aliases = {}
    if before is not None:
        operands.append(before)
        specs.append(pl.BlockSpec(memory_space=pl.ANY))
        aliases = {4: 0}
    return pl.pallas_call(
        functools.partial(back_kernel, n, halo, group),
        grid=(n,),
        in_specs=specs,
        out_specs=pl.BlockSpec((channels, width), lambda b: (0, b * chunks + chunk)),
        out_shape=jax.ShapeDtypeStruct((channels, length * chunks), jnp.bfloat16),
        scratch_shapes=[VMEM((channels, (n + 2 * halo) * width), jnp.bfloat16)],
        input_output_aliases=aliases,
        compiler_params=params(24),
        name="backward",
    )(*operands)


def mix_kernel(n, ch_ref, pw_ref, *rest):
    piece_refs, (out_ref, gathered) = rest[:n], rest[-2:]
    channels = piece_refs[0].shape[0]

    @pl.when(pl.program_id(0) == 0)
    def _():
        for k in range(n):
            b = ch_ref[0] ^ k
            gathered[pl.ds(pl.multiple_of(b * channels, channels), channels), :] = piece_refs[k][...]

    out_ref[...] = jnp.dot(
        pw_ref[...], gathered[...], preferred_element_type=jnp.float32
    ).astype(jnp.bfloat16)


def mix(ch, pw_weight, pieces, before, chunk, chunks):
    n, (channels, width) = len(pieces), pieces[0].shape
    total = pw_weight.shape[0]
    rows = 256
    operands = [ch, pw_weight, *pieces]
    specs = [pl.BlockSpec(memory_space=pltpu.SMEM), pl.BlockSpec((rows, total), lambda m: (m, 0))]
    specs += [pl.BlockSpec(p.shape, lambda m: (0, 0)) for p in pieces]
    aliases = {}
    if before is not None:
        operands.append(before)
        specs.append(pl.BlockSpec(memory_space=pl.ANY))
        aliases = {n + 2: 0}
    return pl.pallas_call(
        functools.partial(mix_kernel, n),
        grid=(total // rows,),
        in_specs=specs,
        out_specs=pl.BlockSpec((rows, width), lambda m: (m, chunk)),
        out_shape=jax.ShapeDtypeStruct((total, width * chunks), jnp.bfloat16),
        scratch_shapes=[VMEM((total, width), jnp.bfloat16)],
        input_output_aliases=aliases,
        compiler_params=params(24),
        name="mix",
    )(*operands)


def exchange(piece, k, n):
    return piece if k == 0 else lax.ppermute(piece, "ch", [(i, i ^ k) for i in range(n)])


def along(values, step):
    size = lax.axis_size("ctx")
    return lax.ppermute(
        values, "ctx", [(i, i + step) for i in range(size) if 0 <= i + step < size]
    )


def body(inputs, conv_weight, pw_weight, cotangent):
    n = lax.axis_size("ch")
    ch = lax.axis_index("ch").astype(jnp.int32)[None]
    channels, length = inputs.shape
    group = conv_weight.shape[2]
    block = cotangent.shape[1]
    halo = DILATION_STEP // block
    chunks = 2 if block % 256 == 0 else 1
    width = block // chunks

    own = lax.dynamic_slice_in_dim(conv_weight, ch[0] * channels, channels, 1)
    weight = jnp.moveaxis(own, 0, 1).reshape(channels, 3 * group)
    turned = own[::-1].reshape(3, channels // group, group, group).transpose(1, 3, 0, 2)
    turned = turned.reshape(channels, 3 * group)

    def edge(first, chunk):
        parts = [
            inputs[:, (first + i) * block + chunk * width:(first + i) * block + (chunk + 1) * width]
            for i in range(halo)
        ]
        return parts[0] if halo == 1 else jnp.concatenate(parts, axis=1)

    halos = [
        (along(edge(n - halo, c), 1), along(edge(0, c), -1)) for c in range(chunks)
    ]
    order = [k for k in range(n - 1, -1, -1)]
    upstreams = []
    for c in range(chunks):
        pieces = dict(zip(order, upstream(ch, pw_weight, cotangent, c, width, channels, order)))
        upstreams.append([exchange(pieces[k], k, n) for k in range(n)])
    mixed = grad_inputs = None
    forwards, grads = [], []
    for c in range(chunks):
        active, slope = forward(ch, inputs, *halos[c], weight, c, n, halo, width, group)
        grad, first, last = grad_conv(ch, slope, upstreams[c], halo)
        grads.append((grad, along(last, 1), along(first, -1)))
        forwards.append([exchange(active[k], k, n) for k in range(n)])
    for c in range(chunks):
        mixed = mix(ch, pw_weight, forwards[c], mixed, c, chunks)
        grad_inputs = backward(*grads[c], turned, grad_inputs, c, chunks, n, halo, group)
    return mixed, grad_inputs


def solution(mesh):
    placed = (P("ch", "ctx"), P(), P(), P(None, ("ctx", "ch")))
    return jax.shard_map(
        body,
        mesh=mesh,
        in_specs=placed,
        out_specs=(P(None, ("ctx", "ch")), P("ch", "ctx")),
        check_vma=False,
    )
```

time: 138 us -> 92.6 us (0.67)
  the two profiles are of different devices: /device:TPU:24 before, /device:TPU:0 now
where the time goes in v1:
time: 92.6 us; the launch traced here: 91.5 us
  starting transfers between devices  32.8 us (35%)
  local copies, waits for them, and re-layouts  27.4 us (30%)
  Pallas kernels  25.9 us (28%)
  waiting for transfers between devices  4.54 us (5%)
    ppermute x8, starting transfers between devices, along(): lax.ppermute(values, 'ctx', [(i, i + step) for i in range(size) if 0 <= i...  24.4 us
    unnamed x56, local copies, waits for them, and re-layouts  17.9 us
    ppermute x12, starting transfers between devices, exchange(): lax.ppermute(piece, 'ch', [(i, i ^ k) for i in range(n)])  8.42 us
    pallas_call x2, Pallas kernels, mix(): pl.pallas_call(functools.partial(mix_kernel, n), grid=(total // rows,), i...  8.21 us
    pallas_call x2, Pallas kernels, upstream(): pl.pallas_call(functools.partial(upstream_kernel, order), grid_spec=pltpu...  6.5 us
    pallas_call x2, Pallas kernels, forward(): pl.pallas_call(functools.partial(forward_kernel, chunk, n, halo, group),...  4.82 us
    pallas_call x2, Pallas kernels, backward(): pl.pallas_call(functools.partial(back_kernel, n, halo, group), grid=(n,),...  4.64 us
    ppermute x8, waiting for transfers between devices, along(): lax.ppermute(values, 'ctx', [(i, i + step) for i in range(size) if 0 <= i...  4.51 us
  transfers between devices with their start and end apart: 20, of which 1 were waited for; matrix products, arithmetic and copies ran while one was open for 10% of the time, Pallas kernels for 20%

profile of v1, /device:TPU:0, one launch (start us, length us, event | category | flops | bytes accessed | tf_op | source)
XLA Modules:
  0.0 91.5 jit_solution(17312188805118165174)
XLA Ops:
  0.7 2.4 %copy-done.1 = bf16[1536,1536]{1,0:T(8,128)(2,1)S(1)} copy-done((bf16[1536,1536]{1,0:T(8,128)(2,1)S(1)}, bf16[1536,1536]{1,0:T(8,128)(2,1)}, u32[]{:S(2)}) %copy-start.1) | copy-done | bytes 4718616
  3.1 1.4 %copy-done.4 = bf16[1536,512]{1,0:T(8,128)(2,1)S(1)} copy-done((bf16[1536,512]{1,0:T(8,128)(2,1)S(1)}, bf16[1536,512]{1,0:T(8,128)(2,1)}, u32[]{:S(2)}) %copy-start.4) | copy-done | bytes 1572888
  4.5 2.8 %upstream.2 = (bf16[384,256]{1,0:T(8,128)(2,1)S(1)}, bf16[384,256]{1,0:T(8,128)(2,1)S(1)}, bf16[384,256]{1,0:T(8,128)(2,1)S(1)}, bf16[384,256]{1,0:T(8,128)(2,1)S(1)}) custom-call(s32[1]{0:T(128)} %bitcast.ch_ref, bf16[1536,1536]{1,0:T(8,128)(2,1)S(1)} %copy-done.1, bf16[1536,512]{1,0:T(8,128)(2,1)S(1)} %copy-done.4), custom_call_target="tpu_custom_call" | custom-call | tf_op jit(solution)/shard_map/upstream/pallas_call | solution.py:60
  7.8 2.6 %collective-permute-start.11 = (bf16[384,256]{1,0:T(8,128)(2,1)S(1)}, bf16[384,256]{1,0:T(8,128)(2,1)S(1)}, u32[]{:S(2)}, u32[]{:S(2)}) collective-permute-start(bf16[384,256]{1,0:T(8,128)(2,1)S(1)} %get-tuple-element.37), channel_id=1, source_target_pairs={{0,2},{1,3},{2,0},{3,1},{4,6},{5,7},{6,4},{7,5},{8,10},{9,11},{10,... | collective-permute-start | bytes 589832 | tf_op jit(solution)/shard_map/ppermute | solution.py:227
  11.3 1.3 %collective-permute-start.1 = (bf16[384,256]{1,0:T(8,128)(2,1)S(1)}, bf16[384,256]{1,0:T(8,128)(2,1)S(1)}, u32[]{:S(2)}, u32[]{:S(2)}) collective-permute-start(bf16[384,256]{1,0:T(8,128)(2,1)S(1)} %get-tuple-element.52), channel_id=1, source_target_pairs={{4,0},{8,4},{12,8},{16,12},{20,16},{24,20},{28,24},{5,1},{9,5},{13... | collective-permute-start | bytes 589832 | tf_op jit(solution)/shard_map/ppermute | solution.py:232
  12.6 4.6 %collective-permute-start = (bf16[384,256]{1,0:T(8,128)(2,1)S(1)}, bf16[384,256]{1,0:T(8,128)(2,1)S(1)}, u32[]{:S(2)}, u32[]{:S(2)}) collective-permute-start(bf16[384,256]{1,0:T(8,128)(2,1)S(1)} %get-tuple-element.53), channel_id=1, source_target_pairs={{0,4},{4,8},{8,12},{12,16},{16,20},{20,24},{24,28},{1,5},{5,9},{9,... | collective-permute-start | bytes 589832 | tf_op jit(solution)/shard_map/ppermute | solution.py:232
  17.1 3.7 %upstream.3 = (bf16[384,256]{1,0:T(8,128)(2,1)}, bf16[384,256]{1,0:T(8,128)(2,1)}, bf16[384,256]{1,0:T(8,128)(2,1)}, bf16[384,256]{1,0:T(8,128)(2,1)S(1)}) custom-call(s32[1]{0:T(128)} %bitcast.ch_ref, bf16[1536,1536]{1,0:T(8,128)(2,1)S(1)} %copy-done.1, bf16[1536,512]{1,0:T(8,128)(2,1)S(1)} %copy-done.4), custom_call_target="tpu_custom_call" | custom-call | tf_op jit(solution)/shard_map/upstream/pallas_call | solution.py:60
  22.2 1.3 %collective-permute-start.6 = (bf16[384,256]{1,0:T(8,128)(2,1)}, bf16[384,256]{1,0:T(8,128)(2,1)}, u32[]{:S(2)}, u32[]{:S(2)}) collective-permute-start(bf16[384,256]{1,0:T(8,128)(2,1)} %get-tuple-element.50), channel_id=1, source_target_pairs={{4,0},{8,4},{12,8},{16,12},{20,16},{24,20},{28,24},{5,1},{9,5},{13... | collective-permute-start | bytes 589832 | tf_op jit(solution)/shard_map/ppermute | solution.py:232
  24.2 5.8 %collective-permute-start.5 = (bf16[384,256]{1,0:T(8,128)(2,1)}, bf16[384,256]{1,0:T(8,128)(2,1)}, u32[]{:S(2)}, u32[]{:S(2)}) collective-permute-start(bf16[384,256]{1,0:T(8,128)(2,1)} %get-tuple-element.51), channel_id=1, source_target_pairs={{0,4},{4,8},{8,12},{12,16},{16,20},{20,24},{24,28},{1,5},{5,9},{9,... | collective-permute-start | bytes 589832 | tf_op jit(solution)/shard_map/ppermute | solution.py:232
  30.6 1.5 %collective-permute-start.16 = (bf16[384,256]{1,0:T(8,128)(2,1)}, bf16[384,256]{1,0:T(8,128)(2,1)}, u32[]{:S(2)}, u32[]{:S(2)}) collective-permute-start(bf16[384,256]{1,0:T(8,128)(2,1)} %get-tuple-element.45), channel_id=1, source_target_pairs={{0,2},{1,3},{2,0},{3,1},{4,6},{5,7},{6,4},{7,5},{8,10},{9,11},{10,... | collective-permute-start | bytes 589832 | tf_op jit(solution)/shard_map/ppermute | solution.py:227
  33.4 1.9 %forward.2 = (bf16[384,256]{1,0:T(8,128)(2,1)S(1)}, bf16[384,256]{1,0:T(8,128)(2,1)}, bf16[384,256]{1,0:T(8,128)(2,1)}, bf16[384,256]{1,0:T(8,128)(2,1)}, f32[4,384,256]{2,1,0:T(8,128)S(1)}) custom-call(s32[1]{0:T(128)} %bitcast.ch_ref, bf16[384,2048]{1,0:T(8,128)(2,1)S(1)} %copy-done.3, bf16[384,256]{1,0:T(8,128)(2,1)S(1)} %collective-permute-done.left_ref, ...), custom_call_target="tpu_custom_call" | custom-call | tf_op jit(solution)/shard_map/forward/pallas_call | solution.py:104
  36.9 0.9 %copy-done.16 = bf16[384,256]{1,0:T(8,128)(2,1)S(1)} copy-done((bf16[384,256]{1,0:T(8,128)(2,1)S(1)}, bf16[384,256]{1,0:T(8,128)(2,1)}, u32[]{:S(2)}) %copy-start.16) | copy-done | bytes 196632
  40.0 4.3 %collective-permute-start.13 = (bf16[384,256]{1,0:T(8,128)(2,1)S(1)}, bf16[384,256]{1,0:T(8,128)(2,1)S(1)}, u32[]{:S(2)}, u32[]{:S(2)}) collective-permute-start(bf16[384,256]{1,0:T(8,128)(2,1)S(1)} %get-tuple-element.40), channel_id=1, source_target_pairs={{0,4},{4,8},{8,12},{12,16},{16,20},{20,24},{24,28},{1,5},{5,9},{9,... | collective-permute-start | bytes 589832 | tf_op jit(solution)/shard_map/ppermute | solution.py:232
  44.3 1.3 %collective-permute-start.14 = (bf16[384,256]{1,0:T(8,128)(2,1)S(1)}, bf16[384,256]{1,0:T(8,128)(2,1)S(1)}, u32[]{:S(2)}, u32[]{:S(2)}) collective-permute-start(bf16[384,256]{1,0:T(8,128)(2,1)S(1)} %get-tuple-element.41), channel_id=1, source_target_pairs={{4,0},{8,4},{12,8},{16,12},{20,16},{24,20},{28,24},{5,1},{9,5},{13... | collective-permute-start | bytes 589832 | tf_op jit(solution)/shard_map/ppermute | solution.py:232
  45.6 2.9 %forward.3 = (bf16[384,256]{1,0:T(8,128)(2,1)S(1)}, bf16[384,256]{1,0:T(8,128)(2,1)S(1)}, bf16[384,256]{1,0:T(8,128)(2,1)}, bf16[384,256]{1,0:T(8,128)(2,1)}, f32[4,384,256]{2,1,0:T(8,128)S(1)}) custom-call(s32[1]{0:T(128)} %bitcast.ch_ref, bf16[384,2048]{1,0:T(8,128)(2,1)S(1)} %copy-done.3, bf16[384,256]{1,0:T(8,128)(2,1)} %collective-permute-done.5.left_ref, ...), custom_call_target="tpu_custom_call" | custom-call | tf_op jit(solution)/shard_map/forward/pallas_call | solution.py:104
  49.3 1.4 %grad_conv.3 = (bf16[384,1024]{1,0:T(8,128)(2,1)S(1)}, bf16[384,256]{1,0:T(8,128)(2,1)S(1)}, bf16[384,256]{1,0:T(8,128)(2,1)S(1)}) custom-call(s32[1]{0:T(128)} %bitcast.ch_ref, f32[4,384,256]{2,1,0:T(8,128)S(1)} %get-tuple-element.42.slope_ref, bf16[384,256]{1,0:T(8,128)(2,1)S(1)} %copy-done.12, bf16[384,256]{1,0:T(8,128)(2,1)} %collective-permute-done.15.rest_1_, ...), custom_call_target="tpu_custom_call" | custom-call | tf_op jit(solution)/shard_map/grad_conv/pallas_call | solution.py:131
  50.7 4.6 %collective-permute-start.18 = (bf16[384,256]{1,0:T(8,128)(2,1)S(1)}, bf16[384,256]{1,0:T(8,128)(2,1)S(1)}, u32[]{:S(2)}, u32[]{:S(2)}) collective-permute-start(bf16[384,256]{1,0:T(8,128)(2,1)S(1)} %get-tuple-element.48), channel_id=1, source_target_pairs={{0,4},{4,8},{8,12},{12,16},{16,20},{20,24},{24,28},{1,5},{5,9},{9,... | collective-permute-start | bytes 589832 | tf_op jit(solution)/shard_map/ppermute | solution.py:232
  55.3 1.3 %collective-permute-start.19 = (bf16[384,256]{1,0:T(8,128)(2,1)S(1)}, bf16[384,256]{1,0:T(8,128)(2,1)S(1)}, u32[]{:S(2)}, u32[]{:S(2)}) collective-permute-start(bf16[384,256]{1,0:T(8,128)(2,1)S(1)} %get-tuple-element.49), channel_id=1, source_target_pairs={{4,0},{8,4},{12,8},{16,12},{20,16},{24,20},{28,24},{5,1},{9,5},{13... | collective-permute-start | bytes 589832 | tf_op jit(solution)/shard_map/ppermute | solution.py:232
  58.2 1.5 %collective-permute-start.8 = (bf16[384,256]{1,0:T(8,128)(2,1)}, bf16[384,256]{1,0:T(8,128)(2,1)S(1)}, u32[]{:S(2)}, u32[]{:S(2)}) collective-permute-start(bf16[384,256]{1,0:T(8,128)(2,1)} %get-tuple-element.32), channel_id=1, source_target_pairs={{0,2},{1,3},{2,0},{3,1},{4,6},{5,7},{6,4},{7,5},{8,10},{9,11},{10,... | collective-permute-start | bytes 589832 | tf_op jit(solution)/shard_map/ppermute | solution.py:227
  59.8 4.5 %collective-permute-done.18.left_ref = bf16[384,256]{1,0:T(8,128)(2,1)S(1)} collective-permute-done((bf16[384,256]{1,0:T(8,128)(2,1)S(1)}, bf16[384,256]{1,0:T(8,128)(2,1)S(1)}, u32[]{:S(2)}, u32[]{:S(2)}) %collective-permute-start.18) | collective-permute-done | bytes 196640 | tf_op jit(solution)/shard_map/ppermute | solution.py:232
  64.3 1.5 %collective-permute-start.3 = (bf16[384,256]{1,0:T(8,128)(2,1)}, bf16[384,256]{1,0:T(8,128)(2,1)}, u32[]{:S(2)}, u32[]{:S(2)}) collective-permute-start(bf16[384,256]{1,0:T(8,128)(2,1)} %get-tuple-element.28), channel_id=1, source_target_pairs={{0,2},{1,3},{2,0},{3,1},{4,6},{5,7},{6,4},{7,5},{8,10},{9,11},{10,... | collective-permute-start | bytes 589832 | tf_op jit(solution)/shard_map/ppermute | solution.py:227
  65.8 1.7 %rev.3 = bf16[3,384,96]{1,2,0:T(8,128)(2,1)} reverse(bf16[3,384,96]{1,2,0:T(8,128)(2,1)} %copy-done.27), dimensions={0} | reverse | bytes 442368 | tf_op jit(solution)/shard_map/rev | solution.py:249
  67.5 1.8 %reshape.14 = bf16[3,4,96,96]{2,1,3,0:T(4,128)(2,1)} reshape(bf16[3,384,96]{1,2,0:T(8,128)(2,1)} %rev.3) | data formatting | bytes 442368 | tf_op jit(solution)/shard_map/reshape | solution.py:249
  69.4 1.9 %copy.12 = bf16[3,4,96,96]{3,1,2,0:T(4,128)(2,1)} copy(bf16[3,4,96,96]{2,1,3,0:T(4,128)(2,1)} %reshape.14) | data formatting | bytes 442368 | tf_op jit(solution)/shard_map/reshape | solution.py:249
  71.3 1.9 %reshape.15 = bf16[384,288]{0,1:T(8,128)(2,1)} reshape(bf16[4,96,3,96]{1,0,3,2:T(4,128)(2,1)} %bitcast.10) | data formatting | bytes 442368 | tf_op jit(solution)/shard_map/reshape | solution.py:250
  73.2 1.1 %copy.14.w_ref = bf16[384,288]{1,0:T(8,128)(2,1)S(1)} copy(bf16[384,288]{0,1:T(8,128)(2,1)} %reshape.15) | data formatting | bytes 442368 | tf_op jit(solution)/shard_map/reshape | solution.py:250
  74.4 1.0 %copy-done.22 = bf16[384,256]{1,0:T(8,128)(2,1)S(1)} copy-done((bf16[384,256]{1,0:T(8,128)(2,1)S(1)}, bf16[384,256]{1,0:T(8,128)(2,1)}, u32[]{:S(2)}) %copy-start.22) | copy-done | bytes 196632
  76.3 2.3 %backward.2.rest_0_ = bf16[384,2048]{1,0:T(8,128)(2,1)} custom-call(bf16[384,1024]{1,0:T(8,128)(2,1)S(1)} %get-tuple-element.47.grad_ref, bf16[384,256]{1,0:T(8,128)(2,1)S(1)} %copy-done.22, bf16[384,256]{1,0:T(8,128)(2,1)S(1)} %copy-done.24, bf16[384,288]{1,0:T(8,128)(2,1)S(1)} %copy.14.w_ref), custom_call_target="tpu_custom_call" | custom-call | tf_op jit(solution)/shard_map/backward/pallas_call | solution.py:173
  78.6 2.3 %backward.3 = bf16[384,2048]{1,0:T(8,128)(2,1)} custom-call(bf16[384,1024]{1,0:T(8,128)(2,1)S(1)} %get-tuple-element.39.grad_ref, bf16[384,256]{1,0:T(8,128)(2,1)S(1)} %copy-done.8, bf16[384,256]{1,0:T(8,128)(2,1)S(1)} %copy-done.10, bf16[384,288]{1,0:T(8,128)(2,1)S(1)} %copy.14.w_ref, bf16[384,2048]{1,0:T(8,128)(2,1)} %backward.2.rest_0_), custom_call_target="tpu_custom_call", output_to_operand_aliasing={{}: (4, {})} | custom-call | tf_op jit(solution)/shard_map/backward/pallas_call | solution.py:173
  81.0 2.3 %copy-done.2 = bf16[1536,1536]{1,0:T(8,128)(2,1)S(1)} copy-done((bf16[1536,1536]{1,0:T(8,128)(2,1)S(1)}, bf16[1536,1536]{1,0:T(8,128)(2,1)}, u32[]{:S(2)}) %copy-start.2) | copy-done | bytes 4718616
  83.3 3.5 %mix.2.rest_4_ = bf16[1536,512]{1,0:T(8,128)(2,1)} custom-call(s32[1]{0:T(128)} %bitcast.ch_ref, bf16[1536,1536]{1,0:T(8,128)(2,1)S(1)} %copy-done.2, bf16[384,256]{1,0:T(8,128)(2,1)S(1)} %copy-done.6, bf16[384,256]{1,0:T(8,128)(2,1)S(1)} %collective-permute-done.7.rest_1_, bf16[384,256]{1,0:T(8,128)(2,1)S(1)} %collective-permute-done.8.rest_2_, ...), custom_call_target="tpu_custom_call" | custom-call | tf_op jit(solution)/shard_map/mix/pallas_call | solution.py:213
  86.8 4.7 %mix.3 = bf16[1536,512]{1,0:T(8,128)(2,1)} custom-call(s32[1]{0:T(128)} %bitcast.ch_ref, bf16[1536,1536]{1,0:T(8,128)(2,1)S(1)} %copy-done.2, bf16[384,256]{1,0:T(8,128)(2,1)S(1)} %copy-done.26, bf16[384,256]{1,0:T(8,128)(2,1)} %collective-permute-done.2.rest_1_, bf16[384,256]{1,0:T(8,128)(2,1)} %collective-permute-done.3.rest_2_, ...), custom_call_target="tpu_custom_call", output_to_operand_aliasing={{}: (6, {})} | custom-call | tf_op jit(solution)/shard_map/mix/pallas_call | solution.py:213
  (82 shorter events, 12.5 us)
Async XLA Ops:
  0.6 31.9 %copy-start = (bf16[3,1536,96]{1,2,0:T(8,128)(2,1)S(1)}, bf16[3,1536,96]{1,2,0:T(8,128)(2,1)}, u32[]{:S(2)}) copy-start(bf16[3,1536,96]{1,2,0:T(8,128)(2,1)} %param.5) | copy-start | bytes 2654212
  0.6 2.4 %copy-start.1 = (bf16[1536,1536]{1,0:T(8,128)(2,1)S(1)}, bf16[1536,1536]{1,0:T(8,128)(2,1)}, u32[]{:S(2)}) copy-start(bf16[1536,1536]{1,0:T(8,128)(2,1)} %pw_ref.7) | copy-start | bytes 14155780
  4.5 6.0 %copy-start.3 = (bf16[384,2048]{1,0:T(8,128)(2,1)S(1)}, bf16[384,2048]{1,0:T(8,128)(2,1)}, u32[]{:S(2)}) copy-start(bf16[384,2048]{1,0:T(8,128)(2,1)} %x_ref.3) | copy-start | bytes 4718596
  7.3 5.3 %copy-start.13 = (bf16[384,256]{1,0:T(8,128)(2,1)}, bf16[384,256]{1,0:T(8,128)(2,1)S(1)}, u32[]{:S(2)}) copy-start(bf16[384,256]{1,0:T(8,128)(2,1)S(1)} %get-tuple-element.35.rest_0_) | copy-start | bytes 589828
  7.3 14.2 %collective-permute-start.10 = (bf16[384,256]{1,0:T(8,128)(2,1)S(1)}, bf16[384,256]{1,0:T(8,128)(2,1)S(1)}, u32[]{:S(2)}, u32[]{:S(2)}) collective-permute-start(bf16[384,256]{1,0:T(8,128)(2,1)S(1)} %get-tuple-element.36), channel_id=1, source_target_pairs={{0,1},{1,0},{2,3},{3,2},{4,5},{5,4},{6,7},{7,6},{8,9},{9,8},{10,11... | collective-permute-start | bytes 589832 | tf_op jit(solution)/shard_map/ppermute | solution.py:227
  7.8 15.6 %collective-permute-start.11 = (bf16[384,256]{1,0:T(8,128)(2,1)S(1)}, bf16[384,256]{1,0:T(8,128)(2,1)S(1)}, u32[]{:S(2)}, u32[]{:S(2)}) collective-permute-start(bf16[384,256]{1,0:T(8,128)(2,1)S(1)} %get-tuple-element.37), channel_id=1, source_target_pairs={{0,2},{1,3},{2,0},{3,1},{4,6},{5,7},{6,4},{7,5},{8,10},{9,11},{10,... | collective-permute-start | bytes 589832 | tf_op jit(solution)/shard_map/ppermute | solution.py:227
  10.4 19.5 %collective-permute-start.12 = (bf16[384,256]{1,0:T(8,128)(2,1)S(1)}, bf16[384,256]{1,0:T(8,128)(2,1)S(1)}, u32[]{:S(2)}, u32[]{:S(2)}) collective-permute-start(bf16[384,256]{1,0:T(8,128)(2,1)S(1)} %get-tuple-element.38), channel_id=1, source_target_pairs={{0,3},{1,2},{2,1},{3,0},{4,7},{5,6},{6,5},{7,4},{8,11},{9,10},{10,... | collective-permute-start | bytes 589832 | tf_op jit(solution)/shard_map/ppermute | solution.py:227
  11.3 19.4 %collective-permute-start.1 = (bf16[384,256]{1,0:T(8,128)(2,1)S(1)}, bf16[384,256]{1,0:T(8,128)(2,1)S(1)}, u32[]{:S(2)}, u32[]{:S(2)}) collective-permute-start(bf16[384,256]{1,0:T(8,128)(2,1)S(1)} %get-tuple-element.52), channel_id=1, source_target_pairs={{4,0},{8,4},{12,8},{16,12},{20,16},{24,20},{28,24},{5,1},{9,5},{13... | collective-permute-start | bytes 589832 | tf_op jit(solution)/shard_map/ppermute | solution.py:232
  12.6 19.6 %collective-permute-start = (bf16[384,256]{1,0:T(8,128)(2,1)S(1)}, bf16[384,256]{1,0:T(8,128)(2,1)S(1)}, u32[]{:S(2)}, u32[]{:S(2)}) collective-permute-start(bf16[384,256]{1,0:T(8,128)(2,1)S(1)} %get-tuple-element.53), channel_id=1, source_target_pairs={{0,4},{4,8},{8,12},{12,16},{16,20},{20,24},{24,28},{1,5},{5,9},{9,... | collective-permute-start | bytes 589832 | tf_op jit(solution)/shard_map/ppermute | solution.py:232
  22.2 17.8 %collective-permute-start.6 = (bf16[384,256]{1,0:T(8,128)(2,1)}, bf16[384,256]{1,0:T(8,128)(2,1)}, u32[]{:S(2)}, u32[]{:S(2)}) collective-permute-start(bf16[384,256]{1,0:T(8,128)(2,1)} %get-tuple-element.50), channel_id=1, source_target_pairs={{4,0},{8,4},{12,8},{16,12},{20,16},{24,20},{28,24},{5,1},{9,5},{13... | collective-permute-start | bytes 589832 | tf_op jit(solution)/shard_map/ppermute | solution.py:232
  24.2 20.2 %collective-permute-start.5 = (bf16[384,256]{1,0:T(8,128)(2,1)}, bf16[384,256]{1,0:T(8,128)(2,1)}, u32[]{:S(2)}, u32[]{:S(2)}) collective-permute-start(bf16[384,256]{1,0:T(8,128)(2,1)} %get-tuple-element.51), channel_id=1, source_target_pairs={{0,4},{4,8},{8,12},{12,16},{16,20},{20,24},{24,28},{1,5},{5,9},{9,... | collective-permute-start | bytes 589832 | tf_op jit(solution)/shard_map/ppermute | solution.py:232
  30.6 18.6 %collective-permute-start.15 = (bf16[384,256]{1,0:T(8,128)(2,1)}, bf16[384,256]{1,0:T(8,128)(2,1)}, u32[]{:S(2)}, u32[]{:S(2)}) collective-permute-start(bf16[384,256]{1,0:T(8,128)(2,1)} %get-tuple-element.44), channel_id=1, source_target_pairs={{0,1},{1,0},{2,3},{3,2},{4,5},{5,4},{6,7},{7,6},{8,9},{9,8},{10,11... | collective-permute-start | bytes 589832 | tf_op jit(solution)/shard_map/ppermute | solution.py:227
  30.6 18.6 %collective-permute-start.16 = (bf16[384,256]{1,0:T(8,128)(2,1)}, bf16[384,256]{1,0:T(8,128)(2,1)}, u32[]{:S(2)}, u32[]{:S(2)}) collective-permute-start(bf16[384,256]{1,0:T(8,128)(2,1)} %get-tuple-element.45), channel_id=1, source_target_pairs={{0,2},{1,3},{2,0},{3,1},{4,6},{5,7},{6,4},{7,5},{8,10},{9,11},{10,... | collective-permute-start | bytes 589832 | tf_op jit(solution)/shard_map/ppermute | solution.py:227
  32.2 17.1 %collective-permute-start.17 = (bf16[384,256]{1,0:T(8,128)(2,1)}, bf16[384,256]{1,0:T(8,128)(2,1)}, u32[]{:S(2)}, u32[]{:S(2)}) collective-permute-start(bf16[384,256]{1,0:T(8,128)(2,1)} %get-tuple-element.46), channel_id=1, source_target_pairs={{0,3},{1,2},{2,1},{3,0},{4,7},{5,6},{6,5},{7,4},{8,11},{9,10},{10,... | collective-permute-start | bytes 589832 | tf_op jit(solution)/shard_map/ppermute | solution.py:227
  40.0 9.3 %copy-start.12 = (bf16[384,256]{1,0:T(8,128)(2,1)S(1)}, bf16[384,256]{1,0:T(8,128)(2,1)}, u32[]{:S(2)}) copy-start(bf16[384,256]{1,0:T(8,128)(2,1)} %copy-done.11) | copy-start | bytes 589828
  40.0 16.5 %collective-permute-start.13 = (bf16[384,256]{1,0:T(8,128)(2,1)S(1)}, bf16[384,256]{1,0:T(8,128)(2,1)S(1)}, u32[]{:S(2)}, u32[]{:S(2)}) collective-permute-start(bf16[384,256]{1,0:T(8,128)(2,1)S(1)} %get-tuple-element.40), channel_id=1, source_target_pairs={{0,4},{4,8},{8,12},{12,16},{16,20},{20,24},{24,28},{1,5},{5,9},{9,... | collective-permute-start | bytes 589832 | tf_op jit(solution)/shard_map/ppermute | solution.py:232
  44.3 13.1 %collective-permute-start.14 = (bf16[384,256]{1,0:T(8,128)(2,1)S(1)}, bf16[384,256]{1,0:T(8,128)(2,1)S(1)}, u32[]{:S(2)}, u32[]{:S(2)}) collective-permute-start(bf16[384,256]{1,0:T(8,128)(2,1)S(1)} %get-tuple-element.41), channel_id=1, source_target_pairs={{4,0},{8,4},{12,8},{16,12},{20,16},{24,20},{28,24},{5,1},{9,5},{13... | collective-permute-start | bytes 589832 | tf_op jit(solution)/shard_map/ppermute | solution.py:232
  49.2 10.4 %collective-permute-start.7 = (bf16[384,256]{1,0:T(8,128)(2,1)S(1)}, bf16[384,256]{1,0:T(8,128)(2,1)S(1)}, u32[]{:S(2)}, u32[]{:S(2)}) collective-permute-start(bf16[384,256]{1,0:T(8,128)(2,1)S(1)} %get-tuple-element.31), channel_id=1, source_target_pairs={{0,1},{1,0},{2,3},{3,2},{4,5},{5,4},{6,7},{7,6},{8,9},{9,8},{10,11... | collective-permute-start | bytes 589832 | tf_op jit(solution)/shard_map/ppermute | solution.py:227
  50.7 13.6 %collective-permute-start.18 = (bf16[384,256]{1,0:T(8,128)(2,1)S(1)}, bf16[384,256]{1,0:T(8,128)(2,1)S(1)}, u32[]{:S(2)}, u32[]{:S(2)}) collective-permute-start(bf16[384,256]{1,0:T(8,128)(2,1)S(1)} %get-tuple-element.48), channel_id=1, source_target_pairs={{0,4},{4,8},{8,12},{12,16},{16,20},{20,24},{24,28},{1,5},{5,9},{9,... | collective-permute-start | bytes 589832 | tf_op jit(solution)/shard_map/ppermute | solution.py:232
  55.3 10.6 %collective-permute-start.19 = (bf16[384,256]{1,0:T(8,128)(2,1)S(1)}, bf16[384,256]{1,0:T(8,128)(2,1)S(1)}, u32[]{:S(2)}, u32[]{:S(2)}) collective-permute-start(bf16[384,256]{1,0:T(8,128)(2,1)S(1)} %get-tuple-element.49), channel_id=1, source_target_pairs={{4,0},{8,4},{12,8},{16,12},{20,16},{24,20},{28,24},{5,1},{9,5},{13... | collective-permute-start | bytes 589832 | tf_op jit(solution)/shard_map/ppermute | solution.py:232
  57.3 29.6 %collective-permute-start.2 = (bf16[384,256]{1,0:T(8,128)(2,1)}, bf16[384,256]{1,0:T(8,128)(2,1)}, u32[]{:S(2)}, u32[]{:S(2)}) collective-permute-start(bf16[384,256]{1,0:T(8,128)(2,1)} %get-tuple-element.27), channel_id=1, source_target_pairs={{0,1},{1,0},{2,3},{3,2},{4,5},{5,4},{6,7},{7,6},{8,9},{9,8},{10,11... | collective-permute-start | bytes 589832 | tf_op jit(solution)/shard_map/ppermute | solution.py:227
  58.2 22.8 %collective-permute-start.8 = (bf16[384,256]{1,0:T(8,128)(2,1)}, bf16[384,256]{1,0:T(8,128)(2,1)S(1)}, u32[]{:S(2)}, u32[]{:S(2)}) collective-permute-start(bf16[384,256]{1,0:T(8,128)(2,1)} %get-tuple-element.32), channel_id=1, source_target_pairs={{0,2},{1,3},{2,0},{3,1},{4,6},{5,7},{6,4},{7,5},{8,10},{9,11},{10,... | collective-permute-start | bytes 589832 | tf_op jit(solution)/shard_map/ppermute | solution.py:227
  59.7 21.3 %collective-permute-start.9 = (bf16[384,256]{1,0:T(8,128)(2,1)}, bf16[384,256]{1,0:T(8,128)(2,1)S(1)}, u32[]{:S(2)}, u32[]{:S(2)}) collective-permute-start(bf16[384,256]{1,0:T(8,128)(2,1)} %get-tuple-element.33), channel_id=1, source_target_pairs={{0,3},{1,2},{2,1},{3,0},{4,7},{5,6},{6,5},{7,4},{8,11},{9,10},{10,... | collective-permute-start | bytes 589832 | tf_op jit(solution)/shard_map/ppermute | solution.py:227
  64.3 8.9 %copy-start.21 = (bf16[384,256]{1,0:T(8,128)(2,1)}, bf16[384,256]{1,0:T(8,128)(2,1)S(1)}, u32[]{:S(2)}) copy-start(bf16[384,256]{1,0:T(8,128)(2,1)S(1)} %collective-permute-done.18.left_ref) | copy-start | bytes 589828
  64.3 22.5 %collective-permute-start.3 = (bf16[384,256]{1,0:T(8,128)(2,1)}, bf16[384,256]{1,0:T(8,128)(2,1)}, u32[]{:S(2)}, u32[]{:S(2)}) collective-permute-start(bf16[384,256]{1,0:T(8,128)(2,1)} %get-tuple-element.28), channel_id=1, source_target_pairs={{0,2},{1,3},{2,0},{3,1},{4,6},{5,7},{6,4},{7,5},{8,10},{9,11},{10,... | collective-permute-start | bytes 589832 | tf_op jit(solution)/shard_map/ppermute | solution.py:227
  65.8 5.5 %copy-start.23 = (bf16[384,256]{1,0:T(8,128)(2,1)}, bf16[384,256]{1,0:T(8,128)(2,1)S(1)}, u32[]{:S(2)}) copy-start(bf16[384,256]{1,0:T(8,128)(2,1)S(1)} %collective-permute-done.19.right_ref) | copy-start | bytes 589828
  65.8 21.0 %collective-permute-start.4 = (bf16[384,256]{1,0:T(8,128)(2,1)}, bf16[384,256]{1,0:T(8,128)(2,1)}, u32[]{:S(2)}, u32[]{:S(2)}) collective-permute-start(bf16[384,256]{1,0:T(8,128)(2,1)} %get-tuple-element.29), channel_id=1, source_target_pairs={{0,3},{1,2},{2,1},{3,0},{4,7},{5,6},{6,5},{7,4},{8,11},{9,10},{10,... | collective-permute-start | bytes 589832 | tf_op jit(solution)/shard_map/ppermute | solution.py:227
  74.4 4.2 %copy-start.8 = (bf16[384,256]{1,0:T(8,128)(2,1)S(1)}, bf16[384,256]{1,0:T(8,128)(2,1)}, u32[]{:S(2)}) copy-start(bf16[384,256]{1,0:T(8,128)(2,1)} %copy-done.7) | copy-start | bytes 589828
  74.4 4.2 %copy-start.10 = (bf16[384,256]{1,0:T(8,128)(2,1)S(1)}, bf16[384,256]{1,0:T(8,128)(2,1)}, u32[]{:S(2)}) copy-start(bf16[384,256]{1,0:T(8,128)(2,1)} %copy-done.9) | copy-start | bytes 589828
  78.6 2.3 %copy-start.6 = (bf16[384,256]{1,0:T(8,128)(2,1)S(1)}, bf16[384,256]{1,0:T(8,128)(2,1)}, u32[]{:S(2)}) copy-start(bf16[384,256]{1,0:T(8,128)(2,1)} %copy-done.5) | copy-start | bytes 589828
  81.0 2.3 %copy-start.2 = (bf16[1536,1536]{1,0:T(8,128)(2,1)S(1)}, bf16[1536,1536]{1,0:T(8,128)(2,1)}, u32[]{:S(2)}) copy-start(bf16[1536,1536]{1,0:T(8,128)(2,1)} %pw_ref.7) | copy-start | bytes 14155780
  83.3 3.5 %copy-start.26 = (bf16[384,256]{1,0:T(8,128)(2,1)S(1)}, bf16[384,256]{1,0:T(8,128)(2,1)}, u32[]{:S(2)}) copy-start(bf16[384,256]{1,0:T(8,128)(2,1)} %copy-done.25) | copy-start | bytes 589828
  (16 other events, 13.1 us)

commit v2 on v0

v2 whole, which is shorter than its diff:
```python
import functools

import jax
import jax.numpy as jnp
from jax import lax
from jax.experimental import pallas as pl
from jax.experimental.pallas import tpu as pltpu
from jax.sharding import PartitionSpec as P

DILATION_STEP = 512
GRANT = 56 << 20
PARAMS = pltpu.CompilerParams(vmem_limit_bytes=GRANT)
BF16 = jnp.bfloat16


def gelu_and_slope(v):
    square = v * v
    inner = v * (0.7978845608 + (0.7978845608 * 0.044715) * square)
    th = jnp.tanh(inner)
    half = 0.5 + 0.5 * th
    active = v * half
    inner_slope = 0.7978845608 + (3.0 * 0.7978845608 * 0.044715) * square
    slope = half + (0.5 * v) * (1.0 - th * th) * inner_slope
    return active, slope


def lanes(start, size):
    return pl.ds(pl.multiple_of(start, 128), size)


def upstream_kernel(order, where_ref, pw_ref, cot_ref, *piece_refs):
    step = pl.program_id(0)
    result = lax.dot_general(
        pw_ref[...], cot_ref[...], (((0,), (0,)), ((), ())), preferred_element_type=jnp.float32
    ).astype(BF16)
    for place in range(len(order)):
        @pl.when(step == place)
        def _(place=place):
            piece_refs[place][...] = result


def upstream(where, pw_weight, cotangent, channels, order):
    total, width = cotangent.shape
    if channels % 128 != 0:
        whole = lax.dot_general(
            pw_weight, cotangent, (((0,), (0,)), ((), ())), preferred_element_type=jnp.float32
        ).astype(BF16)
        return [lax.dynamic_slice_in_dim(whole, (where[0] ^ k) * channels, channels, 0) for k in order]

    def pw_index(step, where_ref):
        k = order[0]
        for place in range(1, len(order)):
            k = jnp.where(step == place, order[place], k)
        return 0, where_ref[0] ^ k

    return pl.pallas_call(
        functools.partial(upstream_kernel, order),
        grid_spec=pltpu.PrefetchScalarGridSpec(
            num_scalar_prefetch=1,
            grid=(len(order),),
            in_specs=[
                pl.BlockSpec((total, channels), pw_index),
                pl.BlockSpec((total, width), lambda step, where_ref: (0, 0)),
            ],
            out_specs=[pl.BlockSpec((channels, width), lambda step, where_ref: (0, 0))] * len(order),
        ),
        out_shape=[jax.ShapeDtypeStruct((channels, width), BF16)] * len(order),
        compiler_params=PARAMS,
        name="upstream",
    )(where, pw_weight, cotangent)


def place_halos(wide, middle, near_ref, far_ref, odd):
    halo, length = near_ref.shape[1], middle.shape[1]
    wide[:, lanes((1 - odd) * (halo + length), halo)] = near_ref[...]
    wide[:, lanes(odd * (halo + length), halo)] = far_ref[...]
    wide[:, halo:halo + length] = middle[...]


def forward_kernel(n, where_ref, x_ref, near_ref, far_ref, w_ref, *rest):
    up_refs, active_refs = rest[:n], rest[n:2 * n]
    grad_ref, near_out, far_out, wide = rest[2 * n:]
    ch, odd = where_ref[0], where_ref[1]
    halo, length = near_ref.shape[1], x_ref.shape[1]
    place_halos(wide, x_ref, near_ref, far_ref, odd)
    block = length // n
    unit = min(block, 256)
    for k in range(n):
        for s in range(block // unit):
            start = (ch ^ k) * block + s * unit
            here = slice(s * unit, (s + 1) * unit)
            conv_out = sum(
                jnp.dot(
                    w_ref[t], wide[:, lanes(start + t * halo, unit)], preferred_element_type=jnp.float32
                )
                for t in range(3)
            )
            active, slope = gelu_and_slope(conv_out)
            active_refs[k][:, here] = active.astype(BF16)
            grad_ref[:, lanes(start, unit)] = (
                up_refs[k][:, here].astype(jnp.float32) * slope
            ).astype(BF16)
    near_out[...] = grad_ref[:, lanes((1 - odd) * (length - halo), halo)]
    far_out[...] = grad_ref[:, lanes(odd * (length - halo), halo)]


def rows_of(array, group):
    return pl.BlockSpec((group, array.shape[1]), lambda g, where_ref: (g, 0))


def forward(where, inputs, near, far, weight, ups):
    n = len(ups)
    channels, length = inputs.shape
    group = weight.shape[2]
    groups = channels // group
    w_spec = pl.BlockSpec((3, group, group), lambda g, where_ref: (0, where_ref[0] * groups + g, 0))
    outs = [ups[0]] * n + [inputs, near, far]
    results = pl.pallas_call(
        functools.partial(forward_kernel, n),
        grid_spec=pltpu.PrefetchScalarGridSpec(
            num_scalar_prefetch=1,
            grid=(groups,),
            in_specs=[rows_of(inputs, group), rows_of(near, group), rows_of(far, group), w_spec]
            + [rows_of(u, group) for u in ups],
            out_specs=[rows_of(o, group) for o in outs],
            scratch_shapes=[pltpu.VMEM((group, length + 2 * near.shape[1]), BF16)],
        ),
        out_shape=[jax.ShapeDtypeStruct(o.shape, BF16) for o in outs],
        compiler_params=PARAMS,
        name="forward",
    )(where, inputs, near, far, weight, *ups)
    return results[:n], *results[n:]


def back_kernel(where_ref, grad_ref, near_ref, far_ref, w_ref, out_ref, wide):
    halo, length = near_ref.shape[1], grad_ref.shape[1]
    place_halos(wide, grad_ref, near_ref, far_ref, where_ref[1])
    unit = 256
    turned = [w_ref[t].T for t in range(3)]
    for s in range(length // unit):
        out_ref[:, s * unit:(s + 1) * unit] = sum(
            jnp.dot(
                turned[2 - t], wide[:, s * unit + t * halo:s * unit + t * halo + unit],
                preferred_element_type=jnp.float32,
            )
            for t in range(3)
        ).astype(BF16)


def backward(where, grad, near, far, weight):
    channels, length = grad.shape
    group = weight.shape[2]
    groups = channels // group
    w_spec = pl.BlockSpec((3, group, group), lambda g, where_ref: (0, where_ref[0] * groups + g, 0))
    return pl.pallas_call(
        back_kernel,
        grid_spec=pltpu.PrefetchScalarGridSpec(
            num_scalar_prefetch=1,
            grid=(groups,),
            in_specs=[rows_of(grad, group), rows_of(near, group), rows_of(far, group), w_spec],
            out_specs=rows_of(grad, group),
            scratch_shapes=[pltpu.VMEM((group, length + 2 * near.shape[1]), BF16)],
        ),
        out_shape=jax.ShapeDtypeStruct(grad.shape, BF16),
        compiler_params=PARAMS,
        name="backward",
    )(where, grad, near, far, weight)


def mix_kernel(n, where_ref, pw_ref, *rest):
    piece_refs, (out_ref, gathered) = rest[:n], rest[n:]
    channels = piece_refs[0].shape[0]

    @pl.when(pl.program_id(0) == 0)
    def _():
        for k in range(n):
            start = (where_ref[0] ^ k) * channels
            gathered[pl.ds(pl.multiple_of(start, 16), channels), :] = piece_refs[k][...]

    out_ref[...] = jnp.dot(
        pw_ref[...], gathered[...], preferred_element_type=jnp.float32
    ).astype(BF16)


def mix(where, pw_weight, pieces):
    n, width = len(pieces), pieces[0].shape[1]
    total = pw_weight.shape[0]
    rows = 256
    return pl.pallas_call(
        functools.partial(mix_kernel, n),
        grid_spec=pltpu.PrefetchScalarGridSpec(
            num_scalar_prefetch=1,
            grid=(total // rows,),
            in_specs=[pl.BlockSpec((rows, total), lambda m, where_ref: (m, 0))]
            + [pl.BlockSpec(p.shape, lambda m, where_ref: (0, 0)) for p in pieces],
            out_specs=pl.BlockSpec((rows, width), lambda m, where_ref: (m, 0)),
            scratch_shapes=[pltpu.VMEM((total, width), BF16)],
        ),
        out_shape=jax.ShapeDtypeStruct((total, width), BF16),
        compiler_params=PARAMS,
        name="mix",
    )(where, pw_weight, *pieces)


def exchange(piece, k):
    if k == 0:
        return piece
    return lax.ppermute(piece, "ch", [(i, i ^ k) for i in range(lax.axis_size("ch"))])


def swap(values, first):
    size = lax.axis_size("ctx")
    pairs = [(i, i + 1) for i in range(first, size - 1, 2)]
    return lax.ppermute(values, "ctx", pairs + [(b, a) for a, b in pairs])


def body(inputs, conv_weight, pw_weight, cotangent):
    n = lax.axis_size("ch")
    odd = lax.axis_index("ctx") % 2
    where = jnp.stack([lax.axis_index("ch"), odd]).astype(jnp.int32)
    channels, length = inputs.shape

    def edge(at_end):
        return lax.dynamic_slice_in_dim(inputs, at_end * (length - DILATION_STEP), DILATION_STEP, 1)

    near, far = swap(edge(1 - odd), 0), swap(edge(odd), 1)
    order = list(range(n - 1, -1, -1))
    ups = {}
    for part in (order[:n // 2], order[n // 2:]):
        pieces = upstream(where, pw_weight, cotangent, channels, part)
        for k, piece in zip(part, pieces):
            ups[k] = exchange(piece, k)
    active, grad, near_grad, far_grad = forward(
        where, inputs, near, far, conv_weight, [ups[k] for k in range(n)]
    )
    near_grad, far_grad = swap(near_grad, 0), swap(far_grad, 1)
    active = {k: exchange(active[k], k) for k in order}
    mixed = mix(where, pw_weight, [active[k] for k in range(n)])
    return mixed, backward(where, grad, near_grad, far_grad, conv_weight)


def solution(mesh):
    placed = (P("ch", "ctx"), P(), P(), P(None, ("ctx", "ch")))
    return jax.shard_map(
        body,
        mesh=mesh,
        in_specs=placed,
        out_specs=(P(None, ("ctx", "ch")), P("ch", "ctx")),
        check_vma=False,
    )
```

time: 138 us -> 74.5 us (0.54)
  the two profiles are of different devices: /device:TPU:24 before, /device:TPU:0 now
where the time goes in v2:
time: 74.5 us; the launch traced here: 73.3 us
  Pallas kernels  30.5 us (41%)
  waiting for transfers between devices  24.8 us (33%)
  starting transfers between devices  11.5 us (15%)
  local copies, waits for them, and re-layouts  5.2 us (7%)
    ppermute x4, waiting for transfers between devices, swap(): return lax.ppermute(values, 'ctx', pairs + [(b, a) for a, b in pairs])  17.1 us
    pallas_call x2, Pallas kernels, upstream(): pl.pallas_call(functools.partial(upstream_kernel, order), grid_spec=pltpu...  10.2 us
    pallas_call x1, Pallas kernels, mix(): pl.pallas_call(functools.partial(mix_kernel, n), grid_spec=pltpu.Prefetch...  8 us
    ppermute x6, waiting for transfers between devices, exchange(): lax.ppermute(piece, 'ch', [(i, i ^ k) for i in range(lax.axis_size('ch'))])  7.73 us
    ppermute x4, starting transfers between devices, swap(): return lax.ppermute(values, 'ctx', pairs + [(b, a) for a, b in pairs])  7.49 us
    pallas_call x1, Pallas kernels, forward(): pl.pallas_call(functools.partial(forward_kernel, n), grid_spec=pltpu.Pref...  6.88 us
    pallas_call x1, Pallas kernels, backward(): pl.pallas_call(back_kernel, grid_spec=pltpu.PrefetchScalarGridSpec(num_sc...  5.39 us
    unnamed x21, local copies, waits for them, and re-layouts  4.02 us
  transfers between devices with their start and end apart: 10, of which 4 were waited for; matrix products, arithmetic and copies ran while one was open for 3% of the time, Pallas kernels for 21%

profile of v2, /device:TPU:0, one launch (start us, length us, event | category | flops | bytes accessed | tf_op | source)
XLA Modules:
  0.0 73.3 jit_solution(1532632804306333327)
XLA Ops:
  0.7 1.2 %constant_dynamic-slice_fusion = (bf16[384,512]{1,0:T(8,128)(2,1)S(1)}, bf16[384,512]{1,0:T(8,128)(2,1)S(1)}) fusion(bf16[384,2048]{1,0:T(8,128)(2,1)} %x_ref.1, s32[]{:T(128)S(6)} %select_n.15, s32[]{:T(128)S(6)} %select_n.14), kind=kLoop, calls=%fused_computation.1 | loop fusion | bytes 1572872 | tf_op jit(solution)/shard_map/dynamic_slice | solution.py:224
  1.8 0.7 collective-permute-start.1
  2.5 5.8 %collective-permute-start = (bf16[384,512]{1,0:T(8,128)(2,1)S(1)}, bf16[384,512]{1,0:T(8,128)(2,1)S(1)}, u32[]{:S(2)}, u32[]{:S(2)}) collective-permute-start(bf16[384,512]{1,0:T(8,128)(2,1)S(1)} %get-tuple-element.25), channel_id=1, source_target_pairs={{0,4},{8,12},{16,20},{24,28},{4,0},{12,8},{20,16},{28,24},{1,5},{9... | collective-permute-start | bytes 1179656 | tf_op jit(solution)/shard_map/ppermute | solution.py:214
  8.3 0.7 pad_add_fusion.where_ref
  9.0 5.0 %upstream.3 = (bf16[384,512]{1,0:T(8,128)(2,1)}, bf16[384,512]{1,0:T(8,128)(2,1)}) custom-call(s32[2]{0:T(128)} %pad_add_fusion.where_ref, bf16[1536,1536]{1,0:T(8,128)(2,1)} %pw_ref.5, bf16[1536,512]{1,0:T(8,128)(2,1)} %cot_ref.3), custom_call_target="tpu_custom_call" | custom-call | tf_op jit(solution)/shard_map/upstream/pallas_call | solution.py:56
  14.0 1.5 %collective-permute-start.3 = (bf16[384,512]{1,0:T(8,128)(2,1)}, bf16[384,512]{1,0:T(8,128)(2,1)S(1)}, u32[]{:S(2)}, u32[]{:S(2)}) collective-permute-start(bf16[384,512]{1,0:T(8,128)(2,1)} %get-tuple-element.15), channel_id=1, source_target_pairs={{0,2},{1,3},{2,0},{3,1},{4,6},{5,7},{6,4},{7,5},{8,10},{9,11},{10,... | collective-permute-start | bytes 1179656 | tf_op jit(solution)/shard_map/ppermute | solution.py:208
  15.5 0.0 collective-permute-start.4
  15.5 5.2 %upstream.2 = (bf16[384,512]{1,0:T(8,128)(2,1)}, bf16[384,512]{1,0:T(8,128)(2,1)}) custom-call(s32[2]{0:T(128)} %pad_add_fusion.where_ref, bf16[1536,1536]{1,0:T(8,128)(2,1)} %pw_ref.5, bf16[1536,512]{1,0:T(8,128)(2,1)} %cot_ref.3), custom_call_target="tpu_custom_call" | custom-call | tf_op jit(solution)/shard_map/upstream/pallas_call | solution.py:56
  20.7 0.5 collective-permute-start.2
  21.2 1.4 %copy.6.w_ref = bf16[3,1536,96]{2,1,0:T(8,128)(2,1)} copy(bf16[3,1536,96]{1,2,0:T(8,128)(2,1)S(1)} %copy-done) | data formatting | bytes 1769472 | tf_op args[1]
  22.6 0.0 collective-permute-done.1.far_ref
  22.6 1.8 %collective-permute-done.near_ref = bf16[384,512]{1,0:T(8,128)(2,1)S(1)} collective-permute-done((bf16[384,512]{1,0:T(8,128)(2,1)S(1)}, bf16[384,512]{1,0:T(8,128)(2,1)S(1)}, u32[]{:S(2)}, u32[]{:S(2)}) %collective-permute-start) | collective-permute-done | bytes 393248 | tf_op jit(solution)/shard_map/ppermute | solution.py:214
  24.4 1.9 %collective-permute-done.3.rest_2_ = bf16[384,512]{1,0:T(8,128)(2,1)S(1)} collective-permute-done((bf16[384,512]{1,0:T(8,128)(2,1)}, bf16[384,512]{1,0:T(8,128)(2,1)S(1)}, u32[]{:S(2)}, u32[]{:S(2)}) %collective-permute-start.3) | collective-permute-done | bytes 393248 | tf_op jit(solution)/shard_map/ppermute | solution.py:208
  26.3 5.8 %collective-permute-done.4.rest_3_ = bf16[384,512]{1,0:T(8,128)(2,1)S(1)} collective-permute-done((bf16[384,512]{1,0:T(8,128)(2,1)}, bf16[384,512]{1,0:T(8,128)(2,1)S(1)}, u32[]{:S(2)}, u32[]{:S(2)}) %collective-permute-start.4) | collective-permute-done | bytes 393248 | tf_op jit(solution)/shard_map/ppermute | solution.py:208
  32.1 0.7 copy-done.7
  32.8 6.9 %forward.1 = (bf16[384,512]{1,0:T(8,128)(2,1)}, bf16[384,512]{1,0:T(8,128)(2,1)}, bf16[384,512]{1,0:T(8,128)(2,1)}, bf16[384,512]{1,0:T(8,128)(2,1)}, bf16[384,2...) custom-call(s32[2]{0:T(128)} %pad_add_fusion.where_ref, bf16[384,2048]{1,0:T(8,128)(2,1)} %x_ref.1, ...), custom_call_target="tpu_custom_call" | custom-call | tf_op jit(solution)/shard_map/forward/pallas_call | solution.py:118
  39.7 0.4 collective-permute-start.8
  40.1 0.7 collective-permute-start.9
  40.8 0.5 collective-permute-start.5
  41.2 1.5 %collective-permute-start.6 = (bf16[384,512]{1,0:T(8,128)(2,1)}, bf16[384,512]{1,0:T(8,128)(2,1)S(1)}, u32[]{:S(2)}, u32[]{:S(2)}) collective-permute-start(bf16[384,512]{1,0:T(8,128)(2,1)} %get-tuple-element.19), channel_id=1, source_target_pairs={{0,2},{1,3},{2,0},{3,1},{4,6},{5,7},{6,4},{7,5},{8,10},{9,11},{10,... | collective-permute-start | bytes 1179656 | tf_op jit(solution)/shard_map/ppermute | solution.py:208
  42.8 0.0 collective-permute-start.7
  42.8 15.3 %collective-permute-done.8.near_ref = bf16[384,512]{1,0:T(8,128)(2,1)S(1)} collective-permute-done((bf16[384,512]{1,0:T(8,128)(2,1)}, bf16[384,512]{1,0:T(8,128)(2,1)S(1)}, u32[]{:S(2)}, u32[]{:S(2)}) %collective-permute-start.8) | collective-permute-done | bytes 393248 | tf_op jit(solution)/shard_map/ppermute | solution.py:214
  58.0 0.0 collective-permute-done.9.far_ref
  58.0 0.7 %copy-done.8 = bf16[384,512]{1,0:T(8,128)(2,1)} copy-done((bf16[384,512]{1,0:T(8,128)(2,1)}, bf16[384,512]{1,0:T(8,128)(2,1)S(1)}, u32[]{:S(2)}) %copy-start.8) | copy-done | bytes 393240
  58.8 0.1 copy-done.9
  58.9 5.4 %backward.1 = bf16[384,2048]{1,0:T(8,128)(2,1)} custom-call(s32[2]{0:T(128)} %pad_add_fusion.where_ref, bf16[384,2048]{1,0:T(8,128)(2,1)} %get-tuple-element.21.grad_ref, bf16[384,512]{1,0:T(8,128)(2,1)} %copy-done.8, bf16[384,512]{1,0:T(8,128)(2,1)} %copy-done.9, bf16[3,1536,96]{2,1,0:T(8,128)(2,1)} %copy.6.w_ref), custom_call_target="tpu_custom_call" | custom-call | tf_op jit(solution)/shard_map/backward/pallas_call | solution.py:155
  64.3 0.0 collective-permute-done.5.rest_1_
  64.3 0.0 collective-permute-done.7.rest_3_
  64.4 0.7 copy-done.1
  65.1 0.1 copy-done.2
  65.2 0.1 copy-done.3
  65.4 8.0 %mix.1 = bf16[1536,512]{1,0:T(8,128)(2,1)} custom-call(s32[2]{0:T(128)} %pad_add_fusion.where_ref, bf16[1536,1536]{1,0:T(8,128)(2,1)} %pw_ref.5, bf16[384,512]{1,0:T(8,128)(2,1)} %get-tuple-element.17.rest_0_, bf16[384,512]{1,0:T(8,128)(2,1)} %copy-done.1, bf16[384,512]{1,0:T(8,128)(2,1)} %copy-done.2, bf16[384,512]{1,0:T(8,128)(2,1)} %copy-done.3), custom_call_target="tpu_custom_call" | custom-call | tf_op jit(solution)/shard_map/mix/pallas_call | solution.py:189
  (16 shorter events, 0.0 us)
Async XLA Ops:
  1.8 20.8 %collective-permute-start.1 = (bf16[384,512]{1,0:T(8,128)(2,1)S(1)}, bf16[384,512]{1,0:T(8,128)(2,1)S(1)}, u32[]{:S(2)}, u32[]{:S(2)}) collective-permute-start(bf16[384,512]{1,0:T(8,128)(2,1)S(1)} %get-tuple-element.24), channel_id=1, source_target_pairs={{4,8},{12,16},{20,24},{8,4},{16,12},{24,20},{5,9},{13,17},{21,25},... | collective-permute-start | bytes 1179656 | tf_op jit(solution)/shard_map/ppermute | solution.py:214
  2.5 21.8 %collective-permute-start = (bf16[384,512]{1,0:T(8,128)(2,1)S(1)}, bf16[384,512]{1,0:T(8,128)(2,1)S(1)}, u32[]{:S(2)}, u32[]{:S(2)}) collective-permute-start(bf16[384,512]{1,0:T(8,128)(2,1)S(1)} %get-tuple-element.25), channel_id=1, source_target_pairs={{0,4},{8,12},{16,20},{24,28},{4,0},{12,8},{20,16},{28,24},{1,5},{9... | collective-permute-start | bytes 1179656 | tf_op jit(solution)/shard_map/ppermute | solution.py:214
  14.0 12.3 %collective-permute-start.3 = (bf16[384,512]{1,0:T(8,128)(2,1)}, bf16[384,512]{1,0:T(8,128)(2,1)S(1)}, u32[]{:S(2)}, u32[]{:S(2)}) collective-permute-start(bf16[384,512]{1,0:T(8,128)(2,1)} %get-tuple-element.15), channel_id=1, source_target_pairs={{0,2},{1,3},{2,0},{3,1},{4,6},{5,7},{6,4},{7,5},{8,10},{9,11},{10,... | collective-permute-start | bytes 1179656 | tf_op jit(solution)/shard_map/ppermute | solution.py:208
  15.5 5.6 %copy-start = (bf16[3,1536,96]{1,2,0:T(8,128)(2,1)S(1)}, bf16[3,1536,96]{1,2,0:T(8,128)(2,1)}, u32[]{:S(2)}) copy-start(bf16[3,1536,96]{1,2,0:T(8,128)(2,1)} %param.5) | copy-start | bytes 2654212
  15.5 16.6 %collective-permute-start.4 = (bf16[384,512]{1,0:T(8,128)(2,1)}, bf16[384,512]{1,0:T(8,128)(2,1)S(1)}, u32[]{:S(2)}, u32[]{:S(2)}) collective-permute-start(bf16[384,512]{1,0:T(8,128)(2,1)} %get-tuple-element.16), channel_id=1, source_target_pairs={{0,3},{1,2},{2,1},{3,0},{4,7},{5,6},{6,5},{7,4},{8,11},{9,10},{10,... | collective-permute-start | bytes 1179656 | tf_op jit(solution)/shard_map/ppermute | solution.py:208
  20.7 11.4 %collective-permute-start.2 = (bf16[384,512]{1,0:T(8,128)(2,1)}, bf16[384,512]{1,0:T(8,128)(2,1)}, u32[]{:S(2)}, u32[]{:S(2)}) collective-permute-start(bf16[384,512]{1,0:T(8,128)(2,1)} %get-tuple-element.14), channel_id=1, source_target_pairs={{0,1},{1,0},{2,3},{3,2},{4,5},{5,4},{6,7},{7,6},{8,9},{9,8},{10,11... | collective-permute-start | bytes 1179656 | tf_op jit(solution)/shard_map/ppermute | solution.py:208
  22.6 9.5 %copy-start.4 = (bf16[384,512]{1,0:T(8,128)(2,1)}, bf16[384,512]{1,0:T(8,128)(2,1)S(1)}, u32[]{:S(2)}) copy-start(bf16[384,512]{1,0:T(8,128)(2,1)S(1)} %collective-permute-done.1.far_ref) | copy-start | bytes 1179652
  24.4 7.7 %copy-start.5 = (bf16[384,512]{1,0:T(8,128)(2,1)}, bf16[384,512]{1,0:T(8,128)(2,1)S(1)}, u32[]{:S(2)}) copy-start(bf16[384,512]{1,0:T(8,128)(2,1)S(1)} %collective-permute-done.near_ref) | copy-start | bytes 1179652
  26.3 5.8 %copy-start.6 = (bf16[384,512]{1,0:T(8,128)(2,1)}, bf16[384,512]{1,0:T(8,128)(2,1)S(1)}, u32[]{:S(2)}) copy-start(bf16[384,512]{1,0:T(8,128)(2,1)S(1)} %collective-permute-done.3.rest_2_) | copy-start | bytes 1179652
  32.1 0.8 %copy-start.7 = (bf16[384,512]{1,0:T(8,128)(2,1)}, bf16[384,512]{1,0:T(8,128)(2,1)S(1)}, u32[]{:S(2)}) copy-start(bf16[384,512]{1,0:T(8,128)(2,1)S(1)} %collective-permute-done.4.rest_3_) | copy-start | bytes 1179652
  39.7 18.3 %collective-permute-start.8 = (bf16[384,512]{1,0:T(8,128)(2,1)}, bf16[384,512]{1,0:T(8,128)(2,1)S(1)}, u32[]{:S(2)}, u32[]{:S(2)}) collective-permute-start(bf16[384,512]{1,0:T(8,128)(2,1)} %get-tuple-element.22), channel_id=1, source_target_pairs={{0,4},{8,12},{16,20},{24,28},{4,0},{12,8},{20,16},{28,24},{1,5},{9... | collective-permute-start | bytes 1179656 | tf_op jit(solution)/shard_map/ppermute | solution.py:214
  40.1 18.0 %collective-permute-start.9 = (bf16[384,512]{1,0:T(8,128)(2,1)}, bf16[384,512]{1,0:T(8,128)(2,1)S(1)}, u32[]{:S(2)}, u32[]{:S(2)}) collective-permute-start(bf16[384,512]{1,0:T(8,128)(2,1)} %get-tuple-element.23), channel_id=1, source_target_pairs={{4,8},{12,16},{20,24},{8,4},{16,12},{24,20},{5,9},{13,17},{21,25},... | collective-permute-start | bytes 1179656 | tf_op jit(solution)/shard_map/ppermute | solution.py:214
  40.8 23.6 %collective-permute-start.5 = (bf16[384,512]{1,0:T(8,128)(2,1)}, bf16[384,512]{1,0:T(8,128)(2,1)S(1)}, u32[]{:S(2)}, u32[]{:S(2)}) collective-permute-start(bf16[384,512]{1,0:T(8,128)(2,1)} %get-tuple-element.18), channel_id=1, source_target_pairs={{0,1},{1,0},{2,3},{3,2},{4,5},{5,4},{6,7},{7,6},{8,9},{9,8},{10,11... | collective-permute-start | bytes 1179656 | tf_op jit(solution)/shard_map/ppermute | solution.py:208
  41.2 23.1 %collective-permute-start.6 = (bf16[384,512]{1,0:T(8,128)(2,1)}, bf16[384,512]{1,0:T(8,128)(2,1)S(1)}, u32[]{:S(2)}, u32[]{:S(2)}) collective-permute-start(bf16[384,512]{1,0:T(8,128)(2,1)} %get-tuple-element.19), channel_id=1, source_target_pairs={{0,2},{1,3},{2,0},{3,1},{4,6},{5,7},{6,4},{7,5},{8,10},{9,11},{10,... | collective-permute-start | bytes 1179656 | tf_op jit(solution)/shard_map/ppermute | solution.py:208
  42.8 21.6 %collective-permute-start.7 = (bf16[384,512]{1,0:T(8,128)(2,1)}, bf16[384,512]{1,0:T(8,128)(2,1)S(1)}, u32[]{:S(2)}, u32[]{:S(2)}) collective-permute-start(bf16[384,512]{1,0:T(8,128)(2,1)} %get-tuple-element.20), channel_id=1, source_target_pairs={{0,3},{1,2},{2,1},{3,0},{4,7},{5,6},{6,5},{7,4},{8,11},{9,10},{10,... | collective-permute-start | bytes 1179656 | tf_op jit(solution)/shard_map/ppermute | solution.py:208
  58.0 0.7 %copy-start.8 = (bf16[384,512]{1,0:T(8,128)(2,1)}, bf16[384,512]{1,0:T(8,128)(2,1)S(1)}, u32[]{:S(2)}) copy-start(bf16[384,512]{1,0:T(8,128)(2,1)S(1)} %collective-permute-done.8.near_ref) | copy-start | bytes 1179652
  58.0 0.9 %copy-start.9 = (bf16[384,512]{1,0:T(8,128)(2,1)}, bf16[384,512]{1,0:T(8,128)(2,1)S(1)}, u32[]{:S(2)}) copy-start(bf16[384,512]{1,0:T(8,128)(2,1)S(1)} %collective-permute-done.9.far_ref) | copy-start | bytes 1179652
  64.3 0.7 %copy-start.1 = (bf16[384,512]{1,0:T(8,128)(2,1)}, bf16[384,512]{1,0:T(8,128)(2,1)S(1)}, u32[]{:S(2)}) copy-start(bf16[384,512]{1,0:T(8,128)(2,1)S(1)} %collective-permute-done.5.rest_1_) | copy-start | bytes 1179652
  64.3 0.9 %copy-start.2 = (bf16[384,512]{1,0:T(8,128)(2,1)}, bf16[384,512]{1,0:T(8,128)(2,1)S(1)}, u32[]{:S(2)}) copy-start(bf16[384,512]{1,0:T(8,128)(2,1)S(1)} %collective-permute-done.6.rest_2_) | copy-start | bytes 1179652
  64.4 1.0 %copy-start.3 = (bf16[384,512]{1,0:T(8,128)(2,1)}, bf16[384,512]{1,0:T(8,128)(2,1)S(1)}, u32[]{:S(2)}) copy-start(bf16[384,512]{1,0:T(8,128)(2,1)S(1)} %collective-permute-done.7.rest_3_) | copy-start | bytes 1179652

commit v3 on v0

v3 whole, which is shorter than its diff:
```python
import functools

import jax
import jax.numpy as jnp
from jax import lax
from jax.experimental import pallas as pl
from jax.experimental.pallas import tpu as pltpu
from jax.sharding import PartitionSpec as P

DILATION_STEP = 512
BF16, F32 = jnp.bfloat16, jnp.float32
ANY = pl.BlockSpec(memory_space=pl.ANY)
INSIDE = pl.BlockSpec(memory_space=pltpu.VMEM)
DMA = pltpu.SemaphoreType.DMA


def kernel_call(name, kernel, operands, outs, scratch=(), aliases=None):
    return pl.pallas_call(
        kernel,
        in_specs=[INSIDE if held else ANY for _, held in operands],
        out_specs=[INSIDE if held else ANY for _, _, held in outs],
        out_shape=[
            pltpu.VMEM(shape, kind) if held else jax.ShapeDtypeStruct(shape, kind)
            for shape, kind, held in outs
        ],
        scratch_shapes=list(scratch),
        input_output_aliases=aliases or {},
        compiler_params=pltpu.CompilerParams(vmem_limit_bytes=16 << 20),
        name=name,
    )(*[
        pltpu.with_memory_space_constraint(array, pltpu.VMEM) if held else array
        for array, held in operands
    ])


def gelu_and_slope(v):
    square = v * v
    inner = v * (0.7978845608 + (0.7978845608 * 0.044715) * square)
    th = jnp.tanh(inner)
    half = 0.5 + 0.5 * th
    active = v * half
    inner_slope = 0.7978845608 + (3.0 * 0.7978845608 * 0.044715) * square
    slope = half + (0.5 * v) * (1.0 - th * th) * inner_slope
    return active, slope


def lanes(start, size):
    return pl.ds(pl.multiple_of(start, 128), size)


def dot(a, b):
    return jnp.dot(a, b, preferred_element_type=F32)


def turned_dot(a, b):
    return lax.dot_general(a, b, (((0,), (0,)), ((), ())), preferred_element_type=F32)


def odd_place():
    return lax.axis_index("ctx") % 2


def upstream_kernel(order, channels, first, pw_ref, cot_ref, *rest):
    count = len(order)
    sems = rest[-1]
    if first:
        x_ref, piece_refs = rest[0], rest[1:1 + count]
        columns_ref, cot_in, near_ref, far_ref = rest[1 + count:-1]
    else:
        piece_refs, columns_ref, cot_in = rest[:count], rest[count], cot_ref
    ch, odd = lax.axis_index("ch"), odd_place()
    copies = []
    if first:
        copies.append(pltpu.make_async_copy(cot_ref, cot_in, sems.at[count]))
        copies[0].start()
    blocks = []
    if channels % 128 == 0:
        for place, k in enumerate(order):
            blocks.append(pltpu.make_async_copy(
                pw_ref.at[:, lanes((ch ^ k) * channels, channels)],
                columns_ref.at[:, place * channels:(place + 1) * channels], sems.at[place],
            ))
    else:
        blocks.append(pltpu.make_async_copy(pw_ref, columns_ref, sems.at[0]))
    for block in blocks:
        block.start()
    if first:
        length, halo = x_ref.shape[1], near_ref.shape[1]
        for place, (edge_ref, at_end) in enumerate(((near_ref, 1 - odd), (far_ref, odd))):
            copies.append(pltpu.make_async_copy(
                x_ref.at[:, lanes(at_end * (length - halo), halo)], edge_ref, sems.at[count + 1 + place]
            ))
            copies[-1].start()
        copies[0].wait()
    if len(blocks) == count:
        for place in range(count):
            blocks[place].wait()
            columns = slice(place * channels, (place + 1) * channels)
            piece_refs[place][...] = turned_dot(columns_ref[:, columns], cot_in[...]).astype(BF16)
    else:
        blocks[0].wait()
        result = turned_dot(columns_ref[...], cot_in[...]).astype(BF16)
        for place in range(count):
            piece_refs[place][...] = result[place * channels:(place + 1) * channels]
    for copy in copies[1:]:
        copy.wait()


def upstream(pw_weight, cotangent, inputs, channels, order):
    total, width = cotangent.shape
    first = inputs is not None
    if channels % 128 != 0:
        ch = lax.axis_index("ch")
        pw_weight = jnp.concatenate(
            [lax.dynamic_slice_in_dim(pw_weight, (ch ^ k) * channels, channels, 1) for k in order], axis=1
        )
    count = len(order)
    operands = [(pw_weight, False), (cotangent, not first)]
    outs = [((channels, width), BF16, True)] * count + [((total, count * channels), BF16, True)]
    if first:
        operands.append((inputs, False))
        outs += [(cotangent.shape, BF16, True)] + [((channels, DILATION_STEP), BF16, True)] * 2
    results = kernel_call(
        "upstream", functools.partial(upstream_kernel, order, channels, first), operands, outs,
        [DMA((count + 3,))],
    )
    return results[:count], *results[count:]


def convolve(w_ref, rows, wide, start, halo, unit):
    return sum(dot(w_ref[t, rows, :], wide[rows, lanes(start + t * halo, unit)]) for t in range(3))


def interior_kernel(n, x_ref, w_ref, *rest):
    active_refs, (slope_ref, wide, plain_ref, turned_ref, sem) = rest[:n], rest[n:]
    ch = lax.axis_index("ch")
    channels, length = x_ref.shape
    group = w_ref.shape[1]
    halo = DILATION_STEP
    block = length // n
    unit = min(block, 256)
    copy = pltpu.make_async_copy(x_ref, wide.at[:, halo:halo + length], sem)
    copy.start()
    groups = [slice(g, g + group) for g in range(0, channels, group)]
    for t in range(3):
        for rows in groups:
            square = w_ref[t, :, rows]
            turned_ref[2 - t, rows, :] = square
            plain_ref[t, rows, :] = square.T
    copy.wait()
    for k in range(n):
        base = (ch ^ k) * block

        @pl.when((base >= halo) & (base < length - halo))
        def _(k=k, base=base):
            for s in range(0, block, unit):
                for rows in groups:
                    active, slope = gelu_and_slope(convolve(plain_ref, rows, wide, base + s, halo, unit))
                    active_refs[k][rows, s:s + unit] = active.astype(BF16)
                    slope_ref[k, rows, s:s + unit] = slope


def interior(inputs, weight, n):
    channels, length = inputs.shape
    group = weight.shape[1]
    block = length // n
    outs = [((channels, block), BF16, True)] * n
    outs += [((n, channels, block), F32, True), ((channels, length + 2 * DILATION_STEP), BF16, True)]
    outs += [((3, channels, group), BF16, True)] * 2
    results = kernel_call(
        "interior", functools.partial(interior_kernel, n), [(inputs, False), (weight, True)], outs, [DMA],
    )
    return results[:n], *results[n:]


def edges_kernel(n, near_ref, far_ref, slope_ref, plain_ref, *rest):
    up_refs, rest = rest[:n], rest[n + n + 1:]
    active_refs, (wide, grad_ref, near_out, far_out) = rest[:n], rest[n:]
    ch, odd = lax.axis_index("ch"), odd_place()
    channels, length = grad_ref.shape
    group = plain_ref.shape[2]
    halo = near_ref.shape[1]
    block = length // n
    unit = min(block, 256)
    groups = [slice(g, g + group) for g in range(0, channels, group)]
    wide[:, lanes((1 - odd) * (halo + length), halo)] = near_ref[...]
    wide[:, lanes(odd * (halo + length), halo)] = far_ref[...]
    for k in range(n):
        base = (ch ^ k) * block
        inner = (base >= halo) & (base < length - halo)

        @pl.when(inner)
        def _(k=k, base=base):
            grad_ref[:, lanes(base, block)] = (
                up_refs[k][...].astype(F32) * slope_ref[k]
            ).astype(BF16)

        @pl.when(jnp.logical_not(inner))
        def _(k=k, base=base):
            for s in range(0, block, unit):
                for rows in groups:
                    active, slope = gelu_and_slope(convolve(plain_ref, rows, wide, base + s, halo, unit))
                    active_refs[k][rows, s:s + unit] = active.astype(BF16)
                    grad_ref[rows, lanes(base + s, unit)] = (
                        up_refs[k][rows, s:s + unit].astype(F32) * slope
                    ).astype(BF16)
    near_out[...] = grad_ref[:, lanes((1 - odd) * (length - halo), halo)]
    far_out[...] = grad_ref[:, lanes(odd * (length - halo), halo)]


def edges(near, far, slope, plain, ups, active, wide):
    n = len(ups)
    channels, halo = near.shape
    length = wide.shape[1] - 2 * halo
    operands = [(o, True) for o in (near, far, slope, plain, *ups, *active, wide)]
    outs = [(a.shape, BF16, True) for a in active] + [(wide.shape, BF16, True)]
    outs += [((channels, length), BF16, True)] + [((channels, halo), BF16, True)] * 2
    results = kernel_call(
        "edges", functools.partial(edges_kernel, n), operands, outs,
        aliases={4 + n + i: i for i in range(n + 1)},
    )
    return results[:n], *results[n + 1:]


def half_mix_kernel(columns_ref, *rest):
    piece_refs, sum_ref = rest[:-1], rest[-1]
    pieces = jnp.concatenate([p[...] for p in piece_refs], axis=0)
    rows = 512
    for m in range(0, sum_ref.shape[0], rows):
        sum_ref[m:m + rows, :] = dot(columns_ref[m:m + rows, :], pieces)


def last_mix_kernel(columns_ref, sum_ref, *rest):
    piece_refs, (out_ref, held, sems) = rest[:-3], rest[-3:]
    pieces = jnp.concatenate([p[...] for p in piece_refs], axis=0)
    rows = 512
    copies = []
    for step, m in enumerate(range(0, sum_ref.shape[0], rows)):
        held[m:m + rows, :] = (sum_ref[m:m + rows, :] + dot(columns_ref[m:m + rows, :], pieces)).astype(BF16)
        copies.append(pltpu.make_async_copy(held.at[m:m + rows, :], out_ref.at[m:m + rows, :], sems.at[step]))
        copies[-1].start()
    for copy in copies:
        copy.wait()


def back(turned_ref, rows, taps):
    return sum(dot(turned_ref[t, rows, :], tap) for t, tap in enumerate(taps)).astype(BF16)


def back_interior_kernel(grad_ref, turned_ref, out_ref, held, sem):
    channels, length = grad_ref.shape
    group, halo, unit = turned_ref.shape[2], DILATION_STEP, 256
    for g in range(0, channels, group):
        rows = slice(g, g + group)
        for s in range(0, length - 2 * halo, unit):
            held[rows, s:s + unit] = back(
                turned_ref, rows, [grad_ref[rows, s + t * halo:s + t * halo + unit] for t in range(3)]
            )
    copy = pltpu.make_async_copy(held, out_ref.at[:, halo:length - halo], sem)
    copy.start()
    copy.wait()


def back_ends_kernel(grad_ref, near_ref, far_ref, turned_ref, _, out_ref, halos, held, sems):
    channels, length = grad_ref.shape
    group, halo, unit = turned_ref.shape[2], DILATION_STEP, 256
    odd = odd_place()
    halos[:, lanes((1 - odd) * halo, halo)] = near_ref[...]
    halos[:, lanes(odd * halo, halo)] = far_ref[...]
    copies = []
    for end in range(2):
        for g in range(0, channels, group):
            rows = slice(g, g + group)
            for s in range(0, halo, unit):
                inner = (length - 2 * halo) * end + s
                taps = [
                    grad_ref[rows, inner:inner + unit],
                    grad_ref[rows, inner + halo:inner + halo + unit],
                ]
                outer = halos[rows, end * halo + s:end * halo + s + unit]
                taps = taps + [outer] if end else [outer] + taps
                held[rows, end * halo + s:end * halo + s + unit] = back(turned_ref, rows, taps)
        copies.append(pltpu.make_async_copy(
            held.at[:, end * halo:(end + 1) * halo],
            out_ref.at[:, end * (length - halo):end * (length - halo) + halo], sems.at[end],
        ))
        copies[-1].start()
    for copy in copies:
        copy.wait()


def exchange(piece, k):
    if k == 0:
        return piece
    return lax.ppermute(piece, "ch", [(i, i ^ k) for i in range(lax.axis_size("ch"))])


def swap(values, first):
    size = lax.axis_size("ctx")
    pairs = [(i, i + 1) for i in range(first, size - 1, 2)]
    return lax.ppermute(values, "ctx", pairs + [(b, a) for a, b in pairs])


def body(inputs, conv_weight, pw_weight, cotangent):
    n = lax.axis_size("ch")
    channels, length = inputs.shape
    total, width = cotangent.shape
    halo = DILATION_STEP
    order = list(range(n - 1, -1, -1))
    parts = order[:n // 2], order[n // 2:]

    ups, columns = {}, []
    pieces, held, cot_in, near, far = upstream(pw_weight, cotangent, inputs, channels, parts[0])
    columns.append(held)
    ups.update({k: exchange(p, k) for k, p in zip(parts[0], pieces)})
    near, far = swap(near, 0), swap(far, 1)
    pieces, held = upstream(pw_weight, cot_in, None, channels, parts[1])
    columns.append(held)
    ups.update({k: exchange(p, k) for k, p in zip(parts[1], pieces)})

    weight = lax.dynamic_slice_in_dim(
        jnp.swapaxes(conv_weight, 1, 2), lax.axis_index("ch") * channels, channels, 2
    )
    active, slope, wide, plain, turned = interior(inputs, weight, n)
    active, grad, near_grad, far_grad = edges(
        near, far, slope, plain, [ups[k] for k in range(n)], active, wide
    )
    active = {k: exchange(active[k], k) for k in order}
    near_grad, far_grad = swap(near_grad, 0), swap(far_grad, 1)

    grad_shape = ((channels, length), BF16, False)
    (grad_inputs,) = kernel_call(
        "back_interior", back_interior_kernel, [(grad, True), (turned, True)], [grad_shape],
        [pltpu.VMEM((channels, length - 2 * halo), BF16), DMA],
    )
    (partial,) = kernel_call(
        "half_mix", half_mix_kernel, [(o, True) for o in (columns[1], *[active[k] for k in parts[1]])],
        [((total, width), F32, True)],
    )
    (mixed,) = kernel_call(
        "last_mix", last_mix_kernel,
        [(o, True) for o in (columns[0], partial, *[active[k] for k in parts[0]])],
        [((total, width), BF16, False)], [pltpu.VMEM((total, width), BF16), DMA((total // 512,))],
    )
    (grad_inputs,) = kernel_call(
        "back_ends", back_ends_kernel,
        [(o, True) for o in (grad, near_grad, far_grad, turned)] + [(grad_inputs, False)], [grad_shape],
        [pltpu.VMEM((channels, 2 * halo), BF16)] * 2 + [DMA((2,))], {4: 0},
    )
    return mixed, grad_inputs


def solution(mesh):
    placed = (P("ch", "ctx"), P(), P(), P(None, ("ctx", "ch")))
    return jax.shard_map(
        body,
        mesh=mesh,
        in_specs=placed,
        out_specs=(P(None, ("ctx", "ch")), P("ch", "ctx")),
        check_vma=False,
    )
```

time: 138 us -> 65.4 us (0.47)
  the two profiles are of different devices: /device:TPU:24 before, /device:TPU:11 now
where the time goes in v3:
time: 65.4 us; the launch traced here: 65.2 us
  waiting for transfers between devices  23.8 us (36%)
  Pallas kernels  17.1 us (26%)
  starting transfers between devices  14.4 us (22%)
  local copies, waits for them, and re-layouts  8.87 us (14%)
  between operations  0.97 us (1%)
    pallas_call x8, Pallas kernels, kernel_call(): pl.pallas_call(kernel, in_specs=[INSIDE if held else ANY for _, held in o...  17.1 us
    ppermute x4, waiting for transfers between devices, swap(): return lax.ppermute(values, 'ctx', pairs + [(b, a) for a, b in pairs])  13.8 us
    ppermute x6, waiting for transfers between devices, exchange(): lax.ppermute(piece, 'ch', [(i, i ^ k) for i in range(lax.axis_size('ch'))])  9.97 us
    ppermute x4, starting transfers between devices, swap(): return lax.ppermute(values, 'ctx', pairs + [(b, a) for a, b in pairs])  8.99 us
    unnamed x22, local copies, waits for them, and re-layouts  8.84 us
    ppermute x6, starting transfers between devices, exchange(): lax.ppermute(piece, 'ch', [(i, i ^ k) for i in range(lax.axis_size('ch'))])  5.42 us
  transfers between devices with their start and end apart: 10, of which 4 were waited for; matrix products, arithmetic and copies ran while one was open for 0% of the time, Pallas kernels for 13%

profile of v3, /device:TPU:11, one launch (start us, length us, event | category | flops | bytes accessed | tf_op | source)
XLA Modules:
  0.0 65.2 jit_solution(6175094330450238016)
XLA Ops:
  0.6 0.0 copy-start
  0.7 2.4 %copy-done.1 = bf16[1536,1536]{1,0:T(8,128)(2,1)S(1)} copy-done((bf16[1536,1536]{1,0:T(8,128)(2,1)S(1)}, bf16[1536,1536]{1,0:T(8,128)(2,1)}, u32[]{:S(2)}) %copy-start.1) | copy-done | bytes 4718616
  3.1 1.4 %copy-done.2 = bf16[384,2048]{1,0:T(8,128)(2,1)S(1)} copy-done((bf16[384,2048]{1,0:T(8,128)(2,1)S(1)}, bf16[384,2048]{1,0:T(8,128)(2,1)}, u32[]{:S(2)}) %copy-start.2) | copy-done | bytes 1572888
  4.5 1.4 %copy-done.8 = bf16[1536,512]{1,0:T(8,128)(2,1)S(1)} copy-done((bf16[1536,512]{1,0:T(8,128)(2,1)S(1)}, bf16[1536,512]{1,0:T(8,128)(2,1)}, u32[]{:S(2)}) %copy-start.8) | copy-done | bytes 1572888
  5.9 3.2 %upstream.2 = (bf16[384,512]{1,0:T(8,128)(2,1)}, bf16[384,512]{1,0:T(8,128)(2,1)}, bf16[1536,768]{1,0:T(8,128)(2,1)S(1)}, bf16[1536,512]{1,0:T(8,128)(2,1)S(1)},...) custom-call(bf16[1536,1536]{1,0:T(8,128)(2,1)S(1)} %copy-done.1, bf16[1536,512]{1,0:T(8,128)(2,1)S(1)} %copy-done.8, ...), custom_call_target="tpu_custom_call" | custom-call | tf_op jit(solution)/shard_map/upstream/pallas_call | solution.py:18
  9.1 1.4 %copy-done.6 = bf16[1536,768]{1,0:T(8,128)(2,1)} copy-done((bf16[1536,768]{1,0:T(8,128)(2,1)}, bf16[1536,768]{1,0:T(8,128)(2,1)S(1)}, u32[]{:S(2)}) %copy-start.6) | copy-done | bytes 2359320
  10.5 0.3 collective-permute-start
  10.8 4.1 %collective-permute-start.1 = (bf16[384,512]{1,0:T(8,128)(2,1)}, bf16[384,512]{1,0:T(8,128)(2,1)S(1)}, u32[]{:S(2)}, u32[]{:S(2)}) collective-permute-start(bf16[384,512]{1,0:T(8,128)(2,1)} %get-tuple-element.30), channel_id=1, source_target_pairs={{4,8},{12,16},{20,24},{8,4},{16,12},{24,20},{5,9},{13,17},{21,25},... | collective-permute-start | bytes 1179656 | tf_op jit(solution)/shard_map/ppermute | solution.py:301
  14.9 1.3 %collective-permute-start.3 = (bf16[384,512]{1,0:T(8,128)(2,1)}, bf16[384,512]{1,0:T(8,128)(2,1)}, u32[]{:S(2)}, u32[]{:S(2)}) collective-permute-start(bf16[384,512]{1,0:T(8,128)(2,1)} %get-tuple-element.35), channel_id=1, source_target_pairs={{0,2},{1,3},{2,0},{3,1},{4,6},{5,7},{6,4},{7,5},{8,10},{9,11},{10,... | collective-permute-start | bytes 1179656 | tf_op jit(solution)/shard_map/ppermute | solution.py:295
  16.2 1.6 %collective-permute-start.4 = (bf16[384,512]{1,0:T(8,128)(2,1)}, bf16[384,512]{1,0:T(8,128)(2,1)}, u32[]{:S(2)}, u32[]{:S(2)}) collective-permute-start(bf16[384,512]{1,0:T(8,128)(2,1)} %get-tuple-element.36), channel_id=1, source_target_pairs={{0,3},{1,2},{2,1},{3,0},{4,7},{5,6},{6,5},{7,4},{8,11},{9,10},{10,... | collective-permute-start | bytes 1179656 | tf_op jit(solution)/shard_map/ppermute | solution.py:295
  17.9 1.9 %upstream.3 = (bf16[384,512]{1,0:T(8,128)(2,1)}, bf16[384,512]{1,0:T(8,128)(2,1)S(1)}, bf16[1536,768]{1,0:T(8,128)(2,1)S(1)}) custom-call(bf16[1536,1536]{1,0:T(8,128)(2,1)S(1)} %copy-done.1, bf16[1536,512]{1,0:T(8,128)(2,1)S(1)} %get-tuple-element.27.cot_ref), custom_call_target="tpu_custom_call" | custom-call | tf_op jit(solution)/shard_map/upstream/pallas_call | solution.py:18
  19.8 1.4 %copy-done.4 = bf16[1536,768]{1,0:T(8,128)(2,1)} copy-done((bf16[1536,768]{1,0:T(8,128)(2,1)}, bf16[1536,768]{1,0:T(8,128)(2,1)S(1)}, u32[]{:S(2)}) %copy-start.4) | copy-done | bytes 2359320
  21.2 0.7 %copy-done.9 = bf16[384,512]{1,0:T(8,128)(2,1)} copy-done((bf16[384,512]{1,0:T(8,128)(2,1)}, bf16[384,512]{1,0:T(8,128)(2,1)S(1)}, u32[]{:S(2)}) %copy-start.9) | copy-done | bytes 393240
  21.9 0.0 collective-permute-start.2
  22.0 2.1 %interior.1 = (bf16[384,512]{1,0:T(8,128)(2,1)S(1)}, bf16[384,512]{1,0:T(8,128)(2,1)S(1)}, bf16[384,512]{1,0:T(8,128)(2,1)S(1)}, bf16[384,512]{1,0:T(8,128)(2,1)...) custom-call(bf16[384,2048]{1,0:T(8,128)(2,1)S(1)} %copy-done.3, ...), custom_call_target="tpu_custom_call" | custom-call | tf_op jit(solution)/shard_map/interior/pallas_call | solution.py:18
  24.1 5.2 %collective-permute-done.near_ref = bf16[384,512]{1,0:T(8,128)(2,1)S(1)} collective-permute-done((bf16[384,512]{1,0:T(8,128)(2,1)}, bf16[384,512]{1,0:T(8,128)(2,1)S(1)}, u32[]{:S(2)}, u32[]{:S(2)}) %collective-permute-start) | collective-permute-done | bytes 393248 | tf_op jit(solution)/shard_map/ppermute | solution.py:301
  29.3 0.0 collective-permute-done.1.far_ref
  29.3 5.3 %collective-permute-done.4.rest_3_ = bf16[384,512]{1,0:T(8,128)(2,1)} collective-permute-done((bf16[384,512]{1,0:T(8,128)(2,1)}, bf16[384,512]{1,0:T(8,128)(2,1)}, u32[]{:S(2)}, u32[]{:S(2)}) %collective-permute-start.4) | collective-permute-done | bytes 393248 | tf_op jit(solution)/shard_map/ppermute | solution.py:295
  34.6 3.1 %edges.1 = (bf16[384,512]{1,0:T(8,128)(2,1)S(1)}, bf16[384,512]{1,0:T(8,128)(2,1)S(1)}, bf16[384,512]{1,0:T(8,128)(2,1)S(1)}, bf16[384,512]{1,0:T(8,128)(2,1)S(1...) custom-call(bf16[384,512]{1,0:T(8,128)(2,1)S(1)} %collective-permute, ...), custom_call_target="tpu_custom_call", output_to_operand_aliasing={{0}: (8, {}), {1}: (9, {}), {2}: (10, {}), {3}: (11, {}), {... | custom-call | tf_op jit(solution)/shard_map/edges/pallas_call | solution.py:18
  37.7 0.1 collective-permute-start.5
  37.7 0.1 collective-permute-start.8
  37.8 4.5 %collective-permute-start.9 = (bf16[384,512]{1,0:T(8,128)(2,1)S(1)}, bf16[384,512]{1,0:T(8,128)(2,1)S(1)}, u32[]{:S(2)}, u32[]{:S(2)}) collective-permute-start(bf16[384,512]{1,0:T(8,128)(2,1)S(1)} %get-tuple-element.48), channel_id=1, source_target_pairs={{4,8},{12,16},{20,24},{8,4},{16,12},{24,20},{5,9},{13,17},{21,25},... | collective-permute-start | bytes 1179656 | tf_op jit(solution)/shard_map/ppermute | solution.py:301
  42.4 2.2 %collective-permute-start.6 = (bf16[384,512]{1,0:T(8,128)(2,1)S(1)}, bf16[384,512]{1,0:T(8,128)(2,1)S(1)}, u32[]{:S(2)}, u32[]{:S(2)}) collective-permute-start(bf16[384,512]{1,0:T(8,128)(2,1)S(1)} %get-tuple-element.44), channel_id=1, source_target_pairs={{0,3},{1,2},{2,1},{3,0},{4,7},{5,6},{6,5},{7,4},{8,11},{9,10},{10,... | collective-permute-start | bytes 1179656 | tf_op jit(solution)/shard_map/ppermute | solution.py:295
  44.6 0.2 collective-permute-start.7
  44.8 1.7 %back_interior.1._ = bf16[384,2048]{1,0:T(8,128)(2,1)} custom-call(bf16[384,2048]{1,0:T(8,128)(2,1)S(1)} %get-tuple-element.46.grad_ref, bf16[3,384,96]{2,1,0:T(8,128)(2,1)S(1)} %get-tuple-element.49.turned_ref), custom_call_target="tpu_custom_call" | custom-call | tf_op jit(solution)/shard_map/back_interior/pallas_call | solution.py:18
  46.5 1.4 %half_mix.1.sum_ref = f32[1536,512]{1,0:T(8,128)S(1)} custom-call(bf16[1536,768]{1,0:T(8,128)(2,1)S(1)} %copy-done.5, bf16[384,512]{1,0:T(8,128)(2,1)S(1)} %collective-permute-done.5.rest_0_, bf16[384,512]{1,0:T(8,128)(2,1)S(1)} %get-tuple-element.43.rest_1_), custom_call_target="tpu_custom_call" | custom-call | tf_op jit(solution)/shard_map/half_mix/pallas_call | solution.py:18
  47.9 8.6 %collective-permute-done.8.near_ref = bf16[384,512]{1,0:T(8,128)(2,1)S(1)} collective-permute-done((bf16[384,512]{1,0:T(8,128)(2,1)S(1)}, bf16[384,512]{1,0:T(8,128)(2,1)S(1)}, u32[]{:S(2)}, u32[]{:S(2)}) %collective-permute-start.8) | collective-permute-done | bytes 393248 | tf_op jit(solution)/shard_map/ppermute | solution.py:301
  56.5 0.0 collective-permute-done.9.far_ref
  56.5 1.6 %back_ends.1 = bf16[384,2048]{1,0:T(8,128)(2,1)} custom-call(bf16[384,2048]{1,0:T(8,128)(2,1)S(1)} %get-tuple-element.46.grad_ref, bf16[384,512]{1,0:T(8,128)(2,1)S(1)} %collective-permute-done.8.near_ref, bf16[384,512]{1,0:T(8,128)(2,1)S(1)} %collective-permute-done.9.far_ref, ...), custom_call_target="tpu_custom_call", output_to_operand_aliasing={{}: (4, {})} | custom-call | tf_op jit(solution)/shard_map/back_ends/pallas_call | solution.py:18
  58.1 0.0 collective-permute-done.6.rest_0_
  58.1 4.7 %collective-permute-done.7.rest_1_ = bf16[384,512]{1,0:T(8,128)(2,1)S(1)} collective-permute-done((bf16[384,512]{1,0:T(8,128)(2,1)S(1)}, bf16[384,512]{1,0:T(8,128)(2,1)S(1)}, u32[]{:S(2)}, u32[]{:S(2)}) %collective-permute-start.7) | collective-permute-done | bytes 393248 | tf_op jit(solution)/shard_map/ppermute | solution.py:295
  62.8 2.2 %last_mix.1 = bf16[1536,512]{1,0:T(8,128)(2,1)} custom-call(bf16[1536,768]{1,0:T(8,128)(2,1)S(1)} %copy-done.7, f32[1536,512]{1,0:T(8,128)S(1)} %half_mix.1.sum_ref, bf16[384,512]{1,0:T(8,128)(2,1)S(1)} %collective-permute-done.6.rest_0_, bf16[384,512]{1,0:T(8,128)(2,1)S(1)} %collective-permute-done.7.rest_1_), custom_call_target="tpu_custom_call" | custom-call | tf_op jit(solution)/shard_map/last_mix/pallas_call | solution.py:18
  (19 shorter events, 0.1 us)
Async XLA Ops:
  0.6 21.3 %copy-start = (bf16[3,1536,96]{1,2,0:T(8,128)(2,1)S(1)}, bf16[3,1536,96]{1,2,0:T(8,128)(2,1)}, u32[]{:S(2)}) copy-start(bf16[3,1536,96]{1,2,0:T(8,128)(2,1)} %param.5) | copy-start | bytes 2654212
  0.6 2.4 %copy-start.1 = (bf16[1536,1536]{1,0:T(8,128)(2,1)S(1)}, bf16[1536,1536]{1,0:T(8,128)(2,1)}, u32[]{:S(2)}) copy-start(bf16[1536,1536]{1,0:T(8,128)(2,1)} %pw_ref.3) | copy-start | bytes 14155780
  3.1 1.4 %copy-start.2 = (bf16[384,2048]{1,0:T(8,128)(2,1)S(1)}, bf16[384,2048]{1,0:T(8,128)(2,1)}, u32[]{:S(2)}) copy-start(bf16[384,2048]{1,0:T(8,128)(2,1)} %x_ref.1) | copy-start | bytes 4718596
  4.5 1.4 %copy-start.8 = (bf16[1536,512]{1,0:T(8,128)(2,1)S(1)}, bf16[1536,512]{1,0:T(8,128)(2,1)}, u32[]{:S(2)}) copy-start(bf16[1536,512]{1,0:T(8,128)(2,1)} %cot_ref.1) | copy-start | bytes 4718596
  9.1 1.4 %copy-start.6 = (bf16[1536,768]{1,0:T(8,128)(2,1)}, bf16[1536,768]{1,0:T(8,128)(2,1)S(1)}, u32[]{:S(2)}) copy-start(bf16[1536,768]{1,0:T(8,128)(2,1)S(1)} %get-tuple-element.26.columns_ref) | copy-start | bytes 7077892
  10.5 18.7 %collective-permute-start = (bf16[384,512]{1,0:T(8,128)(2,1)}, bf16[384,512]{1,0:T(8,128)(2,1)S(1)}, u32[]{:S(2)}, u32[]{:S(2)}) collective-permute-start(bf16[384,512]{1,0:T(8,128)(2,1)} %get-tuple-element.29), channel_id=1, source_target_pairs={{0,4},{8,12},{16,20},{24,28},{4,0},{12,8},{20,16},{28,24},{1,5},{9... | collective-permute-start | bytes 1179656 | tf_op jit(solution)/shard_map/ppermute | solution.py:301
  10.8 18.5 %collective-permute-start.1 = (bf16[384,512]{1,0:T(8,128)(2,1)}, bf16[384,512]{1,0:T(8,128)(2,1)S(1)}, u32[]{:S(2)}, u32[]{:S(2)}) collective-permute-start(bf16[384,512]{1,0:T(8,128)(2,1)} %get-tuple-element.30), channel_id=1, source_target_pairs={{4,8},{12,16},{20,24},{8,4},{16,12},{24,20},{5,9},{13,17},{21,25},... | collective-permute-start | bytes 1179656 | tf_op jit(solution)/shard_map/ppermute | solution.py:301
  14.9 14.4 %collective-permute-start.3 = (bf16[384,512]{1,0:T(8,128)(2,1)}, bf16[384,512]{1,0:T(8,128)(2,1)}, u32[]{:S(2)}, u32[]{:S(2)}) collective-permute-start(bf16[384,512]{1,0:T(8,128)(2,1)} %get-tuple-element.35), channel_id=1, source_target_pairs={{0,2},{1,3},{2,0},{3,1},{4,6},{5,7},{6,4},{7,5},{8,10},{9,11},{10,... | collective-permute-start | bytes 1179656 | tf_op jit(solution)/shard_map/ppermute | solution.py:295
  16.2 18.3 %collective-permute-start.4 = (bf16[384,512]{1,0:T(8,128)(2,1)}, bf16[384,512]{1,0:T(8,128)(2,1)}, u32[]{:S(2)}, u32[]{:S(2)}) collective-permute-start(bf16[384,512]{1,0:T(8,128)(2,1)} %get-tuple-element.36), channel_id=1, source_target_pairs={{0,3},{1,2},{2,1},{3,0},{4,7},{5,6},{6,5},{7,4},{8,11},{9,10},{10,... | collective-permute-start | bytes 1179656 | tf_op jit(solution)/shard_map/ppermute | solution.py:295
  17.9 4.1 %copy-start.3 = (bf16[384,2048]{1,0:T(8,128)(2,1)S(1)}, bf16[384,2048]{1,0:T(8,128)(2,1)}, u32[]{:S(2)}) copy-start(bf16[384,2048]{1,0:T(8,128)(2,1)} %x_ref.1) | copy-start | bytes 4718596
  19.8 1.4 %copy-start.4 = (bf16[1536,768]{1,0:T(8,128)(2,1)}, bf16[1536,768]{1,0:T(8,128)(2,1)S(1)}, u32[]{:S(2)}) copy-start(bf16[1536,768]{1,0:T(8,128)(2,1)S(1)} %get-tuple-element.28.columns_ref) | copy-start | bytes 7077892
  21.2 0.7 %copy-start.9 = (bf16[384,512]{1,0:T(8,128)(2,1)}, bf16[384,512]{1,0:T(8,128)(2,1)S(1)}, u32[]{:S(2)}) copy-start(bf16[384,512]{1,0:T(8,128)(2,1)S(1)} %get-tuple-element.33.rest_0_) | copy-start | bytes 1179652
  21.9 12.6 %collective-permute-start.2 = (bf16[384,512]{1,0:T(8,128)(2,1)}, bf16[384,512]{1,0:T(8,128)(2,1)}, u32[]{:S(2)}, u32[]{:S(2)}) collective-permute-start(bf16[384,512]{1,0:T(8,128)(2,1)} %get-tuple-element.34), channel_id=1, source_target_pairs={{0,1},{1,0},{2,3},{3,2},{4,5},{5,4},{6,7},{7,6},{8,9},{9,8},{10,11... | collective-permute-start | bytes 1179656 | tf_op jit(solution)/shard_map/ppermute | solution.py:295
  21.9 12.6 %copy-start.10 = (bf16[384,512]{1,0:T(8,128)(2,1)S(1)}, bf16[384,512]{1,0:T(8,128)(2,1)}, u32[]{:S(2)}) copy-start(bf16[384,512]{1,0:T(8,128)(2,1)} %copy-done.9) | copy-start | bytes 1179652
  37.6 8.8 %copy-start.5 = (bf16[1536,768]{1,0:T(8,128)(2,1)S(1)}, bf16[1536,768]{1,0:T(8,128)(2,1)}, u32[]{:S(2)}) copy-start(bf16[1536,768]{1,0:T(8,128)(2,1)} %copy-done.4) | copy-start | bytes 7077892
  37.7 8.8 %collective-permute-start.5 = (bf16[384,512]{1,0:T(8,128)(2,1)S(1)}, bf16[384,512]{1,0:T(8,128)(2,1)S(1)}, u32[]{:S(2)}, u32[]{:S(2)}) collective-permute-start(bf16[384,512]{1,0:T(8,128)(2,1)S(1)} %get-tuple-element.42), channel_id=1, source_target_pairs={{0,1},{1,0},{2,3},{3,2},{4,5},{5,4},{6,7},{7,6},{8,9},{9,8},{10,11... | collective-permute-start | bytes 1179656 | tf_op jit(solution)/shard_map/ppermute | solution.py:295
  37.7 18.7 %collective-permute-start.8 = (bf16[384,512]{1,0:T(8,128)(2,1)S(1)}, bf16[384,512]{1,0:T(8,128)(2,1)S(1)}, u32[]{:S(2)}, u32[]{:S(2)}) collective-permute-start(bf16[384,512]{1,0:T(8,128)(2,1)S(1)} %get-tuple-element.47), channel_id=1, source_target_pairs={{0,4},{8,12},{16,20},{24,28},{4,0},{12,8},{20,16},{28,24},{1,5},{9... | collective-permute-start | bytes 1179656 | tf_op jit(solution)/shard_map/ppermute | solution.py:301
  37.8 18.7 %collective-permute-start.9 = (bf16[384,512]{1,0:T(8,128)(2,1)S(1)}, bf16[384,512]{1,0:T(8,128)(2,1)S(1)}, u32[]{:S(2)}, u32[]{:S(2)}) collective-permute-start(bf16[384,512]{1,0:T(8,128)(2,1)S(1)} %get-tuple-element.48), channel_id=1, source_target_pairs={{4,8},{12,16},{20,24},{8,4},{16,12},{24,20},{5,9},{13,17},{21,25},... | collective-permute-start | bytes 1179656 | tf_op jit(solution)/shard_map/ppermute | solution.py:301
  42.4 15.7 %collective-permute-start.6 = (bf16[384,512]{1,0:T(8,128)(2,1)S(1)}, bf16[384,512]{1,0:T(8,128)(2,1)S(1)}, u32[]{:S(2)}, u32[]{:S(2)}) collective-permute-start(bf16[384,512]{1,0:T(8,128)(2,1)S(1)} %get-tuple-element.44), channel_id=1, source_target_pairs={{0,3},{1,2},{2,1},{3,0},{4,7},{5,6},{6,5},{7,4},{8,11},{9,10},{10,... | collective-permute-start | bytes 1179656 | tf_op jit(solution)/shard_map/ppermute | solution.py:295
  44.6 18.2 %collective-permute-start.7 = (bf16[384,512]{1,0:T(8,128)(2,1)S(1)}, bf16[384,512]{1,0:T(8,128)(2,1)S(1)}, u32[]{:S(2)}, u32[]{:S(2)}) collective-permute-start(bf16[384,512]{1,0:T(8,128)(2,1)S(1)} %get-tuple-element.45), channel_id=1, source_target_pairs={{0,2},{1,3},{2,0},{3,1},{4,6},{5,7},{6,4},{7,5},{8,10},{9,11},{10,... | collective-permute-start | bytes 1179656 | tf_op jit(solution)/shard_map/ppermute | solution.py:295
  47.8 14.9 %copy-start.7 = (bf16[1536,768]{1,0:T(8,128)(2,1)S(1)}, bf16[1536,768]{1,0:T(8,128)(2,1)}, u32[]{:S(2)}) copy-start(bf16[1536,768]{1,0:T(8,128)(2,1)} %copy-done.6) | copy-start | bytes 7077892

commit v4 on v3

v4 whole, which is shorter than its diff:
```python
import functools

import jax
import jax.numpy as jnp
from jax import lax
from jax.experimental import pallas as pl
from jax.experimental.pallas import tpu as pltpu
from jax.sharding import PartitionSpec as P

DILATION_STEP = 512
BF16, F32 = jnp.bfloat16, jnp.float32
ANY = pl.BlockSpec(memory_space=pl.ANY)
INSIDE = pl.BlockSpec(memory_space=pltpu.VMEM)
DMA = pltpu.SemaphoreType.DMA


def kernel_call(name, kernel, operands, outs, scratch=(), aliases=None):
    return pl.pallas_call(
        kernel,
        in_specs=[INSIDE if held else ANY for _, held in operands],
        out_specs=[INSIDE if held else ANY for _, _, held in outs],
        out_shape=[
            pltpu.VMEM(shape, kind) if held else jax.ShapeDtypeStruct(shape, kind)
            for shape, kind, held in outs
        ],
        scratch_shapes=list(scratch),
        input_output_aliases=aliases or {},
        compiler_params=pltpu.CompilerParams(vmem_limit_bytes=16 << 20),
        name=name,
    )(*[
        pltpu.with_memory_space_constraint(array, pltpu.VMEM if held else pltpu.HBM)
        for array, held in operands
    ])


def gelu_and_slope(v):
    square = v * v
    inner = v * (0.7978845608 + (0.7978845608 * 0.044715) * square)
    th = jnp.tanh(inner)
    half = 0.5 + 0.5 * th
    active = v * half
    inner_slope = 0.7978845608 + (3.0 * 0.7978845608 * 0.044715) * square
    slope = half + (0.5 * v) * (1.0 - th * th) * inner_slope
    return active, slope


def lanes(start, size):
    return pl.ds(pl.multiple_of(start, 128), size)


def dot(a, b):
    return jnp.dot(a, b, preferred_element_type=F32)


def turned_dot(a, b):
    return lax.dot_general(a, b, (((0,), (0,)), ((), ())), preferred_element_type=F32)


def odd_place():
    return lax.axis_index("ctx") % 2


def ends_kernel(x_ref, near_ref, far_ref, sems):
    odd = odd_place()
    length, halo = x_ref.shape[1], near_ref.shape[1]
    copies = [
        pltpu.make_async_copy(x_ref.at[:, lanes(at_end * (length - halo), halo)], end_ref, sems.at[place])
        for place, (end_ref, at_end) in enumerate(((near_ref, 1 - odd), (far_ref, odd)))
    ]
    for copy in copies:
        copy.start()
    for copy in copies:
        copy.wait()


def upstream_kernel(order, channels, pw_ref, cot_ref, *piece_refs):
    if channels % 128 == 0:
        for k, piece_ref in zip(order, piece_refs):
            columns = lanes((lax.axis_index("ch") ^ k) * channels, channels)
            piece_ref[...] = turned_dot(pw_ref[:, columns], cot_ref[...]).astype(BF16)
    else:
        result = turned_dot(pw_ref[...], cot_ref[...]).astype(BF16)
        for place, piece_ref in enumerate(piece_refs):
            piece_ref[...] = result[place * channels:(place + 1) * channels]


def columns_of(pw_weight, channels, order):
    if channels % 128 == 0:
        return pw_weight
    ch = lax.axis_index("ch")
    return jnp.concatenate(
        [lax.dynamic_slice_in_dim(pw_weight, (ch ^ k) * channels, channels, 1) for k in order], axis=1
    )


def upstream(pw_weight, cotangent, channels, order):
    return kernel_call(
        "upstream", functools.partial(upstream_kernel, order, channels),
        [(columns_of(pw_weight, channels, order), True), (cotangent, True)],
        [((channels, cotangent.shape[1]), BF16, True)] * len(order),
    )


def convolve(w_ref, rows, wide, start, halo, unit):
    return sum(dot(w_ref[t, rows, :], wide[rows, lanes(start + t * halo, unit)]) for t in range(3))


def interior_kernel(n, x_ref, w_ref, *rest):
    active_refs, (slope_ref, wide, plain_ref, turned_ref, sem) = rest[:n], rest[n:]
    ch = lax.axis_index("ch")
    channels, length = x_ref.shape
    group = w_ref.shape[1]
    halo = DILATION_STEP
    block = length // n
    unit = min(block, 256)
    copy = pltpu.make_async_copy(x_ref, wide.at[:, halo:halo + length], sem)
    copy.start()
    groups = [slice(g, g + group) for g in range(0, channels, group)]
    for t in range(3):
        for rows in groups:
            square = w_ref[t, :, rows]
            turned_ref[2 - t, rows, :] = square
            plain_ref[t, rows, :] = square.T
    copy.wait()
    for k in range(n):
        base = (ch ^ k) * block

        @pl.when((base >= halo) & (base < length - halo))
        def _(k=k, base=base):
            for s in range(0, block, unit):
                for rows in groups:
                    active, slope = gelu_and_slope(convolve(plain_ref, rows, wide, base + s, halo, unit))
                    active_refs[k][rows, s:s + unit] = active.astype(BF16)
                    slope_ref[rows, lanes(base + s, unit)] = slope


def interior(inputs, weight, n):
    channels, length = inputs.shape
    group = weight.shape[1]
    block = length // n
    outs = [((channels, block), BF16, True)] * n
    outs += [((channels, length), F32, True), ((channels, length + 2 * DILATION_STEP), BF16, True)]
    outs += [((3, channels, group), BF16, True)] * 2
    results = kernel_call(
        "interior", functools.partial(interior_kernel, n), [(inputs, False), (weight, True)], outs, [DMA],
    )
    return results[:n], *results[n:]


def near_kernel(n, near_ref, plain_ref, *rest):
    active_refs, (slope_ref, wide) = rest[n + 2:n + 2 + n], rest[n + 2 + n:]
    ch, odd = lax.axis_index("ch"), odd_place()
    channels, length = slope_ref.shape
    group = plain_ref.shape[2]
    halo = near_ref.shape[1]
    block = length // n
    unit = min(block, 256)
    groups = [slice(g, g + group) for g in range(0, channels, group)]
    wide[:, lanes((1 - odd) * (halo + length), halo)] = near_ref[...]
    first = (1 - odd) * (length - halo)
    for k in range(n):
        base = (ch ^ k) * block

        @pl.when((base >= first) & (base < first + halo))
        def _(k=k, base=base):
            for s in range(0, block, unit):
                for rows in groups:
                    active, slope = gelu_and_slope(convolve(plain_ref, rows, wide, base + s, halo, unit))
                    active_refs[k][rows, s:s + unit] = active.astype(BF16)
                    slope_ref[rows, lanes(base + s, unit)] = slope


def near_end(near, plain, active, slope, wide):
    n = len(active)
    operands = [(o, True) for o in (near, plain, *active, slope, wide)]
    outs = [(a.shape, a.dtype, True) for a in (*active, slope, wide)]
    results = kernel_call(
        "near_end", functools.partial(near_kernel, n), operands, outs,
        aliases={2 + i: i for i in range(n + 2)},
    )
    return results[:n], *results[n:]


def grad_kernel(n, slope_ref, *rest):
    up_refs, (grad_ref, near_out) = rest[:n], rest[n:]
    ch, odd = lax.axis_index("ch"), odd_place()
    length, halo = grad_ref.shape[1], near_out.shape[1]
    block = length // n
    first = odd * (length - halo)
    for k in range(n):
        base = (ch ^ k) * block

        @pl.when((base < first) | (base >= first + halo))
        def _(k=k, base=base):
            here = lanes(base, block)
            grad_ref[:, here] = (up_refs[k][...].astype(F32) * slope_ref[:, here]).astype(BF16)
    near_out[...] = grad_ref[:, lanes((1 - odd) * (length - halo), halo)]


def grad_conv(slope, ups):
    channels = slope.shape[0]
    return kernel_call(
        "grad_conv", functools.partial(grad_kernel, len(ups)), [(o, True) for o in (slope, *ups)],
        [(slope.shape, BF16, True), ((channels, DILATION_STEP), BF16, True)],
    )


def far_kernel(n, far_ref, plain_ref, *rest):
    up_refs, rest = rest[:n], rest[n + n + 2:]
    active_refs, (wide, grad_ref, far_out) = rest[:n], rest[n:]
    ch, odd = lax.axis_index("ch"), odd_place()
    channels, length = grad_ref.shape
    group = plain_ref.shape[2]
    halo = far_ref.shape[1]
    block = length // n
    unit = min(block, 256)
    groups = [slice(g, g + group) for g in range(0, channels, group)]
    wide[:, lanes(odd * (halo + length), halo)] = far_ref[...]
    first = odd * (length - halo)
    for k in range(n):
        base = (ch ^ k) * block

        @pl.when((base >= first) & (base < first + halo))
        def _(k=k, base=base):
            for s in range(0, block, unit):
                for rows in groups:
                    active, slope = gelu_and_slope(convolve(plain_ref, rows, wide, base + s, halo, unit))
                    active_refs[k][rows, s:s + unit] = active.astype(BF16)
                    grad = (up_refs[k][rows, s:s + unit].astype(F32) * slope).astype(BF16)
                    grad_ref[rows, lanes(base + s, unit)] = grad
                    far_out[rows, lanes(base + s - first, unit)] = grad


def far_end(far, plain, ups, active, wide, grad):
    n = len(active)
    operands = [(o, True) for o in (far, plain, *ups, *active, wide, grad)]
    outs = [(a.shape, BF16, True) for a in (*active, wide, grad, far)]
    results = kernel_call(
        "far_end", functools.partial(far_kernel, n), operands, outs,
        aliases={2 + n + i: i for i in range(n + 2)},
    )
    return results[:n], *results[n + 1:]


def columns_times(order, pw_ref, rows, pieces):
    channels = pieces.shape[0] // len(order)
    if channels % 128 != 0:
        return dot(pw_ref[rows, :], pieces)
    return sum(
        dot(
            pw_ref[rows, lanes((lax.axis_index("ch") ^ k) * channels, channels)],
            pieces[place * channels:(place + 1) * channels],
        )
        for place, k in enumerate(order)
    )


def half_mix_kernel(order, pw_ref, *rest):
    piece_refs, sum_ref = rest[:-1], rest[-1]
    pieces = jnp.concatenate([p[...] for p in piece_refs], axis=0)
    step = 512
    for m in range(0, sum_ref.shape[0], step):
        rows = slice(m, m + step)
        sum_ref[rows, :] = columns_times(order, pw_ref, rows, pieces)


def last_mix_kernel(order, pw_ref, sum_ref, *rest):
    piece_refs, (out_ref, done_ref, held, sems) = rest[:-4], rest[-4:]
    pieces = jnp.concatenate([p[...] for p in piece_refs], axis=0)
    step = 512
    copies = []
    for m in range(0, sum_ref.shape[0], step):
        rows = slice(m, m + step)
        held[rows, :] = (sum_ref[rows, :] + columns_times(order, pw_ref, rows, pieces)).astype(BF16)
        copies.append(pltpu.make_async_copy(held.at[rows, :], out_ref.at[rows, :], sems.at[len(copies)]))
        copies[-1].start()
    done_ref[...] = jnp.zeros_like(done_ref)
    for copy in copies:
        copy.wait()


def back(turned_ref, rows, taps):
    return sum(dot(turned_ref[t, rows, :], tap) for t, tap in enumerate(taps)).astype(BF16)


def back_interior_kernel(grad_ref, turned_ref, out_ref, held, sem):
    channels, length = grad_ref.shape
    group, halo, unit = turned_ref.shape[2], DILATION_STEP, 256
    for g in range(0, channels, group):
        rows = slice(g, g + group)
        for s in range(0, length - 2 * halo, unit):
            held[rows, s:s + unit] = back(
                turned_ref, rows, [grad_ref[rows, s + t * halo:s + t * halo + unit] for t in range(3)]
            )
    copy = pltpu.make_async_copy(held, out_ref.at[:, halo:length - halo], sem)
    copy.start()
    copy.wait()


def back_ends_kernel(grad_ref, near_ref, far_ref, turned_ref, _, __, out_ref, halos, held, sems):
    channels, length = grad_ref.shape
    group, halo, unit = turned_ref.shape[2], DILATION_STEP, 256
    odd = odd_place()
    halos[:, lanes((1 - odd) * halo, halo)] = near_ref[...]
    halos[:, lanes(odd * halo, halo)] = far_ref[...]
    copies = []
    for end in range(2):
        for g in range(0, channels, group):
            rows = slice(g, g + group)
            for s in range(0, halo, unit):
                inner = (length - 2 * halo) * end + s
                taps = [
                    grad_ref[rows, inner:inner + unit],
                    grad_ref[rows, inner + halo:inner + halo + unit],
                ]
                outer = halos[rows, end * halo + s:end * halo + s + unit]
                taps = taps + [outer] if end else [outer] + taps
                held[rows, end * halo + s:end * halo + s + unit] = back(turned_ref, rows, taps)
        copies.append(pltpu.make_async_copy(
            held.at[:, end * halo:(end + 1) * halo],
            out_ref.at[:, end * (length - halo):end * (length - halo) + halo], sems.at[end],
        ))
        copies[-1].start()
    for copy in copies:
        copy.wait()


def exchange(piece, k):
    if k == 0:
        return piece
    return lax.ppermute(piece, "ch", [(i, i ^ k) for i in range(lax.axis_size("ch"))])


def swap(values, first):
    size = lax.axis_size("ctx")
    pairs = [(i, i + 1) for i in range(first, size - 1, 2)]
    return lax.ppermute(values, "ctx", pairs + [(b, a) for a, b in pairs])


def body(inputs, conv_weight, pw_weight, cotangent):
    n = lax.axis_size("ch")
    channels, length = inputs.shape
    total, width = cotangent.shape
    halo = DILATION_STEP
    order = list(range(n - 1, -1, -1))
    parts = order[:n // 2], order[n // 2:]

    near, far = kernel_call(
        "ends", ends_kernel, [(inputs, False)], [((channels, halo), BF16, True)] * 2, [DMA((2,))]
    )
    near, far = swap(near, 0), swap(far, 1)
    ups = {}
    for part in parts:
        pieces = upstream(pw_weight, cotangent, channels, part)
        ups.update({k: exchange(p, k) for k, p in zip(part, pieces)})
    ups = [ups[k] for k in range(n)]

    weight = lax.dynamic_slice_in_dim(
        jnp.swapaxes(conv_weight, 1, 2), lax.axis_index("ch") * channels, channels, 2
    )
    active, slope, wide, plain, turned = interior(inputs, weight, n)
    active, slope, wide = near_end(near, plain, active, slope, wide)
    grad, near_grad = grad_conv(slope, ups)
    near_grad = swap(near_grad, 0)
    active, grad, far_grad = far_end(far, plain, ups, active, wide, grad)
    active = {k: exchange(active[k], k) for k in order}
    far_grad = swap(far_grad, 1)

    grad_shape = ((channels, length), BF16, False)
    (grad_inputs,) = kernel_call(
        "back_interior", back_interior_kernel, [(grad, True), (turned, True)], [grad_shape],
        [pltpu.VMEM((channels, length - 2 * halo), BF16), DMA],
    )
    (partial,) = kernel_call(
        "half_mix", functools.partial(half_mix_kernel, parts[1]),
        [(o, True) for o in (columns_of(pw_weight, channels, parts[1]), *[active[k] for k in parts[1]])],
        [((total, width), F32, True)],
    )
    mixed, done = kernel_call(
        "last_mix", functools.partial(last_mix_kernel, parts[0]),
        [(o, True) for o in (columns_of(pw_weight, channels, parts[0]), partial, *[active[k] for k in parts[0]])],
        [((total, width), BF16, False), ((8, 128), F32, True)],
        [pltpu.VMEM((total, width), BF16), DMA((total // 512,))],
    )
    (grad_inputs,) = kernel_call(
        "back_ends", back_ends_kernel,
        [(o, True) for o in (grad, near_grad, far_grad, turned, done)] + [(grad_inputs, False)], [grad_shape],
        [pltpu.VMEM((channels, 2 * halo), BF16)] * 2 + [DMA((2,))], {5: 0},
    )
    return mixed, grad_inputs


def solution(mesh):
    placed = (P("ch", "ctx"), P(), P(), P(None, ("ctx", "ch")))
    return jax.shard_map(
        body,
        mesh=mesh,
        in_specs=placed,
        out_specs=(P(None, ("ctx", "ch")), P("ch", "ctx")),
        check_vma=False,
    )
```

time: 65.4 us -> 58 us (0.89)
  the two profiles are of different devices: /device:TPU:11 before, /device:TPU:0 now
where the time goes in v4:
time: 58 us; the launch traced here: 57.5 us
  waiting for transfers between devices  22.4 us (39%)
  Pallas kernels  18.7 us (32%)
  starting transfers between devices  12.9 us (22%)
  local copies, waits for them, and re-layouts  2.39 us (4%)
  between operations  0.99 us (2%)
    ppermute x6, waiting for transfers between devices, exchange(): lax.ppermute(piece, 'ch', [(i, i ^ k) for i in range(lax.axis_size('ch'))])  22.4 us
    pallas_call x11, Pallas kernels, kernel_call(): pl.pallas_call(kernel, in_specs=[INSIDE if held else ANY for _, held in o...  18.7 us
    ppermute x4, starting transfers between devices, swap(): return lax.ppermute(values, 'ctx', pairs + [(b, a) for a, b in pairs])  8.86 us
    ppermute x6, starting transfers between devices, exchange(): lax.ppermute(piece, 'ch', [(i, i ^ k) for i in range(lax.axis_size('ch'))])  4.07 us
    unnamed x10, local copies, waits for them, and re-layouts  2.36 us
  transfers between devices with their start and end apart: 10, of which 4 were waited for; matrix products, arithmetic and copies ran while one was open for 0% of the time, Pallas kernels for 25%

profile of v4, /device:TPU:0, one launch (start us, length us, event | category | flops | bytes accessed | tf_op | source)
XLA Modules:
  0.0 57.5 jit_solution(11369174959314533715)
XLA Ops:
  0.6 0.0 copy-start
  0.7 2.2 %ends.1 = (bf16[384,512]{1,0:T(8,128)(2,1)}, bf16[384,512]{1,0:T(8,128)(2,1)}) custom-call(bf16[384,2048]{1,0:T(8,128)(2,1)} %x_ref.3), custom_call_target="tpu_custom_call" | custom-call | tf_op jit(solution)/shard_map/ends/pallas_call | solution.py:18
  2.8 3.0 %collective-permute-start.4 = (bf16[384,512]{1,0:T(8,128)(2,1)}, bf16[384,512]{1,0:T(8,128)(2,1)S(1)}, u32[]{:S(2)}, u32[]{:S(2)}) collective-permute-start(bf16[384,512]{1,0:T(8,128)(2,1)} %get-tuple-element.38), channel_id=1, source_target_pairs={{0,4},{8,12},{16,20},{24,28},{4,0},{12,8},{20,16},{28,24},{1,5},{9... | collective-permute-start | bytes 1179656 | tf_op jit(solution)/shard_map/ppermute | solution.py:337
  5.8 2.3 %copy-done.1 = bf16[1536,1536]{1,0:T(8,128)(2,1)S(1)} copy-done((bf16[1536,1536]{1,0:T(8,128)(2,1)S(1)}, bf16[1536,1536]{1,0:T(8,128)(2,1)}, u32[]{:S(2)}) %copy-start.1) | copy-done | bytes 4718616
  8.2 1.6 %upstream.2 = (bf16[384,512]{1,0:T(8,128)(2,1)}, bf16[384,512]{1,0:T(8,128)(2,1)S(1)}) custom-call(bf16[1536,1536]{1,0:T(8,128)(2,1)S(1)} %copy-done.1, bf16[1536,512]{1,0:T(8,128)(2,1)S(1)} %copy-done.2), custom_call_target="tpu_custom_call" | custom-call | tf_op jit(solution)/shard_map/upstream/pallas_call | solution.py:18
  9.8 2.2 %upstream.3 = (bf16[384,512]{1,0:T(8,128)(2,1)}, bf16[384,512]{1,0:T(8,128)(2,1)}) custom-call(bf16[1536,1536]{1,0:T(8,128)(2,1)S(1)} %copy-done.1, bf16[1536,512]{1,0:T(8,128)(2,1)S(1)} %copy-done.2), custom_call_target="tpu_custom_call" | custom-call | tf_op jit(solution)/shard_map/upstream/pallas_call | solution.py:18
  12.0 1.5 %collective-permute-start.2 = (bf16[384,512]{1,0:T(8,128)(2,1)}, bf16[384,512]{1,0:T(8,128)(2,1)S(1)}, u32[]{:S(2)}, u32[]{:S(2)}) collective-permute-start(bf16[384,512]{1,0:T(8,128)(2,1)} %get-tuple-element.36), channel_id=1, source_target_pairs={{0,2},{1,3},{2,0},{3,1},{4,6},{5,7},{6,4},{7,5},{8,10},{9,11},{10,... | collective-permute-start | bytes 1179656 | tf_op jit(solution)/shard_map/ppermute | solution.py:331
  13.5 0.3 collective-permute-start.3
  13.8 0.7 %collective-permute-start = (bf16[384,512]{1,0:T(8,128)(2,1)}, bf16[384,512]{1,0:T(8,128)(2,1)S(1)}, u32[]{:S(2)}, u32[]{:S(2)}) collective-permute-start(bf16[384,512]{1,0:T(8,128)(2,1)} %get-tuple-element.32), channel_id=1, source_target_pairs={{4,8},{12,16},{20,24},{8,4},{16,12},{24,20},{5,9},{13,17},{21,25},... | collective-permute-start | bytes 1179656 | tf_op jit(solution)/shard_map/ppermute | solution.py:337
  14.6 3.2 %interior.1 = (bf16[384,512]{1,0:T(8,128)(2,1)S(1)}, bf16[384,512]{1,0:T(8,128)(2,1)S(1)}, bf16[384,512]{1,0:T(8,128)(2,1)S(1)}, bf16[384,512]{1,0:T(8,128)(2,1)...) custom-call(bf16[384,2048]{1,0:T(8,128)(2,1)} %x_ref.3, ...), custom_call_target="tpu_custom_call" | custom-call | tf_op jit(solution)/shard_map/interior/pallas_call | solution.py:18
  17.8 0.0 collective-permute-done.4.near_ref
  17.8 0.8 %near_end.1 = (bf16[384,512]{1,0:T(8,128)(2,1)S(1)}, bf16[384,512]{1,0:T(8,128)(2,1)S(1)}, bf16[384,512]{1,0:T(8,128)(2,1)S(1)}, bf16[384,512]{1,0:T(8,128)(2,1)...) custom-call(bf16[384,512]{1,0:T(8,128)(2,1)S(1)} %collective-permute, ...), custom_call_target="tpu_custom_call", output_to_operand_aliasing={{0}: (2, {}), {1}: (3, {}), {2}: (4, {}), {3}: (5, {}), {4}... | custom-call | tf_op jit(solution)/shard_map/near_end/pallas_call | solution.py:18
  18.5 0.0 collective-permute-done.1.rest_1_
  18.6 5.5 %collective-permute-done.2.rest_2_ = bf16[384,512]{1,0:T(8,128)(2,1)S(1)} collective-permute-done((bf16[384,512]{1,0:T(8,128)(2,1)}, bf16[384,512]{1,0:T(8,128)(2,1)S(1)}, u32[]{:S(2)}, u32[]{:S(2)}) %collective-permute-start.2) | collective-permute-done | bytes 393248 | tf_op jit(solution)/shard_map/ppermute | solution.py:331
  24.1 7.7 %collective-permute-done.3.rest_3_ = bf16[384,512]{1,0:T(8,128)(2,1)S(1)} collective-permute-done((bf16[384,512]{1,0:T(8,128)(2,1)}, bf16[384,512]{1,0:T(8,128)(2,1)S(1)}, u32[]{:S(2)}, u32[]{:S(2)}) %collective-permute-start.3) | collective-permute-done | bytes 393248 | tf_op jit(solution)/shard_map/ppermute | solution.py:331
  31.8 0.3 grad_conv.1
  32.1 0.0 slice-start
  32.1 0.0 slice-start.1
  32.1 0.9 %far_end.1 = (bf16[384,512]{1,0:T(8,128)(2,1)S(1)}, bf16[384,512]{1,0:T(8,128)(2,1)S(1)}, bf16[384,512]{1,0:T(8,128)(2,1)S(1)}, bf16[384,512]{1,0:T(8,128)(2,1)S...) custom-call(bf16[384,512]{1,0:T(8,128)(2,1)S(1)} %collective-permute, ...), custom_call_target="tpu_custom_call", output_to_operand_aliasing={{0}: (6, {}), {1}: (7, {}), {2}: (8, {}), {3}: (9, {}), {4}... | custom-call | tf_op jit(solution)/shard_map/far_end/pallas_call | solution.py:18
  33.0 0.3 collective-permute-start.5
  33.2 1.4 %collective-permute-start.6 = (bf16[384,512]{1,0:T(8,128)(2,1)S(1)}, bf16[384,512]{1,0:T(8,128)(2,1)S(1)}, u32[]{:S(2)}, u32[]{:S(2)}) collective-permute-start(bf16[384,512]{1,0:T(8,128)(2,1)S(1)} %get-tuple-element.54), channel_id=1, source_target_pairs={{0,3},{1,2},{2,1},{3,0},{4,7},{5,6},{6,5},{7,4},{8,11},{9,10},{10,... | collective-permute-start | bytes 1179656 | tf_op jit(solution)/shard_map/ppermute | solution.py:331
  34.6 0.5 collective-permute-start.7
  35.2 0.9 %collective-permute-start.9 = (bf16[384,512]{1,0:T(8,128)(2,1)S(1)}, bf16[384,512]{1,0:T(8,128)(2,1)S(1)}, u32[]{:S(2)}, u32[]{:S(2)}) collective-permute-start(bf16[384,512]{1,0:T(8,128)(2,1)S(1)} %get-tuple-element.59), channel_id=1, source_target_pairs={{4,8},{12,16},{20,24},{8,4},{16,12},{24,20},{5,9},{13,17},{21,25},... | collective-permute-start | bytes 1179656 | tf_op jit(solution)/shard_map/ppermute | solution.py:337
  36.0 4.3 %collective-permute-start.8 = (bf16[384,512]{1,0:T(8,128)(2,1)S(1)}, bf16[384,512]{1,0:T(8,128)(2,1)S(1)}, u32[]{:S(2)}, u32[]{:S(2)}) collective-permute-start(bf16[384,512]{1,0:T(8,128)(2,1)S(1)} %get-tuple-element.58), channel_id=1, source_target_pairs={{0,4},{8,12},{16,20},{24,28},{4,0},{12,8},{20,16},{28,24},{1,5},{9... | collective-permute-start | bytes 1179656 | tf_op jit(solution)/shard_map/ppermute | solution.py:337
  40.4 1.7 %back_interior.1.__ = bf16[384,2048]{1,0:T(8,128)(2,1)} custom-call(bf16[384,2048]{1,0:T(8,128)(2,1)S(1)} %get-tuple-element.57.grad_ref, bf16[3,384,96]{2,1,0:T(8,128)(2,1)S(1)} %get-tuple-element.60.turned_ref), custom_call_target="tpu_custom_call" | custom-call | tf_op jit(solution)/shard_map/back_interior/pallas_call | solution.py:18
  42.0 0.0 collective-permute-done.5.rest_0_
  42.1 1.8 %half_mix.1.sum_ref = f32[1536,512]{1,0:T(8,128)S(1)} custom-call(bf16[1536,1536]{1,0:T(8,128)(2,1)S(1)} %bitcast.3, bf16[384,512]{1,0:T(8,128)(2,1)S(1)} %collective-permute-done.5.rest_0_, bf16[384,512]{1,0:T(8,128)(2,1)S(1)} %get-tuple-element.53.rest_1_), custom_call_target="tpu_custom_call" | custom-call | tf_op jit(solution)/shard_map/half_mix/pallas_call | solution.py:18
  43.9 0.4 collective-permute-done.6.rest_0_
  44.2 8.8 %collective-permute-done.7.rest_1_ = bf16[384,512]{1,0:T(8,128)(2,1)S(1)} collective-permute-done((bf16[384,512]{1,0:T(8,128)(2,1)S(1)}, bf16[384,512]{1,0:T(8,128)(2,1)S(1)}, u32[]{:S(2)}, u32[]{:S(2)}) %collective-permute-start.7) | collective-permute-done | bytes 393248 | tf_op jit(solution)/shard_map/ppermute | solution.py:331
  53.1 2.6 %last_mix.1 = (bf16[1536,512]{1,0:T(8,128)(2,1)}, f32[8,128]{1,0:T(8,128)S(1)}) custom-call(bf16[1536,1536]{1,0:T(8,128)(2,1)S(1)} %bitcast.3, f32[1536,512]{1,0:T(8,128)S(1)} %half_mix.1.sum_ref, bf16[384,512]{1,0:T(8,128)(2,1)S(1)} %collective-permute-done.6.rest_0_, bf16[384,512]{1,0:T(8,128)(2,1)S(1)} %collective-permute-done.7.rest_1_), custom_call_target="tpu_custom_call" | custom-call | tf_op jit(solution)/shard_map/last_mix/pallas_call | solution.py:18
  55.7 0.0 collective-permute-done.8.near_ref
  55.7 1.6 %back_ends.1 = bf16[384,2048]{1,0:T(8,128)(2,1)} custom-call(bf16[384,2048]{1,0:T(8,128)(2,1)S(1)} %get-tuple-element.57.grad_ref, bf16[384,512]{1,0:T(8,128)(2,1)S(1)} %collective-permute-done.8.near_ref, bf16[384,512]{1,0:T(8,128)(2,1)S(1)} %collective-permute-done.9.far_ref, ...), custom_call_target="tpu_custom_call", output_to_operand_aliasing={{}: (5, {})} | custom-call | tf_op jit(solution)/shard_map/back_ends/pallas_call | solution.py:18
  (11 shorter events, 0.1 us)
Async XLA Ops:
  0.6 13.9 %copy-start = (bf16[3,1536,96]{1,2,0:T(8,128)(2,1)S(1)}, bf16[3,1536,96]{1,2,0:T(8,128)(2,1)}, u32[]{:S(2)}) copy-start(bf16[3,1536,96]{1,2,0:T(8,128)(2,1)} %param.5) | copy-start | bytes 2654212
  0.6 5.2 %copy-start.2 = (bf16[1536,512]{1,0:T(8,128)(2,1)S(1)}, bf16[1536,512]{1,0:T(8,128)(2,1)}, u32[]{:S(2)}) copy-start(bf16[1536,512]{1,0:T(8,128)(2,1)} %cot_ref.3) | copy-start | bytes 4718596
  2.8 14.9 %collective-permute-start.4 = (bf16[384,512]{1,0:T(8,128)(2,1)}, bf16[384,512]{1,0:T(8,128)(2,1)S(1)}, u32[]{:S(2)}, u32[]{:S(2)}) collective-permute-start(bf16[384,512]{1,0:T(8,128)(2,1)} %get-tuple-element.38), channel_id=1, source_target_pairs={{0,4},{8,12},{16,20},{24,28},{4,0},{12,8},{20,16},{28,24},{1,5},{9... | collective-permute-start | bytes 1179656 | tf_op jit(solution)/shard_map/ppermute | solution.py:337
  5.8 2.3 %copy-start.1 = (bf16[1536,1536]{1,0:T(8,128)(2,1)S(1)}, bf16[1536,1536]{1,0:T(8,128)(2,1)}, u32[]{:S(2)}) copy-start(bf16[1536,1536]{1,0:T(8,128)(2,1)} %pw_ref.7) | copy-start | bytes 14155780
  9.8 8.8 %collective-permute-start.1 = (bf16[384,512]{1,0:T(8,128)(2,1)}, bf16[384,512]{1,0:T(8,128)(2,1)S(1)}, u32[]{:S(2)}, u32[]{:S(2)}) collective-permute-start(bf16[384,512]{1,0:T(8,128)(2,1)} %get-tuple-element.35), channel_id=1, source_target_pairs={{0,1},{1,0},{2,3},{3,2},{4,5},{5,4},{6,7},{7,6},{8,9},{9,8},{10,11... | collective-permute-start | bytes 1179656 | tf_op jit(solution)/shard_map/ppermute | solution.py:331
  12.0 12.1 %collective-permute-start.2 = (bf16[384,512]{1,0:T(8,128)(2,1)}, bf16[384,512]{1,0:T(8,128)(2,1)S(1)}, u32[]{:S(2)}, u32[]{:S(2)}) collective-permute-start(bf16[384,512]{1,0:T(8,128)(2,1)} %get-tuple-element.36), channel_id=1, source_target_pairs={{0,2},{1,3},{2,0},{3,1},{4,6},{5,7},{6,4},{7,5},{8,10},{9,11},{10,... | collective-permute-start | bytes 1179656 | tf_op jit(solution)/shard_map/ppermute | solution.py:331
  13.5 18.3 %collective-permute-start.3 = (bf16[384,512]{1,0:T(8,128)(2,1)}, bf16[384,512]{1,0:T(8,128)(2,1)S(1)}, u32[]{:S(2)}, u32[]{:S(2)}) collective-permute-start(bf16[384,512]{1,0:T(8,128)(2,1)} %get-tuple-element.37), channel_id=1, source_target_pairs={{0,3},{1,2},{2,1},{3,0},{4,7},{5,6},{6,5},{7,4},{8,11},{9,10},{10,... | collective-permute-start | bytes 1179656 | tf_op jit(solution)/shard_map/ppermute | solution.py:331
  13.8 18.2 %collective-permute-start = (bf16[384,512]{1,0:T(8,128)(2,1)}, bf16[384,512]{1,0:T(8,128)(2,1)S(1)}, u32[]{:S(2)}, u32[]{:S(2)}) collective-permute-start(bf16[384,512]{1,0:T(8,128)(2,1)} %get-tuple-element.32), channel_id=1, source_target_pairs={{4,8},{12,16},{20,24},{8,4},{16,12},{24,20},{5,9},{13,17},{21,25},... | collective-permute-start | bytes 1179656 | tf_op jit(solution)/shard_map/ppermute | solution.py:337
  32.1 10.0 %slice-start = ((s8[4718592]{0:T(1024)(128)(4,1)}), s8[4194304]{0:T(1024)(128)(4,1)S(1)}, s32[]{:S(2)}) async-start(s8[4718592]{0:T(1024)(128)(4,1)} %bitcast.2), calls=%async_computation | async-start | bytes 8388608
  32.1 10.0 %slice-start.1 = ((s8[4718592]{0:T(1024)(128)(4,1)}), s8[524288]{0:T(1024)(128)(4,1)S(1)}, s32[]{:S(2)}) async-start(s8[4718592]{0:T(1024)(128)(4,1)} %bitcast.2), calls=%async_computation.1 | async-start | bytes 1048576
  33.0 9.1 %collective-permute-start.5 = (bf16[384,512]{1,0:T(8,128)(2,1)S(1)}, bf16[384,512]{1,0:T(8,128)(2,1)S(1)}, u32[]{:S(2)}, u32[]{:S(2)}) collective-permute-start(bf16[384,512]{1,0:T(8,128)(2,1)S(1)} %get-tuple-element.52), channel_id=1, source_target_pairs={{0,1},{1,0},{2,3},{3,2},{4,5},{5,4},{6,7},{7,6},{8,9},{9,8},{10,11... | collective-permute-start | bytes 1179656 | tf_op jit(solution)/shard_map/ppermute | solution.py:331
  33.2 11.0 %collective-permute-start.6 = (bf16[384,512]{1,0:T(8,128)(2,1)S(1)}, bf16[384,512]{1,0:T(8,128)(2,1)S(1)}, u32[]{:S(2)}, u32[]{:S(2)}) collective-permute-start(bf16[384,512]{1,0:T(8,128)(2,1)S(1)} %get-tuple-element.54), channel_id=1, source_target_pairs={{0,3},{1,2},{2,1},{3,0},{4,7},{5,6},{6,5},{7,4},{8,11},{9,10},{10,... | collective-permute-start | bytes 1179656 | tf_op jit(solution)/shard_map/ppermute | solution.py:331
  34.6 18.4 %collective-permute-start.7 = (bf16[384,512]{1,0:T(8,128)(2,1)S(1)}, bf16[384,512]{1,0:T(8,128)(2,1)S(1)}, u32[]{:S(2)}, u32[]{:S(2)}) collective-permute-start(bf16[384,512]{1,0:T(8,128)(2,1)S(1)} %get-tuple-element.55), channel_id=1, source_target_pairs={{0,2},{1,3},{2,0},{3,1},{4,6},{5,7},{6,4},{7,5},{8,10},{9,11},{10,... | collective-permute-start | bytes 1179656 | tf_op jit(solution)/shard_map/ppermute | solution.py:331
  35.2 20.5 %collective-permute-start.9 = (bf16[384,512]{1,0:T(8,128)(2,1)S(1)}, bf16[384,512]{1,0:T(8,128)(2,1)S(1)}, u32[]{:S(2)}, u32[]{:S(2)}) collective-permute-start(bf16[384,512]{1,0:T(8,128)(2,1)S(1)} %get-tuple-element.59), channel_id=1, source_target_pairs={{4,8},{12,16},{20,24},{8,4},{16,12},{24,20},{5,9},{13,17},{21,25},... | collective-permute-start | bytes 1179656 | tf_op jit(solution)/shard_map/ppermute | solution.py:337
  36.0 19.7 %collective-permute-start.8 = (bf16[384,512]{1,0:T(8,128)(2,1)S(1)}, bf16[384,512]{1,0:T(8,128)(2,1)S(1)}, u32[]{:S(2)}, u32[]{:S(2)}) collective-permute-start(bf16[384,512]{1,0:T(8,128)(2,1)S(1)} %get-tuple-element.58), channel_id=1, source_target_pairs={{0,4},{8,12},{16,20},{24,28},{4,0},{12,8},{20,16},{28,24},{1,5},{9... | collective-permute-start | bytes 1179656 | tf_op jit(solution)/shard_map/ppermute | solution.py:337

commit v5 on v4

--- a/solution.py
+++ b/solution.py
@@ -60,28 +60,41 @@
     return lax.axis_index("ctx") % 2
 
 
-def ends_kernel(x_ref, near_ref, far_ref, sems):
-    odd = odd_place()
-    length, halo = x_ref.shape[1], near_ref.shape[1]
-    copies = [
-        pltpu.make_async_copy(x_ref.at[:, lanes(at_end * (length - halo), halo)], end_ref, sems.at[place])
-        for place, (end_ref, at_end) in enumerate(((near_ref, 1 - odd), (far_ref, odd)))
-    ]
-    for copy in copies:
-        copy.start()
-    for copy in copies:
-        copy.wait()
-
-
-def upstream_kernel(order, channels, pw_ref, cot_ref, *piece_refs):
+def upstream_kernel(order, channels, near, pw_ref, cot_ref, x_ref, *rest):
+    count = len(order)
+    piece_refs, (end_ref, columns_ref, cot_in, sems) = rest[:count], rest[count:]
+    ch, odd = lax.axis_index("ch"), odd_place()
+    length, halo = x_ref.shape[1], end_ref.shape[1]
+    whole = pltpu.make_async_copy(cot_ref, cot_in, sems.at[count])
+    whole.start()
+    blocks = []
     if channels % 128 == 0:
-        for k, piece_ref in zip(order, piece_refs):
-            columns = lanes((lax.axis_index("ch") ^ k) * channels, channels)
-            piece_ref[...] = turned_dot(pw_ref[:, columns], cot_ref[...]).astype(BF16)
+        for place, k in enumerate(order):
+            blocks.append(pltpu.make_async_copy(
+                pw_ref.at[:, lanes((ch ^ k) * channels, channels)],
+                columns_ref.at[:, place * channels:(place + 1) * channels], sems.at[place],
+            ))
     else:
-        result = turned_dot(pw_ref[...], cot_ref[...]).astype(BF16)
-        for place, piece_ref in enumerate(piece_refs):
-            piece_ref[...] = result[place * channels:(place + 1) * channels]
+        blocks.append(pltpu.make_async_copy(pw_ref, columns_ref, sems.at[0]))
+    for block in blocks:
+        block.start()
+    at_end = 1 - odd if near else odd
+    end = pltpu.make_async_copy(
+        x_ref.at[:, lanes(at_end * (length - halo), halo)], end_ref, sems.at[count + 1]
+    )
+    end.start()
+    whole.wait()
+    if len(blocks) == count:
+        for place in range(count):
+            blocks[place].wait()
+            columns = slice(place * channels, (place + 1) * channels)
+            piece_refs[place][...] = turned_dot(columns_ref[:, columns], cot_in[...]).astype(BF16)
+    else:
+        blocks[0].wait()
+        result = turned_dot(columns_ref[...], cot_in[...]).astype(BF16)
+        for place in range(count):
+            piece_refs[place][...] = result[place * channels:(place + 1) * channels]
+    end.wait()
 
 
 def columns_of(pw_weight, channels, order):
@@ -93,12 +106,17 @@
     )
 
 
-def upstream(pw_weight, cotangent, channels, order):
-    return kernel_call(
-        "upstream", functools.partial(upstream_kernel, order, channels),
-        [(columns_of(pw_weight, channels, order), True), (cotangent, True)],
-        [((channels, cotangent.shape[1]), BF16, True)] * len(order),
-    )
+def upstream(pw_weight, cotangent, inputs, order, near):
+    channels = inputs.shape[0]
+    total, width = cotangent.shape
+    count = len(order)
+    results = kernel_call(
+        "upstream", functools.partial(upstream_kernel, order, channels, near),
+        [(columns_of(pw_weight, channels, order), False), (cotangent, False), (inputs, False)],
+        [((channels, width), BF16, True)] * count + [((channels, DILATION_STEP), BF16, True)],
+        [pltpu.VMEM((total, count * channels), BF16), pltpu.VMEM(cotangent.shape, BF16), DMA((count + 2,))],
+    )
+    return results[:count], results[count]
 
 
 def convolve(w_ref, rows, wide, start, halo, unit):
@@ -147,8 +165,9 @@
     return results[:n], *results[n:]
 
 
-def near_kernel(n, near_ref, plain_ref, *rest):
-    active_refs, (slope_ref, wide) = rest[n + 2:n + 2 + n], rest[n + 2 + n:]
+def near_kernel(n, *refs):
+    up_refs, near_ref, plain_ref, rest = refs[:n], refs[n], refs[n + 1], refs[n + 2 + n + 2:]
+    active_refs, (slope_ref, wide, grad_ref, near_out) = rest[:n], rest[n:]
     ch, odd = lax.axis_index("ch"), odd_place()
     channels, length = slope_ref.shape
     group = plain_ref.shape[2]
@@ -157,7 +176,7 @@
     unit = min(block, 256)
     groups = [slice(g, g + group) for g in range(0, channels, group)]
     wide[:, lanes((1 - odd) * (halo + length), halo)] = near_ref[...]
-    first = (1 - odd) * (length - halo)
+    first, far = (1 - odd) * (length - halo), odd * (length - halo)
     for k in range(n):
         base = (ch ^ k) * block
 
@@ -167,42 +186,26 @@
                 for rows in groups:
                     active, slope = gelu_and_slope(convolve(plain_ref, rows, wide, base + s, halo, unit))
                     active_refs[k][rows, s:s + unit] = active.astype(BF16)
-                    slope_ref[rows, lanes(base + s, unit)] = slope
-
-
-def near_end(near, plain, active, slope, wide):
-    n = len(active)
-    operands = [(o, True) for o in (near, plain, *active, slope, wide)]
-    outs = [(a.shape, a.dtype, True) for a in (*active, slope, wide)]
-    results = kernel_call(
-        "near_end", functools.partial(near_kernel, n), operands, outs,
-        aliases={2 + i: i for i in range(n + 2)},
-    )
-    return results[:n], *results[n:]
-
-
-def grad_kernel(n, slope_ref, *rest):
-    up_refs, (grad_ref, near_out) = rest[:n], rest[n:]
-    ch, odd = lax.axis_index("ch"), odd_place()
-    length, halo = grad_ref.shape[1], near_out.shape[1]
-    block = length // n
-    first = odd * (length - halo)
-    for k in range(n):
-        base = (ch ^ k) * block
-
-        @pl.when((base < first) | (base >= first + halo))
+                    grad = (up_refs[k][rows, s:s + unit].astype(F32) * slope).astype(BF16)
+                    grad_ref[rows, lanes(base + s, unit)] = grad
+                    near_out[rows, lanes(base + s - first, unit)] = grad
+
+        @pl.when((base >= halo) & (base < length - halo))
         def _(k=k, base=base):
             here = lanes(base, block)
             grad_ref[:, here] = (up_refs[k][...].astype(F32) * slope_ref[:, here]).astype(BF16)
-    near_out[...] = grad_ref[:, lanes((1 - odd) * (length - halo), halo)]
-
-
-def grad_conv(slope, ups):
-    channels = slope.shape[0]
-    return kernel_call(
-        "grad_conv", functools.partial(grad_kernel, len(ups)), [(o, True) for o in (slope, *ups)],
-        [(slope.shape, BF16, True), ((channels, DILATION_STEP), BF16, True)],
-    )
+
+
+def near_end(order, ups, near, plain, active, slope, wide):
+    n = len(active)
+    operands = [(o, True) for o in (*ups, near, plain, *active, slope, wide)]
+    outs = [(a.shape, a.dtype, True) for a in (*active, slope, wide)]
+    outs += [(slope.shape, BF16, True), (near.shape, BF16, True)]
+    results = kernel_call(
+        "near_end", functools.partial(near_kernel, n), operands, outs,
+        aliases={n + 2 + i: i for i in range(n + 2)},
+    )
+    return results[:n], *results[n + 1:]
 
 
 def far_kernel(n, far_ref, plain_ref, *rest):
@@ -255,13 +258,24 @@
     )
 
 
-def half_mix_kernel(order, pw_ref, *rest):
-    piece_refs, sum_ref = rest[:-1], rest[-1]
+def mix_kernel(order, pw_ref, *rest):
+    piece_refs, before, sum_ref = rest[:len(order)], rest[len(order):-1], rest[-1]
     pieces = jnp.concatenate([p[...] for p in piece_refs], axis=0)
     step = 512
     for m in range(0, sum_ref.shape[0], step):
         rows = slice(m, m + step)
-        sum_ref[rows, :] = columns_times(order, pw_ref, rows, pieces)
+        part = columns_times(order, pw_ref, rows, pieces)
+        sum_ref[rows, :] = part + before[0][rows, :] if before else part
+
+
+def mix(name, pw_weight, order, active, before):
+    channels, width = active[order[0]].shape
+    operands = [columns_of(pw_weight, channels, order), *[active[k] for k in order], *before]
+    return kernel_call(
+        name, functools.partial(mix_kernel, order), [(o, True) for o in operands],
+        [((pw_weight.shape[0], width), F32, True)],
+        aliases={len(operands) - 1: 0} if before else {},
+    )
 
 
 def last_mix_kernel(order, pw_ref, sum_ref, *rest):
@@ -297,32 +311,36 @@
     copy.wait()
 
 
-def back_ends_kernel(grad_ref, near_ref, far_ref, turned_ref, _, __, out_ref, halos, held, sems):
+def back_end_kernel(near, grad_ref, halo_ref, turned_ref, _, __, out_ref, held, sem):
     channels, length = grad_ref.shape
     group, halo, unit = turned_ref.shape[2], DILATION_STEP, 256
     odd = odd_place()
-    halos[:, lanes((1 - odd) * halo, halo)] = near_ref[...]
-    halos[:, lanes(odd * halo, halo)] = far_ref[...]
-    copies = []
     for end in range(2):
-        for g in range(0, channels, group):
-            rows = slice(g, g + group)
-            for s in range(0, halo, unit):
-                inner = (length - 2 * halo) * end + s
-                taps = [
-                    grad_ref[rows, inner:inner + unit],
-                    grad_ref[rows, inner + halo:inner + halo + unit],
-                ]
-                outer = halos[rows, end * halo + s:end * halo + s + unit]
-                taps = taps + [outer] if end else [outer] + taps
-                held[rows, end * halo + s:end * halo + s + unit] = back(turned_ref, rows, taps)
-        copies.append(pltpu.make_async_copy(
-            held.at[:, end * halo:(end + 1) * halo],
-            out_ref.at[:, end * (length - halo):end * (length - halo) + halo], sems.at[end],
-        ))
-        copies[-1].start()
-    for copy in copies:
-        copy.wait()
+        @pl.when(odd == (1 - end if near else end))
+        def _(end=end):
+            for g in range(0, channels, group):
+                rows = slice(g, g + group)
+                for s in range(0, halo, unit):
+                    inner = (length - 2 * halo) * end + s
+                    taps = [
+                        grad_ref[rows, inner:inner + unit],
+                        grad_ref[rows, inner + halo:inner + halo + unit],
+                    ]
+                    outer = halo_ref[rows, s:s + unit]
+                    taps = taps + [outer] if end else [outer] + taps
+                    held[rows, s:s + unit] = back(turned_ref, rows, taps)
+    at_end = 1 - odd if near else odd
+    copy = pltpu.make_async_copy(held, out_ref.at[:, lanes(at_end * (length - halo), halo)], sem)
+    copy.start()
+    copy.wait()
+
+
+def back_end(name, near, grad, halo, turned, token, grad_inputs):
+    operands = [(o, True) for o in (grad, halo, turned, token)] + [(grad_inputs, False)]
+    return kernel_call(
+        name, functools.partial(back_end_kernel, near), operands, [(grad_inputs.shape, BF16, False)],
+        [pltpu.VMEM(halo.shape, BF16), DMA], {4: 0},
+    )
 
 
 def exchange(piece, k):
@@ -345,48 +363,38 @@
     order = list(range(n - 1, -1, -1))
     parts = order[:n // 2], order[n // 2:]
 
-    near, far = kernel_call(
-        "ends", ends_kernel, [(inputs, False)], [((channels, halo), BF16, True)] * 2, [DMA((2,))]
-    )
-    near, far = swap(near, 0), swap(far, 1)
-    ups = {}
-    for part in parts:
-        pieces = upstream(pw_weight, cotangent, channels, part)
-        ups.update({k: exchange(p, k) for k, p in zip(part, pieces)})
-    ups = [ups[k] for k in range(n)]
-
     weight = lax.dynamic_slice_in_dim(
         jnp.swapaxes(conv_weight, 1, 2), lax.axis_index("ch") * channels, channels, 2
     )
+    ups, halos = {}, []
+    for place, part in enumerate(parts):
+        pieces, end = upstream(pw_weight, cotangent, inputs, part, place == 0)
+        ups.update({k: exchange(p, k) for k, p in zip(part, pieces)})
+        halos.append(swap(end, place))
+    ups = [ups[k] for k in range(n)]
+
     active, slope, wide, plain, turned = interior(inputs, weight, n)
-    active, slope, wide = near_end(near, plain, active, slope, wide)
-    grad, near_grad = grad_conv(slope, ups)
+    active, wide, grad, near_grad = near_end(order, ups, halos[0], plain, active, slope, wide)
     near_grad = swap(near_grad, 0)
-    active, grad, far_grad = far_end(far, plain, ups, active, wide, grad)
+    active, grad, far_grad = far_end(halos[1], plain, ups, active, wide, grad)
     active = {k: exchange(active[k], k) for k in order}
     far_grad = swap(far_grad, 1)
 
-    grad_shape = ((channels, length), BF16, False)
     (grad_inputs,) = kernel_call(
-        "back_interior", back_interior_kernel, [(grad, True), (turned, True)], [grad_shape],
-        [pltpu.VMEM((channels, length - 2 * halo), BF16), DMA],
-    )
-    (partial,) = kernel_call(
-        "half_mix", functools.partial(half_mix_kernel, parts[1]),
-        [(o, True) for o in (columns_of(pw_weight, channels, parts[1]), *[active[k] for k in parts[1]])],
-        [((total, width), F32, True)],
-    )
+        "back_interior", back_interior_kernel, [(grad, True), (turned, True)],
+        [((channels, length), BF16, False)], [pltpu.VMEM((channels, length - 2 * halo), BF16), DMA],
+    )
+    (grad_inputs,) = back_end("back_near", True, grad, near_grad, turned, turned, grad_inputs)
+    early, late = parts[0][:n // 4], parts[0][n // 4:]
+    partial = mix("half_mix", pw_weight, parts[1], active, [])
+    partial = mix("more_mix", pw_weight, early, active, partial)
     mixed, done = kernel_call(
-        "last_mix", functools.partial(last_mix_kernel, parts[0]),
-        [(o, True) for o in (columns_of(pw_weight, channels, parts[0]), partial, *[active[k] for k in parts[0]])],
+        "last_mix", functools.partial(last_mix_kernel, late),
+        [(o, True) for o in (columns_of(pw_weight, channels, late), *partial, *[active[k] for k in late])],
         [((total, width), BF16, False), ((8, 128), F32, True)],
         [pltpu.VMEM((total, width), BF16), DMA((total // 512,))],
     )
-    (grad_inputs,) = kernel_call(
-        "back_ends", back_ends_kernel,
-        [(o, True) for o in (grad, near_grad, far_grad, turned, done)] + [(grad_inputs, False)], [grad_shape],
-        [pltpu.VMEM((channels, 2 * halo), BF16)] * 2 + [DMA((2,))], {5: 0},
-    )
+    (grad_inputs,) = back_end("back_far", False, grad, far_grad, turned, done, grad_inputs)
     return mixed, grad_inputs
 
 

time: 58 us -> 55.3 us (0.953)
  Pallas kernels: 18.7 us -> 22.5 us
  local copies, waits for them, and re-layouts: 2.39 us -> 0.05 us
  waiting for transfers between devices: 22.4 us -> 20.5 us
  starting transfers between devices: 12.9 us -> 11.1 us
    ppermute x6, waiting for transfers between devices: 22.4 us -> 7.03 us  [exchange(): lax.ppermute(piece, 'ch', [(i, i ^ k) for i in range(lax.axis_size('ch'))])]
    ppermute x4, waiting for transfers between devices: 0.01 us -> 13.4 us  [swap(): return lax.ppermute(values, 'ctx', pairs + [(b, a) for a, b in pairs])]
    pallas_call x11, Pallas kernels: 18.7 us -> 22.5 us  [kernel_call(): pl.pallas_call(kernel, in_specs=[INSIDE if held else ANY for _, held in o...]
    ppermute x4, starting transfers between devices: 8.86 us -> 5.49 us  [swap(): return lax.ppermute(values, 'ctx', pairs + [(b, a) for a, b in pairs])]
    unnamed x10 -> x6, local copies, waits for them, and re-layouts: 2.36 us -> 0.02 us
    ppermute x6, starting transfers between devices: 4.07 us -> 5.65 us  [exchange(): lax.ppermute(piece, 'ch', [(i, i ^ k) for i in range(lax.axis_size('ch'))])]
  transfers between devices with their start and end apart: 10 -> 10, of which waited for: 4 -> 3; matrix products, arithmetic and copies ran while one was open for 0% -> 0% of each run, Pallas kernels for 25% -> 30%
where the time goes in v5:
time: 55.3 us; the launch traced here: 55.2 us
  Pallas kernels  22.5 us (41%)
  waiting for transfers between devices  20.5 us (37%)
  starting transfers between devices  11.1 us (20%)
  between operations  0.99 us (2%)
    pallas_call x11, Pallas kernels, kernel_call(): pl.pallas_call(kernel, in_specs=[INSIDE if held else ANY for _, held in o...  22.5 us
    ppermute x4, waiting for transfers between devices, swap(): return lax.ppermute(values, 'ctx', pairs + [(b, a) for a, b in pairs])  13.4 us
    ppermute x6, waiting for transfers between devices, exchange(): lax.ppermute(piece, 'ch', [(i, i ^ k) for i in range(lax.axis_size('ch'))])  7.03 us
    ppermute x6, starting transfers between devices, exchange(): lax.ppermute(piece, 'ch', [(i, i ^ k) for i in range(lax.axis_size('ch'))])  5.65 us
    ppermute x4, starting transfers between devices, swap(): return lax.ppermute(values, 'ctx', pairs + [(b, a) for a, b in pairs])  5.49 us
  transfers between devices with their start and end apart: 10, of which 3 were waited for; matrix products, arithmetic and copies ran while one was open for 0% of the time, Pallas kernels for 30%

profile of v5, /device:TPU:0, one launch (start us, length us, event | category | flops | bytes accessed | tf_op | source)
XLA Modules:
  0.0 55.2 jit_solution(16082096056898128537)
XLA Ops:
  0.6 0.0 copy-start
  0.6 4.5 %upstream.3 = (bf16[384,512]{1,0:T(8,128)(2,1)}, bf16[384,512]{1,0:T(8,128)(2,1)}, bf16[384,512]{1,0:T(8,128)(2,1)}) custom-call(bf16[1536,1536]{1,0:T(8,128)(2,1)} %pw_ref.9, bf16[1536,512]{1,0:T(8,128)(2,1)} %cot_ref.3, bf16[384,2048]{1,0:T(8,128)(2,1)} %x_ref.5), custom_call_target="tpu_custom_call" | custom-call | tf_op jit(solution)/shard_map/upstream/pallas_call | solution.py:18
  5.1 3.0 %collective-permute-start.2 = (bf16[384,512]{1,0:T(8,128)(2,1)}, bf16[384,512]{1,0:T(8,128)(2,1)S(1)}, u32[]{:S(2)}, u32[]{:S(2)}) collective-permute-start(bf16[384,512]{1,0:T(8,128)(2,1)} %get-tuple-element.35), channel_id=1, source_target_pairs={{0,2},{1,3},{2,0},{3,1},{4,6},{5,7},{6,4},{7,5},{8,10},{9,11},{10,... | collective-permute-start | bytes 1179656 | tf_op jit(solution)/shard_map/ppermute | solution.py:349
  8.2 0.0 collective-permute-start.3
  8.2 1.5 %collective-permute-start.4 = (bf16[384,512]{1,0:T(8,128)(2,1)}, bf16[384,512]{1,0:T(8,128)(2,1)S(1)}, u32[]{:S(2)}, u32[]{:S(2)}) collective-permute-start(bf16[384,512]{1,0:T(8,128)(2,1)} %get-tuple-element.37), channel_id=1, source_target_pairs={{0,4},{8,12},{16,20},{24,28},{4,0},{12,8},{20,16},{28,24},{1,5},{9... | collective-permute-start | bytes 1179656 | tf_op jit(solution)/shard_map/ppermute | solution.py:355
  9.7 4.3 %upstream.2 = (bf16[384,512]{1,0:T(8,128)(2,1)}, bf16[384,512]{1,0:T(8,128)(2,1)S(1)}, bf16[384,512]{1,0:T(8,128)(2,1)}) custom-call(bf16[1536,1536]{1,0:T(8,128)(2,1)} %pw_ref.9, bf16[1536,512]{1,0:T(8,128)(2,1)} %cot_ref.3, bf16[384,2048]{1,0:T(8,128)(2,1)} %x_ref.5), custom_call_target="tpu_custom_call" | custom-call | tf_op jit(solution)/shard_map/upstream/pallas_call | solution.py:18
  13.9 0.4 collective-permute-start.1
  14.3 0.7 %collective-permute-start = (bf16[384,512]{1,0:T(8,128)(2,1)}, bf16[384,512]{1,0:T(8,128)(2,1)S(1)}, u32[]{:S(2)}, u32[]{:S(2)}) collective-permute-start(bf16[384,512]{1,0:T(8,128)(2,1)} %get-tuple-element.31), channel_id=1, source_target_pairs={{4,8},{12,16},{20,24},{8,4},{16,12},{24,20},{5,9},{13,17},{21,25},... | collective-permute-start | bytes 1179656 | tf_op jit(solution)/shard_map/ppermute | solution.py:355
  15.1 3.2 %interior.1 = (bf16[384,512]{1,0:T(8,128)(2,1)S(1)}, bf16[384,512]{1,0:T(8,128)(2,1)S(1)}, bf16[384,512]{1,0:T(8,128)(2,1)S(1)}, bf16[384,512]{1,0:T(8,128)(2,1)...) custom-call(bf16[384,2048]{1,0:T(8,128)(2,1)} %x_ref.5, ...), custom_call_target="tpu_custom_call" | custom-call | tf_op jit(solution)/shard_map/interior/pallas_call | solution.py:18
  18.3 0.0 collective-permute-done.2.refs_2_.rest_2_
  18.3 7.0 %collective-permute-done.3.refs_3_.rest_3_ = bf16[384,512]{1,0:T(8,128)(2,1)S(1)} collective-permute-done((bf16[384,512]{1,0:T(8,128)(2,1)}, bf16[384,512]{1,0:T(8,128)(2,1)S(1)}, u32[]{:S(2)}, u32[]{:S(2)}) %collective-permute-start.3) | collective-permute-done | bytes 393248 | tf_op jit(solution)/shard_map/ppermute | solution.py:349
  25.3 2.3 %collective-permute-done.4.refs_4_ = bf16[384,512]{1,0:T(8,128)(2,1)S(1)} collective-permute-done((bf16[384,512]{1,0:T(8,128)(2,1)}, bf16[384,512]{1,0:T(8,128)(2,1)S(1)}, u32[]{:S(2)}, u32[]{:S(2)}) %collective-permute-start.4) | collective-permute-done | bytes 393248 | tf_op jit(solution)/shard_map/ppermute | solution.py:355
  27.6 0.0 collective-permute-done.1.refs_1_.rest_1_
  27.6 1.0 %near_end.1 = (bf16[384,512]{1,0:T(8,128)(2,1)S(1)}, bf16[384,512]{1,0:T(8,128)(2,1)S(1)}, bf16[384,512]{1,0:T(8,128)(2,1)S(1)}, bf16[384,512]{1,0:T(8,128)(2,1)...) custom-call(bf16[384,512]{1,0:T(8,128)(2,1)S(1)} %get-tuple-element., ...), custom_call_target="tpu_custom_call", output_to_operand_aliasing={{0}: (6, {}), {1}: (7, {}), {2}: (8, {}), {3}: (9, {}), {4}... | custom-call | tf_op jit(solution)/shard_map/near_end/pallas_call | solution.py:18
  28.6 2.5 %collective-permute-start.9 = (bf16[384,512]{1,0:T(8,128)(2,1)S(1)}, bf16[384,512]{1,0:T(8,128)(2,1)S(1)}, u32[]{:S(2)}, u32[]{:S(2)}) collective-permute-start(bf16[384,512]{1,0:T(8,128)(2,1)S(1)} %get-tuple-element.59), channel_id=1, source_target_pairs={{0,4},{8,12},{16,20},{24,28},{4,0},{12,8},{20,16},{28,24},{1,5},{9... | collective-permute-start | bytes 1179656 | tf_op jit(solution)/shard_map/ppermute | solution.py:355
  31.0 0.0 collective-permute-done.far_ref
  31.0 0.9 %far_end.1 = (bf16[384,512]{1,0:T(8,128)(2,1)S(1)}, bf16[384,512]{1,0:T(8,128)(2,1)S(1)}, bf16[384,512]{1,0:T(8,128)(2,1)S(1)}, bf16[384,512]{1,0:T(8,128)(2,1)S...) custom-call(bf16[384,512]{1,0:T(8,128)(2,1)S(1)} %collective-permute, ...), custom_call_target="tpu_custom_call", output_to_operand_aliasing={{0}: (6, {}), {1}: (7, {}), {2}: (8, {}), {3}: (9, {}), {4}... | custom-call | tf_op jit(solution)/shard_map/far_end/pallas_call | solution.py:18
  31.9 0.1 collective-permute-start.6
  32.0 1.6 %collective-permute-start.5 = (bf16[384,512]{1,0:T(8,128)(2,1)S(1)}, bf16[384,512]{1,0:T(8,128)(2,1)S(1)}, u32[]{:S(2)}, u32[]{:S(2)}) collective-permute-start(bf16[384,512]{1,0:T(8,128)(2,1)S(1)} %get-tuple-element.50), channel_id=1, source_target_pairs={{0,3},{1,2},{2,1},{3,0},{4,7},{5,6},{6,5},{7,4},{8,11},{9,10},{10,... | collective-permute-start | bytes 1179656 | tf_op jit(solution)/shard_map/ppermute | solution.py:349
  33.6 0.5 collective-permute-start.7
  34.1 0.9 %collective-permute-start.8 = (bf16[384,512]{1,0:T(8,128)(2,1)S(1)}, bf16[384,512]{1,0:T(8,128)(2,1)S(1)}, u32[]{:S(2)}, u32[]{:S(2)}) collective-permute-start(bf16[384,512]{1,0:T(8,128)(2,1)S(1)} %get-tuple-element.56), channel_id=1, source_target_pairs={{4,8},{12,16},{20,24},{8,4},{16,12},{24,20},{5,9},{13,17},{21,25},... | collective-permute-start | bytes 1179656 | tf_op jit(solution)/shard_map/ppermute | solution.py:355
  35.0 0.0 slice-start.1
  35.0 1.7 %back_interior.1.__ = bf16[384,2048]{1,0:T(8,128)(2,1)} custom-call(bf16[384,2048]{1,0:T(8,128)(2,1)S(1)} %get-tuple-element.55.grad_ref, bf16[3,384,96]{2,1,0:T(8,128)(2,1)S(1)} %get-tuple-element.57.turned_ref._), custom_call_target="tpu_custom_call" | custom-call | tf_op jit(solution)/shard_map/back_interior/pallas_call | solution.py:18
  36.7 11.2 %collective-permute-done.9.halo_ref = bf16[384,512]{1,0:T(8,128)(2,1)S(1)} collective-permute-done((bf16[384,512]{1,0:T(8,128)(2,1)S(1)}, bf16[384,512]{1,0:T(8,128)(2,1)S(1)}, u32[]{:S(2)}, u32[]{:S(2)}) %collective-permute-start.9) | collective-permute-done | bytes 393248 | tf_op jit(solution)/shard_map/ppermute | solution.py:355
  47.8 1.2 %back_near.1.__ = bf16[384,2048]{1,0:T(8,128)(2,1)} custom-call(bf16[384,2048]{1,0:T(8,128)(2,1)S(1)} %get-tuple-element.55.grad_ref, bf16[384,512]{1,0:T(8,128)(2,1)S(1)} %collective-permute-done.9.halo_ref, bf16[3,384,96]{2,1,0:T(8,128)(2,1)S(1)} %get-tuple-element.57.turned_ref._, ...), custom_call_target="tpu_custom_call", output_to_operand_aliasing={{}: (4, {})} | custom-call | tf_op jit(solution)/shard_map/back_near/pallas_call | solution.py:18
  49.1 0.0 collective-permute-done.6.rest_0_
  49.1 1.8 %half_mix.1.rest_1_ = f32[1536,512]{1,0:T(8,128)S(1)} custom-call(bf16[1536,1536]{1,0:T(8,128)(2,1)S(1)} %bitcast.3, bf16[384,512]{1,0:T(8,128)(2,1)S(1)} %collective-permute-done.6.rest_0_, bf16[384,512]{1,0:T(8,128)(2,1)S(1)} %get-tuple-element.52.rest_1_), custom_call_target="tpu_custom_call" | custom-call | tf_op jit(solution)/shard_map/half_mix/pallas_call | solution.py:18
  50.9 0.0 collective-permute-done.5.rest_0_
  50.9 1.0 %more_mix.1.sum_ref = f32[1536,512]{1,0:T(8,128)S(1)} custom-call(bf16[1536,1536]{1,0:T(8,128)(2,1)S(1)} %bitcast.3, bf16[384,512]{1,0:T(8,128)(2,1)S(1)} %collective-permute-done.5.rest_0_, f32[1536,512]{1,0:T(8,128)S(1)} %half_mix.1.rest_1_), custom_call_target="tpu_custom_call", output_to_operand_aliasing={{}: (2, {})} | custom-call | tf_op jit(solution)/shard_map/more_mix/pallas_call | solution.py:18
  51.9 0.0 collective-permute-done.7.rest_0_
  51.9 1.8 %last_mix.1 = (bf16[1536,512]{1,0:T(8,128)(2,1)}, f32[8,128]{1,0:T(8,128)S(1)}) custom-call(bf16[1536,1536]{1,0:T(8,128)(2,1)S(1)} %bitcast.3, f32[1536,512]{1,0:T(8,128)S(1)} %more_mix.1.sum_ref, bf16[384,512]{1,0:T(8,128)(2,1)S(1)} %collective-permute-done.7.rest_0_), custom_call_target="tpu_custom_call" | custom-call | tf_op jit(solution)/shard_map/last_mix/pallas_call | solution.py:18
  53.8 1.2 %back_far.1 = bf16[384,2048]{1,0:T(8,128)(2,1)} custom-call(bf16[384,2048]{1,0:T(8,128)(2,1)S(1)} %get-tuple-element.55.grad_ref, bf16[384,512]{1,0:T(8,128)(2,1)S(1)} %collective-permute-done.8.halo_ref, bf16[3,384,96]{2,1,0:T(8,128)(2,1)S(1)} %get-tuple-element.57.turned_ref._, f32[8,128]{1,0:T(8,128)S(1)} %get-tuple-element.58._, ...), custom_call_target="tpu_custom_call", output_to_operand_aliasing={{}: (4, {})} | custom-call | tf_op jit(solution)/shard_map/back_far/pallas_call | solution.py:18
  (7 shorter events, 0.0 us)
Async XLA Ops:
  0.6 14.4 %copy-start = (bf16[3,1536,96]{1,2,0:T(8,128)(2,1)S(1)}, bf16[3,1536,96]{1,2,0:T(8,128)(2,1)}, u32[]{:S(2)}) copy-start(bf16[3,1536,96]{1,2,0:T(8,128)(2,1)} %param.5) | copy-start | bytes 2654212
  5.1 13.2 %collective-permute-start.2 = (bf16[384,512]{1,0:T(8,128)(2,1)}, bf16[384,512]{1,0:T(8,128)(2,1)S(1)}, u32[]{:S(2)}, u32[]{:S(2)}) collective-permute-start(bf16[384,512]{1,0:T(8,128)(2,1)} %get-tuple-element.35), channel_id=1, source_target_pairs={{0,2},{1,3},{2,0},{3,1},{4,6},{5,7},{6,4},{7,5},{8,10},{9,11},{10,... | collective-permute-start | bytes 1179656 | tf_op jit(solution)/shard_map/ppermute | solution.py:349
  8.2 17.1 %collective-permute-start.3 = (bf16[384,512]{1,0:T(8,128)(2,1)}, bf16[384,512]{1,0:T(8,128)(2,1)S(1)}, u32[]{:S(2)}, u32[]{:S(2)}) collective-permute-start(bf16[384,512]{1,0:T(8,128)(2,1)} %get-tuple-element.36), channel_id=1, source_target_pairs={{0,3},{1,2},{2,1},{3,0},{4,7},{5,6},{6,5},{7,4},{8,11},{9,10},{10,... | collective-permute-start | bytes 1179656 | tf_op jit(solution)/shard_map/ppermute | solution.py:349
  8.2 19.4 %collective-permute-start.4 = (bf16[384,512]{1,0:T(8,128)(2,1)}, bf16[384,512]{1,0:T(8,128)(2,1)S(1)}, u32[]{:S(2)}, u32[]{:S(2)}) collective-permute-start(bf16[384,512]{1,0:T(8,128)(2,1)} %get-tuple-element.37), channel_id=1, source_target_pairs={{0,4},{8,12},{16,20},{24,28},{4,0},{12,8},{20,16},{28,24},{1,5},{9... | collective-permute-start | bytes 1179656 | tf_op jit(solution)/shard_map/ppermute | solution.py:355
  13.9 13.6 %collective-permute-start.1 = (bf16[384,512]{1,0:T(8,128)(2,1)}, bf16[384,512]{1,0:T(8,128)(2,1)S(1)}, u32[]{:S(2)}, u32[]{:S(2)}) collective-permute-start(bf16[384,512]{1,0:T(8,128)(2,1)} %get-tuple-element.34), channel_id=1, source_target_pairs={{0,1},{1,0},{2,3},{3,2},{4,5},{5,4},{6,7},{7,6},{8,9},{9,8},{10,11... | collective-permute-start | bytes 1179656 | tf_op jit(solution)/shard_map/ppermute | solution.py:349
  14.3 16.7 %collective-permute-start = (bf16[384,512]{1,0:T(8,128)(2,1)}, bf16[384,512]{1,0:T(8,128)(2,1)S(1)}, u32[]{:S(2)}, u32[]{:S(2)}) collective-permute-start(bf16[384,512]{1,0:T(8,128)(2,1)} %get-tuple-element.31), channel_id=1, source_target_pairs={{4,8},{12,16},{20,24},{8,4},{16,12},{24,20},{5,9},{13,17},{21,25},... | collective-permute-start | bytes 1179656 | tf_op jit(solution)/shard_map/ppermute | solution.py:355
  28.6 19.3 %collective-permute-start.9 = (bf16[384,512]{1,0:T(8,128)(2,1)S(1)}, bf16[384,512]{1,0:T(8,128)(2,1)S(1)}, u32[]{:S(2)}, u32[]{:S(2)}) collective-permute-start(bf16[384,512]{1,0:T(8,128)(2,1)S(1)} %get-tuple-element.59), channel_id=1, source_target_pairs={{0,4},{8,12},{16,20},{24,28},{4,0},{12,8},{20,16},{28,24},{1,5},{9... | collective-permute-start | bytes 1179656 | tf_op jit(solution)/shard_map/ppermute | solution.py:355
  31.0 18.0 %slice-start = ((s8[4718592]{0:T(1024)(128)(4,1)}), s8[4194304]{0:T(1024)(128)(4,1)S(1)}, s32[]{:S(2)}) async-start(s8[4718592]{0:T(1024)(128)(4,1)} %bitcast.2), calls=%async_computation | async-start | bytes 8388608
  31.9 17.2 %collective-permute-start.6 = (bf16[384,512]{1,0:T(8,128)(2,1)S(1)}, bf16[384,512]{1,0:T(8,128)(2,1)S(1)}, u32[]{:S(2)}, u32[]{:S(2)}) collective-permute-start(bf16[384,512]{1,0:T(8,128)(2,1)S(1)} %get-tuple-element.51), channel_id=1, source_target_pairs={{0,1},{1,0},{2,3},{3,2},{4,5},{5,4},{6,7},{7,6},{8,9},{9,8},{10,11... | collective-permute-start | bytes 1179656 | tf_op jit(solution)/shard_map/ppermute | solution.py:349
  32.0 18.9 %collective-permute-start.5 = (bf16[384,512]{1,0:T(8,128)(2,1)S(1)}, bf16[384,512]{1,0:T(8,128)(2,1)S(1)}, u32[]{:S(2)}, u32[]{:S(2)}) collective-permute-start(bf16[384,512]{1,0:T(8,128)(2,1)S(1)} %get-tuple-element.50), channel_id=1, source_target_pairs={{0,3},{1,2},{2,1},{3,0},{4,7},{5,6},{6,5},{7,4},{8,11},{9,10},{10,... | collective-permute-start | bytes 1179656 | tf_op jit(solution)/shard_map/ppermute | solution.py:349
  33.6 18.3 %collective-permute-start.7 = (bf16[384,512]{1,0:T(8,128)(2,1)S(1)}, bf16[384,512]{1,0:T(8,128)(2,1)S(1)}, u32[]{:S(2)}, u32[]{:S(2)}) collective-permute-start(bf16[384,512]{1,0:T(8,128)(2,1)S(1)} %get-tuple-element.53), channel_id=1, source_target_pairs={{0,2},{1,3},{2,0},{3,1},{4,6},{5,7},{6,4},{7,5},{8,10},{9,11},{10,... | collective-permute-start | bytes 1179656 | tf_op jit(solution)/shard_map/ppermute | solution.py:349
  34.1 19.6 %collective-permute-start.8 = (bf16[384,512]{1,0:T(8,128)(2,1)S(1)}, bf16[384,512]{1,0:T(8,128)(2,1)S(1)}, u32[]{:S(2)}, u32[]{:S(2)}) collective-permute-start(bf16[384,512]{1,0:T(8,128)(2,1)S(1)} %get-tuple-element.56), channel_id=1, source_target_pairs={{4,8},{12,16},{20,24},{8,4},{16,12},{24,20},{5,9},{13,17},{21,25},... | collective-permute-start | bytes 1179656 | tf_op jit(solution)/shard_map/ppermute | solution.py:355
  35.0 14.1 %slice-start.1 = ((s8[4718592]{0:T(1024)(128)(4,1)}), s8[524288]{0:T(1024)(128)(4,1)S(1)}, s32[]{:S(2)}) async-start(s8[4718592]{0:T(1024)(128)(4,1)} %bitcast.2), calls=%async_computation.1 | async-start | bytes 1048576

commit v6 on v5

--- a/solution.py
+++ b/solution.py
@@ -8,6 +8,7 @@
 from jax.sharding import PartitionSpec as P
 
 DILATION_STEP = 512
+UPSTREAM_ROWS = 512
 BF16, F32 = jnp.bfloat16, jnp.float32
 ANY = pl.BlockSpec(memory_space=pl.ANY)
 INSIDE = pl.BlockSpec(memory_space=pltpu.VMEM)
@@ -62,38 +63,44 @@
 
 def upstream_kernel(order, channels, near, pw_ref, cot_ref, x_ref, *rest):
     count = len(order)
-    piece_refs, (end_ref, columns_ref, cot_in, sems) = rest[:count], rest[count:]
+    piece_refs, (end_ref, columns_ref, cot_in, total_ref, sems) = rest[:count], rest[count:]
     ch, odd = lax.axis_index("ch"), odd_place()
     length, halo = x_ref.shape[1], end_ref.shape[1]
-    whole = pltpu.make_async_copy(cot_ref, cot_in, sems.at[count])
-    whole.start()
     blocks = []
-    if channels % 128 == 0:
-        for place, k in enumerate(order):
-            blocks.append(pltpu.make_async_copy(
-                pw_ref.at[:, lanes((ch ^ k) * channels, channels)],
-                columns_ref.at[:, place * channels:(place + 1) * channels], sems.at[place],
-            ))
-    else:
-        blocks.append(pltpu.make_async_copy(pw_ref, columns_ref, sems.at[0]))
-    for block in blocks:
-        block.start()
+    for m in range(0, cot_in.shape[0], UPSTREAM_ROWS):
+        rows = slice(m, m + UPSTREAM_ROWS)
+        pairs = [(cot_ref.at[rows], cot_in.at[rows])]
+        if channels % 128 == 0:
+            for place, k in enumerate(order):
+                columns = lanes((ch ^ k) * channels, channels)
+                held = slice(place * channels, (place + 1) * channels)
+                pairs.append((pw_ref.at[rows, columns], columns_ref.at[rows, held]))
+        else:
+            pairs.append((pw_ref.at[rows], columns_ref.at[rows]))
+        copies = [
+            pltpu.make_async_copy(source, place, sems.at[len(blocks), i])
+            for i, (source, place) in enumerate(pairs)
+        ]
+        for copy in copies:
+            copy.start()
+        blocks.append((rows, copies))
     at_end = 1 - odd if near else odd
     end = pltpu.make_async_copy(
-        x_ref.at[:, lanes(at_end * (length - halo), halo)], end_ref, sems.at[count + 1]
+        x_ref.at[:, lanes(at_end * (length - halo), halo)], end_ref, sems.at[0, count + 1]
     )
     end.start()
-    whole.wait()
-    if len(blocks) == count:
+    for step, (rows, copies) in enumerate(blocks):
+        for copy in copies:
+            copy.wait()
         for place in range(count):
-            blocks[place].wait()
-            columns = slice(place * channels, (place + 1) * channels)
-            piece_refs[place][...] = turned_dot(columns_ref[:, columns], cot_in[...]).astype(BF16)
-    else:
-        blocks[0].wait()
-        result = turned_dot(columns_ref[...], cot_in[...]).astype(BF16)
-        for place in range(count):
-            piece_refs[place][...] = result[place * channels:(place + 1) * channels]
+            held = slice(place * channels, (place + 1) * channels)
+            part = turned_dot(columns_ref[rows, held], cot_in[rows, :])
+            if step > 0:
+                part = part + total_ref[held, :]
+            if step < len(blocks) - 1:
+                total_ref[held, :] = part
+            else:
+                piece_refs[place][...] = part.astype(BF16)
     end.wait()
 
 
@@ -114,7 +121,10 @@
         "upstream", functools.partial(upstream_kernel, order, channels, near),
         [(columns_of(pw_weight, channels, order), False), (cotangent, False), (inputs, False)],
         [((channels, width), BF16, True)] * count + [((channels, DILATION_STEP), BF16, True)],
-        [pltpu.VMEM((total, count * channels), BF16), pltpu.VMEM(cotangent.shape, BF16), DMA((count + 2,))],
+        [
+            pltpu.VMEM((total, count * channels), BF16), pltpu.VMEM(cotangent.shape, BF16),
+            pltpu.VMEM((count * channels, width), F32), DMA((total // UPSTREAM_ROWS, count + 2)),
+        ],
     )
     return results[:count], results[count]
 
@@ -165,9 +175,10 @@
     return results[:n], *results[n:]
 
 
-def near_kernel(n, *refs):
-    up_refs, near_ref, plain_ref, rest = refs[:n], refs[n], refs[n + 1], refs[n + 2 + n + 2:]
-    active_refs, (slope_ref, wide, grad_ref, near_out) = rest[:n], rest[n:]
+def near_kernel(order, n, *refs):
+    up_refs = {k: refs[i + (i > 0)] for i, k in enumerate(order)}
+    near_ref, plain_ref, rest = refs[1], refs[n + 1], refs[n + 2 + n + 2:]
+    active_refs, (slope_ref, wide, grad_ref) = rest[:n], rest[n:]
     ch, odd = lax.axis_index("ch"), odd_place()
     channels, length = slope_ref.shape
     group = plain_ref.shape[2]
@@ -186,9 +197,9 @@
                 for rows in groups:
                     active, slope = gelu_and_slope(convolve(plain_ref, rows, wide, base + s, halo, unit))
                     active_refs[k][rows, s:s + unit] = active.astype(BF16)
-                    grad = (up_refs[k][rows, s:s + unit].astype(F32) * slope).astype(BF16)
-                    grad_ref[rows, lanes(base + s, unit)] = grad
-                    near_out[rows, lanes(base + s - first, unit)] = grad
+                    grad_ref[rows, lanes(base + s, unit)] = (
+                        up_refs[k][rows, s:s + unit].astype(F32) * slope
+                    ).astype(BF16)
 
         @pl.when((base >= halo) & (base < length - halo))
         def _(k=k, base=base):
@@ -198,11 +209,11 @@
 
 def near_end(order, ups, near, plain, active, slope, wide):
     n = len(active)
-    operands = [(o, True) for o in (*ups, near, plain, *active, slope, wide)]
-    outs = [(a.shape, a.dtype, True) for a in (*active, slope, wide)]
-    outs += [(slope.shape, BF16, True), (near.shape, BF16, True)]
+    lead = [ups[k] for k in order]
+    operands = [(o, True) for o in (lead[0], near, *lead[1:], plain, *active, slope, wide)]
+    outs = [(a.shape, a.dtype, True) for a in (*active, slope, wide)] + [(slope.shape, BF16, True)]
     results = kernel_call(
-        "near_end", functools.partial(near_kernel, n), operands, outs,
+        "near_end", functools.partial(near_kernel, order, n), operands, outs,
         aliases={n + 2 + i: i for i in range(n + 2)},
     )
     return results[:n], *results[n + 1:]
@@ -210,7 +221,7 @@
 
 def far_kernel(n, far_ref, plain_ref, *rest):
     up_refs, rest = rest[:n], rest[n + n + 2:]
-    active_refs, (wide, grad_ref, far_out) = rest[:n], rest[n:]
+    active_refs, (wide, grad_ref, near_out, far_out) = rest[:n], rest[n:]
     ch, odd = lax.axis_index("ch"), odd_place()
     channels, length = grad_ref.shape
     group = plain_ref.shape[2]
@@ -232,12 +243,13 @@
                     grad = (up_refs[k][rows, s:s + unit].astype(F32) * slope).astype(BF16)
                     grad_ref[rows, lanes(base + s, unit)] = grad
                     far_out[rows, lanes(base + s - first, unit)] = grad
+    near_out[...] = grad_ref[:, lanes((1 - odd) * (length - halo), halo)]
 
 
 def far_end(far, plain, ups, active, wide, grad):
     n = len(active)
     operands = [(o, True) for o in (far, plain, *ups, *active, wide, grad)]
-    outs = [(a.shape, BF16, True) for a in (*active, wide, grad, far)]
+    outs = [(a.shape, BF16, True) for a in (*active, wide, grad, far, far)]
     results = kernel_call(
         "far_end", functools.partial(far_kernel, n), operands, outs,
         aliases={2 + n + i: i for i in range(n + 2)},
@@ -276,21 +288,6 @@
         [((pw_weight.shape[0], width), F32, True)],
         aliases={len(operands) - 1: 0} if before else {},
     )
-
-
-def last_mix_kernel(order, pw_ref, sum_ref, *rest):
-    piece_refs, (out_ref, done_ref, held, sems) = rest[:-4], rest[-4:]
-    pieces = jnp.concatenate([p[...] for p in piece_refs], axis=0)
-    step = 512
-    copies = []
-    for m in range(0, sum_ref.shape[0], step):
-        rows = slice(m, m + step)
-        held[rows, :] = (sum_ref[rows, :] + columns_times(order, pw_ref, rows, pieces)).astype(BF16)
-        copies.append(pltpu.make_async_copy(held.at[rows, :], out_ref.at[rows, :], sems.at[len(copies)]))
-        copies[-1].start()
-    done_ref[...] = jnp.zeros_like(done_ref)
-    for copy in copies:
-        copy.wait()
 
 
 def back(turned_ref, rows, taps):
@@ -311,35 +308,56 @@
     copy.wait()
 
 
-def back_end_kernel(near, grad_ref, halo_ref, turned_ref, _, __, out_ref, held, sem):
+def tail_kernel(order, pw_ref, sum_ref, *rest):
+    piece_refs, rest = rest[:len(order)], rest[len(order):]
+    grad_ref, near_ref, far_ref, turned_ref, _, mixed_ref, out_ref, held, ends, halos, sems = rest
     channels, length = grad_ref.shape
     group, halo, unit = turned_ref.shape[2], DILATION_STEP, 256
+    pieces = jnp.concatenate([p[...] for p in piece_refs], axis=0)
+    copies = []
+
+    def send(source, place):
+        copies.append(pltpu.make_async_copy(source, place, sems.at[len(copies)]))
+        copies[-1].start()
+
+    step = 512
+    for m in range(0, sum_ref.shape[0], step):
+        rows = slice(m, m + step)
+        held[rows, :] = (sum_ref[rows, :] + columns_times(order, pw_ref, rows, pieces)).astype(BF16)
+        send(held.at[rows, :], mixed_ref.at[rows, :])
     odd = odd_place()
+    halos[:, lanes((1 - odd) * halo, halo)] = near_ref[...]
+    halos[:, lanes(odd * halo, halo)] = far_ref[...]
     for end in range(2):
-        @pl.when(odd == (1 - end if near else end))
-        def _(end=end):
-            for g in range(0, channels, group):
-                rows = slice(g, g + group)
-                for s in range(0, halo, unit):
-                    inner = (length - 2 * halo) * end + s
-                    taps = [
-                        grad_ref[rows, inner:inner + unit],
-                        grad_ref[rows, inner + halo:inner + halo + unit],
-                    ]
-                    outer = halo_ref[rows, s:s + unit]
-                    taps = taps + [outer] if end else [outer] + taps
-                    held[rows, s:s + unit] = back(turned_ref, rows, taps)
-    at_end = 1 - odd if near else odd
-    copy = pltpu.make_async_copy(held, out_ref.at[:, lanes(at_end * (length - halo), halo)], sem)
-    copy.start()
-    copy.wait()
-
-
-def back_end(name, near, grad, halo, turned, token, grad_inputs):
-    operands = [(o, True) for o in (grad, halo, turned, token)] + [(grad_inputs, False)]
+        for g in range(0, channels, group):
+            rows = slice(g, g + group)
+            for s in range(0, halo, unit):
+                inner = (length - 2 * halo) * end + s
+                taps = [
+                    grad_ref[rows, inner:inner + unit],
+                    grad_ref[rows, inner + halo:inner + halo + unit],
+                ]
+                outer = halos[rows, end * halo + s:end * halo + s + unit]
+                taps = taps + [outer] if end else [outer] + taps
+                ends[rows, end * halo + s:end * halo + s + unit] = back(turned_ref, rows, taps)
+        send(
+            ends.at[:, end * halo:(end + 1) * halo],
+            out_ref.at[:, end * (length - halo):end * (length - halo) + halo],
+        )
+    for copy in copies:
+        copy.wait()
+
+
+def tail(pw_weight, order, partial, active, grad, near, far, turned, grad_inputs):
+    channels, halo = near.shape
+    operands = [columns_of(pw_weight, channels, order), partial, *[active[k] for k in order]]
+    operands = [(o, True) for o in (*operands, grad, near, far, turned)] + [(grad_inputs, False)]
     return kernel_call(
-        name, functools.partial(back_end_kernel, near), operands, [(grad_inputs.shape, BF16, False)],
-        [pltpu.VMEM(halo.shape, BF16), DMA], {4: 0},
+        "tail", functools.partial(tail_kernel, order), operands,
+        [(partial.shape, BF16, False), (grad_inputs.shape, BF16, False)],
+        [pltpu.VMEM(partial.shape, BF16)] + [pltpu.VMEM((channels, 2 * halo), BF16)] * 2
+        + [DMA((partial.shape[0] // 512 + 2,))],
+        {len(operands) - 1: 1},
     )
 
 
@@ -358,7 +376,6 @@
 def body(inputs, conv_weight, pw_weight, cotangent):
     n = lax.axis_size("ch")
     channels, length = inputs.shape
-    total, width = cotangent.shape
     halo = DILATION_STEP
     order = list(range(n - 1, -1, -1))
     parts = order[:n // 2], order[n // 2:]
@@ -374,28 +391,19 @@
     ups = [ups[k] for k in range(n)]
 
     active, slope, wide, plain, turned = interior(inputs, weight, n)
-    active, wide, grad, near_grad = near_end(order, ups, halos[0], plain, active, slope, wide)
-    near_grad = swap(near_grad, 0)
-    active, grad, far_grad = far_end(halos[1], plain, ups, active, wide, grad)
+    active, wide, grad = near_end(order, ups, halos[0], plain, active, slope, wide)
+    active, grad, near_grad, far_grad = far_end(halos[1], plain, ups, active, wide, grad)
     active = {k: exchange(active[k], k) for k in order}
-    far_grad = swap(far_grad, 1)
+    near_grad, far_grad = swap(near_grad, 0), swap(far_grad, 1)
 
     (grad_inputs,) = kernel_call(
         "back_interior", back_interior_kernel, [(grad, True), (turned, True)],
         [((channels, length), BF16, False)], [pltpu.VMEM((channels, length - 2 * halo), BF16), DMA],
     )
-    (grad_inputs,) = back_end("back_near", True, grad, near_grad, turned, turned, grad_inputs)
     early, late = parts[0][:n // 4], parts[0][n // 4:]
-    partial = mix("half_mix", pw_weight, parts[1], active, [])
-    partial = mix("more_mix", pw_weight, early, active, partial)
-    mixed, done = kernel_call(
-        "last_mix", functools.partial(last_mix_kernel, late),
-        [(o, True) for o in (columns_of(pw_weight, channels, late), *partial, *[active[k] for k in late])],
-        [((total, width), BF16, False), ((8, 128), F32, True)],
-        [pltpu.VMEM((total, width), BF16), DMA((total // 512,))],
-    )
-    (grad_inputs,) = back_end("back_far", False, grad, far_grad, turned, done, grad_inputs)
-    return mixed, grad_inputs
+    partial = mix("early_mix", pw_weight, early, active, [])
+    (partial,) = mix("half_mix", pw_weight, parts[1], active, partial)
+    return tuple(tail(pw_weight, late, partial, active, grad, near_grad, far_grad, turned, grad_inputs))
 
 
 def solution(mesh):

time: 55.3 us -> 53.1 us (0.960)
  Pallas kernels: 22.5 us -> 19.8 us
  waiting for transfers between devices: 20.5 us -> 21.1 us
    ppermute x6, waiting for transfers between devices: 7.03 us -> 17.4 us  [exchange(): lax.ppermute(piece, 'ch', [(i, i ^ k) for i in range(lax.axis_size('ch'))])]
    ppermute x4, waiting for transfers between devices: 13.4 us -> 3.64 us  [swap(): return lax.ppermute(values, 'ctx', pairs + [(b, a) for a, b in pairs])]
    pallas_call x11 -> x9, Pallas kernels: 22.5 us -> 19.8 us  [kernel_call(): pl.pallas_call(kernel, in_specs=[INSIDE if held else ANY for _, held in o...]
  transfers between devices with their start and end apart: 10 -> 10, of which waited for: 3 -> 6; matrix products, arithmetic and copies ran while one was open for 0% -> 0% of each run, Pallas kernels for 30% -> 24%
where the time goes in v6:
time: 53.1 us; the launch traced here: 52.9 us
  waiting for transfers between devices  21.1 us (40%)
  Pallas kernels  19.8 us (37%)
  starting transfers between devices  11 us (21%)
  between operations  0.93 us (2%)
    pallas_call x9, Pallas kernels, kernel_call(): pl.pallas_call(kernel, in_specs=[INSIDE if held else ANY for _, held in o...  19.8 us
    ppermute x6, waiting for transfers between devices, exchange(): lax.ppermute(piece, 'ch', [(i, i ^ k) for i in range(lax.axis_size('ch'))])  17.4 us
    ppermute x6, starting transfers between devices, exchange(): lax.ppermute(piece, 'ch', [(i, i ^ k) for i in range(lax.axis_size('ch'))])  5.64 us
    ppermute x4, starting transfers between devices, swap(): return lax.ppermute(values, 'ctx', pairs + [(b, a) for a, b in pairs])  5.4 us
    ppermute x4, waiting for transfers between devices, swap(): return lax.ppermute(values, 'ctx', pairs + [(b, a) for a, b in pairs])  3.64 us
  transfers between devices with their start and end apart: 10, of which 6 were waited for; matrix products, arithmetic and copies ran while one was open for 0% of the time, Pallas kernels for 24%

profile of v6, /device:TPU:0, one launch (start us, length us, event | category | flops | bytes accessed | tf_op | source)
XLA Modules:
  0.0 52.9 jit_solution(17187340384752562557)
XLA Ops:
  0.6 0.0 copy-start
  0.6 4.1 %upstream.3 = (bf16[384,512]{1,0:T(8,128)(2,1)}, bf16[384,512]{1,0:T(8,128)(2,1)}, bf16[384,512]{1,0:T(8,128)(2,1)}) custom-call(bf16[1536,1536]{1,0:T(8,128)(2,1)} %pw_ref.9, bf16[1536,512]{1,0:T(8,128)(2,1)} %cot_ref.3, bf16[384,2048]{1,0:T(8,128)(2,1)} %x_ref.5), custom_call_target="tpu_custom_call" | custom-call | tf_op jit(solution)/shard_map/upstream/pallas_call | solution.py:19
  4.7 3.0 %collective-permute-start.2 = (bf16[384,512]{1,0:T(8,128)(2,1)}, bf16[384,512]{1,0:T(8,128)(2,1)S(1)}, u32[]{:S(2)}, u32[]{:S(2)}) collective-permute-start(bf16[384,512]{1,0:T(8,128)(2,1)} %get-tuple-element.33), channel_id=1, source_target_pairs={{0,2},{1,3},{2,0},{3,1},{4,6},{5,7},{6,4},{7,5},{8,10},{9,11},{10,... | collective-permute-start | bytes 1179656 | tf_op jit(solution)/shard_map/ppermute | solution.py:367
  7.8 0.0 collective-permute-start.3
  7.8 1.5 %collective-permute-start.4 = (bf16[384,512]{1,0:T(8,128)(2,1)}, bf16[384,512]{1,0:T(8,128)(2,1)S(1)}, u32[]{:S(2)}, u32[]{:S(2)}) collective-permute-start(bf16[384,512]{1,0:T(8,128)(2,1)} %get-tuple-element.35), channel_id=1, source_target_pairs={{0,4},{8,12},{16,20},{24,28},{4,0},{12,8},{20,16},{28,24},{1,5},{9... | collective-permute-start | bytes 1179656 | tf_op jit(solution)/shard_map/ppermute | solution.py:373
  9.3 3.8 %upstream.2 = (bf16[384,512]{1,0:T(8,128)(2,1)}, bf16[384,512]{1,0:T(8,128)(2,1)S(1)}, bf16[384,512]{1,0:T(8,128)(2,1)}) custom-call(bf16[1536,1536]{1,0:T(8,128)(2,1)} %pw_ref.9, bf16[1536,512]{1,0:T(8,128)(2,1)} %cot_ref.3, bf16[384,2048]{1,0:T(8,128)(2,1)} %x_ref.5), custom_call_target="tpu_custom_call" | custom-call | tf_op jit(solution)/shard_map/upstream/pallas_call | solution.py:19
  13.1 0.4 collective-permute-start.1
  13.5 0.7 %collective-permute-start = (bf16[384,512]{1,0:T(8,128)(2,1)}, bf16[384,512]{1,0:T(8,128)(2,1)S(1)}, u32[]{:S(2)}, u32[]{:S(2)}) collective-permute-start(bf16[384,512]{1,0:T(8,128)(2,1)} %get-tuple-element.29), channel_id=1, source_target_pairs={{4,8},{12,16},{20,24},{8,4},{16,12},{24,20},{5,9},{13,17},{21,25},... | collective-permute-start | bytes 1179656 | tf_op jit(solution)/shard_map/ppermute | solution.py:373
  14.2 3.2 %interior.1 = (bf16[384,512]{1,0:T(8,128)(2,1)S(1)}, bf16[384,512]{1,0:T(8,128)(2,1)S(1)}, bf16[384,512]{1,0:T(8,128)(2,1)S(1)}, bf16[384,512]{1,0:T(8,128)(2,1)...) custom-call(bf16[384,2048]{1,0:T(8,128)(2,1)} %x_ref.5, ...), custom_call_target="tpu_custom_call" | custom-call | tf_op jit(solution)/shard_map/interior/pallas_call | solution.py:19
  17.5 0.5 collective-permute-done.2.refs_2_.rest_2_
  17.9 7.0 %collective-permute-done.3.refs_0_.rest_3_ = bf16[384,512]{1,0:T(8,128)(2,1)S(1)} collective-permute-done((bf16[384,512]{1,0:T(8,128)(2,1)}, bf16[384,512]{1,0:T(8,128)(2,1)S(1)}, u32[]{:S(2)}, u32[]{:S(2)}) %collective-permute-start.3) | collective-permute-done | bytes 393248 | tf_op jit(solution)/shard_map/ppermute | solution.py:367
  24.9 2.3 %collective-permute-done.4.refs_1_ = bf16[384,512]{1,0:T(8,128)(2,1)S(1)} collective-permute-done((bf16[384,512]{1,0:T(8,128)(2,1)}, bf16[384,512]{1,0:T(8,128)(2,1)S(1)}, u32[]{:S(2)}, u32[]{:S(2)}) %collective-permute-start.4) | collective-permute-done | bytes 393248 | tf_op jit(solution)/shard_map/ppermute | solution.py:373
  27.2 0.0 collective-permute-done.1.refs_3_.rest_1_
  27.2 1.0 %near_end.1 = (bf16[384,512]{1,0:T(8,128)(2,1)S(1)}, bf16[384,512]{1,0:T(8,128)(2,1)S(1)}, bf16[384,512]{1,0:T(8,128)(2,1)S(1)}, bf16[384,512]{1,0:T(8,128)(2,1)...) custom-call(bf16[384,512]{1,0:T(8,128)(2,1)S(1)} %collective-permute, ...), custom_call_target="tpu_custom_call", output_to_operand_aliasing={{0}: (6, {}), {1}: (7, {}), {2}: (8, {}), {3}: (9, {}), {4}... | custom-call | tf_op jit(solution)/shard_map/near_end/pallas_call | solution.py:19
  28.1 0.0 collective-permute-done.far_ref
  28.2 0.0 slice-start
  28.2 0.0 slice-start.1
  28.2 0.9 %far_end.1 = (bf16[384,512]{1,0:T(8,128)(2,1)S(1)}, bf16[384,512]{1,0:T(8,128)(2,1)S(1)}, bf16[384,512]{1,0:T(8,128)(2,1)S(1)}, bf16[384,512]{1,0:T(8,128)(2,1)S...) custom-call(bf16[384,512]{1,0:T(8,128)(2,1)S(1)} %collective-permute, ...), custom_call_target="tpu_custom_call", output_to_operand_aliasing={{0}: (6, {}), {1}: (7, {}), {2}: (8, {}), {3}: (9, {}), {4}... | custom-call | tf_op jit(solution)/shard_map/far_end/pallas_call | solution.py:19
  29.1 1.3 %collective-permute-start.6 = (bf16[384,512]{1,0:T(8,128)(2,1)S(1)}, bf16[384,512]{1,0:T(8,128)(2,1)S(1)}, u32[]{:S(2)}, u32[]{:S(2)}) collective-permute-start(bf16[384,512]{1,0:T(8,128)(2,1)S(1)} %get-tuple-element.50), channel_id=1, source_target_pairs={{0,3},{1,2},{2,1},{3,0},{4,7},{5,6},{6,5},{7,4},{8,11},{9,10},{10,... | collective-permute-start | bytes 1179656 | tf_op jit(solution)/shard_map/ppermute | solution.py:367
  30.4 0.4 collective-permute-start.5
  30.8 0.5 collective-permute-start.7
  31.3 2.4 %collective-permute-start.8 = (bf16[384,512]{1,0:T(8,128)(2,1)S(1)}, bf16[384,512]{1,0:T(8,128)(2,1)S(1)}, u32[]{:S(2)}, u32[]{:S(2)}) collective-permute-start(bf16[384,512]{1,0:T(8,128)(2,1)S(1)} %get-tuple-element.53), channel_id=1, source_target_pairs={{0,4},{8,12},{16,20},{24,28},{4,0},{12,8},{20,16},{28,24},{1,5},{9... | collective-permute-start | bytes 1179656 | tf_op jit(solution)/shard_map/ppermute | solution.py:373
  33.7 0.9 %collective-permute-start.9 = (bf16[384,512]{1,0:T(8,128)(2,1)S(1)}, bf16[384,512]{1,0:T(8,128)(2,1)S(1)}, u32[]{:S(2)}, u32[]{:S(2)}) collective-permute-start(bf16[384,512]{1,0:T(8,128)(2,1)S(1)} %get-tuple-element.54), channel_id=1, source_target_pairs={{4,8},{12,16},{20,24},{8,4},{16,12},{24,20},{5,9},{13,17},{21,25},... | collective-permute-start | bytes 1179656 | tf_op jit(solution)/shard_map/ppermute | solution.py:373
  34.5 1.7 %back_interior.1.rest_5_ = bf16[384,2048]{1,0:T(8,128)(2,1)} custom-call(bf16[384,2048]{1,0:T(8,128)(2,1)S(1)} %get-tuple-element.52.grad_ref.rest_1_, bf16[3,384,96]{2,1,0:T(8,128)(2,1)S(1)} %get-tuple-element.55.turned_ref.rest_4_), custom_call_target="tpu_custom_call" | custom-call | tf_op jit(solution)/shard_map/back_interior/pallas_call | solution.py:19
  36.2 4.3 %collective-permute-done.6.rest_0_ = bf16[384,512]{1,0:T(8,128)(2,1)S(1)} collective-permute-done((bf16[384,512]{1,0:T(8,128)(2,1)S(1)}, bf16[384,512]{1,0:T(8,128)(2,1)S(1)}, u32[]{:S(2)}, u32[]{:S(2)}) %collective-permute-start.6) | collective-permute-done | bytes 393248 | tf_op jit(solution)/shard_map/ppermute | solution.py:367
  40.5 1.0 %early_mix.1.rest_2_ = f32[1536,512]{1,0:T(8,128)S(1)} custom-call(bf16[1536,1536]{1,0:T(8,128)(2,1)S(1)} %bitcast.3, bf16[384,512]{1,0:T(8,128)(2,1)S(1)} %collective-permute-done.6.rest_0_), custom_call_target="tpu_custom_call" | custom-call | tf_op jit(solution)/shard_map/early_mix/pallas_call | solution.py:19
  41.5 0.0 collective-permute-done.5.rest_0_
  41.5 1.8 %half_mix.1.sum_ref = f32[1536,512]{1,0:T(8,128)S(1)} custom-call(bf16[1536,1536]{1,0:T(8,128)(2,1)S(1)} %bitcast.3, bf16[384,512]{1,0:T(8,128)(2,1)S(1)} %collective-permute-done.5.rest_0_, bf16[384,512]{1,0:T(8,128)(2,1)S(1)} %get-tuple-element.49.rest_1_, f32[1536,512]{1,0:T(8,128)S(1)} %early_mix.1.rest_2_), custom_call_target="tpu_custom_call", output_to_operand_aliasing={{}: (3, {})} | custom-call | tf_op jit(solution)/shard_map/half_mix/pallas_call | solution.py:19
  43.3 5.7 %collective-permute-done.7.rest_0_ = bf16[384,512]{1,0:T(8,128)(2,1)S(1)} collective-permute-done((bf16[384,512]{1,0:T(8,128)(2,1)S(1)}, bf16[384,512]{1,0:T(8,128)(2,1)S(1)}, u32[]{:S(2)}, u32[]{:S(2)}) %collective-permute-start.7) | collective-permute-done | bytes 393248 | tf_op jit(solution)/shard_map/ppermute | solution.py:367
  49.0 1.4 %collective-permute-done.8.rest_2_ = bf16[384,512]{1,0:T(8,128)(2,1)S(1)} collective-permute-done((bf16[384,512]{1,0:T(8,128)(2,1)S(1)}, bf16[384,512]{1,0:T(8,128)(2,1)S(1)}, u32[]{:S(2)}, u32[]{:S(2)}) %collective-permute-start.8) | collective-permute-done | bytes 393248 | tf_op jit(solution)/shard_map/ppermute | solution.py:373
  50.3 0.0 collective-permute-done.9.rest_3_
  50.4 2.4 %tail.1 = (bf16[1536,512]{1,0:T(8,128)(2,1)}, bf16[384,2048]{1,0:T(8,128)(2,1)}) custom-call(bf16[1536,1536]{1,0:T(8,128)(2,1)S(1)} %bitcast.3, f32[1536,512]{1,0:T(8,128)S(1)} %half_mix.1.sum_ref, bf16[384,512]{1,0:T(8,128)(2,1)S(1)} %collective-permute-done.7.rest_0_, ...), custom_call_target="tpu_custom_call", output_to_operand_aliasing={{1}: (7, {})} | custom-call | tf_op jit(solution)/shard_map/tail/pallas_call | solution.py:19
  (5 shorter events, 0.0 us)
Async XLA Ops:
  0.6 13.6 %copy-start = (bf16[3,1536,96]{1,2,0:T(8,128)(2,1)S(1)}, bf16[3,1536,96]{1,2,0:T(8,128)(2,1)}, u32[]{:S(2)}) copy-start(bf16[3,1536,96]{1,2,0:T(8,128)(2,1)} %param.5) | copy-start | bytes 2654212
  4.7 13.2 %collective-permute-start.2 = (bf16[384,512]{1,0:T(8,128)(2,1)}, bf16[384,512]{1,0:T(8,128)(2,1)S(1)}, u32[]{:S(2)}, u32[]{:S(2)}) collective-permute-start(bf16[384,512]{1,0:T(8,128)(2,1)} %get-tuple-element.33), channel_id=1, source_target_pairs={{0,2},{1,3},{2,0},{3,1},{4,6},{5,7},{6,4},{7,5},{8,10},{9,11},{10,... | collective-permute-start | bytes 1179656 | tf_op jit(solution)/shard_map/ppermute | solution.py:367
  7.8 17.1 %collective-permute-start.3 = (bf16[384,512]{1,0:T(8,128)(2,1)}, bf16[384,512]{1,0:T(8,128)(2,1)S(1)}, u32[]{:S(2)}, u32[]{:S(2)}) collective-permute-start(bf16[384,512]{1,0:T(8,128)(2,1)} %get-tuple-element.34), channel_id=1, source_target_pairs={{0,3},{1,2},{2,1},{3,0},{4,7},{5,6},{6,5},{7,4},{8,11},{9,10},{10,... | collective-permute-start | bytes 1179656 | tf_op jit(solution)/shard_map/ppermute | solution.py:367
  7.8 19.4 %collective-permute-start.4 = (bf16[384,512]{1,0:T(8,128)(2,1)}, bf16[384,512]{1,0:T(8,128)(2,1)S(1)}, u32[]{:S(2)}, u32[]{:S(2)}) collective-permute-start(bf16[384,512]{1,0:T(8,128)(2,1)} %get-tuple-element.35), channel_id=1, source_target_pairs={{0,4},{8,12},{16,20},{24,28},{4,0},{12,8},{20,16},{28,24},{1,5},{9... | collective-permute-start | bytes 1179656 | tf_op jit(solution)/shard_map/ppermute | solution.py:373
  13.1 14.0 %collective-permute-start.1 = (bf16[384,512]{1,0:T(8,128)(2,1)}, bf16[384,512]{1,0:T(8,128)(2,1)S(1)}, u32[]{:S(2)}, u32[]{:S(2)}) collective-permute-start(bf16[384,512]{1,0:T(8,128)(2,1)} %get-tuple-element.32), channel_id=1, source_target_pairs={{0,1},{1,0},{2,3},{3,2},{4,5},{5,4},{6,7},{7,6},{8,9},{9,8},{10,11... | collective-permute-start | bytes 1179656 | tf_op jit(solution)/shard_map/ppermute | solution.py:367
  13.5 14.6 %collective-permute-start = (bf16[384,512]{1,0:T(8,128)(2,1)}, bf16[384,512]{1,0:T(8,128)(2,1)S(1)}, u32[]{:S(2)}, u32[]{:S(2)}) collective-permute-start(bf16[384,512]{1,0:T(8,128)(2,1)} %get-tuple-element.29), channel_id=1, source_target_pairs={{4,8},{12,16},{20,24},{8,4},{16,12},{24,20},{5,9},{13,17},{21,25},... | collective-permute-start | bytes 1179656 | tf_op jit(solution)/shard_map/ppermute | solution.py:373
  28.2 12.3 %slice-start = ((s8[4718592]{0:T(1024)(128)(4,1)}), s8[4194304]{0:T(1024)(128)(4,1)S(1)}, s32[]{:S(2)}) async-start(s8[4718592]{0:T(1024)(128)(4,1)} %bitcast.2), calls=%async_computation | async-start | bytes 8388608
  28.2 12.3 %slice-start.1 = ((s8[4718592]{0:T(1024)(128)(4,1)}), s8[524288]{0:T(1024)(128)(4,1)S(1)}, s32[]{:S(2)}) async-start(s8[4718592]{0:T(1024)(128)(4,1)} %bitcast.2), calls=%async_computation.1 | async-start | bytes 1048576
  29.1 11.4 %collective-permute-start.6 = (bf16[384,512]{1,0:T(8,128)(2,1)S(1)}, bf16[384,512]{1,0:T(8,128)(2,1)S(1)}, u32[]{:S(2)}, u32[]{:S(2)}) collective-permute-start(bf16[384,512]{1,0:T(8,128)(2,1)S(1)} %get-tuple-element.50), channel_id=1, source_target_pairs={{0,3},{1,2},{2,1},{3,0},{4,7},{5,6},{6,5},{7,4},{8,11},{9,10},{10,... | collective-permute-start | bytes 1179656 | tf_op jit(solution)/shard_map/ppermute | solution.py:367
  30.4 11.1 %collective-permute-start.5 = (bf16[384,512]{1,0:T(8,128)(2,1)S(1)}, bf16[384,512]{1,0:T(8,128)(2,1)S(1)}, u32[]{:S(2)}, u32[]{:S(2)}) collective-permute-start(bf16[384,512]{1,0:T(8,128)(2,1)S(1)} %get-tuple-element.48), channel_id=1, source_target_pairs={{0,1},{1,0},{2,3},{3,2},{4,5},{5,4},{6,7},{7,6},{8,9},{9,8},{10,11... | collective-permute-start | bytes 1179656 | tf_op jit(solution)/shard_map/ppermute | solution.py:367
  30.8 18.2 %collective-permute-start.7 = (bf16[384,512]{1,0:T(8,128)(2,1)S(1)}, bf16[384,512]{1,0:T(8,128)(2,1)S(1)}, u32[]{:S(2)}, u32[]{:S(2)}) collective-permute-start(bf16[384,512]{1,0:T(8,128)(2,1)S(1)} %get-tuple-element.51), channel_id=1, source_target_pairs={{0,2},{1,3},{2,0},{3,1},{4,6},{5,7},{6,4},{7,5},{8,10},{9,11},{10,... | collective-permute-start | bytes 1179656 | tf_op jit(solution)/shard_map/ppermute | solution.py:367
  31.3 19.1 %collective-permute-start.8 = (bf16[384,512]{1,0:T(8,128)(2,1)S(1)}, bf16[384,512]{1,0:T(8,128)(2,1)S(1)}, u32[]{:S(2)}, u32[]{:S(2)}) collective-permute-start(bf16[384,512]{1,0:T(8,128)(2,1)S(1)} %get-tuple-element.53), channel_id=1, source_target_pairs={{0,4},{8,12},{16,20},{24,28},{4,0},{12,8},{20,16},{28,24},{1,5},{9... | collective-permute-start | bytes 1179656 | tf_op jit(solution)/shard_map/ppermute | solution.py:373
  33.7 16.7 %collective-permute-start.9 = (bf16[384,512]{1,0:T(8,128)(2,1)S(1)}, bf16[384,512]{1,0:T(8,128)(2,1)S(1)}, u32[]{:S(2)}, u32[]{:S(2)}) collective-permute-start(bf16[384,512]{1,0:T(8,128)(2,1)S(1)} %get-tuple-element.54), channel_id=1, source_target_pairs={{4,8},{12,16},{20,24},{8,4},{16,12},{24,20},{5,9},{13,17},{21,25},... | collective-permute-start | bytes 1179656 | tf_op jit(solution)/shard_map/ppermute | solution.py:373

commit v7 on v6

--- a/solution.py
+++ b/solution.py
@@ -61,15 +61,16 @@
     return lax.axis_index("ctx") % 2
 
 
-def upstream_kernel(order, channels, near, pw_ref, cot_ref, x_ref, *rest):
+def upstream_kernel(order, channels, near, far, pw_ref, cot_ref, x_ref, *rest):
     count = len(order)
-    piece_refs, (end_ref, columns_ref, cot_in, total_ref, sems) = rest[:count], rest[count:]
+    piece_refs, rest = rest[:count], rest[count:]
+    columns_ref, total_ref, sems = rest[-3:]
+    cot_in = rest[0] if near else cot_ref
     ch, odd = lax.axis_index("ch"), odd_place()
-    length, halo = x_ref.shape[1], end_ref.shape[1]
     blocks = []
     for m in range(0, cot_in.shape[0], UPSTREAM_ROWS):
         rows = slice(m, m + UPSTREAM_ROWS)
-        pairs = [(cot_ref.at[rows], cot_in.at[rows])]
+        pairs = [(cot_ref.at[rows], cot_in.at[rows])] if near else []
         if channels % 128 == 0:
             for place, k in enumerate(order):
                 columns = lanes((ch ^ k) * channels, channels)
@@ -84,11 +85,15 @@
         for copy in copies:
             copy.start()
         blocks.append((rows, copies))
-    at_end = 1 - odd if near else odd
-    end = pltpu.make_async_copy(
-        x_ref.at[:, lanes(at_end * (length - halo), halo)], end_ref, sems.at[0, count + 1]
-    )
-    end.start()
+    end = None
+    if near or far:
+        end_ref = rest[-4]
+        length, halo = x_ref.shape[1], end_ref.shape[1]
+        at_end = 1 - odd if near else odd
+        end = pltpu.make_async_copy(
+            x_ref.at[:, lanes(at_end * (length - halo), halo)], end_ref, sems.at[0, count + 1]
+        )
+        end.start()
     for step, (rows, copies) in enumerate(blocks):
         for copy in copies:
             copy.wait()
@@ -101,7 +106,8 @@
                 total_ref[held, :] = part
             else:
                 piece_refs[place][...] = part.astype(BF16)
-    end.wait()
+    if end is not None:
+        end.wait()
 
 
 def columns_of(pw_weight, channels, order):
@@ -113,20 +119,21 @@
     )
 
 
-def upstream(pw_weight, cotangent, inputs, order, near):
+def upstream(pw_weight, cotangent, inputs, order, near, far):
     channels = inputs.shape[0]
     total, width = cotangent.shape
     count = len(order)
+    outs = [((channels, width), BF16, True)] * count
+    outs += [(cotangent.shape, BF16, True)] * near + [((channels, DILATION_STEP), BF16, True)] * (near or far)
     results = kernel_call(
-        "upstream", functools.partial(upstream_kernel, order, channels, near),
-        [(columns_of(pw_weight, channels, order), False), (cotangent, False), (inputs, False)],
-        [((channels, width), BF16, True)] * count + [((channels, DILATION_STEP), BF16, True)],
+        "upstream", functools.partial(upstream_kernel, order, channels, near, far),
+        [(columns_of(pw_weight, channels, order), False), (cotangent, not near), (inputs, False)], outs,
         [
-            pltpu.VMEM((total, count * channels), BF16), pltpu.VMEM(cotangent.shape, BF16),
-            pltpu.VMEM((count * channels, width), F32), DMA((total // UPSTREAM_ROWS, count + 2)),
+            pltpu.VMEM((total, count * channels), BF16), pltpu.VMEM((count * channels, width), F32),
+            DMA((total // UPSTREAM_ROWS, count + 2)),
         ],
     )
-    return results[:count], results[count]
+    return results[:count], *results[count:]
 
 
 def convolve(w_ref, rows, wide, start, halo, unit):
@@ -175,10 +182,8 @@
     return results[:n], *results[n:]
 
 
-def near_kernel(order, n, *refs):
-    up_refs = {k: refs[i + (i > 0)] for i, k in enumerate(order)}
-    near_ref, plain_ref, rest = refs[1], refs[n + 1], refs[n + 2 + n + 2:]
-    active_refs, (slope_ref, wide, grad_ref) = rest[:n], rest[n:]
+def ends_kernel(n, _, near_ref, __, far_ref, plain_ref, *rest):
+    active_refs, (slope_ref, wide) = rest[n + 2:n + 2 + n], rest[n + 2 + n:]
     ch, odd = lax.axis_index("ch"), odd_place()
     channels, length = slope_ref.shape
     group = plain_ref.shape[2]
@@ -187,74 +192,49 @@
     unit = min(block, 256)
     groups = [slice(g, g + group) for g in range(0, channels, group)]
     wide[:, lanes((1 - odd) * (halo + length), halo)] = near_ref[...]
-    first, far = (1 - odd) * (length - halo), odd * (length - halo)
+    wide[:, lanes(odd * (halo + length), halo)] = far_ref[...]
     for k in range(n):
         base = (ch ^ k) * block
 
-        @pl.when((base >= first) & (base < first + halo))
+        @pl.when((base < halo) | (base >= length - halo))
         def _(k=k, base=base):
             for s in range(0, block, unit):
                 for rows in groups:
                     active, slope = gelu_and_slope(convolve(plain_ref, rows, wide, base + s, halo, unit))
                     active_refs[k][rows, s:s + unit] = active.astype(BF16)
-                    grad_ref[rows, lanes(base + s, unit)] = (
-                        up_refs[k][rows, s:s + unit].astype(F32) * slope
-                    ).astype(BF16)
-
-        @pl.when((base >= halo) & (base < length - halo))
-        def _(k=k, base=base):
-            here = lanes(base, block)
-            grad_ref[:, here] = (up_refs[k][...].astype(F32) * slope_ref[:, here]).astype(BF16)
-
-
-def near_end(order, ups, near, plain, active, slope, wide):
+                    slope_ref[rows, lanes(base + s, unit)] = slope
+
+
+def both_ends(first, near, second, far, plain, active, slope, wide):
     n = len(active)
-    lead = [ups[k] for k in order]
-    operands = [(o, True) for o in (lead[0], near, *lead[1:], plain, *active, slope, wide)]
-    outs = [(a.shape, a.dtype, True) for a in (*active, slope, wide)] + [(slope.shape, BF16, True)]
+    operands = [(o, True) for o in (first, near, second, far, plain, *active, slope, wide)]
     results = kernel_call(
-        "near_end", functools.partial(near_kernel, order, n), operands, outs,
-        aliases={n + 2 + i: i for i in range(n + 2)},
-    )
-    return results[:n], *results[n + 1:]
-
-
-def far_kernel(n, far_ref, plain_ref, *rest):
-    up_refs, rest = rest[:n], rest[n + n + 2:]
-    active_refs, (wide, grad_ref, near_out, far_out) = rest[:n], rest[n:]
+        "ends", functools.partial(ends_kernel, n), operands,
+        [(a.shape, a.dtype, True) for a in (*active, slope, wide)],
+        aliases={5 + i: i for i in range(n + 2)},
+    )
+    return results[:n], results[n]
+
+
+def grad_kernel(order, slope_ref, *rest):
+    up_refs, (grad_ref, near_out, far_out) = rest[:-3], rest[-3:]
     ch, odd = lax.axis_index("ch"), odd_place()
-    channels, length = grad_ref.shape
-    group = plain_ref.shape[2]
-    halo = far_ref.shape[1]
-    block = length // n
-    unit = min(block, 256)
-    groups = [slice(g, g + group) for g in range(0, channels, group)]
-    wide[:, lanes(odd * (halo + length), halo)] = far_ref[...]
-    first = odd * (length - halo)
-    for k in range(n):
-        base = (ch ^ k) * block
-
-        @pl.when((base >= first) & (base < first + halo))
-        def _(k=k, base=base):
-            for s in range(0, block, unit):
-                for rows in groups:
-                    active, slope = gelu_and_slope(convolve(plain_ref, rows, wide, base + s, halo, unit))
-                    active_refs[k][rows, s:s + unit] = active.astype(BF16)
-                    grad = (up_refs[k][rows, s:s + unit].astype(F32) * slope).astype(BF16)
-                    grad_ref[rows, lanes(base + s, unit)] = grad
-                    far_out[rows, lanes(base + s - first, unit)] = grad
+    length, halo = grad_ref.shape[1], near_out.shape[1]
+    block = up_refs[0].shape[1]
+    for k, up_ref in zip(order, up_refs):
+        here = lanes((ch ^ k) * block, block)
+        grad_ref[:, here] = (up_ref[...].astype(F32) * slope_ref[:, here]).astype(BF16)
     near_out[...] = grad_ref[:, lanes((1 - odd) * (length - halo), halo)]
-
-
-def far_end(far, plain, ups, active, wide, grad):
-    n = len(active)
-    operands = [(o, True) for o in (far, plain, *ups, *active, wide, grad)]
-    outs = [(a.shape, BF16, True) for a in (*active, wide, grad, far, far)]
-    results = kernel_call(
-        "far_end", functools.partial(far_kernel, n), operands, outs,
-        aliases={2 + n + i: i for i in range(n + 2)},
-    )
-    return results[:n], *results[n + 1:]
+    far_out[...] = grad_ref[:, lanes(odd * (length - halo), halo)]
+
+
+def grad_conv(slope, order, ups):
+    channels = slope.shape[0]
+    return kernel_call(
+        "grad_conv", functools.partial(grad_kernel, order),
+        [(o, True) for o in (slope, *[ups[k] for k in order])],
+        [(slope.shape, BF16, True)] + [((channels, DILATION_STEP), BF16, True)] * 2,
+    )
 
 
 def columns_times(order, pw_ref, rows, pieces):
@@ -308,9 +288,9 @@
     copy.wait()
 
 
-def tail_kernel(order, pw_ref, sum_ref, *rest):
+def tail_kernel(order, pw_ref, sum_ref, near_ref, *rest):
     piece_refs, rest = rest[:len(order)], rest[len(order):]
-    grad_ref, near_ref, far_ref, turned_ref, _, mixed_ref, out_ref, held, ends, halos, sems = rest
+    far_ref, grad_ref, turned_ref, _, mixed_ref, out_ref, held, ends, halos, sems = rest
     channels, length = grad_ref.shape
     group, halo, unit = turned_ref.shape[2], DILATION_STEP, 256
     pieces = jnp.concatenate([p[...] for p in piece_refs], axis=0)
@@ -350,8 +330,8 @@
 
 def tail(pw_weight, order, partial, active, grad, near, far, turned, grad_inputs):
     channels, halo = near.shape
-    operands = [columns_of(pw_weight, channels, order), partial, *[active[k] for k in order]]
-    operands = [(o, True) for o in (*operands, grad, near, far, turned)] + [(grad_inputs, False)]
+    operands = [columns_of(pw_weight, channels, order), partial, near, *[active[k] for k in order]]
+    operands = [(o, True) for o in (*operands, far, grad, turned)] + [(grad_inputs, False)]
     return kernel_call(
         "tail", functools.partial(tail_kernel, order), operands,
         [(partial.shape, BF16, False), (grad_inputs.shape, BF16, False)],
@@ -378,21 +358,23 @@
     channels, length = inputs.shape
     halo = DILATION_STEP
     order = list(range(n - 1, -1, -1))
-    parts = order[:n // 2], order[n // 2:]
+    first, second, rest = order[:n // 4], order[n // 4:n // 2], order[n // 2:]
 
     weight = lax.dynamic_slice_in_dim(
         jnp.swapaxes(conv_weight, 1, 2), lax.axis_index("ch") * channels, channels, 2
     )
-    ups, halos = {}, []
-    for place, part in enumerate(parts):
-        pieces, end = upstream(pw_weight, cotangent, inputs, part, place == 0)
-        ups.update({k: exchange(p, k) for k, p in zip(part, pieces)})
-        halos.append(swap(end, place))
-    ups = [ups[k] for k in range(n)]
+    pieces, cot_in, near = upstream(pw_weight, cotangent, inputs, first, True, False)
+    ups = {k: exchange(p, k) for k, p in zip(first, pieces)}
+    near = swap(near, 0)
+    pieces, far = upstream(pw_weight, cot_in, inputs, second, False, True)
+    ups.update({k: exchange(p, k) for k, p in zip(second, pieces)})
+    far = swap(far, 1)
+    (pieces,) = upstream(pw_weight, cot_in, inputs, rest, False, False)
+    ups.update({k: exchange(p, k) for k, p in zip(rest, pieces)})
 
     active, slope, wide, plain, turned = interior(inputs, weight, n)
-    active, wide, grad = near_end(order, ups, halos[0], plain, active, slope, wide)
-    active, grad, near_grad, far_grad = far_end(halos[1], plain, ups, active, wide, grad)
+    active, slope = both_ends(ups[first[0]], near, ups[second[0]], far, plain, active, slope, wide)
+    grad, near_grad, far_grad = grad_conv(slope, order, ups)
     active = {k: exchange(active[k], k) for k in order}
     near_grad, far_grad = swap(near_grad, 0), swap(far_grad, 1)
 
@@ -400,10 +382,9 @@
         "back_interior", back_interior_kernel, [(grad, True), (turned, True)],
         [((channels, length), BF16, False)], [pltpu.VMEM((channels, length - 2 * halo), BF16), DMA],
     )
-    early, late = parts[0][:n // 4], parts[0][n // 4:]
-    partial = mix("early_mix", pw_weight, early, active, [])
-    (partial,) = mix("half_mix", pw_weight, parts[1], active, partial)
-    return tuple(tail(pw_weight, late, partial, active, grad, near_grad, far_grad, turned, grad_inputs))
+    partial = mix("early_mix", pw_weight, first, active, [])
+    (partial,) = mix("half_mix", pw_weight, rest, active, partial)
+    return tuple(tail(pw_weight, second, partial, active, grad, near_grad, far_grad, turned, grad_inputs))
 
 
 def solution(mesh):

time: 53.1 us -> 52 us (0.979)
  waiting for transfers between devices: 21.1 us -> 18.1 us
  Pallas kernels: 19.8 us -> 21.8 us
    ppermute x6, waiting for transfers between devices: 17.4 us -> 9.37 us  [exchange(): lax.ppermute(piece, 'ch', [(i, i ^ k) for i in range(lax.axis_size('ch'))])]
    ppermute x4, waiting for transfers between devices: 3.64 us -> 8.76 us  [swap(): return lax.ppermute(values, 'ctx', pairs + [(b, a) for a, b in pairs])]
    pallas_call x9 -> x10, Pallas kernels: 19.8 us -> 21.8 us  [kernel_call(): pl.pallas_call(kernel, in_specs=[INSIDE if held else ANY for _, held in o...]
  transfers between devices with their start and end apart: 10 -> 10, of which waited for: 6 -> 4; matrix products, arithmetic and copies ran while one was open for 0% -> 0% of each run, Pallas kernels for 24% -> 31%
where the time goes in v7:
time: 52 us; the launch traced here: 51.8 us
  Pallas kernels  21.8 us (42%)
  waiting for transfers between devices  18.1 us (35%)
  starting transfers between devices  10.9 us (21%)
  between operations  0.94 us (2%)
    pallas_call x10, Pallas kernels, kernel_call(): pl.pallas_call(kernel, in_specs=[INSIDE if held else ANY for _, held in o...  21.8 us
    ppermute x6, waiting for transfers between devices, exchange(): lax.ppermute(piece, 'ch', [(i, i ^ k) for i in range(lax.axis_size('ch'))])  9.37 us
    ppermute x4, waiting for transfers between devices, swap(): return lax.ppermute(values, 'ctx', pairs + [(b, a) for a, b in pairs])  8.76 us
    ppermute x4, starting transfers between devices, swap(): return lax.ppermute(values, 'ctx', pairs + [(b, a) for a, b in pairs])  5.47 us
    ppermute x6, starting transfers between devices, exchange(): lax.ppermute(piece, 'ch', [(i, i ^ k) for i in range(lax.axis_size('ch'))])  5.46 us
  transfers between devices with their start and end apart: 10, of which 4 were waited for; matrix products, arithmetic and copies ran while one was open for 0% of the time, Pallas kernels for 31%

profile of v7, /device:TPU:0, one launch (start us, length us, event | category | flops | bytes accessed | tf_op | source)
XLA Modules:
  0.0 51.8 jit_solution(10826352874273421981)
XLA Ops:
  0.6 0.0 copy-start
  0.6 3.2 %upstream.3 = (bf16[384,512]{1,0:T(8,128)(2,1)}, bf16[1536,512]{1,0:T(8,128)(2,1)S(1)}, bf16[384,512]{1,0:T(8,128)(2,1)}) custom-call(bf16[1536,1536]{1,0:T(8,128)(2,1)} %pw_ref.11, bf16[1536,512]{1,0:T(8,128)(2,1)} %cot_ref.1, bf16[384,2048]{1,0:T(8,128)(2,1)} %x_ref.7), custom_call_target="tpu_custom_call" | custom-call | tf_op jit(solution)/shard_map/upstream/pallas_call | solution.py:19
  3.8 2.5 %collective-permute-start = (bf16[384,512]{1,0:T(8,128)(2,1)}, bf16[384,512]{1,0:T(8,128)(2,1)S(1)}, u32[]{:S(2)}, u32[]{:S(2)}) collective-permute-start(bf16[384,512]{1,0:T(8,128)(2,1)} %get-tuple-element.25), channel_id=1, source_target_pairs={{0,3},{1,2},{2,1},{3,0},{4,7},{5,6},{6,5},{7,4},{8,11},{9,10},{10,... | collective-permute-start | bytes 1179656 | tf_op jit(solution)/shard_map/ppermute | solution.py:347
  6.3 1.5 %collective-permute-start.1 = (bf16[384,512]{1,0:T(8,128)(2,1)}, bf16[384,512]{1,0:T(8,128)(2,1)S(1)}, u32[]{:S(2)}, u32[]{:S(2)}) collective-permute-start(bf16[384,512]{1,0:T(8,128)(2,1)} %get-tuple-element.26), channel_id=1, source_target_pairs={{0,4},{8,12},{16,20},{24,28},{4,0},{12,8},{20,16},{28,24},{1,5},{9... | collective-permute-start | bytes 1179656 | tf_op jit(solution)/shard_map/ppermute | solution.py:353
  7.8 2.9 %upstream.4 = (bf16[384,512]{1,0:T(8,128)(2,1)}, bf16[384,512]{1,0:T(8,128)(2,1)}) custom-call(bf16[1536,1536]{1,0:T(8,128)(2,1)} %pw_ref.11, bf16[1536,512]{1,0:T(8,128)(2,1)S(1)} %get-tuple-element.27.cot_ref, bf16[384,2048]{1,0:T(8,128)(2,1)} %x_ref.7), custom_call_target="tpu_custom_call" | custom-call | tf_op jit(solution)/shard_map/upstream/pallas_call | solution.py:19
  10.7 0.7 %collective-permute-start.2 = (bf16[384,512]{1,0:T(8,128)(2,1)}, bf16[384,512]{1,0:T(8,128)(2,1)S(1)}, u32[]{:S(2)}, u32[]{:S(2)}) collective-permute-start(bf16[384,512]{1,0:T(8,128)(2,1)} %get-tuple-element.28), channel_id=1, source_target_pairs={{0,2},{1,3},{2,0},{3,1},{4,6},{5,7},{6,4},{7,5},{8,10},{9,11},{10,... | collective-permute-start | bytes 1179656 | tf_op jit(solution)/shard_map/ppermute | solution.py:347
  11.4 0.7 %collective-permute-start.3 = (bf16[384,512]{1,0:T(8,128)(2,1)}, bf16[384,512]{1,0:T(8,128)(2,1)S(1)}, u32[]{:S(2)}, u32[]{:S(2)}) collective-permute-start(bf16[384,512]{1,0:T(8,128)(2,1)} %get-tuple-element.29), channel_id=1, source_target_pairs={{4,8},{12,16},{20,24},{8,4},{16,12},{24,20},{5,9},{13,17},{21,25},... | collective-permute-start | bytes 1179656 | tf_op jit(solution)/shard_map/ppermute | solution.py:353
  12.1 3.4 %upstream.5 = (bf16[384,512]{1,0:T(8,128)(2,1)}, bf16[384,512]{1,0:T(8,128)(2,1)S(1)}) custom-call(bf16[1536,1536]{1,0:T(8,128)(2,1)} %pw_ref.11, bf16[1536,512]{1,0:T(8,128)(2,1)S(1)} %get-tuple-element.27.cot_ref, bf16[384,2048]{1,0:T(8,128)(2,1)} %x_ref.7), custom_call_target="tpu_custom_call" | custom-call | tf_op jit(solution)/shard_map/upstream/pallas_call | solution.py:19
  15.5 0.1 collective-permute-start.6
  15.6 0.0 slice-start
  15.6 3.4 %interior.1 = (bf16[384,512]{1,0:T(8,128)(2,1)S(1)}, bf16[384,512]{1,0:T(8,128)(2,1)S(1)}, bf16[384,512]{1,0:T(8,128)(2,1)S(1)}, bf16[384,512]{1,0:T(8,128)(2,1)...) custom-call(bf16[384,2048]{1,0:T(8,128)(2,1)} %x_ref.7, ...), custom_call_target="tpu_custom_call" | custom-call | tf_op jit(solution)/shard_map/interior/pallas_call | solution.py:19
  19.0 0.0 collective-permute-done._.rest_0_
  19.0 6.7 %collective-permute-done.1.near_ref = bf16[384,512]{1,0:T(8,128)(2,1)S(1)} collective-permute-done((bf16[384,512]{1,0:T(8,128)(2,1)}, bf16[384,512]{1,0:T(8,128)(2,1)S(1)}, u32[]{:S(2)}, u32[]{:S(2)}) %collective-permute-start.1) | collective-permute-done | bytes 393248 | tf_op jit(solution)/shard_map/ppermute | solution.py:353
  25.7 0.0 collective-permute-done.2.__.rest_1_
  25.7 0.0 collective-permute-done.3.far_ref
  25.7 1.5 %ends.1 = (bf16[384,512]{1,0:T(8,128)(2,1)S(1)}, bf16[384,512]{1,0:T(8,128)(2,1)S(1)}, bf16[384,512]{1,0:T(8,128)(2,1)S(1)}, bf16[384,512]{1,0:T(8,128)(2,1)S(1)...) custom-call(bf16[384,512]{1,0:T(8,128)(2,1)S(1)} %collective-permute, ...), custom_call_target="tpu_custom_call", output_to_operand_aliasing={{0}: (5, {}), {1}: (6, {}), {2}: (7, {}), {3}: (8, {}), {4}... | custom-call | tf_op jit(solution)/shard_map/ends/pallas_call | solution.py:19
  27.2 0.1 collective-permute-start.4
  27.3 1.3 %collective-permute-start.5 = (bf16[384,512]{1,0:T(8,128)(2,1)S(1)}, bf16[384,512]{1,0:T(8,128)(2,1)S(1)}, u32[]{:S(2)}, u32[]{:S(2)}) collective-permute-start(bf16[384,512]{1,0:T(8,128)(2,1)S(1)} %get-tuple-element.39), channel_id=1, source_target_pairs={{0,3},{1,2},{2,1},{3,0},{4,7},{5,6},{6,5},{7,4},{8,11},{9,10},{10,... | collective-permute-start | bytes 1179656 | tf_op jit(solution)/shard_map/ppermute | solution.py:347
  28.6 0.8 %collective-permute-start.8 = (bf16[384,512]{1,0:T(8,128)(2,1)S(1)}, bf16[384,512]{1,0:T(8,128)(2,1)S(1)}, u32[]{:S(2)}, u32[]{:S(2)}) collective-permute-start(bf16[384,512]{1,0:T(8,128)(2,1)S(1)} %get-tuple-element.44), channel_id=1, source_target_pairs={{0,2},{1,3},{2,0},{3,1},{4,6},{5,7},{6,4},{7,5},{8,10},{9,11},{10,... | collective-permute-start | bytes 1179656 | tf_op jit(solution)/shard_map/ppermute | solution.py:347
  29.5 0.0 collective-permute-done.6.rest_2_
  29.5 0.6 %grad_conv.1 = (bf16[384,2048]{1,0:T(8,128)(2,1)S(1)}, bf16[384,512]{1,0:T(8,128)(2,1)S(1)}, bf16[384,512]{1,0:T(8,128)(2,1)S(1)}) custom-call(f32[384,2048]{1,0:T(8,128)S(1)} %get-tuple-element.40.slope_ref, bf16[384,512]{1,0:T(8,128)(2,1)S(1)} %collective-permute-done._.rest_0_, bf16[384,512]{1,0:T(8,128)(2,1)S(1)} %collective-permute-done.2.__.rest_1_, ...), custom_call_target="tpu_custom_call" | custom-call | tf_op jit(solution)/shard_map/grad_conv/pallas_call | solution.py:19
  30.1 2.5 %collective-permute-start.7 = (bf16[384,512]{1,0:T(8,128)(2,1)S(1)}, bf16[384,512]{1,0:T(8,128)(2,1)S(1)}, u32[]{:S(2)}, u32[]{:S(2)}) collective-permute-start(bf16[384,512]{1,0:T(8,128)(2,1)S(1)} %get-tuple-element.43), channel_id=1, source_target_pairs={{0,4},{8,12},{16,20},{24,28},{4,0},{12,8},{20,16},{28,24},{1,5},{9... | collective-permute-start | bytes 1179656 | tf_op jit(solution)/shard_map/ppermute | solution.py:353
  32.5 0.9 %collective-permute-start.9 = (bf16[384,512]{1,0:T(8,128)(2,1)S(1)}, bf16[384,512]{1,0:T(8,128)(2,1)S(1)}, u32[]{:S(2)}, u32[]{:S(2)}) collective-permute-start(bf16[384,512]{1,0:T(8,128)(2,1)S(1)} %get-tuple-element.45), channel_id=1, source_target_pairs={{4,8},{12,16},{20,24},{8,4},{16,12},{24,20},{5,9},{13,17},{21,25},... | collective-permute-start | bytes 1179656 | tf_op jit(solution)/shard_map/ppermute | solution.py:353
  33.4 1.7 %back_interior.1.rest_4_ = bf16[384,2048]{1,0:T(8,128)(2,1)} custom-call(bf16[384,2048]{1,0:T(8,128)(2,1)S(1)} %get-tuple-element.46.grad_ref.rest_2_, bf16[3,384,96]{2,1,0:T(8,128)(2,1)S(1)} %get-tuple-element.47.turned_ref.rest_3_), custom_call_target="tpu_custom_call" | custom-call | tf_op jit(solution)/shard_map/back_interior/pallas_call | solution.py:19
  35.0 3.2 %collective-permute-done.5.rest_0_ = bf16[384,512]{1,0:T(8,128)(2,1)S(1)} collective-permute-done((bf16[384,512]{1,0:T(8,128)(2,1)S(1)}, bf16[384,512]{1,0:T(8,128)(2,1)S(1)}, u32[]{:S(2)}, u32[]{:S(2)}) %collective-permute-start.5) | collective-permute-done | bytes 393248 | tf_op jit(solution)/shard_map/ppermute | solution.py:347
  38.2 1.0 %early_mix.1.rest_2_ = f32[1536,512]{1,0:T(8,128)S(1)} custom-call(bf16[1536,1536]{1,0:T(8,128)(2,1)S(1)} %bitcast.3, bf16[384,512]{1,0:T(8,128)(2,1)S(1)} %collective-permute-done.5.rest_0_), custom_call_target="tpu_custom_call" | custom-call | tf_op jit(solution)/shard_map/early_mix/pallas_call | solution.py:19
  39.2 0.0 collective-permute-done.4.rest_0_
  39.2 1.8 %half_mix.1.sum_ref = f32[1536,512]{1,0:T(8,128)S(1)} custom-call(bf16[1536,1536]{1,0:T(8,128)(2,1)S(1)} %bitcast.3, bf16[384,512]{1,0:T(8,128)(2,1)S(1)} %collective-permute-done.4.rest_0_, bf16[384,512]{1,0:T(8,128)(2,1)S(1)} %get-tuple-element.38.rest_1_, f32[1536,512]{1,0:T(8,128)S(1)} %early_mix.1.rest_2_), custom_call_target="tpu_custom_call", output_to_operand_aliasing={{}: (3, {})} | custom-call | tf_op jit(solution)/shard_map/half_mix/pallas_call | solution.py:19
  41.0 6.2 %collective-permute-done.8.rest_0_ = bf16[384,512]{1,0:T(8,128)(2,1)S(1)} collective-permute-done((bf16[384,512]{1,0:T(8,128)(2,1)S(1)}, bf16[384,512]{1,0:T(8,128)(2,1)S(1)}, u32[]{:S(2)}, u32[]{:S(2)}) %collective-permute-start.8) | collective-permute-done | bytes 393248 | tf_op jit(solution)/shard_map/ppermute | solution.py:347
  47.2 2.0 %collective-permute-done.7.near_ref = bf16[384,512]{1,0:T(8,128)(2,1)S(1)} collective-permute-done((bf16[384,512]{1,0:T(8,128)(2,1)S(1)}, bf16[384,512]{1,0:T(8,128)(2,1)S(1)}, u32[]{:S(2)}, u32[]{:S(2)}) %collective-permute-start.7) | collective-permute-done | bytes 393248 | tf_op jit(solution)/shard_map/ppermute | solution.py:353
  49.3 0.0 collective-permute-done.9.rest_1_
  49.3 2.4 %tail.1 = (bf16[1536,512]{1,0:T(8,128)(2,1)}, bf16[384,2048]{1,0:T(8,128)(2,1)}) custom-call(bf16[1536,1536]{1,0:T(8,128)(2,1)S(1)} %bitcast.3, f32[1536,512]{1,0:T(8,128)S(1)} %half_mix.1.sum_ref, bf16[384,512]{1,0:T(8,128)(2,1)S(1)} %collective-permute-done.7.near_ref, ...), custom_call_target="tpu_custom_call", output_to_operand_aliasing={{1}: (7, {})} | custom-call | tf_op jit(solution)/shard_map/tail/pallas_call | solution.py:19
  (6 shorter events, 0.0 us)
Async XLA Ops:
  0.6 14.9 %copy-start = (bf16[3,1536,96]{1,2,0:T(8,128)(2,1)S(1)}, bf16[3,1536,96]{1,2,0:T(8,128)(2,1)}, u32[]{:S(2)}) copy-start(bf16[3,1536,96]{1,2,0:T(8,128)(2,1)} %param.5) | copy-start | bytes 2654212
  3.8 15.2 %collective-permute-start = (bf16[384,512]{1,0:T(8,128)(2,1)}, bf16[384,512]{1,0:T(8,128)(2,1)S(1)}, u32[]{:S(2)}, u32[]{:S(2)}) collective-permute-start(bf16[384,512]{1,0:T(8,128)(2,1)} %get-tuple-element.25), channel_id=1, source_target_pairs={{0,3},{1,2},{2,1},{3,0},{4,7},{5,6},{6,5},{7,4},{8,11},{9,10},{10,... | collective-permute-start | bytes 1179656 | tf_op jit(solution)/shard_map/ppermute | solution.py:347
  6.3 19.4 %collective-permute-start.1 = (bf16[384,512]{1,0:T(8,128)(2,1)}, bf16[384,512]{1,0:T(8,128)(2,1)S(1)}, u32[]{:S(2)}, u32[]{:S(2)}) collective-permute-start(bf16[384,512]{1,0:T(8,128)(2,1)} %get-tuple-element.26), channel_id=1, source_target_pairs={{0,4},{8,12},{16,20},{24,28},{4,0},{12,8},{20,16},{28,24},{1,5},{9... | collective-permute-start | bytes 1179656 | tf_op jit(solution)/shard_map/ppermute | solution.py:353
  10.7 15.0 %collective-permute-start.2 = (bf16[384,512]{1,0:T(8,128)(2,1)}, bf16[384,512]{1,0:T(8,128)(2,1)S(1)}, u32[]{:S(2)}, u32[]{:S(2)}) collective-permute-start(bf16[384,512]{1,0:T(8,128)(2,1)} %get-tuple-element.28), channel_id=1, source_target_pairs={{0,2},{1,3},{2,0},{3,1},{4,6},{5,7},{6,4},{7,5},{8,10},{9,11},{10,... | collective-permute-start | bytes 1179656 | tf_op jit(solution)/shard_map/ppermute | solution.py:347
  11.4 14.3 %collective-permute-start.3 = (bf16[384,512]{1,0:T(8,128)(2,1)}, bf16[384,512]{1,0:T(8,128)(2,1)S(1)}, u32[]{:S(2)}, u32[]{:S(2)}) collective-permute-start(bf16[384,512]{1,0:T(8,128)(2,1)} %get-tuple-element.29), channel_id=1, source_target_pairs={{4,8},{12,16},{20,24},{8,4},{16,12},{24,20},{5,9},{13,17},{21,25},... | collective-permute-start | bytes 1179656 | tf_op jit(solution)/shard_map/ppermute | solution.py:353
  15.5 14.0 %collective-permute-start.6 = (bf16[384,512]{1,0:T(8,128)(2,1)}, bf16[384,512]{1,0:T(8,128)(2,1)S(1)}, u32[]{:S(2)}, u32[]{:S(2)}) collective-permute-start(bf16[384,512]{1,0:T(8,128)(2,1)} %get-tuple-element.41), channel_id=1, source_target_pairs={{0,1},{1,0},{2,3},{3,2},{4,5},{5,4},{6,7},{7,6},{8,9},{9,8},{10,11... | collective-permute-start | bytes 1179656 | tf_op jit(solution)/shard_map/ppermute | solution.py:347
  15.6 22.6 %slice-start = ((s8[4718592]{0:T(1024)(128)(4,1)}), s8[4194304]{0:T(1024)(128)(4,1)S(1)}, s32[]{:S(2)}) async-start(s8[4718592]{0:T(1024)(128)(4,1)} %bitcast.2), calls=%async_computation | async-start | bytes 8388608
  25.7 12.5 %slice-start.1 = ((s8[4718592]{0:T(1024)(128)(4,1)}), s8[524288]{0:T(1024)(128)(4,1)S(1)}, s32[]{:S(2)}) async-start(s8[4718592]{0:T(1024)(128)(4,1)} %bitcast.2), calls=%async_computation.1 | async-start | bytes 1048576
  27.2 12.0 %collective-permute-start.4 = (bf16[384,512]{1,0:T(8,128)(2,1)S(1)}, bf16[384,512]{1,0:T(8,128)(2,1)S(1)}, u32[]{:S(2)}, u32[]{:S(2)}) collective-permute-start(bf16[384,512]{1,0:T(8,128)(2,1)S(1)} %get-tuple-element.37), channel_id=1, source_target_pairs={{0,1},{1,0},{2,3},{3,2},{4,5},{5,4},{6,7},{7,6},{8,9},{9,8},{10,11... | collective-permute-start | bytes 1179656 | tf_op jit(solution)/shard_map/ppermute | solution.py:347
  27.3 10.9 %collective-permute-start.5 = (bf16[384,512]{1,0:T(8,128)(2,1)S(1)}, bf16[384,512]{1,0:T(8,128)(2,1)S(1)}, u32[]{:S(2)}, u32[]{:S(2)}) collective-permute-start(bf16[384,512]{1,0:T(8,128)(2,1)S(1)} %get-tuple-element.39), channel_id=1, source_target_pairs={{0,3},{1,2},{2,1},{3,0},{4,7},{5,6},{6,5},{7,4},{8,11},{9,10},{10,... | collective-permute-start | bytes 1179656 | tf_op jit(solution)/shard_map/ppermute | solution.py:347
  28.6 18.6 %collective-permute-start.8 = (bf16[384,512]{1,0:T(8,128)(2,1)S(1)}, bf16[384,512]{1,0:T(8,128)(2,1)S(1)}, u32[]{:S(2)}, u32[]{:S(2)}) collective-permute-start(bf16[384,512]{1,0:T(8,128)(2,1)S(1)} %get-tuple-element.44), channel_id=1, source_target_pairs={{0,2},{1,3},{2,0},{3,1},{4,6},{5,7},{6,4},{7,5},{8,10},{9,11},{10,... | collective-permute-start | bytes 1179656 | tf_op jit(solution)/shard_map/ppermute | solution.py:347
  30.1 19.2 %collective-permute-start.7 = (bf16[384,512]{1,0:T(8,128)(2,1)S(1)}, bf16[384,512]{1,0:T(8,128)(2,1)S(1)}, u32[]{:S(2)}, u32[]{:S(2)}) collective-permute-start(bf16[384,512]{1,0:T(8,128)(2,1)S(1)} %get-tuple-element.43), channel_id=1, source_target_pairs={{0,4},{8,12},{16,20},{24,28},{4,0},{12,8},{20,16},{28,24},{1,5},{9... | collective-permute-start | bytes 1179656 | tf_op jit(solution)/shard_map/ppermute | solution.py:353
  32.5 16.8 %collective-permute-start.9 = (bf16[384,512]{1,0:T(8,128)(2,1)S(1)}, bf16[384,512]{1,0:T(8,128)(2,1)S(1)}, u32[]{:S(2)}, u32[]{:S(2)}) collective-permute-start(bf16[384,512]{1,0:T(8,128)(2,1)S(1)} %get-tuple-element.45), channel_id=1, source_target_pairs={{4,8},{12,16},{20,24},{8,4},{16,12},{24,20},{5,9},{13,17},{21,25},... | collective-permute-start | bytes 1179656 | tf_op jit(solution)/shard_map/ppermute | solution.py:353

commit v8 on v7

--- a/solution.py
+++ b/solution.py
@@ -61,16 +61,27 @@
     return lax.axis_index("ctx") % 2
 
 
-def upstream_kernel(order, channels, near, far, pw_ref, cot_ref, x_ref, *rest):
+def end_copy(x_ref, end_ref, which, sem):
+    length, halo = x_ref.shape[1], end_ref.shape[1]
+    return pltpu.make_async_copy(x_ref.at[:, lanes(which * (length - halo), halo)], end_ref, sem)
+
+
+def near_source_kernel(x_ref, near_ref, sem):
+    copy = end_copy(x_ref, near_ref, 1 - odd_place(), sem)
+    copy.start()
+    copy.wait()
+
+
+def upstream_kernel(order, channels, first, with_far, pw_ref, cot_ref, x_ref, *rest):
     count = len(order)
     piece_refs, rest = rest[:count], rest[count:]
     columns_ref, total_ref, sems = rest[-3:]
-    cot_in = rest[0] if near else cot_ref
-    ch, odd = lax.axis_index("ch"), odd_place()
+    cot_in = rest[0] if first else cot_ref
+    ch = lax.axis_index("ch")
     blocks = []
     for m in range(0, cot_in.shape[0], UPSTREAM_ROWS):
         rows = slice(m, m + UPSTREAM_ROWS)
-        pairs = [(cot_ref.at[rows], cot_in.at[rows])] if near else []
+        pairs = [(cot_ref.at[rows], cot_in.at[rows])] if first else []
         if channels % 128 == 0:
             for place, k in enumerate(order):
                 columns = lanes((ch ^ k) * channels, channels)
@@ -85,15 +96,9 @@
         for copy in copies:
             copy.start()
         blocks.append((rows, copies))
-    end = None
-    if near or far:
-        end_ref = rest[-4]
-        length, halo = x_ref.shape[1], end_ref.shape[1]
-        at_end = 1 - odd if near else odd
-        end = pltpu.make_async_copy(
-            x_ref.at[:, lanes(at_end * (length - halo), halo)], end_ref, sems.at[0, count + 1]
-        )
-        end.start()
+    if with_far:
+        far = end_copy(x_ref, rest[-4], odd_place(), sems.at[0, count + 1])
+        far.start()
     for step, (rows, copies) in enumerate(blocks):
         for copy in copies:
             copy.wait()
@@ -106,8 +111,8 @@
                 total_ref[held, :] = part
             else:
                 piece_refs[place][...] = part.astype(BF16)
-    if end is not None:
-        end.wait()
+    if with_far:
+        far.wait()
 
 
 def columns_of(pw_weight, channels, order):
@@ -119,15 +124,15 @@
     )
 
 
-def upstream(pw_weight, cotangent, inputs, order, near, far):
+def upstream(pw_weight, cotangent, inputs, order, first, with_far):
     channels = inputs.shape[0]
     total, width = cotangent.shape
     count = len(order)
     outs = [((channels, width), BF16, True)] * count
-    outs += [(cotangent.shape, BF16, True)] * near + [((channels, DILATION_STEP), BF16, True)] * (near or far)
+    outs += [(cotangent.shape, BF16, True)] * first + [((channels, DILATION_STEP), BF16, True)] * with_far
     results = kernel_call(
-        "upstream", functools.partial(upstream_kernel, order, channels, near, far),
-        [(columns_of(pw_weight, channels, order), False), (cotangent, not near), (inputs, False)], outs,
+        "upstream", functools.partial(upstream_kernel, order, channels, first, with_far),
+        [(columns_of(pw_weight, channels, order), False), (cotangent, not first), (inputs, False)], outs,
         [
             pltpu.VMEM((total, count * channels), BF16), pltpu.VMEM((count * channels, width), F32),
             DMA((total // UPSTREAM_ROWS, count + 2)),
@@ -141,19 +146,23 @@
 
 
 def interior_kernel(n, x_ref, w_ref, *rest):
-    active_refs, (slope_ref, wide, plain_ref, turned_ref, sem) = rest[:n], rest[n:]
+    active_refs, (slope_ref, wide, plain_ref, turned_ref, own_ref, sem, own_sem) = rest[:n], rest[n:]
     ch = lax.axis_index("ch")
     channels, length = x_ref.shape
     group = w_ref.shape[1]
+    own = w_ref.at[:, :, lanes(ch * channels, channels)] if w_ref.shape[2] > channels else w_ref
+    own_copy = pltpu.make_async_copy(own, own_ref, own_sem)
+    own_copy.start()
     halo = DILATION_STEP
     block = length // n
     unit = min(block, 256)
     copy = pltpu.make_async_copy(x_ref, wide.at[:, halo:halo + length], sem)
     copy.start()
     groups = [slice(g, g + group) for g in range(0, channels, group)]
+    own_copy.wait()
     for t in range(3):
         for rows in groups:
-            square = w_ref[t, :, rows]
+            square = own_ref[t, :, rows]
             turned_ref[2 - t, rows, :] = square
             plain_ref[t, rows, :] = square.T
     copy.wait()
@@ -177,26 +186,29 @@
     outs += [((channels, length), F32, True), ((channels, length + 2 * DILATION_STEP), BF16, True)]
     outs += [((3, channels, group), BF16, True)] * 2
     results = kernel_call(
-        "interior", functools.partial(interior_kernel, n), [(inputs, False), (weight, True)], outs, [DMA],
+        "interior", functools.partial(interior_kernel, n), [(inputs, False), (weight, False)], outs,
+        [pltpu.VMEM((3, group, channels), BF16), DMA, DMA],
     )
     return results[:n], *results[n:]
 
 
-def ends_kernel(n, _, near_ref, __, far_ref, plain_ref, *rest):
-    active_refs, (slope_ref, wide) = rest[n + 2:n + 2 + n], rest[n + 2 + n:]
+def end_kernel(n, near, waits, *refs):
+    halo_ref, plain_ref, rest = refs[waits], refs[waits + 1], refs[-(n + 2):]
+    active_refs, (slope_ref, wide) = rest[:n], rest[n:]
     ch, odd = lax.axis_index("ch"), odd_place()
     channels, length = slope_ref.shape
     group = plain_ref.shape[2]
-    halo = near_ref.shape[1]
+    halo = halo_ref.shape[1]
     block = length // n
     unit = min(block, 256)
     groups = [slice(g, g + group) for g in range(0, channels, group)]
-    wide[:, lanes((1 - odd) * (halo + length), halo)] = near_ref[...]
-    wide[:, lanes(odd * (halo + length), halo)] = far_ref[...]
+    at_end = 1 - odd if near else odd
+    wide[:, lanes(at_end * (halo + length), halo)] = halo_ref[...]
+    first = at_end * (length - halo)
     for k in range(n):
         base = (ch ^ k) * block
 
-        @pl.when((base < halo) | (base >= length - halo))
+        @pl.when((base >= first) & (base < first + halo))
         def _(k=k, base=base):
             for s in range(0, block, unit):
                 for rows in groups:
@@ -205,15 +217,15 @@
                     slope_ref[rows, lanes(base + s, unit)] = slope
 
 
-def both_ends(first, near, second, far, plain, active, slope, wide):
+def one_end(near, halo, plain, active, slope, wide, waited):
     n = len(active)
-    operands = [(o, True) for o in (first, near, second, far, plain, *active, slope, wide)]
+    operands = [(o, True) for o in (*waited, halo, plain, *active, slope, wide)]
     results = kernel_call(
-        "ends", functools.partial(ends_kernel, n), operands,
+        "near_end" if near else "far_end", functools.partial(end_kernel, n, near, len(waited)), operands,
         [(a.shape, a.dtype, True) for a in (*active, slope, wide)],
-        aliases={5 + i: i for i in range(n + 2)},
-    )
-    return results[:n], results[n]
+        aliases={len(waited) + 2 + i: i for i in range(n + 2)},
+    )
+    return results[:n], *results[n:]
 
 
 def grad_kernel(order, slope_ref, *rest):
@@ -288,26 +300,37 @@
     copy.wait()
 
 
-def tail_kernel(order, pw_ref, sum_ref, near_ref, *rest):
-    piece_refs, rest = rest[:len(order)], rest[len(order):]
-    far_ref, grad_ref, turned_ref, _, mixed_ref, out_ref, held, ends, halos, sems = rest
-    channels, length = grad_ref.shape
-    group, halo, unit = turned_ref.shape[2], DILATION_STEP, 256
+def late_mix_kernel(order, pw_ref, sum_ref, *rest):
+    piece_refs, (out_ref, done_ref, held, sems) = rest[:len(order)], rest[len(order):]
     pieces = jnp.concatenate([p[...] for p in piece_refs], axis=0)
+    step = 512
     copies = []
-
-    def send(source, place):
-        copies.append(pltpu.make_async_copy(source, place, sems.at[len(copies)]))
-        copies[-1].start()
-
-    step = 512
     for m in range(0, sum_ref.shape[0], step):
         rows = slice(m, m + step)
         held[rows, :] = (sum_ref[rows, :] + columns_times(order, pw_ref, rows, pieces)).astype(BF16)
-        send(held.at[rows, :], mixed_ref.at[rows, :])
+        copies.append(pltpu.make_async_copy(held.at[rows, :], out_ref.at[rows, :], sems.at[len(copies)]))
+        copies[-1].start()
+    done_ref[...] = jnp.zeros_like(done_ref)
+    for copy in copies:
+        copy.wait()
+
+
+def late_mix(pw_weight, order, active, partial):
+    operands = [columns_of(pw_weight, active[order[0]].shape[0], order), partial, *[active[k] for k in order]]
+    return kernel_call(
+        "late_mix", functools.partial(late_mix_kernel, order), [(o, True) for o in operands],
+        [(partial.shape, BF16, False), ((8, 128), F32, True)],
+        [pltpu.VMEM(partial.shape, BF16), DMA((partial.shape[0] // 512,))],
+    )
+
+
+def back_ends_kernel(near_ref, far_ref, grad_ref, turned_ref, _, __, out_ref, ends, halos, sems):
+    channels, length = grad_ref.shape
+    group, halo, unit = turned_ref.shape[2], DILATION_STEP, 256
     odd = odd_place()
     halos[:, lanes((1 - odd) * halo, halo)] = near_ref[...]
     halos[:, lanes(odd * halo, halo)] = far_ref[...]
+    copies = []
     for end in range(2):
         for g in range(0, channels, group):
             rows = slice(g, g + group)
@@ -320,24 +343,21 @@
                 outer = halos[rows, end * halo + s:end * halo + s + unit]
                 taps = taps + [outer] if end else [outer] + taps
                 ends[rows, end * halo + s:end * halo + s + unit] = back(turned_ref, rows, taps)
-        send(
+        copies.append(pltpu.make_async_copy(
             ends.at[:, end * halo:(end + 1) * halo],
-            out_ref.at[:, end * (length - halo):end * (length - halo) + halo],
-        )
+            out_ref.at[:, end * (length - halo):end * (length - halo) + halo], sems.at[end],
+        ))
+        copies[-1].start()
     for copy in copies:
         copy.wait()
 
 
-def tail(pw_weight, order, partial, active, grad, near, far, turned, grad_inputs):
+def back_ends(near, far, grad, turned, done, grad_inputs):
     channels, halo = near.shape
-    operands = [columns_of(pw_weight, channels, order), partial, near, *[active[k] for k in order]]
-    operands = [(o, True) for o in (*operands, far, grad, turned)] + [(grad_inputs, False)]
+    operands = [(o, True) for o in (near, far, grad, turned, done)] + [(grad_inputs, False)]
     return kernel_call(
-        "tail", functools.partial(tail_kernel, order), operands,
-        [(partial.shape, BF16, False), (grad_inputs.shape, BF16, False)],
-        [pltpu.VMEM(partial.shape, BF16)] + [pltpu.VMEM((channels, 2 * halo), BF16)] * 2
-        + [DMA((partial.shape[0] // 512 + 2,))],
-        {len(operands) - 1: 1},
+        "back_ends", back_ends_kernel, operands, [(grad_inputs.shape, BF16, False)],
+        [pltpu.VMEM((channels, 2 * halo), BF16)] * 2 + [DMA((2,))], {5: 0},
     )
 
 
@@ -360,12 +380,15 @@
     order = list(range(n - 1, -1, -1))
     first, second, rest = order[:n // 4], order[n // 4:n // 2], order[n // 2:]
 
-    weight = lax.dynamic_slice_in_dim(
-        jnp.swapaxes(conv_weight, 1, 2), lax.axis_index("ch") * channels, channels, 2
-    )
-    pieces, cot_in, near = upstream(pw_weight, cotangent, inputs, first, True, False)
+    weight = jnp.swapaxes(conv_weight, 1, 2)
+    if channels % 128 != 0:
+        weight = lax.dynamic_slice_in_dim(weight, lax.axis_index("ch") * channels, channels, 2)
+    (near,) = kernel_call(
+        "near_source", near_source_kernel, [(inputs, False)], [((channels, halo), BF16, True)], [DMA]
+    )
+    near = swap(near, 0)
+    pieces, cot_in = upstream(pw_weight, cotangent, inputs, first, True, False)
     ups = {k: exchange(p, k) for k, p in zip(first, pieces)}
-    near = swap(near, 0)
     pieces, far = upstream(pw_weight, cot_in, inputs, second, False, True)
     ups.update({k: exchange(p, k) for k, p in zip(second, pieces)})
     far = swap(far, 1)
@@ -373,7 +396,10 @@
     ups.update({k: exchange(p, k) for k, p in zip(rest, pieces)})
 
     active, slope, wide, plain, turned = interior(inputs, weight, n)
-    active, slope = both_ends(ups[first[0]], near, ups[second[0]], far, plain, active, slope, wide)
+    active, slope, wide = one_end(True, near, plain, active, slope, wide, [])
+    active, slope, wide = one_end(
+        False, far, plain, active, slope, wide, [ups[first[0]], ups[second[0]]]
+    )
     grad, near_grad, far_grad = grad_conv(slope, order, ups)
     active = {k: exchange(active[k], k) for k in order}
     near_grad, far_grad = swap(near_grad, 0), swap(far_grad, 1)
@@ -384,7 +410,9 @@
     )
     partial = mix("early_mix", pw_weight, first, active, [])
     (partial,) = mix("half_mix", pw_weight, rest, active, partial)
-    return tuple(tail(pw_weight, second, partial, active, grad, near_grad, far_grad, turned, grad_inputs))
+    mixed, done = late_mix(pw_weight, second, active, partial)
+    (grad_inputs,) = back_ends(near_grad, far_grad, grad, turned, done, grad_inputs)
+    return mixed, grad_inputs
 
 
 def solution(mesh):

time: 52 us -> 51.4 us (0.988)
  starting transfers between devices: 10.9 us -> 8.89 us
  waiting for transfers between devices: 18.1 us -> 19.9 us
    ppermute x6, waiting for transfers between devices: 9.37 us -> 19.9 us  [exchange(): lax.ppermute(piece, 'ch', [(i, i ^ k) for i in range(lax.axis_size('ch'))])]
    ppermute x4, waiting for transfers between devices: 8.76 us -> 0.01 us  [swap(): return lax.ppermute(values, 'ctx', pairs + [(b, a) for a, b in pairs])]
    ppermute x6, starting transfers between devices: 5.46 us -> 4.28 us  [exchange(): lax.ppermute(piece, 'ch', [(i, i ^ k) for i in range(lax.axis_size('ch'))])]
    ppermute x4, starting transfers between devices: 5.47 us -> 4.61 us  [swap(): return lax.ppermute(values, 'ctx', pairs + [(b, a) for a, b in pairs])]
    pallas_call x10 -> x13, Pallas kernels: 21.8 us -> 21.4 us  [kernel_call(): pl.pallas_call(kernel, in_specs=[INSIDE if held else ANY for _, held in o...]
  transfers between devices with their start and end apart: 10 -> 10, of which waited for: 4 -> 3; matrix products, arithmetic and copies ran while one was open for 0% -> 0% of each run, Pallas kernels for 31% -> 37%
where the time goes in v8:
time: 51.4 us; the launch traced here: 51.1 us
  Pallas kernels  21.4 us (42%)
  waiting for transfers between devices  19.9 us (39%)
  starting transfers between devices  8.89 us (17%)
  between operations  0.95 us (2%)
    pallas_call x13, Pallas kernels, kernel_call(): pl.pallas_call(kernel, in_specs=[INSIDE if held else ANY for _, held in o...  21.4 us
    ppermute x6, waiting for transfers between devices, exchange(): lax.ppermute(piece, 'ch', [(i, i ^ k) for i in range(lax.axis_size('ch'))])  19.9 us
    ppermute x4, starting transfers between devices, swap(): return lax.ppermute(values, 'ctx', pairs + [(b, a) for a, b in pairs])  4.61 us
    ppermute x6, starting transfers between devices, exchange(): lax.ppermute(piece, 'ch', [(i, i ^ k) for i in range(lax.axis_size('ch'))])  4.28 us
  transfers between devices with their start and end apart: 10, of which 3 were waited for; matrix products, arithmetic and copies ran while one was open for 0% of the time, Pallas kernels for 37%

profile of v8, /device:TPU:0, one launch (start us, length us, event | category | flops | bytes accessed | tf_op | source)
XLA Modules:
  0.0 51.1 jit_solution(5533028978817949466)
XLA Ops:
  0.6 1.0 %near_source.1 = bf16[384,512]{1,0:T(8,128)(2,1)S(1)} custom-call(bf16[384,2048]{1,0:T(8,128)(2,1)} %x_ref.9), custom_call_target="tpu_custom_call" | custom-call | tf_op jit(solution)/shard_map/near_source/pallas_call | solution.py:19
  1.7 3.0 %collective-permute-start.3 = (bf16[384,512]{1,0:T(8,128)(2,1)S(1)}, bf16[384,512]{1,0:T(8,128)(2,1)S(1)}, u32[]{:S(2)}, u32[]{:S(2)}) collective-permute-start(bf16[384,512]{1,0:T(8,128)(2,1)S(1)} %near_source.1), channel_id=1, source_target_pairs={{0,4},{8,12},{16,20},{24,28},{4,0},{12,8},{20,16},{28,24},{1,5},{9... | collective-permute-start | bytes 1179656 | tf_op jit(solution)/shard_map/ppermute | solution.py:373
  4.7 2.2 %upstream.3 = (bf16[384,512]{1,0:T(8,128)(2,1)S(1)}, bf16[1536,512]{1,0:T(8,128)(2,1)S(1)}) custom-call(bf16[1536,1536]{1,0:T(8,128)(2,1)} %pw_ref.11, bf16[1536,512]{1,0:T(8,128)(2,1)} %cot_ref.1, bf16[384,2048]{1,0:T(8,128)(2,1)} %x_ref.9), custom_call_target="tpu_custom_call" | custom-call | tf_op jit(solution)/shard_map/upstream/pallas_call | solution.py:19
  6.9 0.7 %collective-permute-start = (bf16[384,512]{1,0:T(8,128)(2,1)S(1)}, bf16[384,512]{1,0:T(8,128)(2,1)S(1)}, u32[]{:S(2)}, u32[]{:S(2)}) collective-permute-start(bf16[384,512]{1,0:T(8,128)(2,1)S(1)} %get-tuple-element.32), channel_id=1, source_target_pairs={{0,3},{1,2},{2,1},{3,0},{4,7},{5,6},{6,5},{7,4},{8,11},{9,10},{10,... | collective-permute-start | bytes 1179656 | tf_op jit(solution)/shard_map/ppermute | solution.py:367
  7.6 2.0 %upstream.4 = (bf16[384,512]{1,0:T(8,128)(2,1)S(1)}, bf16[384,512]{1,0:T(8,128)(2,1)S(1)}) custom-call(bf16[1536,1536]{1,0:T(8,128)(2,1)} %pw_ref.11, bf16[1536,512]{1,0:T(8,128)(2,1)S(1)} %get-tuple-element.33.cot_ref, bf16[384,2048]{1,0:T(8,128)(2,1)} %x_ref.9), custom_call_target="tpu_custom_call" | custom-call | tf_op jit(solution)/shard_map/upstream/pallas_call | solution.py:19
  9.7 0.9 %collective-permute-start.1 = (bf16[384,512]{1,0:T(8,128)(2,1)S(1)}, bf16[384,512]{1,0:T(8,128)(2,1)S(1)}, u32[]{:S(2)}, u32[]{:S(2)}) collective-permute-start(bf16[384,512]{1,0:T(8,128)(2,1)S(1)} %get-tuple-element.34), channel_id=1, source_target_pairs={{0,2},{1,3},{2,0},{3,1},{4,6},{5,7},{6,4},{7,5},{8,10},{9,11},{10,... | collective-permute-start | bytes 1179656 | tf_op jit(solution)/shard_map/ppermute | solution.py:367
  10.6 0.7 %collective-permute-start.2 = (bf16[384,512]{1,0:T(8,128)(2,1)S(1)}, bf16[384,512]{1,0:T(8,128)(2,1)S(1)}, u32[]{:S(2)}, u32[]{:S(2)}) collective-permute-start(bf16[384,512]{1,0:T(8,128)(2,1)S(1)} %get-tuple-element.35), channel_id=1, source_target_pairs={{4,8},{12,16},{20,24},{8,4},{16,12},{24,20},{5,9},{13,17},{21,25},... | collective-permute-start | bytes 1179656 | tf_op jit(solution)/shard_map/ppermute | solution.py:373
  11.3 2.8 %upstream.5 = (bf16[384,512]{1,0:T(8,128)(2,1)S(1)}, bf16[384,512]{1,0:T(8,128)(2,1)S(1)}) custom-call(bf16[1536,1536]{1,0:T(8,128)(2,1)} %pw_ref.11, bf16[1536,512]{1,0:T(8,128)(2,1)S(1)} %get-tuple-element.33.cot_ref, bf16[384,2048]{1,0:T(8,128)(2,1)} %x_ref.9), custom_call_target="tpu_custom_call" | custom-call | tf_op jit(solution)/shard_map/upstream/pallas_call | solution.py:19
  14.1 0.4 collective-permute-start.7
  14.5 3.3 %interior.1 = (bf16[384,512]{1,0:T(8,128)(2,1)S(1)}, bf16[384,512]{1,0:T(8,128)(2,1)S(1)}, bf16[384,512]{1,0:T(8,128)(2,1)S(1)}, bf16[384,512]{1,0:T(8,128)(2,1)...) custom-call(bf16[384,2048]{1,0:T(8,128)(2,1)} %x_ref.9, ...), custom_call_target="tpu_custom_call" | custom-call | tf_op jit(solution)/shard_map/interior/pallas_call | solution.py:19
  17.8 0.0 collective-permute-done.3.refs_0_
  17.8 0.0 slice-start
  17.8 0.8 %near_end.1 = (bf16[384,512]{1,0:T(8,128)(2,1)S(1)}, bf16[384,512]{1,0:T(8,128)(2,1)S(1)}, bf16[384,512]{1,0:T(8,128)(2,1)S(1)}, bf16[384,512]{1,0:T(8,128)(2,1)...) custom-call(bf16[384,512]{1,0:T(8,128)(2,1)S(1)} %collective-permute, ...), custom_call_target="tpu_custom_call", output_to_operand_aliasing={{0}: (2, {}), {1}: (3, {}), {2}: (4, {}), {3}: (5, {}), {4}... | custom-call | tf_op jit(solution)/shard_map/near_end/pallas_call | solution.py:19
  18.6 0.0 collective-permute-done.refs_0_.rest_0_
  18.6 8.2 %collective-permute-done.1.refs_1_.rest_1_ = bf16[384,512]{1,0:T(8,128)(2,1)S(1)} collective-permute-done((bf16[384,512]{1,0:T(8,128)(2,1)S(1)}, bf16[384,512]{1,0:T(8,128)(2,1)S(1)}, u32[]{:S(2)}, u32[]{:S(2)}) %collective-permute-start.1) | collective-permute-done | bytes 393248 | tf_op jit(solution)/shard_map/ppermute | solution.py:367
  26.8 0.0 collective-permute-done.2.refs_2_
  26.8 0.8 %far_end.1 = (bf16[384,512]{1,0:T(8,128)(2,1)S(1)}, bf16[384,512]{1,0:T(8,128)(2,1)S(1)}, bf16[384,512]{1,0:T(8,128)(2,1)S(1)}, bf16[384,512]{1,0:T(8,128)(2,1)S...) custom-call(bf16[384,512]{1,0:T(8,128)(2,1)S(1)} %collective-permute, ...), custom_call_target="tpu_custom_call", output_to_operand_aliasing={{0}: (4, {}), {1}: (5, {}), {2}: (6, {}), {3}: (7, {}), {4}... | custom-call | tf_op jit(solution)/shard_map/far_end/pallas_call | solution.py:19
  27.6 0.1 collective-permute-start.4
  27.7 1.1 %collective-permute-start.5 = (bf16[384,512]{1,0:T(8,128)(2,1)S(1)}, bf16[384,512]{1,0:T(8,128)(2,1)S(1)}, u32[]{:S(2)}, u32[]{:S(2)}) collective-permute-start(bf16[384,512]{1,0:T(8,128)(2,1)S(1)} %get-tuple-element.51), channel_id=1, source_target_pairs={{0,3},{1,2},{2,1},{3,0},{4,7},{5,6},{6,5},{7,4},{8,11},{9,10},{10,... | collective-permute-start | bytes 1179656 | tf_op jit(solution)/shard_map/ppermute | solution.py:367
  28.7 1.0 %collective-permute-start.6 = (bf16[384,512]{1,0:T(8,128)(2,1)S(1)}, bf16[384,512]{1,0:T(8,128)(2,1)S(1)}, u32[]{:S(2)}, u32[]{:S(2)}) collective-permute-start(bf16[384,512]{1,0:T(8,128)(2,1)S(1)} %get-tuple-element.52), channel_id=1, source_target_pairs={{0,2},{1,3},{2,0},{3,1},{4,6},{5,7},{6,4},{7,5},{8,10},{9,11},{10,... | collective-permute-start | bytes 1179656 | tf_op jit(solution)/shard_map/ppermute | solution.py:367
  29.8 0.0 collective-permute-done.7.rest_2_
  29.8 0.6 %grad_conv.1 = (bf16[384,2048]{1,0:T(8,128)(2,1)S(1)}, bf16[384,512]{1,0:T(8,128)(2,1)S(1)}, bf16[384,512]{1,0:T(8,128)(2,1)S(1)}) custom-call(f32[384,2048]{1,0:T(8,128)S(1)} %get-tuple-element.54.slope_ref, bf16[384,512]{1,0:T(8,128)(2,1)S(1)} %collective-permute-done.refs_0_.rest_0_, bf16[384,512]{1,0:T(8,128)(2,1)S(1)} %collective-permute-done.1.refs_1_.rest_1_, ...), custom_call_target="tpu_custom_call" | custom-call | tf_op jit(solution)/shard_map/grad_conv/pallas_call | solution.py:19
  30.4 0.1 collective-permute-start.8
  30.5 0.9 %collective-permute-start.9 = (bf16[384,512]{1,0:T(8,128)(2,1)S(1)}, bf16[384,512]{1,0:T(8,128)(2,1)S(1)}, u32[]{:S(2)}, u32[]{:S(2)}) collective-permute-start(bf16[384,512]{1,0:T(8,128)(2,1)S(1)} %get-tuple-element.58), channel_id=1, source_target_pairs={{4,8},{12,16},{20,24},{8,4},{16,12},{24,20},{5,9},{13,17},{21,25},... | collective-permute-start | bytes 1179656 | tf_op jit(solution)/shard_map/ppermute | solution.py:373
  31.4 1.7 %back_interior.1.__ = bf16[384,2048]{1,0:T(8,128)(2,1)} custom-call(bf16[384,2048]{1,0:T(8,128)(2,1)S(1)} %get-tuple-element.59.grad_ref, bf16[3,384,96]{2,1,0:T(8,128)(2,1)S(1)} %get-tuple-element.60.turned_ref), custom_call_target="tpu_custom_call" | custom-call | tf_op jit(solution)/shard_map/back_interior/pallas_call | solution.py:19
  33.0 5.5 %collective-permute-done.5.rest_0_ = bf16[384,512]{1,0:T(8,128)(2,1)S(1)} collective-permute-done((bf16[384,512]{1,0:T(8,128)(2,1)S(1)}, bf16[384,512]{1,0:T(8,128)(2,1)S(1)}, u32[]{:S(2)}, u32[]{:S(2)}) %collective-permute-start.5) | collective-permute-done | bytes 393248 | tf_op jit(solution)/shard_map/ppermute | solution.py:367
  38.6 1.0 %early_mix.1.rest_2_ = f32[1536,512]{1,0:T(8,128)S(1)} custom-call(bf16[1536,1536]{1,0:T(8,128)(2,1)S(1)} %bitcast.2, bf16[384,512]{1,0:T(8,128)(2,1)S(1)} %collective-permute-done.5.rest_0_), custom_call_target="tpu_custom_call" | custom-call | tf_op jit(solution)/shard_map/early_mix/pallas_call | solution.py:19
  39.6 1.8 %half_mix.1.sum_ref = f32[1536,512]{1,0:T(8,128)S(1)} custom-call(bf16[1536,1536]{1,0:T(8,128)(2,1)S(1)} %bitcast.2, bf16[384,512]{1,0:T(8,128)(2,1)S(1)} %collective-permute-done.4.rest_0_, bf16[384,512]{1,0:T(8,128)(2,1)S(1)} %get-tuple-element.50.rest_1_, f32[1536,512]{1,0:T(8,128)S(1)} %early_mix.1.rest_2_), custom_call_target="tpu_custom_call", output_to_operand_aliasing={{}: (3, {})} | custom-call | tf_op jit(solution)/shard_map/half_mix/pallas_call | solution.py:19
  41.4 6.2 %collective-permute-done.6.rest_0_ = bf16[384,512]{1,0:T(8,128)(2,1)S(1)} collective-permute-done((bf16[384,512]{1,0:T(8,128)(2,1)S(1)}, bf16[384,512]{1,0:T(8,128)(2,1)S(1)}, u32[]{:S(2)}, u32[]{:S(2)}) %collective-permute-start.6) | collective-permute-done | bytes 393248 | tf_op jit(solution)/shard_map/ppermute | solution.py:367
  47.6 1.8 %late_mix.1 = (bf16[1536,512]{1,0:T(8,128)(2,1)}, f32[8,128]{1,0:T(8,128)S(1)}) custom-call(bf16[1536,1536]{1,0:T(8,128)(2,1)S(1)} %bitcast.2, f32[1536,512]{1,0:T(8,128)S(1)} %half_mix.1.sum_ref, bf16[384,512]{1,0:T(8,128)(2,1)S(1)} %collective-permute-done.6.rest_0_), custom_call_target="tpu_custom_call" | custom-call | tf_op jit(solution)/shard_map/late_mix/pallas_call | solution.py:19
  49.4 0.0 collective-permute-done.8.near_ref
  49.4 1.6 %back_ends.1 = bf16[384,2048]{1,0:T(8,128)(2,1)} custom-call(bf16[384,512]{1,0:T(8,128)(2,1)S(1)} %collective-permute-done.8.near_ref, bf16[384,512]{1,0:T(8,128)(2,1)S(1)} %collective-permute-done.9.far_ref, bf16[384,2048]{1,0:T(8,128)(2,1)S(1)} %get-tuple-element.59.grad_ref, ...), custom_call_target="tpu_custom_call", output_to_operand_aliasing={{}: (5, {})} | custom-call | tf_op jit(solution)/shard_map/back_ends/pallas_call | solution.py:19
  (6 shorter events, 0.0 us)
Async XLA Ops:
  1.7 16.2 %collective-permute-start.3 = (bf16[384,512]{1,0:T(8,128)(2,1)S(1)}, bf16[384,512]{1,0:T(8,128)(2,1)S(1)}, u32[]{:S(2)}, u32[]{:S(2)}) collective-permute-start(bf16[384,512]{1,0:T(8,128)(2,1)S(1)} %near_source.1), channel_id=1, source_target_pairs={{0,4},{8,12},{16,20},{24,28},{4,0},{12,8},{20,16},{28,24},{1,5},{9... | collective-permute-start | bytes 1179656 | tf_op jit(solution)/shard_map/ppermute | solution.py:373
  6.9 11.7 %collective-permute-start = (bf16[384,512]{1,0:T(8,128)(2,1)S(1)}, bf16[384,512]{1,0:T(8,128)(2,1)S(1)}, u32[]{:S(2)}, u32[]{:S(2)}) collective-permute-start(bf16[384,512]{1,0:T(8,128)(2,1)S(1)} %get-tuple-element.32), channel_id=1, source_target_pairs={{0,3},{1,2},{2,1},{3,0},{4,7},{5,6},{6,5},{7,4},{8,11},{9,10},{10,... | collective-permute-start | bytes 1179656 | tf_op jit(solution)/shard_map/ppermute | solution.py:367
  9.7 17.1 %collective-permute-start.1 = (bf16[384,512]{1,0:T(8,128)(2,1)S(1)}, bf16[384,512]{1,0:T(8,128)(2,1)S(1)}, u32[]{:S(2)}, u32[]{:S(2)}) collective-permute-start(bf16[384,512]{1,0:T(8,128)(2,1)S(1)} %get-tuple-element.34), channel_id=1, source_target_pairs={{0,2},{1,3},{2,0},{3,1},{4,6},{5,7},{6,4},{7,5},{8,10},{9,11},{10,... | collective-permute-start | bytes 1179656 | tf_op jit(solution)/shard_map/ppermute | solution.py:367
  10.6 16.2 %collective-permute-start.2 = (bf16[384,512]{1,0:T(8,128)(2,1)S(1)}, bf16[384,512]{1,0:T(8,128)(2,1)S(1)}, u32[]{:S(2)}, u32[]{:S(2)}) collective-permute-start(bf16[384,512]{1,0:T(8,128)(2,1)S(1)} %get-tuple-element.35), channel_id=1, source_target_pairs={{4,8},{12,16},{20,24},{8,4},{16,12},{24,20},{5,9},{13,17},{21,25},... | collective-permute-start | bytes 1179656 | tf_op jit(solution)/shard_map/ppermute | solution.py:373
  14.1 15.7 %collective-permute-start.7 = (bf16[384,512]{1,0:T(8,128)(2,1)S(1)}, bf16[384,512]{1,0:T(8,128)(2,1)S(1)}, u32[]{:S(2)}, u32[]{:S(2)}) collective-permute-start(bf16[384,512]{1,0:T(8,128)(2,1)S(1)} %get-tuple-element.55), channel_id=1, source_target_pairs={{0,1},{1,0},{2,3},{3,2},{4,5},{5,4},{6,7},{7,6},{8,9},{9,8},{10,11... | collective-permute-start | bytes 1179656 | tf_op jit(solution)/shard_map/ppermute | solution.py:367
  17.8 20.7 %slice-start = ((s8[4718592]{0:T(1024)(128)(4,1)}), s8[4194304]{0:T(1024)(128)(4,1)S(1)}, s32[]{:S(2)}) async-start(s8[4718592]{0:T(1024)(128)(4,1)} %bitcast.1), calls=%async_computation | async-start | bytes 8388608
  26.8 11.8 %slice-start.1 = ((s8[4718592]{0:T(1024)(128)(4,1)}), s8[524288]{0:T(1024)(128)(4,1)S(1)}, s32[]{:S(2)}) async-start(s8[4718592]{0:T(1024)(128)(4,1)} %bitcast.1), calls=%async_computation.1 | async-start | bytes 1048576
  27.6 12.0 %collective-permute-start.4 = (bf16[384,512]{1,0:T(8,128)(2,1)S(1)}, bf16[384,512]{1,0:T(8,128)(2,1)S(1)}, u32[]{:S(2)}, u32[]{:S(2)}) collective-permute-start(bf16[384,512]{1,0:T(8,128)(2,1)S(1)} %get-tuple-element.49), channel_id=1, source_target_pairs={{0,1},{1,0},{2,3},{3,2},{4,5},{5,4},{6,7},{7,6},{8,9},{9,8},{10,11... | collective-permute-start | bytes 1179656 | tf_op jit(solution)/shard_map/ppermute | solution.py:367
  27.7 10.9 %collective-permute-start.5 = (bf16[384,512]{1,0:T(8,128)(2,1)S(1)}, bf16[384,512]{1,0:T(8,128)(2,1)S(1)}, u32[]{:S(2)}, u32[]{:S(2)}) collective-permute-start(bf16[384,512]{1,0:T(8,128)(2,1)S(1)} %get-tuple-element.51), channel_id=1, source_target_pairs={{0,3},{1,2},{2,1},{3,0},{4,7},{5,6},{6,5},{7,4},{8,11},{9,10},{10,... | collective-permute-start | bytes 1179656 | tf_op jit(solution)/shard_map/ppermute | solution.py:367
  28.7 18.8 %collective-permute-start.6 = (bf16[384,512]{1,0:T(8,128)(2,1)S(1)}, bf16[384,512]{1,0:T(8,128)(2,1)S(1)}, u32[]{:S(2)}, u32[]{:S(2)}) collective-permute-start(bf16[384,512]{1,0:T(8,128)(2,1)S(1)} %get-tuple-element.52), channel_id=1, source_target_pairs={{0,2},{1,3},{2,0},{3,1},{4,6},{5,7},{6,4},{7,5},{8,10},{9,11},{10,... | collective-permute-start | bytes 1179656 | tf_op jit(solution)/shard_map/ppermute | solution.py:367
  30.4 19.0 %collective-permute-start.8 = (bf16[384,512]{1,0:T(8,128)(2,1)S(1)}, bf16[384,512]{1,0:T(8,128)(2,1)S(1)}, u32[]{:S(2)}, u32[]{:S(2)}) collective-permute-start(bf16[384,512]{1,0:T(8,128)(2,1)S(1)} %get-tuple-element.57), channel_id=1, source_target_pairs={{0,4},{8,12},{16,20},{24,28},{4,0},{12,8},{20,16},{28,24},{1,5},{9... | collective-permute-start | bytes 1179656 | tf_op jit(solution)/shard_map/ppermute | solution.py:373
  30.5 18.9 %collective-permute-start.9 = (bf16[384,512]{1,0:T(8,128)(2,1)S(1)}, bf16[384,512]{1,0:T(8,128)(2,1)S(1)}, u32[]{:S(2)}, u32[]{:S(2)}) collective-permute-start(bf16[384,512]{1,0:T(8,128)(2,1)S(1)} %get-tuple-element.58), channel_id=1, source_target_pairs={{4,8},{12,16},{20,24},{8,4},{16,12},{24,20},{5,9},{13,17},{21,25},... | collective-permute-start | bytes 1179656 | tf_op jit(solution)/shard_map/ppermute | solution.py:373

commit v9 on v8

--- a/solution.py
+++ b/solution.py
@@ -61,18 +61,7 @@
     return lax.axis_index("ctx") % 2
 
 
-def end_copy(x_ref, end_ref, which, sem):
-    length, halo = x_ref.shape[1], end_ref.shape[1]
-    return pltpu.make_async_copy(x_ref.at[:, lanes(which * (length - halo), halo)], end_ref, sem)
-
-
-def near_source_kernel(x_ref, near_ref, sem):
-    copy = end_copy(x_ref, near_ref, 1 - odd_place(), sem)
-    copy.start()
-    copy.wait()
-
-
-def upstream_kernel(order, channels, first, with_far, pw_ref, cot_ref, x_ref, *rest):
+def upstream_kernel(order, channels, first, pw_ref, cot_ref, x_ref, *rest):
     count = len(order)
     piece_refs, rest = rest[:count], rest[count:]
     columns_ref, total_ref, sems = rest[-3:]
@@ -96,9 +85,12 @@
         for copy in copies:
             copy.start()
         blocks.append((rows, copies))
-    if with_far:
-        far = end_copy(x_ref, rest[-4], odd_place(), sems.at[0, count + 1])
-        far.start()
+    which = 1 - odd_place() if first else odd_place()
+    length, halo = x_ref.shape[1], rest[-4].shape[1]
+    end = pltpu.make_async_copy(
+        x_ref.at[:, lanes(which * (length - halo), halo)], rest[-4], sems.at[0, count + 1]
+    )
+    end.start()
     for step, (rows, copies) in enumerate(blocks):
         for copy in copies:
             copy.wait()
@@ -111,8 +103,7 @@
                 total_ref[held, :] = part
             else:
                 piece_refs[place][...] = part.astype(BF16)
-    if with_far:
-        far.wait()
+    end.wait()
 
 
 def columns_of(pw_weight, channels, order):
@@ -124,14 +115,15 @@
     )
 
 
-def upstream(pw_weight, cotangent, inputs, order, first, with_far):
+def upstream(pw_weight, cotangent, inputs, order, first):
     channels = inputs.shape[0]
     total, width = cotangent.shape
     count = len(order)
     outs = [((channels, width), BF16, True)] * count
-    outs += [(cotangent.shape, BF16, True)] * first + [((channels, DILATION_STEP), BF16, True)] * with_far
+    outs += [(cotangent.shape, BF16, True)] * first
+    outs += [((channels, DILATION_STEP), BF16, True)]
     results = kernel_call(
-        "upstream", functools.partial(upstream_kernel, order, channels, first, with_far),
+        "upstream", functools.partial(upstream_kernel, order, channels, first),
         [(columns_of(pw_weight, channels, order), False), (cotangent, not first), (inputs, False)], outs,
         [
             pltpu.VMEM((total, count * channels), BF16), pltpu.VMEM((count * channels, width), F32),
@@ -300,37 +292,26 @@
     copy.wait()
 
 
-def late_mix_kernel(order, pw_ref, sum_ref, *rest):
-    piece_refs, (out_ref, done_ref, held, sems) = rest[:len(order)], rest[len(order):]
+def tail_kernel(order, pw_ref, sum_ref, *rest):
+    piece_refs, rest = rest[:len(order)], rest[len(order):]
+    near_ref, far_ref, grad_ref, turned_ref, _, mixed_ref, out_ref, held, ends, halos, sems = rest
+    channels, length = grad_ref.shape
+    group, halo, unit = turned_ref.shape[2], DILATION_STEP, 256
     pieces = jnp.concatenate([p[...] for p in piece_refs], axis=0)
+    copies = []
+
+    def send(source, place):
+        copies.append(pltpu.make_async_copy(source, place, sems.at[len(copies)]))
+        copies[-1].start()
+
     step = 512
-    copies = []
     for m in range(0, sum_ref.shape[0], step):
         rows = slice(m, m + step)
         held[rows, :] = (sum_ref[rows, :] + columns_times(order, pw_ref, rows, pieces)).astype(BF16)
-        copies.append(pltpu.make_async_copy(held.at[rows, :], out_ref.at[rows, :], sems.at[len(copies)]))
-        copies[-1].start()
-    done_ref[...] = jnp.zeros_like(done_ref)
-    for copy in copies:
-        copy.wait()
-
-
-def late_mix(pw_weight, order, active, partial):
-    operands = [columns_of(pw_weight, active[order[0]].shape[0], order), partial, *[active[k] for k in order]]
-    return kernel_call(
-        "late_mix", functools.partial(late_mix_kernel, order), [(o, True) for o in operands],
-        [(partial.shape, BF16, False), ((8, 128), F32, True)],
-        [pltpu.VMEM(partial.shape, BF16), DMA((partial.shape[0] // 512,))],
-    )
-
-
-def back_ends_kernel(near_ref, far_ref, grad_ref, turned_ref, _, __, out_ref, ends, halos, sems):
-    channels, length = grad_ref.shape
-    group, halo, unit = turned_ref.shape[2], DILATION_STEP, 256
+        send(held.at[rows, :], mixed_ref.at[rows, :])
     odd = odd_place()
     halos[:, lanes((1 - odd) * halo, halo)] = near_ref[...]
     halos[:, lanes(odd * halo, halo)] = far_ref[...]
-    copies = []
     for end in range(2):
         for g in range(0, channels, group):
             rows = slice(g, g + group)
@@ -343,21 +324,24 @@
                 outer = halos[rows, end * halo + s:end * halo + s + unit]
                 taps = taps + [outer] if end else [outer] + taps
                 ends[rows, end * halo + s:end * halo + s + unit] = back(turned_ref, rows, taps)
-        copies.append(pltpu.make_async_copy(
+        send(
             ends.at[:, end * halo:(end + 1) * halo],
-            out_ref.at[:, end * (length - halo):end * (length - halo) + halo], sems.at[end],
-        ))
-        copies[-1].start()
+            out_ref.at[:, end * (length - halo):end * (length - halo) + halo],
+        )
     for copy in copies:
         copy.wait()
 
 
-def back_ends(near, far, grad, turned, done, grad_inputs):
+def tail(pw_weight, order, partial, active, near, far, grad, turned, grad_inputs):
     channels, halo = near.shape
-    operands = [(o, True) for o in (near, far, grad, turned, done)] + [(grad_inputs, False)]
+    operands = [columns_of(pw_weight, channels, order), partial, *[active[k] for k in order]]
+    operands = [(o, True) for o in (*operands, near, far, grad, turned)] + [(grad_inputs, False)]
     return kernel_call(
-        "back_ends", back_ends_kernel, operands, [(grad_inputs.shape, BF16, False)],
-        [pltpu.VMEM((channels, 2 * halo), BF16)] * 2 + [DMA((2,))], {5: 0},
+        "tail", functools.partial(tail_kernel, order), operands,
+        [(partial.shape, BF16, False), (grad_inputs.shape, BF16, False)],
+        [pltpu.VMEM(partial.shape, BF16)] + [pltpu.VMEM((channels, 2 * halo), BF16)] * 2
+        + [DMA((partial.shape[0] // 512 + 2,))],
+        {len(operands) - 1: 1},
     )
 
 
@@ -383,22 +367,17 @@
     weight = jnp.swapaxes(conv_weight, 1, 2)
     if channels % 128 != 0:
         weight = lax.dynamic_slice_in_dim(weight, lax.axis_index("ch") * channels, channels, 2)
-    (near,) = kernel_call(
-        "near_source", near_source_kernel, [(inputs, False)], [((channels, halo), BF16, True)], [DMA]
-    )
+    pieces, cot_in, near = upstream(pw_weight, cotangent, inputs, first, True)
     near = swap(near, 0)
-    pieces, cot_in = upstream(pw_weight, cotangent, inputs, first, True, False)
     ups = {k: exchange(p, k) for k, p in zip(first, pieces)}
-    pieces, far = upstream(pw_weight, cot_in, inputs, second, False, True)
-    ups.update({k: exchange(p, k) for k, p in zip(second, pieces)})
+    pieces, far = upstream(pw_weight, cot_in, inputs, second + rest, False)
+    ups.update({k: exchange(p, k) for k, p in zip(second + rest, pieces)})
     far = swap(far, 1)
-    (pieces,) = upstream(pw_weight, cot_in, inputs, rest, False, False)
-    ups.update({k: exchange(p, k) for k, p in zip(rest, pieces)})
 
     active, slope, wide, plain, turned = interior(inputs, weight, n)
     active, slope, wide = one_end(True, near, plain, active, slope, wide, [])
     active, slope, wide = one_end(
-        False, far, plain, active, slope, wide, [ups[first[0]], ups[second[0]]]
+        False, far, plain, active, slope, wide, [ups[first[0]]]
     )
     grad, near_grad, far_grad = grad_conv(slope, order, ups)
     active = {k: exchange(active[k], k) for k in order}
@@ -410,9 +389,7 @@
     )
     partial = mix("early_mix", pw_weight, first, active, [])
     (partial,) = mix("half_mix", pw_weight, rest, active, partial)
-    mixed, done = late_mix(pw_weight, second, active, partial)
-    (grad_inputs,) = back_ends(near_grad, far_grad, grad, turned, done, grad_inputs)
-    return mixed, grad_inputs
+    return tuple(tail(pw_weight, second, partial, active, near_grad, far_grad, grad, turned, grad_inputs))
 
 
 def solution(mesh):

time: 51.4 us -> 49.2 us (0.957)
  starting transfers between devices: 8.89 us -> 17.1 us
  waiting for transfers between devices: 19.9 us -> 12.6 us
  Pallas kernels: 21.4 us -> 18.2 us
    ppermute x6, waiting for transfers between devices: 19.9 us -> 10.5 us  [exchange(): lax.ppermute(piece, 'ch', [(i, i ^ k) for i in range(lax.axis_size('ch'))])]
    ppermute x6, starting transfers between devices: 4.28 us -> 9.93 us  [exchange(): lax.ppermute(piece, 'ch', [(i, i ^ k) for i in range(lax.axis_size('ch'))])]
    pallas_call x13 -> x10, Pallas kernels: 21.4 us -> 18.2 us  [kernel_call(): pl.pallas_call(kernel, in_specs=[INSIDE if held else ANY for _, held in o...]
    ppermute x4, starting transfers between devices: 4.61 us -> 7.12 us  [swap(): return lax.ppermute(values, 'ctx', pairs + [(b, a) for a, b in pairs])]
    ppermute x4, waiting for transfers between devices: 0.01 us -> 2.19 us  [swap(): return lax.ppermute(values, 'ctx', pairs + [(b, a) for a, b in pairs])]
  transfers between devices with their start and end apart: 10 -> 10, of which waited for: 3 -> 4; matrix products, arithmetic and copies ran while one was open for 0% -> 0% of each run, Pallas kernels for 37% -> 28%
where the time goes in v9:
time: 49.2 us; the launch traced here: 48.8 us
  Pallas kernels  18.2 us (37%)
  starting transfers between devices  17.1 us (35%)
  waiting for transfers between devices  12.6 us (26%)
  between operations  0.9 us (2%)
    pallas_call x10, Pallas kernels, kernel_call(): pl.pallas_call(kernel, in_specs=[INSIDE if held else ANY for _, held in o...  18.2 us
    ppermute x6, waiting for transfers between devices, exchange(): lax.ppermute(piece, 'ch', [(i, i ^ k) for i in range(lax.axis_size('ch'))])  10.5 us
    ppermute x6, starting transfers between devices, exchange(): lax.ppermute(piece, 'ch', [(i, i ^ k) for i in range(lax.axis_size('ch'))])  9.93 us
    ppermute x4, starting transfers between devices, swap(): return lax.ppermute(values, 'ctx', pairs + [(b, a) for a, b in pairs])  7.12 us
    ppermute x4, waiting for transfers between devices, swap(): return lax.ppermute(values, 'ctx', pairs + [(b, a) for a, b in pairs])  2.19 us
  transfers between devices with their start and end apart: 10, of which 4 were waited for; matrix products, arithmetic and copies ran while one was open for 0% of the time, Pallas kernels for 28%

profile of v9, /device:TPU:0, one launch (start us, length us, event | category | flops | bytes accessed | tf_op | source)
XLA Modules:
  0.0 48.8 jit_solution(9191964121061005997)
XLA Ops:
  0.6 2.2 %upstream.2 = (bf16[384,512]{1,0:T(8,128)(2,1)S(1)}, bf16[1536,512]{1,0:T(8,128)(2,1)S(1)}, bf16[384,512]{1,0:T(8,128)(2,1)S(1)}) custom-call(bf16[1536,1536]{1,0:T(8,128)(2,1)} %pw_ref.9, bf16[1536,512]{1,0:T(8,128)(2,1)} %cot_ref.1, bf16[384,2048]{1,0:T(8,128)(2,1)} %x_ref.5), custom_call_target="tpu_custom_call" | custom-call | tf_op jit(solution)/shard_map/upstream/pallas_call | solution.py:19
  2.8 3.0 %collective-permute-start.2 = (bf16[384,512]{1,0:T(8,128)(2,1)S(1)}, bf16[384,512]{1,0:T(8,128)(2,1)S(1)}, u32[]{:S(2)}, u32[]{:S(2)}) collective-permute-start(bf16[384,512]{1,0:T(8,128)(2,1)S(1)} %get-tuple-element.35), channel_id=1, source_target_pairs={{0,4},{8,12},{16,20},{24,28},{4,0},{12,8},{20,16},{28,24},{1,5},{9... | collective-permute-start | bytes 1179656 | tf_op jit(solution)/shard_map/ppermute | solution.py:357
  5.8 0.7 %collective-permute-start = (bf16[384,512]{1,0:T(8,128)(2,1)S(1)}, bf16[384,512]{1,0:T(8,128)(2,1)S(1)}, u32[]{:S(2)}, u32[]{:S(2)}) collective-permute-start(bf16[384,512]{1,0:T(8,128)(2,1)S(1)} %get-tuple-element.31), channel_id=1, source_target_pairs={{0,3},{1,2},{2,1},{3,0},{4,7},{5,6},{6,5},{7,4},{8,11},{9,10},{10,... | collective-permute-start | bytes 1179656 | tf_op jit(solution)/shard_map/ppermute | solution.py:351
  6.5 3.6 %upstream.3 = (bf16[384,512]{1,0:T(8,128)(2,1)S(1)}, bf16[384,512]{1,0:T(8,128)(2,1)S(1)}, bf16[384,512]{1,0:T(8,128)(2,1)S(1)}, bf16[384,512]{1,0:T(8,128)(2,1)S(1)}) custom-call(bf16[1536,1536]{1,0:T(8,128)(2,1)} %pw_ref.9, bf16[1536,512]{1,0:T(8,128)(2,1)S(1)} %get-tuple-element.32.cot_ref, bf16[384,2048]{1,0:T(8,128)(2,1)} %x_ref.5), custom_call_target="tpu_custom_call" | custom-call | tf_op jit(solution)/shard_map/upstream/pallas_call | solution.py:19
  10.2 0.7 %collective-permute-start.1 = (bf16[384,512]{1,0:T(8,128)(2,1)S(1)}, bf16[384,512]{1,0:T(8,128)(2,1)S(1)}, u32[]{:S(2)}, u32[]{:S(2)}) collective-permute-start(bf16[384,512]{1,0:T(8,128)(2,1)S(1)} %get-tuple-element.33), channel_id=1, source_target_pairs={{4,8},{12,16},{20,24},{8,4},{16,12},{24,20},{5,9},{13,17},{21,25},... | collective-permute-start | bytes 1179656 | tf_op jit(solution)/shard_map/ppermute | solution.py:357
  10.9 0.9 %collective-permute-start.6 = (bf16[384,512]{1,0:T(8,128)(2,1)S(1)}, bf16[384,512]{1,0:T(8,128)(2,1)S(1)}, u32[]{:S(2)}, u32[]{:S(2)}) collective-permute-start(bf16[384,512]{1,0:T(8,128)(2,1)S(1)} %get-tuple-element.53), channel_id=1, source_target_pairs={{0,2},{1,3},{2,0},{3,1},{4,6},{5,7},{6,4},{7,5},{8,10},{9,11},{10,... | collective-permute-start | bytes 1179656 | tf_op jit(solution)/shard_map/ppermute | solution.py:351
  11.8 0.3 collective-permute-start.7
  12.1 3.3 %interior.1 = (bf16[384,512]{1,0:T(8,128)(2,1)S(1)}, bf16[384,512]{1,0:T(8,128)(2,1)S(1)}, bf16[384,512]{1,0:T(8,128)(2,1)S(1)}, bf16[384,512]{1,0:T(8,128)(2,1)...) custom-call(bf16[384,2048]{1,0:T(8,128)(2,1)} %x_ref.5, ...), custom_call_target="tpu_custom_call" | custom-call | tf_op jit(solution)/shard_map/interior/pallas_call | solution.py:19
  15.5 0.0 collective-permute-done.2.refs_0_
  15.5 0.8 %near_end.1 = (bf16[384,512]{1,0:T(8,128)(2,1)S(1)}, bf16[384,512]{1,0:T(8,128)(2,1)S(1)}, bf16[384,512]{1,0:T(8,128)(2,1)S(1)}, bf16[384,512]{1,0:T(8,128)(2,1)...) custom-call(bf16[384,512]{1,0:T(8,128)(2,1)S(1)} %collective-permute, ...), custom_call_target="tpu_custom_call", output_to_operand_aliasing={{0}: (2, {}), {1}: (3, {}), {2}: (4, {}), {3}: (5, {}), {4}... | custom-call | tf_op jit(solution)/shard_map/near_end/pallas_call | solution.py:19
  16.2 1.0 %collective-permute-done.refs_0_.rest_0_ = bf16[384,512]{1,0:T(8,128)(2,1)S(1)} collective-permute-done((bf16[384,512]{1,0:T(8,128)(2,1)S(1)}, bf16[384,512]{1,0:T(8,128)(2,1)S(1)}, u32[]{:S(2)}, u32[]{:S(2)}) %collective-permute-start) | collective-permute-done | bytes 393248 | tf_op jit(solution)/shard_map/ppermute | solution.py:351
  17.2 0.0 collective-permute-done.1.refs_1_
  17.2 0.8 %far_end.1 = (bf16[384,512]{1,0:T(8,128)(2,1)S(1)}, bf16[384,512]{1,0:T(8,128)(2,1)S(1)}, bf16[384,512]{1,0:T(8,128)(2,1)S(1)}, bf16[384,512]{1,0:T(8,128)(2,1)S...) custom-call(bf16[384,512]{1,0:T(8,128)(2,1)S(1)} %collective-permute, ...), custom_call_target="tpu_custom_call", output_to_operand_aliasing={{0}: (3, {}), {1}: (4, {}), {2}: (5, {}), {3}: (6, {}), {4}... | custom-call | tf_op jit(solution)/shard_map/far_end/pallas_call | solution.py:19
  18.0 0.2 collective-permute-start.3
  18.1 7.8 %collective-permute-start.4 = (bf16[384,512]{1,0:T(8,128)(2,1)S(1)}, bf16[384,512]{1,0:T(8,128)(2,1)S(1)}, u32[]{:S(2)}, u32[]{:S(2)}) collective-permute-start(bf16[384,512]{1,0:T(8,128)(2,1)S(1)} %get-tuple-element.50), channel_id=1, source_target_pairs={{0,3},{1,2},{2,1},{3,0},{4,7},{5,6},{6,5},{7,4},{8,11},{9,10},{10,... | collective-permute-start | bytes 1179656 | tf_op jit(solution)/shard_map/ppermute | solution.py:351
  25.9 0.0 collective-permute-start.5
  26.0 0.0 collective-permute-done.6.rest_1_
  26.0 0.0 collective-permute-done.7.rest_2_
  26.0 0.6 %grad_conv.1 = (bf16[384,2048]{1,0:T(8,128)(2,1)S(1)}, bf16[384,512]{1,0:T(8,128)(2,1)S(1)}, bf16[384,512]{1,0:T(8,128)(2,1)S(1)}) custom-call(f32[384,2048]{1,0:T(8,128)S(1)} %get-tuple-element.52.slope_ref, bf16[384,512]{1,0:T(8,128)(2,1)S(1)} %collective-permute-done.refs_0_.rest_0_, bf16[384,512]{1,0:T(8,128)(2,1)S(1)} %collective-permute-done.6.rest_1_, ...), custom_call_target="tpu_custom_call" | custom-call | tf_op jit(solution)/shard_map/grad_conv/pallas_call | solution.py:19
  26.6 2.6 %collective-permute-start.8 = (bf16[384,512]{1,0:T(8,128)(2,1)S(1)}, bf16[384,512]{1,0:T(8,128)(2,1)S(1)}, u32[]{:S(2)}, u32[]{:S(2)}) collective-permute-start(bf16[384,512]{1,0:T(8,128)(2,1)S(1)} %get-tuple-element.56), channel_id=1, source_target_pairs={{0,4},{8,12},{16,20},{24,28},{4,0},{12,8},{20,16},{28,24},{1,5},{9... | collective-permute-start | bytes 1179656 | tf_op jit(solution)/shard_map/ppermute | solution.py:357
  29.2 0.9 %collective-permute-start.9 = (bf16[384,512]{1,0:T(8,128)(2,1)S(1)}, bf16[384,512]{1,0:T(8,128)(2,1)S(1)}, u32[]{:S(2)}, u32[]{:S(2)}) collective-permute-start(bf16[384,512]{1,0:T(8,128)(2,1)S(1)} %get-tuple-element.57), channel_id=1, source_target_pairs={{4,8},{12,16},{20,24},{8,4},{16,12},{24,20},{5,9},{13,17},{21,25},... | collective-permute-start | bytes 1179656 | tf_op jit(solution)/shard_map/ppermute | solution.py:357
  30.0 1.7 %back_interior.1.rest_5_ = bf16[384,2048]{1,0:T(8,128)(2,1)} custom-call(bf16[384,2048]{1,0:T(8,128)(2,1)S(1)} %get-tuple-element.58.grad_ref.rest_3_, bf16[3,384,96]{2,1,0:T(8,128)(2,1)S(1)} %get-tuple-element.59.turned_ref.rest_4_), custom_call_target="tpu_custom_call" | custom-call | tf_op jit(solution)/shard_map/back_interior/pallas_call | solution.py:19
  31.7 3.7 %collective-permute-done.4.rest_0_ = bf16[384,512]{1,0:T(8,128)(2,1)S(1)} collective-permute-done((bf16[384,512]{1,0:T(8,128)(2,1)S(1)}, bf16[384,512]{1,0:T(8,128)(2,1)S(1)}, u32[]{:S(2)}, u32[]{:S(2)}) %collective-permute-start.4) | collective-permute-done | bytes 393248 | tf_op jit(solution)/shard_map/ppermute | solution.py:351
  35.4 0.0 slice-done
  35.4 0.0 slice-done.1
  35.4 1.0 %early_mix.1.rest_2_ = f32[1536,512]{1,0:T(8,128)S(1)} custom-call(bf16[1536,1536]{1,0:T(8,128)(2,1)S(1)} %bitcast.2, bf16[384,512]{1,0:T(8,128)(2,1)S(1)} %collective-permute-done.4.rest_0_), custom_call_target="tpu_custom_call" | custom-call | tf_op jit(solution)/shard_map/early_mix/pallas_call | solution.py:19
  36.4 0.0 collective-permute-done.3.rest_0_
  36.4 1.8 %half_mix.1.sum_ref = f32[1536,512]{1,0:T(8,128)S(1)} custom-call(bf16[1536,1536]{1,0:T(8,128)(2,1)S(1)} %bitcast.2, bf16[384,512]{1,0:T(8,128)(2,1)S(1)} %collective-permute-done.3.rest_0_, bf16[384,512]{1,0:T(8,128)(2,1)S(1)} %get-tuple-element.49.rest_1_, f32[1536,512]{1,0:T(8,128)S(1)} %early_mix.1.rest_2_), custom_call_target="tpu_custom_call", output_to_operand_aliasing={{}: (3, {})} | custom-call | tf_op jit(solution)/shard_map/half_mix/pallas_call | solution.py:19
  38.2 5.8 %collective-permute-done.5.rest_0_ = bf16[384,512]{1,0:T(8,128)(2,1)S(1)} collective-permute-done((bf16[384,512]{1,0:T(8,128)(2,1)S(1)}, bf16[384,512]{1,0:T(8,128)(2,1)S(1)}, u32[]{:S(2)}, u32[]{:S(2)}) %collective-permute-start.5) | collective-permute-done | bytes 393248 | tf_op jit(solution)/shard_map/ppermute | solution.py:351
  44.0 2.2 %collective-permute-done.8.rest_1_ = bf16[384,512]{1,0:T(8,128)(2,1)S(1)} collective-permute-done((bf16[384,512]{1,0:T(8,128)(2,1)S(1)}, bf16[384,512]{1,0:T(8,128)(2,1)S(1)}, u32[]{:S(2)}, u32[]{:S(2)}) %collective-permute-start.8) | collective-permute-done | bytes 393248 | tf_op jit(solution)/shard_map/ppermute | solution.py:357
  46.2 0.0 collective-permute-done.9.rest_2_
  46.2 2.4 %tail.1 = (bf16[1536,512]{1,0:T(8,128)(2,1)}, bf16[384,2048]{1,0:T(8,128)(2,1)}) custom-call(bf16[1536,1536]{1,0:T(8,128)(2,1)S(1)} %bitcast.2, f32[1536,512]{1,0:T(8,128)S(1)} %half_mix.1.sum_ref, bf16[384,512]{1,0:T(8,128)(2,1)S(1)} %collective-permute-done.5.rest_0_, ...), custom_call_target="tpu_custom_call", output_to_operand_aliasing={{1}: (7, {})} | custom-call | tf_op jit(solution)/shard_map/tail/pallas_call | solution.py:19
  (3 shorter events, 0.0 us)
Async XLA Ops:
  2.8 12.6 %collective-permute-start.2 = (bf16[384,512]{1,0:T(8,128)(2,1)S(1)}, bf16[384,512]{1,0:T(8,128)(2,1)S(1)}, u32[]{:S(2)}, u32[]{:S(2)}) collective-permute-start(bf16[384,512]{1,0:T(8,128)(2,1)S(1)} %get-tuple-element.35), channel_id=1, source_target_pairs={{0,4},{8,12},{16,20},{24,28},{4,0},{12,8},{20,16},{28,24},{1,5},{9... | collective-permute-start | bytes 1179656 | tf_op jit(solution)/shard_map/ppermute | solution.py:357
  5.8 11.3 %collective-permute-start = (bf16[384,512]{1,0:T(8,128)(2,1)S(1)}, bf16[384,512]{1,0:T(8,128)(2,1)S(1)}, u32[]{:S(2)}, u32[]{:S(2)}) collective-permute-start(bf16[384,512]{1,0:T(8,128)(2,1)S(1)} %get-tuple-element.31), channel_id=1, source_target_pairs={{0,3},{1,2},{2,1},{3,0},{4,7},{5,6},{6,5},{7,4},{8,11},{9,10},{10,... | collective-permute-start | bytes 1179656 | tf_op jit(solution)/shard_map/ppermute | solution.py:351
  10.2 7.0 %collective-permute-start.1 = (bf16[384,512]{1,0:T(8,128)(2,1)S(1)}, bf16[384,512]{1,0:T(8,128)(2,1)S(1)}, u32[]{:S(2)}, u32[]{:S(2)}) collective-permute-start(bf16[384,512]{1,0:T(8,128)(2,1)S(1)} %get-tuple-element.33), channel_id=1, source_target_pairs={{4,8},{12,16},{20,24},{8,4},{16,12},{24,20},{5,9},{13,17},{21,25},... | collective-permute-start | bytes 1179656 | tf_op jit(solution)/shard_map/ppermute | solution.py:357
  10.9 15.1 %collective-permute-start.6 = (bf16[384,512]{1,0:T(8,128)(2,1)S(1)}, bf16[384,512]{1,0:T(8,128)(2,1)S(1)}, u32[]{:S(2)}, u32[]{:S(2)}) collective-permute-start(bf16[384,512]{1,0:T(8,128)(2,1)S(1)} %get-tuple-element.53), channel_id=1, source_target_pairs={{0,2},{1,3},{2,0},{3,1},{4,6},{5,7},{6,4},{7,5},{8,10},{9,11},{10,... | collective-permute-start | bytes 1179656 | tf_op jit(solution)/shard_map/ppermute | solution.py:351
  11.8 14.2 %collective-permute-start.7 = (bf16[384,512]{1,0:T(8,128)(2,1)S(1)}, bf16[384,512]{1,0:T(8,128)(2,1)S(1)}, u32[]{:S(2)}, u32[]{:S(2)}) collective-permute-start(bf16[384,512]{1,0:T(8,128)(2,1)S(1)} %get-tuple-element.54), channel_id=1, source_target_pairs={{0,1},{1,0},{2,3},{3,2},{4,5},{5,4},{6,7},{7,6},{8,9},{9,8},{10,11... | collective-permute-start | bytes 1179656 | tf_op jit(solution)/shard_map/ppermute | solution.py:351
  17.2 18.2 %slice-start = ((s8[4718592]{0:T(1024)(128)(4,1)}), s8[4194304]{0:T(1024)(128)(4,1)S(1)}, s32[]{:S(2)}) async-start(s8[4718592]{0:T(1024)(128)(4,1)} %bitcast.1), calls=%async_computation | async-start | bytes 8388608
  18.0 18.4 %collective-permute-start.3 = (bf16[384,512]{1,0:T(8,128)(2,1)S(1)}, bf16[384,512]{1,0:T(8,128)(2,1)S(1)}, u32[]{:S(2)}, u32[]{:S(2)}) collective-permute-start(bf16[384,512]{1,0:T(8,128)(2,1)S(1)} %get-tuple-element.48), channel_id=1, source_target_pairs={{0,1},{1,0},{2,3},{3,2},{4,5},{5,4},{6,7},{7,6},{8,9},{9,8},{10,11... | collective-permute-start | bytes 1179656 | tf_op jit(solution)/shard_map/ppermute | solution.py:351
  18.1 17.2 %collective-permute-start.4 = (bf16[384,512]{1,0:T(8,128)(2,1)S(1)}, bf16[384,512]{1,0:T(8,128)(2,1)S(1)}, u32[]{:S(2)}, u32[]{:S(2)}) collective-permute-start(bf16[384,512]{1,0:T(8,128)(2,1)S(1)} %get-tuple-element.50), channel_id=1, source_target_pairs={{0,3},{1,2},{2,1},{3,0},{4,7},{5,6},{6,5},{7,4},{8,11},{9,10},{10,... | collective-permute-start | bytes 1179656 | tf_op jit(solution)/shard_map/ppermute | solution.py:351
  25.9 18.1 %collective-permute-start.5 = (bf16[384,512]{1,0:T(8,128)(2,1)S(1)}, bf16[384,512]{1,0:T(8,128)(2,1)S(1)}, u32[]{:S(2)}, u32[]{:S(2)}) collective-permute-start(bf16[384,512]{1,0:T(8,128)(2,1)S(1)} %get-tuple-element.51), channel_id=1, source_target_pairs={{0,2},{1,3},{2,0},{3,1},{4,6},{5,7},{6,4},{7,5},{8,10},{9,11},{10,... | collective-permute-start | bytes 1179656 | tf_op jit(solution)/shard_map/ppermute | solution.py:351
  26.0 9.4 %slice-start.1 = ((s8[4718592]{0:T(1024)(128)(4,1)}), s8[524288]{0:T(1024)(128)(4,1)S(1)}, s32[]{:S(2)}) async-start(s8[4718592]{0:T(1024)(128)(4,1)} %bitcast.1), calls=%async_computation.1 | async-start | bytes 1048576
  26.6 19.6 %collective-permute-start.8 = (bf16[384,512]{1,0:T(8,128)(2,1)S(1)}, bf16[384,512]{1,0:T(8,128)(2,1)S(1)}, u32[]{:S(2)}, u32[]{:S(2)}) collective-permute-start(bf16[384,512]{1,0:T(8,128)(2,1)S(1)} %get-tuple-element.56), channel_id=1, source_target_pairs={{0,4},{8,12},{16,20},{24,28},{4,0},{12,8},{20,16},{28,24},{1,5},{9... | collective-permute-start | bytes 1179656 | tf_op jit(solution)/shard_map/ppermute | solution.py:357
  29.2 17.0 %collective-permute-start.9 = (bf16[384,512]{1,0:T(8,128)(2,1)S(1)}, bf16[384,512]{1,0:T(8,128)(2,1)S(1)}, u32[]{:S(2)}, u32[]{:S(2)}) collective-permute-start(bf16[384,512]{1,0:T(8,128)(2,1)S(1)} %get-tuple-element.57), channel_id=1, source_target_pairs={{4,8},{12,16},{20,24},{8,4},{16,12},{24,20},{5,9},{13,17},{21,25},... | collective-permute-start | bytes 1179656 | tf_op jit(solution)/shard_map/ppermute | solution.py:357

commit v10 on v9

v10 whole, which is shorter than its diff:
```python
import functools

import jax
import jax.numpy as jnp
from jax import lax
from jax.experimental import pallas as pl
from jax.experimental.pallas import tpu as pltpu
from jax.sharding import PartitionSpec as P

DILATION_STEP = 512
UPSTREAM_ROWS = 512
BF16, F32 = jnp.bfloat16, jnp.float32
ANY = pl.BlockSpec(memory_space=pl.ANY)
INSIDE = pl.BlockSpec(memory_space=pltpu.VMEM)
DMA = pltpu.SemaphoreType.DMA


def kernel_call(name, kernel, operands, outs, scratch=(), aliases=None):
    return pl.pallas_call(
        kernel,
        in_specs=[INSIDE if held else ANY for _, held in operands],
        out_specs=[INSIDE if held else ANY for _, _, held in outs],
        out_shape=[
            pltpu.VMEM(shape, kind) if held else jax.ShapeDtypeStruct(shape, kind)
            for shape, kind, held in outs
        ],
        scratch_shapes=list(scratch),
        input_output_aliases=aliases or {},
        compiler_params=pltpu.CompilerParams(vmem_limit_bytes=16 << 20),
        name=name,
    )(*[
        pltpu.with_memory_space_constraint(array, pltpu.VMEM if held else pltpu.HBM)
        for array, held in operands
    ])


def gelu_and_slope(v):
    square = v * v
    inner = v * (0.7978845608 + (0.7978845608 * 0.044715) * square)
    th = jnp.tanh(inner)
    half = 0.5 + 0.5 * th
    active = v * half
    inner_slope = 0.7978845608 + (3.0 * 0.7978845608 * 0.044715) * square
    slope = half + (0.5 * v) * (1.0 - th * th) * inner_slope
    return active, slope


def lanes(start, size):
    return pl.ds(pl.multiple_of(start, 128), size)


def dot(a, b):
    return jnp.dot(a, b, preferred_element_type=F32)


def turned_dot(a, b):
    return lax.dot_general(a, b, (((0,), (0,)), ((), ())), preferred_element_type=F32)


def odd_place():
    return lax.axis_index("ctx") % 2


def upstream_kernel(order, channels, first, pw_ref, cot_ref, x_ref, *rest):
    count = len(order)
    piece_refs, rest = rest[:count], rest[count:]
    columns_ref, total_ref, sems = rest[-3:]
    cot_in = rest[0] if first else cot_ref
    ch = lax.axis_index("ch")
    blocks = []
    for m in range(0, cot_in.shape[0], UPSTREAM_ROWS):
        rows = slice(m, m + UPSTREAM_ROWS)
        pairs = [(cot_ref.at[rows], cot_in.at[rows])] if first else []
        if channels % 128 == 0:
            for place, k in enumerate(order):
                columns = lanes((ch ^ k) * channels, channels)
                held = slice(place * channels, (place + 1) * channels)
                pairs.append((pw_ref.at[rows, columns], columns_ref.at[rows, held]))
        else:
            pairs.append((pw_ref.at[rows], columns_ref.at[rows]))
        copies = [
            pltpu.make_async_copy(source, place, sems.at[len(blocks), i])
            for i, (source, place) in enumerate(pairs)
        ]
        for copy in copies:
            copy.start()
        blocks.append((rows, copies))
    which = 1 - odd_place() if first else odd_place()
    length, halo = x_ref.shape[1], rest[-4].shape[1]
    end = pltpu.make_async_copy(
        x_ref.at[:, lanes(which * (length - halo), halo)], rest[-4], sems.at[0, count + 1]
    )
    end.start()
    for step, (rows, copies) in enumerate(blocks):
        for copy in copies:
            copy.wait()
        for place in range(count):
            held = slice(place * channels, (place + 1) * channels)
            part = turned_dot(columns_ref[rows, held], cot_in[rows, :])
            if step > 0:
                part = part + total_ref[held, :]
            if step < len(blocks) - 1:
                total_ref[held, :] = part
            else:
                piece_refs[place][...] = part.astype(BF16)
    end.wait()


def columns_of(pw_weight, channels, order):
    if channels % 128 == 0:
        return pw_weight
    ch = lax.axis_index("ch")
    return jnp.concatenate(
        [lax.dynamic_slice_in_dim(pw_weight, (ch ^ k) * channels, channels, 1) for k in order], axis=1
    )


def upstream(pw_weight, cotangent, inputs, order, first):
    channels = inputs.shape[0]
    total, width = cotangent.shape
    count = len(order)
    outs = [((channels, width), BF16, True)] * count
    outs += [(cotangent.shape, BF16, True)] * first
    outs += [((channels, DILATION_STEP), BF16, True)]
    results = kernel_call(
        "upstream", functools.partial(upstream_kernel, order, channels, first),
        [(columns_of(pw_weight, channels, order), False), (cotangent, not first), (inputs, False)], outs,
        [
            pltpu.VMEM((total, count * channels), BF16), pltpu.VMEM((count * channels, width), F32),
            DMA((total // UPSTREAM_ROWS, count + 2)),
        ],
    )
    return results[:count], *results[count:]


def is_inner(block_index, block, length):
    base = block_index * block
    return (base >= DILATION_STEP) & (base < length - DILATION_STEP)


def convolve_block(plain_ref, wide, base, active_ref, slope_ref):
    group, width = plain_ref.shape[2], active_ref.shape[1]
    unit = min(width, 256)
    for s in range(0, width, unit):
        for g in range(0, active_ref.shape[0], group):
            rows = slice(g, g + group)
            conv_out = sum(
                dot(plain_ref[t, rows, :], wide[rows, lanes(base + s + t * DILATION_STEP, unit)])
                for t in range(3)
            )
            active, slope = gelu_and_slope(conv_out)
            active_ref[rows, s:s + unit] = active.astype(BF16)
            slope_ref[rows, lanes(base + s, unit)] = slope


def interior_kernel(n, x_ref, w_ref, *rest):
    active_refs, (slope_ref, wide, plain_ref, turned_ref, own_ref, sem, own_sem) = rest[:n], rest[n:]
    ch = lax.axis_index("ch")
    channels, length = x_ref.shape
    group, halo = w_ref.shape[1], DILATION_STEP
    block = length // n
    own = w_ref.at[:, :, lanes(ch * channels, channels)] if w_ref.shape[2] > channels else w_ref
    own_copy = pltpu.make_async_copy(own, own_ref, own_sem)
    own_copy.start()
    copy = pltpu.make_async_copy(x_ref, wide.at[:, halo:halo + length], sem)
    copy.start()
    own_copy.wait()
    for t in range(3):
        for g in range(0, channels, group):
            square = own_ref[t, :, g:g + group]
            turned_ref[2 - t, g:g + group, :] = square
            plain_ref[t, g:g + group, :] = square.T
    copy.wait()
    for k in range(n):
        @pl.when(is_inner(ch ^ k, block, length))
        def _(k=k):
            convolve_block(plain_ref, wide, (ch ^ k) * block, active_refs[k], slope_ref)


def interior(inputs, weight, n):
    channels, length = inputs.shape
    group = weight.shape[1]
    outs = [((channels, length // n), BF16, True)] * n
    outs += [((channels, length), F32, True), ((channels, length + 2 * DILATION_STEP), BF16, True)]
    outs += [((3, channels, group), BF16, True)] * 2
    results = kernel_call(
        "interior", functools.partial(interior_kernel, n), [(inputs, False), (weight, False)], outs,
        [pltpu.VMEM((3, group, channels), BF16), DMA, DMA],
    )
    return results[:n], *results[n:]


def in_end(block_index, block, at_end, length):
    first = at_end * (length - DILATION_STEP)
    return (block_index * block >= first) & (block_index * block < first + DILATION_STEP)


def near_kernel(ks, waits, near_ref, *rest):
    plain_ref = rest[waits]
    n = len(ks)
    slope_ref, wide = rest[-(n + 2):-n]
    active_refs = rest[-n:]
    ch, at_end = lax.axis_index("ch"), 1 - odd_place()
    length, halo = slope_ref.shape[1], near_ref.shape[1]
    block = length // n
    wide[:, lanes(at_end * (halo + length), halo)] = near_ref[...]
    for k, active_ref in zip(ks, active_refs):
        @pl.when(in_end(ch ^ k, block, at_end, length))
        def _(k=k, active_ref=active_ref):
            convolve_block(plain_ref, wide, (ch ^ k) * block, active_ref, slope_ref)


def near_end(near, waited, plain, slope, wide, away, here, active):
    held = [active[k] for k in here]
    operands = [(o, True) for o in (near, *waited, plain, slope, wide, *held)]
    outs = [slope, wide, *[active[k] for k in away], *held]
    first_held, at = 2 + len(away), 2 + len(waited)
    results = kernel_call(
        "near_end", functools.partial(near_kernel, away + here, len(waited)), operands,
        [(o.shape, o.dtype, True) for o in outs],
        aliases={at: 0, at + 1: 1, **{at + 2 + i: first_held + i for i in range(len(here))}},
    )
    return results[0], results[1], dict(zip(away + here, results[2:]))


def grad_kernel(ks, slope_ref, *rest):
    up_refs, (grad_ref, near_out) = rest[:-2], rest[-2:]
    ch, odd = lax.axis_index("ch"), odd_place()
    length, halo = grad_ref.shape[1], near_out.shape[1]
    block = length // len(ks)
    for k, up_ref in zip(ks, up_refs):
        @pl.when(jnp.logical_not(in_end(ch ^ k, block, odd, length)))
        def _(k=k, up_ref=up_ref):
            here = lanes((ch ^ k) * block, block)
            grad_ref[:, here] = (up_ref[...].astype(F32) * slope_ref[:, here]).astype(BF16)
    near_out[...] = grad_ref[:, lanes((1 - odd) * (length - halo), halo)]


def grad_conv(slope, ks, ups):
    return kernel_call(
        "grad_conv", functools.partial(grad_kernel, ks),
        [(o, True) for o in (slope, *[ups[k] for k in ks])],
        [(slope.shape, BF16, True), ((slope.shape[0], DILATION_STEP), BF16, True)],
    )


def far_kernel(ks, _, __, far_ref, plain_ref, *rest):
    n = len(ks)
    up_refs, (slope_ref, far_out, wide, grad_ref), active_refs = rest[:n], rest[-(n + 4):-n], rest[-n:]
    ch, at_end = lax.axis_index("ch"), odd_place()
    length, halo = slope_ref.shape[1], far_ref.shape[1]
    block = length // n
    wide[:, lanes(at_end * (halo + length), halo)] = far_ref[...]
    for k, up_ref, active_ref in zip(ks, up_refs, active_refs):
        @pl.when(in_end(ch ^ k, block, at_end, length))
        def _(k=k, up_ref=up_ref, active_ref=active_ref):
            convolve_block(plain_ref, wide, (ch ^ k) * block, active_ref, slope_ref)
            here = lanes((ch ^ k) * block, block)
            grad = (up_ref[...].astype(F32) * slope_ref[:, here]).astype(BF16)
            grad_ref[:, here] = grad
            far_out[:, lanes((ch ^ k) * block - at_end * (length - halo), block)] = grad


def far_end(far, plain, slope, wide, grad, ks, ups, active):
    n = len(ks)
    operands = [(o, True) for o in (slope, wide, far, plain, *[ups[k] for k in ks], grad)]
    operands += [(active[k], True) for k in ks]
    outs = [slope, far, wide, grad, *[active[k] for k in ks]]
    results = kernel_call(
        "far_end", functools.partial(far_kernel, ks), operands, [(o.shape, o.dtype, True) for o in outs],
        aliases={0: 0, 1: 2, 4 + n: 3, **{5 + n + i: 4 + i for i in range(n)}},
    )
    return results[1], results[3], dict(zip(ks, results[4:]))


def columns_times(order, pw_ref, rows, pieces):
    channels = pieces.shape[0] // len(order)
    if channels % 128 != 0:
        return dot(pw_ref[rows, :], pieces)
    return sum(
        dot(
            pw_ref[rows, lanes((lax.axis_index("ch") ^ k) * channels, channels)],
            pieces[place * channels:(place + 1) * channels],
        )
        for place, k in enumerate(order)
    )


def gather(counts, refs, gathered):
    width = gathered.shape[1]
    inner = is_inner(lax.axis_index("ch"), width, lax.axis_size("ch") * width)
    refs, at = list(refs), 0
    channels = refs[0].shape[0]
    for count in counts:
        rows = slice(at, at + channels)
        if count == 1:
            gathered[rows, :] = refs.pop(0)[...]
        else:
            early, late = refs.pop(0), refs.pop(0)

            @pl.when(inner)
            def _(rows=rows, early=early):
                gathered[rows, :] = early[...]

            @pl.when(jnp.logical_not(inner))
            def _(rows=rows, late=late):
                gathered[rows, :] = late[...]
        at += channels


def mix_kernel(order, counts, adds, *refs):
    before, refs = refs[:adds], refs[-sum(counts) - 3:]
    pw_ref, piece_refs, sum_ref, gathered = refs[0], refs[1:-2], refs[-2], refs[-1]
    gather(counts, piece_refs, gathered)
    pieces = gathered[...]
    step = 512
    for m in range(0, sum_ref.shape[0], step):
        rows = slice(m, m + step)
        part = columns_times(order, pw_ref, rows, pieces)
        sum_ref[rows, :] = part + before[0][rows, :] if before else part


def mix(name, pw_weight, order, active, before, waited=()):
    channels, width = active[order[0]][0].shape
    operands = [*before, *waited, columns_of(pw_weight, channels, order), *[p for k in order for p in active[k]]]
    return kernel_call(
        name, functools.partial(mix_kernel, order, [len(active[k]) for k in order], len(before)),
        [(o, True) for o in operands], [((pw_weight.shape[0], width), F32, True)],
        [pltpu.VMEM((len(order) * channels, width), BF16)], {0: 0} if before else {},
    )


def back_interior_kernel(grad_ref, turned_ref, *rest):
    out_ref, ends_ref, held, sem = rest[-4:]
    channels, length = grad_ref.shape
    group, halo, unit = turned_ref.shape[2], DILATION_STEP, 256

    def taps(rows, start, which):
        return sum(
            dot(turned_ref[t, rows, :], grad_ref[rows, start + (t - 1) * halo:start + (t - 1) * halo + unit])
            for t in which
        )

    groups = [slice(g, g + group) for g in range(0, channels, group)]
    for rows in groups:
        for s in range(0, length - 2 * halo, unit):
            held[rows, s:s + unit] = taps(rows, halo + s, (0, 1, 2)).astype(BF16)
    copy = pltpu.make_async_copy(held, out_ref.at[:, halo:length - halo], sem)
    copy.start()
    for rows in groups:
        for s in range(0, halo, unit):
            ends_ref[rows, s:s + unit] = taps(rows, s, (1, 2))
            ends_ref[rows, halo + s:halo + s + unit] = taps(rows, length - halo + s, (0, 1))
    copy.wait()


def back_end(halo_ref, ends_ref, turned_ref, at_end, held):
    channels, halo = halo_ref.shape
    group, unit = turned_ref.shape[2], 256
    for g in range(0, channels, group):
        rows = slice(g, g + group)
        for s in range(0, halo, unit):
            outer = dot(turned_ref[2 * at_end, rows, :], halo_ref[rows, s:s + unit])
            held[rows, s:s + unit] = (ends_ref[rows, lanes(at_end * halo + s, unit)] + outer).astype(BF16)


def end_of(out_ref, at_end):
    return out_ref.at[:, lanes(at_end * (out_ref.shape[1] - DILATION_STEP), DILATION_STEP)]


def back_near_kernel(near_ref, ends_ref, turned_ref, _, out_ref, done_ref, held, sem):
    at_end = 1 - odd_place()
    back_end(near_ref, ends_ref, turned_ref, at_end, held)
    copy = pltpu.make_async_copy(held, end_of(out_ref, at_end), sem)
    copy.start()
    done_ref[...] = jnp.zeros_like(done_ref)
    copy.wait()


def back_near(near, ends, turned, grad_inputs):
    return kernel_call(
        "back_near", back_near_kernel, [(near, True), (ends, True), (turned, True), (grad_inputs, False)],
        [(grad_inputs.shape, BF16, False), ((8, 128), F32, True)], [pltpu.VMEM(near.shape, BF16), DMA], {3: 0},
    )


def tail_kernel(order, counts, far_ref, sum_ref, pw_ref, *rest):
    piece_refs, rest = rest[:-10], rest[-10:]
    ends_ref, turned_ref, _, mixed_ref, out_ref, gathered, held, end, sems, end_sem = rest
    copies = []

    def send(source, place, sem):
        copies.append(pltpu.make_async_copy(source, place, sem))
        copies[-1].start()

    gather(counts, piece_refs, gathered)
    pieces = gathered[...]
    step = 512
    for m in range(0, sum_ref.shape[0], step):
        rows = slice(m, m + step)
        held[rows, :] = (sum_ref[rows, :] + columns_times(order, pw_ref, rows, pieces)).astype(BF16)
        send(held.at[rows, :], mixed_ref.at[rows, :], sems.at[m // step])
    at_end = odd_place()
    back_end(far_ref, ends_ref, turned_ref, at_end, end)
    send(end, end_of(out_ref, at_end), end_sem)
    for copy in copies:
        copy.wait()


def tail(far, partial, pw_weight, order, active, ends, turned, grad_inputs):
    channels = far.shape[0]
    operands = [far, partial, columns_of(pw_weight, channels, order)]
    operands += [*[p for k in order for p in active[k]], ends, turned]
    operands = [(o, True) for o in operands] + [(grad_inputs, False)]
    return kernel_call(
        "tail", functools.partial(tail_kernel, order, [len(active[k]) for k in order]), operands,
        [(partial.shape, BF16, False), (grad_inputs.shape, BF16, False)],
        [
            pltpu.VMEM((len(order) * channels, partial.shape[1]), BF16), pltpu.VMEM(partial.shape, BF16),
            pltpu.VMEM(far.shape, BF16), DMA((partial.shape[0] // 512,)), DMA,
        ],
        {len(operands) - 1: 1},
    )


def exchange(piece, k):
    if k == 0:
        return piece
    return lax.ppermute(piece, "ch", [(i, i ^ k) for i in range(lax.axis_size("ch"))])


def exchange_part(piece, k, inner):
    n, block = lax.axis_size("ch"), piece.shape[1]
    return lax.ppermute(
        piece, "ch", [(i, i ^ k) for i in range(n) if is_inner(i ^ k, block, n * block) == inner]
    )


def swap(values, first):
    size = lax.axis_size("ctx")
    pairs = [(i, i + 1) for i in range(first, size - 1, 2)]
    return lax.ppermute(values, "ctx", pairs + [(b, a) for a, b in pairs])


def body(inputs, conv_weight, pw_weight, cotangent):
    n = lax.axis_size("ch")
    channels, length = inputs.shape
    halo = DILATION_STEP
    order = list(range(n - 1, -1, -1))
    first, second, rest = order[:n // 4], order[n // 4:n // 2], order[n // 2:]

    weight = jnp.swapaxes(conv_weight, 1, 2)
    if channels % 128 != 0:
        weight = lax.dynamic_slice_in_dim(weight, lax.axis_index("ch") * channels, channels, 2)
    pieces, cot_in, near = upstream(pw_weight, cotangent, inputs, first, True)
    near = swap(near, 0)
    ups = {k: exchange(p, k) for k, p in zip(first, pieces)}
    pieces, far = upstream(pw_weight, cot_in, inputs, second + rest, False)
    ups.update({k: exchange(p, k) for k, p in zip(second + rest, pieces)})
    far = swap(far, 1)

    active, slope, wide, plain, turned = interior(inputs, weight, n)
    inner = {k: exchange_part(active[k], k, True) for k in first}
    waited = [ups[k] for k in first + [k for k in rest if k > 0]]
    slope, wide, active = near_end(near, waited, plain, slope, wide, first, second + rest, active)
    grad, near_grad = grad_conv(slope, order, ups)
    near_grad = swap(near_grad, 0)
    far_grad, grad, active = far_end(far, plain, slope, wide, grad, order, ups, active)
    far_grad = swap(far_grad, 1)
    active = {
        k: (inner[k], exchange_part(active[k], k, False)) if k in first else (exchange(active[k], k),)
        for k in order
    }

    grad_inputs, ends = kernel_call(
        "back_interior", back_interior_kernel,
        [(grad, True), (turned, True), *[(inner[k], True) for k in first]],
        [((channels, length), BF16, False), ((channels, 2 * halo), F32, True)],
        [pltpu.VMEM((channels, length - 2 * halo), BF16), DMA],
    )
    grad_inputs, done = back_near(near_grad, ends, turned, grad_inputs)
    partial = mix("half_mix", pw_weight, rest, active, [], [done])
    (partial,) = mix("early_mix", pw_weight, second, active, partial)
    return tuple(tail(far_grad, partial, pw_weight, first, active, ends, turned, grad_inputs))


def solution(mesh):
    placed = (P("ch", "ctx"), P(), P(), P(None, ("ctx", "ch")))
    return jax.shard_map(
        body,
        mesh=mesh,
        in_specs=placed,
        out_specs=(P(None, ("ctx", "ch")), P("ch", "ctx")),
        check_vma=False,
    )
```

time: 49.2 us -> 50.3 us (1.022); the launches traced: 48.8 us -> 49.3 us
  starting transfers between devices: 17.1 us -> 11.3 us
  waiting for transfers between devices: 12.6 us -> 18.3 us
    ppermute x4, waiting for transfers between devices: 2.19 us -> 9.85 us  [swap(): return lax.ppermute(values, 'ctx', pairs + [(b, a) for a, b in pairs])]
    ppermute x6 -> x5, starting transfers between devices: 9.93 us -> 3.76 us  [exchange(): lax.ppermute(piece, 'ch', [(i, i ^ k) for i in range(lax.axis_size('ch'))])]
    ppermute x0 -> x2, starting transfers between devices: none -> 3 us  [exchange_part(): lax.ppermute(piece, 'ch', [(i, i ^ k) for i in range(n) if is_inner(i ^ k...]
    ppermute x4, starting transfers between devices: 7.12 us -> 4.5 us  [swap(): return lax.ppermute(values, 'ctx', pairs + [(b, a) for a, b in pairs])]
    ppermute x6 -> x5, waiting for transfers between devices: 10.5 us -> 8.49 us  [exchange(): lax.ppermute(piece, 'ch', [(i, i ^ k) for i in range(lax.axis_size('ch'))])]
    pallas_call x10 -> x11, Pallas kernels: 18.2 us -> 18.7 us  [kernel_call(): pl.pallas_call(kernel, in_specs=[INSIDE if held else ANY for _, held in o...]
  transfers between devices with their start and end apart: 10 -> 11, of which waited for: 4 -> 3; matrix products, arithmetic and copies ran while one was open for 0% -> 0% of each run, Pallas kernels for 28% -> 30%
where the time goes in v10:
time: 50.3 us; the launch traced here: 49.3 us
  Pallas kernels  18.7 us (37%)
  waiting for transfers between devices  18.3 us (36%)
  starting transfers between devices  11.3 us (22%)
  between operations  0.97 us (2%)
    pallas_call x11, Pallas kernels, kernel_call(): pl.pallas_call(kernel, in_specs=[INSIDE if held else ANY for _, held in o...  18.7 us
    ppermute x4, waiting for transfers between devices, swap(): return lax.ppermute(values, 'ctx', pairs + [(b, a) for a, b in pairs])  9.85 us
    ppermute x5, waiting for transfers between devices, exchange(): lax.ppermute(piece, 'ch', [(i, i ^ k) for i in range(lax.axis_size('ch'))])  8.49 us
    ppermute x4, starting transfers between devices, swap(): return lax.ppermute(values, 'ctx', pairs + [(b, a) for a, b in pairs])  4.5 us
    ppermute x5, starting transfers between devices, exchange(): lax.ppermute(piece, 'ch', [(i, i ^ k) for i in range(lax.axis_size('ch'))])  3.76 us
    ppermute x2, starting transfers between devices, exchange_part(): lax.ppermute(piece, 'ch', [(i, i ^ k) for i in range(n) if is_inner(i ^ k...  3 us
  transfers between devices with their start and end apart: 11, of which 3 were waited for; matrix products, arithmetic and copies ran while one was open for 0% of the time, Pallas kernels for 30%

profile of v10, /device:TPU:0, one launch (start us, length us, event | category | flops | bytes accessed | tf_op | source)
XLA Modules:
  0.0 49.3 jit_solution(5026697759885667074)
XLA Ops:
  0.6 2.2 %upstream.2 = (bf16[384,512]{1,0:T(8,128)(2,1)S(1)}, bf16[1536,512]{1,0:T(8,128)(2,1)S(1)}, bf16[384,512]{1,0:T(8,128)(2,1)S(1)}) custom-call(bf16[1536,1536]{1,0:T(8,128)(2,1)} %pw_ref.5, bf16[1536,512]{1,0:T(8,128)(2,1)} %cot_ref.1, bf16[384,2048]{1,0:T(8,128)(2,1)} %x_ref.5), custom_call_target="tpu_custom_call" | custom-call | tf_op jit(solution)/shard_map/upstream/pallas_call | solution.py:19
  2.8 3.0 %collective-permute-start = (bf16[384,512]{1,0:T(8,128)(2,1)S(1)}, bf16[384,512]{1,0:T(8,128)(2,1)S(1)}, u32[]{:S(2)}, u32[]{:S(2)}) collective-permute-start(bf16[384,512]{1,0:T(8,128)(2,1)S(1)} %get-tuple-element.35), channel_id=1, source_target_pairs={{0,4},{8,12},{16,20},{24,28},{4,0},{12,8},{20,16},{28,24},{1,5},{9... | collective-permute-start | bytes 1179656 | tf_op jit(solution)/shard_map/ppermute | solution.py:442
  5.8 0.7 %collective-permute-start.1 = (bf16[384,512]{1,0:T(8,128)(2,1)S(1)}, bf16[384,512]{1,0:T(8,128)(2,1)S(1)}, u32[]{:S(2)}, u32[]{:S(2)}) collective-permute-start(bf16[384,512]{1,0:T(8,128)(2,1)S(1)} %get-tuple-element.36), channel_id=1, source_target_pairs={{0,3},{1,2},{2,1},{3,0},{4,7},{5,6},{6,5},{7,4},{8,11},{9,10},{10,... | collective-permute-start | bytes 1179656 | tf_op jit(solution)/shard_map/ppermute | solution.py:429
  6.5 3.6 %upstream.3 = (bf16[384,512]{1,0:T(8,128)(2,1)S(1)}, bf16[384,512]{1,0:T(8,128)(2,1)S(1)}, bf16[384,512]{1,0:T(8,128)(2,1)S(1)}, bf16[384,512]{1,0:T(8,128)(2,1)S(1)}) custom-call(bf16[1536,1536]{1,0:T(8,128)(2,1)} %pw_ref.5, bf16[1536,512]{1,0:T(8,128)(2,1)S(1)} %get-tuple-element.37.cot_ref, bf16[384,2048]{1,0:T(8,128)(2,1)} %x_ref.5), custom_call_target="tpu_custom_call" | custom-call | tf_op jit(solution)/shard_map/upstream/pallas_call | solution.py:19
  10.2 1.0 %collective-permute-start.2 = (bf16[384,512]{1,0:T(8,128)(2,1)S(1)}, bf16[384,512]{1,0:T(8,128)(2,1)S(1)}, u32[]{:S(2)}, u32[]{:S(2)}) collective-permute-start(bf16[384,512]{1,0:T(8,128)(2,1)S(1)} %get-tuple-element.38), channel_id=1, source_target_pairs={{0,1},{1,0},{2,3},{3,2},{4,5},{5,4},{6,7},{7,6},{8,9},{9,8},{10,11... | collective-permute-start | bytes 1179656 | tf_op jit(solution)/shard_map/ppermute | solution.py:429
  11.2 0.5 %collective-permute-start.4 = (bf16[384,512]{1,0:T(8,128)(2,1)S(1)}, bf16[384,512]{1,0:T(8,128)(2,1)S(1)}, u32[]{:S(2)}, u32[]{:S(2)}) collective-permute-start(bf16[384,512]{1,0:T(8,128)(2,1)S(1)} %get-tuple-element.48), channel_id=1, source_target_pairs={{0,2},{1,3},{2,0},{3,1},{4,6},{5,7},{6,4},{7,5},{8,10},{9,11},{10,... | collective-permute-start | bytes 1179656 | tf_op jit(solution)/shard_map/ppermute | solution.py:429
  11.7 0.7 %collective-permute-start.3 = (bf16[384,512]{1,0:T(8,128)(2,1)S(1)}, bf16[384,512]{1,0:T(8,128)(2,1)S(1)}, u32[]{:S(2)}, u32[]{:S(2)}) collective-permute-start(bf16[384,512]{1,0:T(8,128)(2,1)S(1)} %get-tuple-element.47), channel_id=1, source_target_pairs={{4,8},{12,16},{20,24},{8,4},{16,12},{24,20},{5,9},{13,17},{21,25},... | collective-permute-start | bytes 1179656 | tf_op jit(solution)/shard_map/ppermute | solution.py:442
  12.4 3.3 %interior.1 = (bf16[384,512]{1,0:T(8,128)(2,1)S(1)}, bf16[384,512]{1,0:T(8,128)(2,1)S(1)}, bf16[384,512]{1,0:T(8,128)(2,1)S(1)}, bf16[384,512]{1,0:T(8,128)(2,1)...) custom-call(bf16[384,2048]{1,0:T(8,128)(2,1)} %x_ref.5, ...), custom_call_target="tpu_custom_call" | custom-call | tf_op jit(solution)/shard_map/interior/pallas_call | solution.py:19
  15.7 0.0 collective-permute-done.near_ref
  15.7 0.7 %collective-permute-start.7 = (bf16[384,512]{1,0:T(8,128)(2,1)S(1)}, bf16[384,512]{1,0:T(8,128)(2,1)S(1)}, u32[]{:S(2)}, u32[]{:S(2)}) collective-permute-start(bf16[384,512]{1,0:T(8,128)(2,1)S(1)} %get-tuple-element.59), channel_id=1, source_target_pairs={{1,2},{2,1},{5,6},{6,5},{9,10},{10,9},{13,14},{14,13},{17,18},{18,... | collective-permute-start | bytes 1179656 | tf_op jit(solution)/shard_map/ppermute | solution.py:434
  16.4 0.8 %collective-permute-done.1.rest_0_ = bf16[384,512]{1,0:T(8,128)(2,1)S(1)} collective-permute-done((bf16[384,512]{1,0:T(8,128)(2,1)S(1)}, bf16[384,512]{1,0:T(8,128)(2,1)S(1)}, u32[]{:S(2)}, u32[]{:S(2)}) %collective-permute-start.1) | collective-permute-done | bytes 393248 | tf_op jit(solution)/shard_map/ppermute | solution.py:429
  17.2 0.0 collective-permute-done.2.rest_1_.rest_2_
  17.2 0.8 %near_end.1 = (f32[384,2048]{1,0:T(8,128)S(1)}, bf16[384,3072]{1,0:T(8,128)(2,1)S(1)}, bf16[384,512]{1,0:T(8,128)(2,1)S(1)}, bf16[384,512]{1,0:T(8,128)(2,1)S(1)...) custom-call(bf16[384,512]{1,0:T(8,128)(2,1)S(1)} %collective-permute, ...), custom_call_target="tpu_custom_call", output_to_operand_aliasing={{0}: (4, {}), {1}: (5, {}), {3}: (6, {}), {4}: (7, {}), {5}... | custom-call | tf_op jit(solution)/shard_map/near_end/pallas_call | solution.py:19
  18.0 7.7 %collective-permute-done.4.rest_1_ = bf16[384,512]{1,0:T(8,128)(2,1)S(1)} collective-permute-done((bf16[384,512]{1,0:T(8,128)(2,1)S(1)}, bf16[384,512]{1,0:T(8,128)(2,1)S(1)}, u32[]{:S(2)}, u32[]{:S(2)}) %collective-permute-start.4) | collective-permute-done | bytes 393248 | tf_op jit(solution)/shard_map/ppermute | solution.py:429
  25.7 0.2 grad_conv.1
  25.9 0.1 collective-permute-start.6
  26.1 0.0 collective-permute-done.3.far_ref
  26.1 1.1 %far_end.1 = (f32[384,2048]{1,0:T(8,128)S(1)}, bf16[384,512]{1,0:T(8,128)(2,1)S(1)}, bf16[384,3072]{1,0:T(8,128)(2,1)S(1)}, bf16[384,2048]{1,0:T(8,128)(2,1)S(1)...) custom-call(f32[384,2048]{1,0:T(8,128)S(1)} %get-tuple-element.45.sl, ...), custom_call_target="tpu_custom_call", output_to_operand_aliasing={{0}: (0, {}), {2}: (1, {}), {3}: (8, {}), {4}: (9, {}), {5}... | custom-call | tf_op jit(solution)/shard_map/far_end/pallas_call | solution.py:19
  27.2 0.1 collective-permute-start.8
  27.3 0.7 %collective-permute-start.5 = (bf16[384,512]{1,0:T(8,128)(2,1)S(1)}, bf16[384,512]{1,0:T(8,128)(2,1)S(1)}, u32[]{:S(2)}, u32[]{:S(2)}) collective-permute-start(bf16[384,512]{1,0:T(8,128)(2,1)S(1)} %get-tuple-element.55), channel_id=1, source_target_pairs={{4,8},{12,16},{20,24},{8,4},{16,12},{24,20},{5,9},{13,17},{21,25},... | collective-permute-start | bytes 1179656 | tf_op jit(solution)/shard_map/ppermute | solution.py:442
  28.0 1.5 %collective-permute-start.9 = (bf16[384,512]{1,0:T(8,128)(2,1)S(1)}, bf16[384,512]{1,0:T(8,128)(2,1)S(1)}, u32[]{:S(2)}, u32[]{:S(2)}) collective-permute-start(bf16[384,512]{1,0:T(8,128)(2,1)S(1)} %get-tuple-element.65), channel_id=1, source_target_pairs={{0,2},{1,3},{2,0},{3,1},{4,6},{5,7},{6,4},{7,5},{8,10},{9,11},{10,... | collective-permute-start | bytes 1179656 | tf_op jit(solution)/shard_map/ppermute | solution.py:429
  29.4 0.0 collective-permute-done.7.rest_0_
  29.4 2.3 %collective-permute-start.10 = (bf16[384,512]{1,0:T(8,128)(2,1)S(1)}, bf16[384,512]{1,0:T(8,128)(2,1)S(1)}, u32[]{:S(2)}, u32[]{:S(2)}) collective-permute-start(bf16[384,512]{1,0:T(8,128)(2,1)S(1)} %get-tuple-element.66), channel_id=1, source_target_pairs={{0,3},{3,0},{4,7},{7,4},{8,11},{11,8},{12,15},{15,12},{16,19},{19,... | collective-permute-start | bytes 1179656 | tf_op jit(solution)/shard_map/ppermute | solution.py:434
  31.8 1.7 %back_interior.1 = (bf16[384,2048]{1,0:T(8,128)(2,1)}, f32[384,1024]{1,0:T(8,128)S(1)}) custom-call(bf16[384,2048]{1,0:T(8,128)(2,1)S(1)} %get-tuple-element.57.grad_ref, bf16[3,384,96]{2,1,0:T(8,128)(2,1)S(1)} %get-tuple-element.58.turned_ref.rest_3_, bf16[384,512]{1,0:T(8,128)(2,1)S(1)} %collective-permute-done.7.rest_0_), custom_call_target="tpu_custom_call" | custom-call | tf_op jit(solution)/shard_map/back_interior/pallas_call | solution.py:19
  33.5 9.8 %collective-permute-done.6.near_ref = bf16[384,512]{1,0:T(8,128)(2,1)S(1)} collective-permute-done((bf16[384,512]{1,0:T(8,128)(2,1)S(1)}, bf16[384,512]{1,0:T(8,128)(2,1)S(1)}, u32[]{:S(2)}, u32[]{:S(2)}) %collective-permute-start.6) | collective-permute-done | bytes 393248 | tf_op jit(solution)/shard_map/ppermute | solution.py:442
  43.3 1.0 %back_near.1 = (bf16[384,2048]{1,0:T(8,128)(2,1)}, f32[8,128]{1,0:T(8,128)S(1)}) custom-call(bf16[384,512]{1,0:T(8,128)(2,1)S(1)} %collective-permute-done.6.near_ref, f32[384,1024]{1,0:T(8,128)S(1)} %get-tuple-element.60.ends_ref.rest_2_, bf16[3,384,96]{2,1,0:T(8,128)(2,1)S(1)} %get-tuple-element.58.turned_ref.rest_3_, ...), custom_call_target="tpu_custom_call", output_to_operand_aliasing={{0}: (3, {})} | custom-call | tf_op jit(solution)/shard_map/back_near/pallas_call | solution.py:19
  44.4 1.8 %half_mix.1.refs_0_ = f32[1536,512]{1,0:T(8,128)S(1)} custom-call(f32[8,128]{1,0:T(8,128)S(1)} %get-tuple-element.62.refs_0_, bf16[1536,1536]{1,0:T(8,128)(2,1)S(1)} %bitcast.2, bf16[384,512]{1,0:T(8,128)(2,1)S(1)} %collective-permute-done.8.refs_2_, bf16[384,512]{1,0:T(8,128)(2,1)S(1)} %get-tuple-element.64.refs_3_), custom_call_target="tpu_custom_call" | custom-call | tf_op jit(solution)/shard_map/half_mix/pallas_call | solution.py:19
  46.1 0.0 collective-permute-done.9.refs_2_
  46.2 1.0 %early_mix.1.sum_ref = f32[1536,512]{1,0:T(8,128)S(1)} custom-call(f32[1536,512]{1,0:T(8,128)S(1)} %half_mix.1.refs_0_, bf16[1536,1536]{1,0:T(8,128)(2,1)S(1)} %bitcast.2, bf16[384,512]{1,0:T(8,128)(2,1)S(1)} %collective-permute-done.9.refs_2_), custom_call_target="tpu_custom_call", output_to_operand_aliasing={{}: (0, {})} | custom-call | tf_op jit(solution)/shard_map/early_mix/pallas_call | solution.py:19
  47.2 0.0 collective-permute-done.5.far_ref
  47.2 0.0 collective-permute-done.10.rest_1_
  47.2 2.0 %tail.1 = (bf16[1536,512]{1,0:T(8,128)(2,1)}, bf16[384,2048]{1,0:T(8,128)(2,1)}) custom-call(bf16[384,512]{1,0:T(8,128)(2,1)S(1)} %collective-permute-done.5.far_ref, f32[1536,512]{1,0:T(8,128)S(1)} %early_mix.1.sum_ref, bf16[1536,1536]{1,0:T(8,128)(2,1)S(1)} %bitcast.2, ...), custom_call_target="tpu_custom_call", output_to_operand_aliasing={{1}: (7, {})} | custom-call | tf_op jit(solution)/shard_map/tail/pallas_call | solution.py:19
  (6 shorter events, 0.0 us)
Async XLA Ops:
  2.8 12.9 %collective-permute-start = (bf16[384,512]{1,0:T(8,128)(2,1)S(1)}, bf16[384,512]{1,0:T(8,128)(2,1)S(1)}, u32[]{:S(2)}, u32[]{:S(2)}) collective-permute-start(bf16[384,512]{1,0:T(8,128)(2,1)S(1)} %get-tuple-element.35), channel_id=1, source_target_pairs={{0,4},{8,12},{16,20},{24,28},{4,0},{12,8},{20,16},{28,24},{1,5},{9... | collective-permute-start | bytes 1179656 | tf_op jit(solution)/shard_map/ppermute | solution.py:442
  5.8 11.3 %collective-permute-start.1 = (bf16[384,512]{1,0:T(8,128)(2,1)S(1)}, bf16[384,512]{1,0:T(8,128)(2,1)S(1)}, u32[]{:S(2)}, u32[]{:S(2)}) collective-permute-start(bf16[384,512]{1,0:T(8,128)(2,1)S(1)} %get-tuple-element.36), channel_id=1, source_target_pairs={{0,3},{1,2},{2,1},{3,0},{4,7},{5,6},{6,5},{7,4},{8,11},{9,10},{10,... | collective-permute-start | bytes 1179656 | tf_op jit(solution)/shard_map/ppermute | solution.py:429
  10.2 7.0 %collective-permute-start.2 = (bf16[384,512]{1,0:T(8,128)(2,1)S(1)}, bf16[384,512]{1,0:T(8,128)(2,1)S(1)}, u32[]{:S(2)}, u32[]{:S(2)}) collective-permute-start(bf16[384,512]{1,0:T(8,128)(2,1)S(1)} %get-tuple-element.38), channel_id=1, source_target_pairs={{0,1},{1,0},{2,3},{3,2},{4,5},{5,4},{6,7},{7,6},{8,9},{9,8},{10,11... | collective-permute-start | bytes 1179656 | tf_op jit(solution)/shard_map/ppermute | solution.py:429
  11.2 14.5 %collective-permute-start.4 = (bf16[384,512]{1,0:T(8,128)(2,1)S(1)}, bf16[384,512]{1,0:T(8,128)(2,1)S(1)}, u32[]{:S(2)}, u32[]{:S(2)}) collective-permute-start(bf16[384,512]{1,0:T(8,128)(2,1)S(1)} %get-tuple-element.48), channel_id=1, source_target_pairs={{0,2},{1,3},{2,0},{3,1},{4,6},{5,7},{6,4},{7,5},{8,10},{9,11},{10,... | collective-permute-start | bytes 1179656 | tf_op jit(solution)/shard_map/ppermute | solution.py:429
  11.7 14.4 %collective-permute-start.3 = (bf16[384,512]{1,0:T(8,128)(2,1)S(1)}, bf16[384,512]{1,0:T(8,128)(2,1)S(1)}, u32[]{:S(2)}, u32[]{:S(2)}) collective-permute-start(bf16[384,512]{1,0:T(8,128)(2,1)S(1)} %get-tuple-element.47), channel_id=1, source_target_pairs={{4,8},{12,16},{20,24},{8,4},{16,12},{24,20},{5,9},{13,17},{21,25},... | collective-permute-start | bytes 1179656 | tf_op jit(solution)/shard_map/ppermute | solution.py:442
  15.7 13.7 %collective-permute-start.7 = (bf16[384,512]{1,0:T(8,128)(2,1)S(1)}, bf16[384,512]{1,0:T(8,128)(2,1)S(1)}, u32[]{:S(2)}, u32[]{:S(2)}) collective-permute-start(bf16[384,512]{1,0:T(8,128)(2,1)S(1)} %get-tuple-element.59), channel_id=1, source_target_pairs={{1,2},{2,1},{5,6},{6,5},{9,10},{10,9},{13,14},{14,13},{17,18},{18,... | collective-permute-start | bytes 1179656 | tf_op jit(solution)/shard_map/ppermute | solution.py:434
  25.7 18.6 %slice-start = ((s8[4718592]{0:T(1024)(128)(4,1)}), s8[4194304]{0:T(1024)(128)(4,1)S(1)}, s32[]{:S(2)}) async-start(s8[4718592]{0:T(1024)(128)(4,1)} %bitcast.1), calls=%async_computation | async-start | bytes 8388608
  25.9 17.4 %collective-permute-start.6 = (bf16[384,512]{1,0:T(8,128)(2,1)S(1)}, bf16[384,512]{1,0:T(8,128)(2,1)S(1)}, u32[]{:S(2)}, u32[]{:S(2)}) collective-permute-start(bf16[384,512]{1,0:T(8,128)(2,1)S(1)} %get-tuple-element.56), channel_id=1, source_target_pairs={{0,4},{8,12},{16,20},{24,28},{4,0},{12,8},{20,16},{28,24},{1,5},{9... | collective-permute-start | bytes 1179656 | tf_op jit(solution)/shard_map/ppermute | solution.py:442
  26.1 18.3 %slice-start.1 = ((s8[4718592]{0:T(1024)(128)(4,1)}), s8[524288]{0:T(1024)(128)(4,1)S(1)}, s32[]{:S(2)}) async-start(s8[4718592]{0:T(1024)(128)(4,1)} %bitcast.1), calls=%async_computation.1 | async-start | bytes 1048576
  27.2 17.1 %collective-permute-start.8 = (bf16[384,512]{1,0:T(8,128)(2,1)S(1)}, bf16[384,512]{1,0:T(8,128)(2,1)S(1)}, u32[]{:S(2)}, u32[]{:S(2)}) collective-permute-start(bf16[384,512]{1,0:T(8,128)(2,1)S(1)} %get-tuple-element.63), channel_id=1, source_target_pairs={{0,1},{1,0},{2,3},{3,2},{4,5},{5,4},{6,7},{7,6},{8,9},{9,8},{10,11... | collective-permute-start | bytes 1179656 | tf_op jit(solution)/shard_map/ppermute | solution.py:429
  27.3 19.9 %collective-permute-start.5 = (bf16[384,512]{1,0:T(8,128)(2,1)S(1)}, bf16[384,512]{1,0:T(8,128)(2,1)S(1)}, u32[]{:S(2)}, u32[]{:S(2)}) collective-permute-start(bf16[384,512]{1,0:T(8,128)(2,1)S(1)} %get-tuple-element.55), channel_id=1, source_target_pairs={{4,8},{12,16},{20,24},{8,4},{16,12},{24,20},{5,9},{13,17},{21,25},... | collective-permute-start | bytes 1179656 | tf_op jit(solution)/shard_map/ppermute | solution.py:442
  28.0 18.2 %collective-permute-start.9 = (bf16[384,512]{1,0:T(8,128)(2,1)S(1)}, bf16[384,512]{1,0:T(8,128)(2,1)S(1)}, u32[]{:S(2)}, u32[]{:S(2)}) collective-permute-start(bf16[384,512]{1,0:T(8,128)(2,1)S(1)} %get-tuple-element.65), channel_id=1, source_target_pairs={{0,2},{1,3},{2,0},{3,1},{4,6},{5,7},{6,4},{7,5},{8,10},{9,11},{10,... | collective-permute-start | bytes 1179656 | tf_op jit(solution)/shard_map/ppermute | solution.py:429
  29.4 17.7 %collective-permute-start.10 = (bf16[384,512]{1,0:T(8,128)(2,1)S(1)}, bf16[384,512]{1,0:T(8,128)(2,1)S(1)}, u32[]{:S(2)}, u32[]{:S(2)}) collective-permute-start(bf16[384,512]{1,0:T(8,128)(2,1)S(1)} %get-tuple-element.66), channel_id=1, source_target_pairs={{0,3},{3,0},{4,7},{7,4},{8,11},{11,8},{12,15},{15,12},{16,19},{19,... | collective-permute-start | bytes 1179656 | tf_op jit(solution)/shard_map/ppermute | solution.py:434

commit v11 on v10

--- a/solution.py
+++ b/solution.py
@@ -13,6 +13,12 @@
 ANY = pl.BlockSpec(memory_space=pl.ANY)
 INSIDE = pl.BlockSpec(memory_space=pltpu.VMEM)
 DMA = pltpu.SemaphoreType.DMA
+
+
+TAKES = {
+    "upstream": 3, "interior": 3, "near_end": 1, "grad_conv": 1, "far_end": 1, "back_interior": 2,
+    "early_mix": 3, "tail": 2,
+}
 
 
 def kernel_call(name, kernel, operands, outs, scratch=(), aliases=None):
@@ -27,6 +33,7 @@
         scratch_shapes=list(scratch),
         input_output_aliases=aliases or {},
         compiler_params=pltpu.CompilerParams(vmem_limit_bytes=16 << 20),
+        cost_estimate=pl.CostEstimate(flops=0, transcendentals=0, bytes_accessed=TAKES[name] * 3_500_000),
         name=name,
     )(*[
         pltpu.with_memory_space_constraint(array, pltpu.VMEM if held else pltpu.HBM)
@@ -223,54 +230,47 @@
     return results[0], results[1], dict(zip(away + here, results[2:]))
 
 
+def far_kernel(ks, _, __, far_ref, plain_ref, *rest):
+    n = len(ks)
+    slope_ref, wide = rest[-(n + 2):-n]
+    ch, at_end = lax.axis_index("ch"), odd_place()
+    length, halo = slope_ref.shape[1], far_ref.shape[1]
+    block = length // n
+    wide[:, lanes(at_end * (halo + length), halo)] = far_ref[...]
+    for k, active_ref in zip(ks, rest[-n:]):
+        @pl.when(in_end(ch ^ k, block, at_end, length))
+        def _(k=k, active_ref=active_ref):
+            convolve_block(plain_ref, wide, (ch ^ k) * block, active_ref, slope_ref)
+
+
+def far_end(far, plain, slope, wide, ks, active):
+    outs = [slope, wide, *[active[k] for k in ks]]
+    results = kernel_call(
+        "far_end", functools.partial(far_kernel, ks), [(o, True) for o in (slope, wide, far, plain, *outs[2:])],
+        [(o.shape, o.dtype, True) for o in outs],
+        aliases={0: 0, 1: 1, **{2 + i: i for i in range(2, len(outs))}},
+    )
+    return results[0], dict(zip(ks, results[2:]))
+
+
 def grad_kernel(ks, slope_ref, *rest):
-    up_refs, (grad_ref, near_out) = rest[:-2], rest[-2:]
+    up_refs, (grad_ref, near_out, far_out) = rest[:-3], rest[-3:]
     ch, odd = lax.axis_index("ch"), odd_place()
     length, halo = grad_ref.shape[1], near_out.shape[1]
     block = length // len(ks)
     for k, up_ref in zip(ks, up_refs):
-        @pl.when(jnp.logical_not(in_end(ch ^ k, block, odd, length)))
-        def _(k=k, up_ref=up_ref):
-            here = lanes((ch ^ k) * block, block)
-            grad_ref[:, here] = (up_ref[...].astype(F32) * slope_ref[:, here]).astype(BF16)
+        here = lanes((ch ^ k) * block, block)
+        grad_ref[:, here] = (up_ref[...].astype(F32) * slope_ref[:, here]).astype(BF16)
     near_out[...] = grad_ref[:, lanes((1 - odd) * (length - halo), halo)]
+    far_out[...] = grad_ref[:, lanes(odd * (length - halo), halo)]
 
 
 def grad_conv(slope, ks, ups):
+    end = (slope.shape[0], DILATION_STEP)
     return kernel_call(
-        "grad_conv", functools.partial(grad_kernel, ks),
-        [(o, True) for o in (slope, *[ups[k] for k in ks])],
-        [(slope.shape, BF16, True), ((slope.shape[0], DILATION_STEP), BF16, True)],
-    )
-
-
-def far_kernel(ks, _, __, far_ref, plain_ref, *rest):
-    n = len(ks)
-    up_refs, (slope_ref, far_out, wide, grad_ref), active_refs = rest[:n], rest[-(n + 4):-n], rest[-n:]
-    ch, at_end = lax.axis_index("ch"), odd_place()
-    length, halo = slope_ref.shape[1], far_ref.shape[1]
-    block = length // n
-    wide[:, lanes(at_end * (halo + length), halo)] = far_ref[...]
-    for k, up_ref, active_ref in zip(ks, up_refs, active_refs):
-        @pl.when(in_end(ch ^ k, block, at_end, length))
-        def _(k=k, up_ref=up_ref, active_ref=active_ref):
-            convolve_block(plain_ref, wide, (ch ^ k) * block, active_ref, slope_ref)
-            here = lanes((ch ^ k) * block, block)
-            grad = (up_ref[...].astype(F32) * slope_ref[:, here]).astype(BF16)
-            grad_ref[:, here] = grad
-            far_out[:, lanes((ch ^ k) * block - at_end * (length - halo), block)] = grad
-
-
-def far_end(far, plain, slope, wide, grad, ks, ups, active):
-    n = len(ks)
-    operands = [(o, True) for o in (slope, wide, far, plain, *[ups[k] for k in ks], grad)]
-    operands += [(active[k], True) for k in ks]
-    outs = [slope, far, wide, grad, *[active[k] for k in ks]]
-    results = kernel_call(
-        "far_end", functools.partial(far_kernel, ks), operands, [(o.shape, o.dtype, True) for o in outs],
-        aliases={0: 0, 1: 2, 4 + n: 3, **{5 + n + i: 4 + i for i in range(n)}},
-    )
-    return results[1], results[3], dict(zip(ks, results[4:]))
+        "grad_conv", functools.partial(grad_kernel, ks), [(o, True) for o in (slope, *[ups[k] for k in ks])],
+        [(slope.shape, BF16, True), (end, BF16, True), (end, BF16, True)],
+    )
 
 
 def columns_times(order, pw_ref, rows, pieces):
@@ -308,25 +308,24 @@
         at += channels
 
 
-def mix_kernel(order, counts, adds, *refs):
-    before, refs = refs[:adds], refs[-sum(counts) - 3:]
+def mix_kernel(order, counts, *refs):
+    refs = refs[-sum(counts) - 3:]
     pw_ref, piece_refs, sum_ref, gathered = refs[0], refs[1:-2], refs[-2], refs[-1]
     gather(counts, piece_refs, gathered)
     pieces = gathered[...]
     step = 512
     for m in range(0, sum_ref.shape[0], step):
         rows = slice(m, m + step)
-        part = columns_times(order, pw_ref, rows, pieces)
-        sum_ref[rows, :] = part + before[0][rows, :] if before else part
-
-
-def mix(name, pw_weight, order, active, before, waited=()):
+        sum_ref[rows, :] = columns_times(order, pw_ref, rows, pieces)
+
+
+def mix(name, pw_weight, order, active, waited):
     channels, width = active[order[0]][0].shape
-    operands = [*before, *waited, columns_of(pw_weight, channels, order), *[p for k in order for p in active[k]]]
+    operands = [*waited, columns_of(pw_weight, channels, order), *[p for k in order for p in active[k]]]
     return kernel_call(
-        name, functools.partial(mix_kernel, order, [len(active[k]) for k in order], len(before)),
+        name, functools.partial(mix_kernel, order, [len(active[k]) for k in order]),
         [(o, True) for o in operands], [((pw_weight.shape[0], width), F32, True)],
-        [pltpu.VMEM((len(order) * channels, width), BF16)], {0: 0} if before else {},
+        [pltpu.VMEM((len(order) * channels, width), BF16)],
     )
 
 
@@ -368,25 +367,9 @@
     return out_ref.at[:, lanes(at_end * (out_ref.shape[1] - DILATION_STEP), DILATION_STEP)]
 
 
-def back_near_kernel(near_ref, ends_ref, turned_ref, _, out_ref, done_ref, held, sem):
-    at_end = 1 - odd_place()
-    back_end(near_ref, ends_ref, turned_ref, at_end, held)
-    copy = pltpu.make_async_copy(held, end_of(out_ref, at_end), sem)
-    copy.start()
-    done_ref[...] = jnp.zeros_like(done_ref)
-    copy.wait()
-
-
-def back_near(near, ends, turned, grad_inputs):
-    return kernel_call(
-        "back_near", back_near_kernel, [(near, True), (ends, True), (turned, True), (grad_inputs, False)],
-        [(grad_inputs.shape, BF16, False), ((8, 128), F32, True)], [pltpu.VMEM(near.shape, BF16), DMA], {3: 0},
-    )
-
-
-def tail_kernel(order, counts, far_ref, sum_ref, pw_ref, *rest):
+def tail_kernel(order, counts, near_ref, far_ref, sum_ref, pw_ref, *rest):
     piece_refs, rest = rest[:-10], rest[-10:]
-    ends_ref, turned_ref, _, mixed_ref, out_ref, gathered, held, end, sems, end_sem = rest
+    ends_ref, turned_ref, _, mixed_ref, out_ref, gathered, held, both, sems, end_sems = rest
     copies = []
 
     def send(source, place, sem):
@@ -400,16 +383,17 @@
         rows = slice(m, m + step)
         held[rows, :] = (sum_ref[rows, :] + columns_times(order, pw_ref, rows, pieces)).astype(BF16)
         send(held.at[rows, :], mixed_ref.at[rows, :], sems.at[m // step])
-    at_end = odd_place()
-    back_end(far_ref, ends_ref, turned_ref, at_end, end)
-    send(end, end_of(out_ref, at_end), end_sem)
+    odd = odd_place()
+    for place, (halo_ref, at_end) in enumerate(((near_ref, 1 - odd), (far_ref, odd))):
+        back_end(halo_ref, ends_ref, turned_ref, at_end, both.at[place])
+        send(both.at[place], end_of(out_ref, at_end), end_sems.at[place])
     for copy in copies:
         copy.wait()
 
 
-def tail(far, partial, pw_weight, order, active, ends, turned, grad_inputs):
+def tail(near, far, partial, pw_weight, order, active, ends, turned, grad_inputs):
     channels = far.shape[0]
-    operands = [far, partial, columns_of(pw_weight, channels, order)]
+    operands = [near, far, partial, columns_of(pw_weight, channels, order)]
     operands += [*[p for k in order for p in active[k]], ends, turned]
     operands = [(o, True) for o in operands] + [(grad_inputs, False)]
     return kernel_call(
@@ -417,7 +401,7 @@
         [(partial.shape, BF16, False), (grad_inputs.shape, BF16, False)],
         [
             pltpu.VMEM((len(order) * channels, partial.shape[1]), BF16), pltpu.VMEM(partial.shape, BF16),
-            pltpu.VMEM(far.shape, BF16), DMA((partial.shape[0] // 512,)), DMA,
+            pltpu.VMEM((2, *far.shape), BF16), DMA((partial.shape[0] // 512,)), DMA((2,)),
         ],
         {len(operands) - 1: 1},
     )
@@ -463,10 +447,9 @@
     inner = {k: exchange_part(active[k], k, True) for k in first}
     waited = [ups[k] for k in first + [k for k in rest if k > 0]]
     slope, wide, active = near_end(near, waited, plain, slope, wide, first, second + rest, active)
-    grad, near_grad = grad_conv(slope, order, ups)
-    near_grad = swap(near_grad, 0)
-    far_grad, grad, active = far_end(far, plain, slope, wide, grad, order, ups, active)
-    far_grad = swap(far_grad, 1)
+    slope, active = far_end(far, plain, slope, wide, order, active)
+    grad, near_grad, far_grad = grad_conv(slope, order, ups)
+    near_grad, far_grad = swap(near_grad, 0), swap(far_grad, 1)
     active = {
         k: (inner[k], exchange_part(active[k], k, False)) if k in first else (exchange(active[k], k),)
         for k in order
@@ -478,10 +461,8 @@
         [((channels, length), BF16, False), ((channels, 2 * halo), F32, True)],
         [pltpu.VMEM((channels, length - 2 * halo), BF16), DMA],
     )
-    grad_inputs, done = back_near(near_grad, ends, turned, grad_inputs)
-    partial = mix("half_mix", pw_weight, rest, active, [], [done])
-    (partial,) = mix("early_mix", pw_weight, second, active, partial)
-    return tuple(tail(far_grad, partial, pw_weight, first, active, ends, turned, grad_inputs))
+    (partial,) = mix("early_mix", pw_weight, second + rest, active, [ends])
+    return tuple(tail(near_grad, far_grad, partial, pw_weight, first, active, ends, turned, grad_inputs))
 
 
 def solution(mesh):

time: 50.3 us -> 50.9 us (1.012); the launches traced: 49.3 us -> 50.7 us
  starting transfers between devices: 11.3 us -> 22.1 us
  waiting for transfers between devices: 18.3 us -> 9.93 us
  Pallas kernels: 18.7 us -> 17.7 us
    ppermute x5, starting transfers between devices: 3.76 us -> 11.5 us  [exchange(): lax.ppermute(piece, 'ch', [(i, i ^ k) for i in range(lax.axis_size('ch'))])]
    ppermute x4, waiting for transfers between devices: 9.85 us -> 4.2 us  [swap(): return lax.ppermute(values, 'ctx', pairs + [(b, a) for a, b in pairs])]
    ppermute x5, waiting for transfers between devices: 8.49 us -> 5.72 us  [exchange(): lax.ppermute(piece, 'ch', [(i, i ^ k) for i in range(lax.axis_size('ch'))])]
    ppermute x4, starting transfers between devices: 4.5 us -> 6.86 us  [swap(): return lax.ppermute(values, 'ctx', pairs + [(b, a) for a, b in pairs])]
    pallas_call x11 -> x9, Pallas kernels: 18.7 us -> 17.7 us  [kernel_call(): pl.pallas_call(kernel, in_specs=[INSIDE if held else ANY for _, held in o...]
    ppermute x2, starting transfers between devices: 3 us -> 3.77 us  [exchange_part(): lax.ppermute(piece, 'ch', [(i, i ^ k) for i in range(n) if is_inner(i ^ k...]
  transfers between devices with their start and end apart: 11 -> 11, of which waited for: 3 -> 3; matrix products, arithmetic and copies ran while one was open for 0% -> 0% of each run, Pallas kernels for 30% -> 26%
where the time goes in v11:
time: 50.9 us; the launch traced here: 50.7 us
  starting transfers between devices  22.1 us (43%)
  Pallas kernels  17.7 us (35%)
  waiting for transfers between devices  9.93 us (20%)
  between operations  0.94 us (2%)
    pallas_call x9, Pallas kernels, kernel_call(): pl.pallas_call(kernel, in_specs=[INSIDE if held else ANY for _, held in o...  17.7 us
    ppermute x5, starting transfers between devices, exchange(): lax.ppermute(piece, 'ch', [(i, i ^ k) for i in range(lax.axis_size('ch'))])  11.5 us
    ppermute x4, starting transfers between devices, swap(): return lax.ppermute(values, 'ctx', pairs + [(b, a) for a, b in pairs])  6.86 us
    ppermute x5, waiting for transfers between devices, exchange(): lax.ppermute(piece, 'ch', [(i, i ^ k) for i in range(lax.axis_size('ch'))])  5.72 us
    ppermute x4, waiting for transfers between devices, swap(): return lax.ppermute(values, 'ctx', pairs + [(b, a) for a, b in pairs])  4.2 us
    ppermute x2, starting transfers between devices, exchange_part(): lax.ppermute(piece, 'ch', [(i, i ^ k) for i in range(n) if is_inner(i ^ k...  3.77 us
  transfers between devices with their start and end apart: 11, of which 3 were waited for; matrix products, arithmetic and copies ran while one was open for 0% of the time, Pallas kernels for 26%

profile of v11, /device:TPU:0, one launch (start us, length us, event | category | flops | bytes accessed | tf_op | source)
XLA Modules:
  0.0 50.7 jit_solution(11000133736528064798)
XLA Ops:
  0.6 2.2 %upstream.2 = (bf16[384,512]{1,0:T(8,128)(2,1)S(1)}, bf16[1536,512]{1,0:T(8,128)(2,1)S(1)}, bf16[384,512]{1,0:T(8,128)(2,1)S(1)}) custom-call(bf16[1536,1536]{1,0:T(8,128)(2,1)} %pw_ref.5, bf16[1536,512]{1,0:T(8,128)(2,1)} %cot_ref.1, bf16[384,2048]{1,0:T(8,128)(2,1)} %x_ref.5), custom_call_target="tpu_custom_call" | custom-call | bytes 10500000 | tf_op jit(solution)/shard_map/upstream/pallas_call | solution.py:25
  2.8 3.0 %collective-permute-start = (bf16[384,512]{1,0:T(8,128)(2,1)S(1)}, bf16[384,512]{1,0:T(8,128)(2,1)S(1)}, u32[]{:S(2)}, u32[]{:S(2)}) collective-permute-start(bf16[384,512]{1,0:T(8,128)(2,1)S(1)} %get-tuple-element.33), channel_id=1, source_target_pairs={{0,4},{8,12},{16,20},{24,28},{4,0},{12,8},{20,16},{28,24},{1,5},{9... | collective-permute-start | bytes 1179656 | tf_op jit(solution)/shard_map/ppermute | solution.py:426
  5.8 0.7 %collective-permute-start.1 = (bf16[384,512]{1,0:T(8,128)(2,1)S(1)}, bf16[384,512]{1,0:T(8,128)(2,1)S(1)}, u32[]{:S(2)}, u32[]{:S(2)}) collective-permute-start(bf16[384,512]{1,0:T(8,128)(2,1)S(1)} %get-tuple-element.34), channel_id=1, source_target_pairs={{0,3},{1,2},{2,1},{3,0},{4,7},{5,6},{6,5},{7,4},{8,11},{9,10},{10,... | collective-permute-start | bytes 1179656 | tf_op jit(solution)/shard_map/ppermute | solution.py:413
  6.5 3.6 %upstream.3 = (bf16[384,512]{1,0:T(8,128)(2,1)S(1)}, bf16[384,512]{1,0:T(8,128)(2,1)S(1)}, bf16[384,512]{1,0:T(8,128)(2,1)S(1)}, bf16[384,512]{1,0:T(8,128)(2,1)S(1)}) custom-call(bf16[1536,1536]{1,0:T(8,128)(2,1)} %pw_ref.5, bf16[1536,512]{1,0:T(8,128)(2,1)S(1)} %get-tuple-element.35.cot_ref, bf16[384,2048]{1,0:T(8,128)(2,1)} %x_ref.5), custom_call_target="tpu_custom_call" | custom-call | bytes 10500000 | tf_op jit(solution)/shard_map/upstream/pallas_call | solution.py:25
  10.2 1.0 %collective-permute-start.2 = (bf16[384,512]{1,0:T(8,128)(2,1)S(1)}, bf16[384,512]{1,0:T(8,128)(2,1)S(1)}, u32[]{:S(2)}, u32[]{:S(2)}) collective-permute-start(bf16[384,512]{1,0:T(8,128)(2,1)S(1)} %get-tuple-element.36), channel_id=1, source_target_pairs={{0,1},{1,0},{2,3},{3,2},{4,5},{5,4},{6,7},{7,6},{8,9},{9,8},{10,11... | collective-permute-start | bytes 1179656 | tf_op jit(solution)/shard_map/ppermute | solution.py:413
  11.2 0.7 %collective-permute-start.3 = (bf16[384,512]{1,0:T(8,128)(2,1)S(1)}, bf16[384,512]{1,0:T(8,128)(2,1)S(1)}, u32[]{:S(2)}, u32[]{:S(2)}) collective-permute-start(bf16[384,512]{1,0:T(8,128)(2,1)S(1)} %get-tuple-element.45), channel_id=1, source_target_pairs={{4,8},{12,16},{20,24},{8,4},{16,12},{24,20},{5,9},{13,17},{21,25},... | collective-permute-start | bytes 1179656 | tf_op jit(solution)/shard_map/ppermute | solution.py:426
  11.9 0.6 %collective-permute-start.4 = (bf16[384,512]{1,0:T(8,128)(2,1)S(1)}, bf16[384,512]{1,0:T(8,128)(2,1)S(1)}, u32[]{:S(2)}, u32[]{:S(2)}) collective-permute-start(bf16[384,512]{1,0:T(8,128)(2,1)S(1)} %get-tuple-element.51), channel_id=1, source_target_pairs={{0,2},{1,3},{2,0},{3,1},{4,6},{5,7},{6,4},{7,5},{8,10},{9,11},{10,... | collective-permute-start | bytes 1179656 | tf_op jit(solution)/shard_map/ppermute | solution.py:413
  12.4 3.3 %interior.1 = (bf16[384,512]{1,0:T(8,128)(2,1)S(1)}, bf16[384,512]{1,0:T(8,128)(2,1)S(1)}, bf16[384,512]{1,0:T(8,128)(2,1)S(1)}, bf16[384,512]{1,0:T(8,128)(2,1)...) custom-call(bf16[384,2048]{1,0:T(8,128)(2,1)} %x_ref.5, ...), custom_call_target="tpu_custom_call" | custom-call | bytes 10500000 | tf_op jit(solution)/shard_map/interior/pallas_call | solution.py:25
  15.8 0.0 collective-permute-done.near_ref
  15.8 0.7 %collective-permute-start.7 = (bf16[384,512]{1,0:T(8,128)(2,1)S(1)}, bf16[384,512]{1,0:T(8,128)(2,1)S(1)}, u32[]{:S(2)}, u32[]{:S(2)}) collective-permute-start(bf16[384,512]{1,0:T(8,128)(2,1)S(1)} %get-tuple-element.57), channel_id=1, source_target_pairs={{1,2},{2,1},{5,6},{6,5},{9,10},{10,9},{13,14},{14,13},{17,18},{18,... | collective-permute-start | bytes 1179656 | tf_op jit(solution)/shard_map/ppermute | solution.py:418
  16.5 0.7 %collective-permute-done.1.rest_0_ = bf16[384,512]{1,0:T(8,128)(2,1)S(1)} collective-permute-done((bf16[384,512]{1,0:T(8,128)(2,1)S(1)}, bf16[384,512]{1,0:T(8,128)(2,1)S(1)}, u32[]{:S(2)}, u32[]{:S(2)}) %collective-permute-start.1) | collective-permute-done | bytes 393248 | tf_op jit(solution)/shard_map/ppermute | solution.py:413
  17.2 0.0 collective-permute-done.2.rest_1_.rest_2_
  17.2 0.8 %near_end.1 = (f32[384,2048]{1,0:T(8,128)S(1)}, bf16[384,3072]{1,0:T(8,128)(2,1)S(1)}, bf16[384,512]{1,0:T(8,128)(2,1)S(1)}, bf16[384,512]{1,0:T(8,128)(2,1)S(1)...) custom-call(bf16[384,512]{1,0:T(8,128)(2,1)S(1)} %collective-permute, ...), custom_call_target="tpu_custom_call", output_to_operand_aliasing={{0}: (4, {}), {1}: (5, {}), {3}: (6, {}), {4}: (7, {}), {5}... | custom-call | bytes 3500000 | tf_op jit(solution)/shard_map/near_end/pallas_call | solution.py:25
  18.0 0.0 collective-permute-done.3.far_ref
  18.0 0.0 slice-start
  18.0 0.0 slice-start.1
  18.0 0.8 %far_end.1 = (f32[384,2048]{1,0:T(8,128)S(1)}, bf16[384,3072]{1,0:T(8,128)(2,1)S(1)}, bf16[384,512]{1,0:T(8,128)(2,1)S(1)}, bf16[384,512]{1,0:T(8,128)(2,1)S(1)}...) custom-call(f32[384,2048]{1,0:T(8,128)S(1)} %get-tuple-element.43._,, ...), custom_call_target="tpu_custom_call", output_to_operand_aliasing={{0}: (0, {}), {1}: (1, {}), {2}: (4, {}), {3}: (5, {}), {4}... | custom-call | bytes 3500000 | tf_op jit(solution)/shard_map/far_end/pallas_call | solution.py:25
  18.8 9.0 %collective-permute-start.8 = (bf16[384,512]{1,0:T(8,128)(2,1)S(1)}, bf16[384,512]{1,0:T(8,128)(2,1)S(1)}, u32[]{:S(2)}, u32[]{:S(2)}) collective-permute-start(bf16[384,512]{1,0:T(8,128)(2,1)S(1)} %get-tuple-element.59), channel_id=1, source_target_pairs={{0,2},{1,3},{2,0},{3,1},{4,6},{5,7},{6,4},{7,5},{8,10},{9,11},{10,... | collective-permute-start | bytes 1179656 | tf_op jit(solution)/shard_map/ppermute | solution.py:413
  27.8 0.2 collective-permute-start.9
  28.0 0.0 collective-permute-done.4.rest_1_
  28.0 0.6 %grad_conv.1 = (bf16[384,2048]{1,0:T(8,128)(2,1)S(1)}, bf16[384,512]{1,0:T(8,128)(2,1)S(1)}, bf16[384,512]{1,0:T(8,128)(2,1)S(1)}) custom-call(f32[384,2048]{1,0:T(8,128)S(1)} %get-tuple-element.50.slope_ref, bf16[384,512]{1,0:T(8,128)(2,1)S(1)} %collective-permute-done.1.rest_0_, bf16[384,512]{1,0:T(8,128)(2,1)S(1)} %collective-permute-done.4.rest_1_, ...), custom_call_target="tpu_custom_call" | custom-call | bytes 3500000 | tf_op jit(solution)/shard_map/grad_conv/pallas_call | solution.py:25
  28.6 2.5 %collective-permute-start.5 = (bf16[384,512]{1,0:T(8,128)(2,1)S(1)}, bf16[384,512]{1,0:T(8,128)(2,1)S(1)}, u32[]{:S(2)}, u32[]{:S(2)}) collective-permute-start(bf16[384,512]{1,0:T(8,128)(2,1)S(1)} %get-tuple-element.53), channel_id=1, source_target_pairs={{0,4},{8,12},{16,20},{24,28},{4,0},{12,8},{20,16},{28,24},{1,5},{9... | collective-permute-start | bytes 1179656 | tf_op jit(solution)/shard_map/ppermute | solution.py:426
  31.1 0.7 %collective-permute-start.6 = (bf16[384,512]{1,0:T(8,128)(2,1)S(1)}, bf16[384,512]{1,0:T(8,128)(2,1)S(1)}, u32[]{:S(2)}, u32[]{:S(2)}) collective-permute-start(bf16[384,512]{1,0:T(8,128)(2,1)S(1)} %get-tuple-element.54), channel_id=1, source_target_pairs={{4,8},{12,16},{20,24},{8,4},{16,12},{24,20},{5,9},{13,17},{21,25},... | collective-permute-start | bytes 1179656 | tf_op jit(solution)/shard_map/ppermute | solution.py:426
  31.8 0.0 collective-permute-done.7.rest_0_
  31.8 3.1 %collective-permute-start.10 = (bf16[384,512]{1,0:T(8,128)(2,1)S(1)}, bf16[384,512]{1,0:T(8,128)(2,1)S(1)}, u32[]{:S(2)}, u32[]{:S(2)}) collective-permute-start(bf16[384,512]{1,0:T(8,128)(2,1)S(1)} %get-tuple-element.62), channel_id=1, source_target_pairs={{0,3},{3,0},{4,7},{7,4},{8,11},{11,8},{12,15},{15,12},{16,19},{19,... | collective-permute-start | bytes 1179656 | tf_op jit(solution)/shard_map/ppermute | solution.py:418
  34.9 1.7 %back_interior.1 = (bf16[384,2048]{1,0:T(8,128)(2,1)}, f32[384,1024]{1,0:T(8,128)S(1)}) custom-call(bf16[384,2048]{1,0:T(8,128)(2,1)S(1)} %get-tuple-element.55.grad_ref, bf16[3,384,96]{2,1,0:T(8,128)(2,1)S(1)} %get-tuple-element.56.turned_ref.rest_3_, bf16[384,512]{1,0:T(8,128)(2,1)S(1)} %collective-permute-done.7.rest_0_), custom_call_target="tpu_custom_call" | custom-call | bytes 7000000 | tf_op jit(solution)/shard_map/back_interior/pallas_call | solution.py:25
  36.5 5.0 %collective-permute-done.8.refs_2_ = bf16[384,512]{1,0:T(8,128)(2,1)S(1)} collective-permute-done((bf16[384,512]{1,0:T(8,128)(2,1)S(1)}, bf16[384,512]{1,0:T(8,128)(2,1)S(1)}, u32[]{:S(2)}, u32[]{:S(2)}) %collective-permute-start.8) | collective-permute-done | bytes 393248 | tf_op jit(solution)/shard_map/ppermute | solution.py:413
  41.6 2.6 %early_mix.1.sum_ref = f32[1536,512]{1,0:T(8,128)S(1)} custom-call(f32[384,1024]{1,0:T(8,128)S(1)} %get-tuple-element.58.refs_0_.rest_2_, bf16[1536,1536]{1,0:T(8,128)(2,1)S(1)} %bitcast.2, bf16[384,512]{1,0:T(8,128)(2,1)S(1)} %collective-permute-done.8.refs_2_, bf16[384,512]{1,0:T(8,128)(2,1)S(1)} %collective-permute-done.9.refs_3_, ...), custom_call_target="tpu_custom_call" | custom-call | bytes 10500000 | tf_op jit(solution)/shard_map/early_mix/pallas_call | solution.py:25
  44.2 4.2 %collective-permute-done.5.near_ref = bf16[384,512]{1,0:T(8,128)(2,1)S(1)} collective-permute-done((bf16[384,512]{1,0:T(8,128)(2,1)S(1)}, bf16[384,512]{1,0:T(8,128)(2,1)S(1)}, u32[]{:S(2)}, u32[]{:S(2)}) %collective-permute-start.5) | collective-permute-done | bytes 393248 | tf_op jit(solution)/shard_map/ppermute | solution.py:426
  48.4 0.0 collective-permute-done.6.far_ref
  48.4 0.0 collective-permute-done.10.rest_1_
  48.4 2.1 %tail.1 = (bf16[1536,512]{1,0:T(8,128)(2,1)}, bf16[384,2048]{1,0:T(8,128)(2,1)}) custom-call(bf16[384,512]{1,0:T(8,128)(2,1)S(1)} %collective-permute-done.5.near_ref, bf16[384,512]{1,0:T(8,128)(2,1)S(1)} %collective-permute-done.6.far_ref, f32[1536,512]{1,0:T(8,128)S(1)} %early_mix.1.sum_ref, ...), custom_call_target="tpu_custom_call", output_to_operand_aliasing={{1}: (8, {})} | custom-call | bytes 7000000 | tf_op jit(solution)/shard_map/tail/pallas_call | solution.py:25
  (4 shorter events, 0.0 us)
Async XLA Ops:
  2.8 13.0 %collective-permute-start = (bf16[384,512]{1,0:T(8,128)(2,1)S(1)}, bf16[384,512]{1,0:T(8,128)(2,1)S(1)}, u32[]{:S(2)}, u32[]{:S(2)}) collective-permute-start(bf16[384,512]{1,0:T(8,128)(2,1)S(1)} %get-tuple-element.33), channel_id=1, source_target_pairs={{0,4},{8,12},{16,20},{24,28},{4,0},{12,8},{20,16},{28,24},{1,5},{9... | collective-permute-start | bytes 1179656 | tf_op jit(solution)/shard_map/ppermute | solution.py:426
  5.8 11.3 %collective-permute-start.1 = (bf16[384,512]{1,0:T(8,128)(2,1)S(1)}, bf16[384,512]{1,0:T(8,128)(2,1)S(1)}, u32[]{:S(2)}, u32[]{:S(2)}) collective-permute-start(bf16[384,512]{1,0:T(8,128)(2,1)S(1)} %get-tuple-element.34), channel_id=1, source_target_pairs={{0,3},{1,2},{2,1},{3,0},{4,7},{5,6},{6,5},{7,4},{8,11},{9,10},{10,... | collective-permute-start | bytes 1179656 | tf_op jit(solution)/shard_map/ppermute | solution.py:413
  10.2 7.0 %collective-permute-start.2 = (bf16[384,512]{1,0:T(8,128)(2,1)S(1)}, bf16[384,512]{1,0:T(8,128)(2,1)S(1)}, u32[]{:S(2)}, u32[]{:S(2)}) collective-permute-start(bf16[384,512]{1,0:T(8,128)(2,1)S(1)} %get-tuple-element.36), channel_id=1, source_target_pairs={{0,1},{1,0},{2,3},{3,2},{4,5},{5,4},{6,7},{7,6},{8,9},{9,8},{10,11... | collective-permute-start | bytes 1179656 | tf_op jit(solution)/shard_map/ppermute | solution.py:413
  11.2 6.8 %collective-permute-start.3 = (bf16[384,512]{1,0:T(8,128)(2,1)S(1)}, bf16[384,512]{1,0:T(8,128)(2,1)S(1)}, u32[]{:S(2)}, u32[]{:S(2)}) collective-permute-start(bf16[384,512]{1,0:T(8,128)(2,1)S(1)} %get-tuple-element.45), channel_id=1, source_target_pairs={{4,8},{12,16},{20,24},{8,4},{16,12},{24,20},{5,9},{13,17},{21,25},... | collective-permute-start | bytes 1179656 | tf_op jit(solution)/shard_map/ppermute | solution.py:426
  11.9 16.1 %collective-permute-start.4 = (bf16[384,512]{1,0:T(8,128)(2,1)S(1)}, bf16[384,512]{1,0:T(8,128)(2,1)S(1)}, u32[]{:S(2)}, u32[]{:S(2)}) collective-permute-start(bf16[384,512]{1,0:T(8,128)(2,1)S(1)} %get-tuple-element.51), channel_id=1, source_target_pairs={{0,2},{1,3},{2,0},{3,1},{4,6},{5,7},{6,4},{7,5},{8,10},{9,11},{10,... | collective-permute-start | bytes 1179656 | tf_op jit(solution)/shard_map/ppermute | solution.py:413
  15.8 16.0 %collective-permute-start.7 = (bf16[384,512]{1,0:T(8,128)(2,1)S(1)}, bf16[384,512]{1,0:T(8,128)(2,1)S(1)}, u32[]{:S(2)}, u32[]{:S(2)}) collective-permute-start(bf16[384,512]{1,0:T(8,128)(2,1)S(1)} %get-tuple-element.57), channel_id=1, source_target_pairs={{1,2},{2,1},{5,6},{6,5},{9,10},{10,9},{13,14},{14,13},{17,18},{18,... | collective-permute-start | bytes 1179656 | tf_op jit(solution)/shard_map/ppermute | solution.py:418
  18.0 23.6 %slice-start = ((s8[4718592]{0:T(1024)(128)(4,1)}), s8[4194304]{0:T(1024)(128)(4,1)S(1)}, s32[]{:S(2)}) async-start(s8[4718592]{0:T(1024)(128)(4,1)} %bitcast.1), calls=%async_computation | async-start | bytes 8388608
  18.0 23.6 %slice-start.1 = ((s8[4718592]{0:T(1024)(128)(4,1)}), s8[524288]{0:T(1024)(128)(4,1)S(1)}, s32[]{:S(2)}) async-start(s8[4718592]{0:T(1024)(128)(4,1)} %bitcast.1), calls=%async_computation.1 | async-start | bytes 1048576
  18.8 22.8 %collective-permute-start.8 = (bf16[384,512]{1,0:T(8,128)(2,1)S(1)}, bf16[384,512]{1,0:T(8,128)(2,1)S(1)}, u32[]{:S(2)}, u32[]{:S(2)}) collective-permute-start(bf16[384,512]{1,0:T(8,128)(2,1)S(1)} %get-tuple-element.59), channel_id=1, source_target_pairs={{0,2},{1,3},{2,0},{3,1},{4,6},{5,7},{6,4},{7,5},{8,10},{9,11},{10,... | collective-permute-start | bytes 1179656 | tf_op jit(solution)/shard_map/ppermute | solution.py:413
  27.8 13.8 %collective-permute-start.9 = (bf16[384,512]{1,0:T(8,128)(2,1)S(1)}, bf16[384,512]{1,0:T(8,128)(2,1)S(1)}, u32[]{:S(2)}, u32[]{:S(2)}) collective-permute-start(bf16[384,512]{1,0:T(8,128)(2,1)S(1)} %get-tuple-element.60), channel_id=1, source_target_pairs={{0,1},{1,0},{2,3},{3,2},{4,5},{5,4},{6,7},{7,6},{8,9},{9,8},{10,11... | collective-permute-start | bytes 1179656 | tf_op jit(solution)/shard_map/ppermute | solution.py:413
  28.6 19.8 %collective-permute-start.5 = (bf16[384,512]{1,0:T(8,128)(2,1)S(1)}, bf16[384,512]{1,0:T(8,128)(2,1)S(1)}, u32[]{:S(2)}, u32[]{:S(2)}) collective-permute-start(bf16[384,512]{1,0:T(8,128)(2,1)S(1)} %get-tuple-element.53), channel_id=1, source_target_pairs={{0,4},{8,12},{16,20},{24,28},{4,0},{12,8},{20,16},{28,24},{1,5},{9... | collective-permute-start | bytes 1179656 | tf_op jit(solution)/shard_map/ppermute | solution.py:426
  31.1 17.3 %collective-permute-start.6 = (bf16[384,512]{1,0:T(8,128)(2,1)S(1)}, bf16[384,512]{1,0:T(8,128)(2,1)S(1)}, u32[]{:S(2)}, u32[]{:S(2)}) collective-permute-start(bf16[384,512]{1,0:T(8,128)(2,1)S(1)} %get-tuple-element.54), channel_id=1, source_target_pairs={{4,8},{12,16},{20,24},{8,4},{16,12},{24,20},{5,9},{13,17},{21,25},... | collective-permute-start | bytes 1179656 | tf_op jit(solution)/shard_map/ppermute | solution.py:426
  31.8 16.6 %collective-permute-start.10 = (bf16[384,512]{1,0:T(8,128)(2,1)S(1)}, bf16[384,512]{1,0:T(8,128)(2,1)S(1)}, u32[]{:S(2)}, u32[]{:S(2)}) collective-permute-start(bf16[384,512]{1,0:T(8,128)(2,1)S(1)} %get-tuple-element.62), channel_id=1, source_target_pairs={{0,3},{3,0},{4,7},{7,4},{8,11},{11,8},{12,15},{15,12},{16,19},{19,... | collective-permute-start | bytes 1179656 | tf_op jit(solution)/shard_map/ppermute | solution.py:418

commit v12 on v9

--- a/solution.py
+++ b/solution.py
@@ -59,6 +59,17 @@
 
 def odd_place():
     return lax.axis_index("ctx") % 2
+
+
+def end_copy(x_ref, end_ref, at_end, sem):
+    length, halo = x_ref.shape[1], end_ref.shape[1]
+    return pltpu.make_async_copy(x_ref.at[:, lanes(at_end * (length - halo), halo)], end_ref, sem)
+
+
+def near_source_kernel(x_ref, near_ref, sem):
+    copy = end_copy(x_ref, near_ref, 1 - odd_place(), sem)
+    copy.start()
+    copy.wait()
 
 
 def upstream_kernel(order, channels, first, pw_ref, cot_ref, x_ref, *rest):
@@ -85,12 +96,9 @@
         for copy in copies:
             copy.start()
         blocks.append((rows, copies))
-    which = 1 - odd_place() if first else odd_place()
-    length, halo = x_ref.shape[1], rest[-4].shape[1]
-    end = pltpu.make_async_copy(
-        x_ref.at[:, lanes(which * (length - halo), halo)], rest[-4], sems.at[0, count + 1]
-    )
-    end.start()
+    if not first:
+        end = end_copy(x_ref, rest[-4], odd_place(), sems.at[0, count + 1])
+        end.start()
     for step, (rows, copies) in enumerate(blocks):
         for copy in copies:
             copy.wait()
@@ -103,7 +111,8 @@
                 total_ref[held, :] = part
             else:
                 piece_refs[place][...] = part.astype(BF16)
-    end.wait()
+    if not first:
+        end.wait()
 
 
 def columns_of(pw_weight, channels, order):
@@ -121,7 +130,7 @@
     count = len(order)
     outs = [((channels, width), BF16, True)] * count
     outs += [(cotangent.shape, BF16, True)] * first
-    outs += [((channels, DILATION_STEP), BF16, True)]
+    outs += [((channels, DILATION_STEP), BF16, True)] * (not first)
     results = kernel_call(
         "upstream", functools.partial(upstream_kernel, order, channels, first),
         [(columns_of(pw_weight, channels, order), False), (cotangent, not first), (inputs, False)], outs,
@@ -274,29 +283,46 @@
     )
 
 
-def back(turned_ref, rows, taps):
-    return sum(dot(turned_ref[t, rows, :], tap) for t, tap in enumerate(taps)).astype(BF16)
-
-
-def back_interior_kernel(grad_ref, turned_ref, out_ref, held, sem):
+def back_interior_kernel(grad_ref, turned_ref, out_ref, ends_ref, held, sem):
     channels, length = grad_ref.shape
     group, halo, unit = turned_ref.shape[2], DILATION_STEP, 256
+
+    def taps(rows, start, which):
+        return sum(
+            dot(turned_ref[t, rows, :], grad_ref[rows, start + (t - 1) * halo:start + (t - 1) * halo + unit])
+            for t in which
+        )
+
+    groups = [slice(g, g + group) for g in range(0, channels, group)]
+    for rows in groups:
+        for s in range(0, length - 2 * halo, unit):
+            held[rows, s:s + unit] = taps(rows, halo + s, (0, 1, 2)).astype(BF16)
+    copy = pltpu.make_async_copy(held, out_ref.at[:, halo:length - halo], sem)
+    copy.start()
+    for rows in groups:
+        for s in range(0, halo, unit):
+            ends_ref[rows, s:s + unit] = taps(rows, s, (1, 2))
+            ends_ref[rows, halo + s:halo + s + unit] = taps(rows, length - halo + s, (0, 1))
+    copy.wait()
+
+
+def back_end(halo_ref, ends_ref, turned_ref, at_end, held):
+    channels, halo = halo_ref.shape
+    group, unit = turned_ref.shape[2], 256
     for g in range(0, channels, group):
         rows = slice(g, g + group)
-        for s in range(0, length - 2 * halo, unit):
-            held[rows, s:s + unit] = back(
-                turned_ref, rows, [grad_ref[rows, s + t * halo:s + t * halo + unit] for t in range(3)]
-            )
-    copy = pltpu.make_async_copy(held, out_ref.at[:, halo:length - halo], sem)
-    copy.start()
-    copy.wait()
-
-
-def tail_kernel(order, pw_ref, sum_ref, *rest):
+        for s in range(0, halo, unit):
+            outer = dot(turned_ref[2 * at_end, rows, :], halo_ref[rows, s:s + unit])
+            held[rows, s:s + unit] = (ends_ref[rows, lanes(at_end * halo + s, unit)] + outer).astype(BF16)
+
+
+def end_of(out_ref, at_end):
+    return out_ref.at[:, lanes(at_end * (out_ref.shape[1] - DILATION_STEP), DILATION_STEP)]
+
+
+def tail_kernel(order, near_ref, far_ref, pw_ref, sum_ref, *rest):
     piece_refs, rest = rest[:len(order)], rest[len(order):]
-    near_ref, far_ref, grad_ref, turned_ref, _, mixed_ref, out_ref, held, ends, halos, sems = rest
-    channels, length = grad_ref.shape
-    group, halo, unit = turned_ref.shape[2], DILATION_STEP, 256
+    ends_ref, turned_ref, _, mixed_ref, out_ref, held, both, sems = rest
     pieces = jnp.concatenate([p[...] for p in piece_refs], axis=0)
     copies = []
 
@@ -310,37 +336,24 @@
         held[rows, :] = (sum_ref[rows, :] + columns_times(order, pw_ref, rows, pieces)).astype(BF16)
         send(held.at[rows, :], mixed_ref.at[rows, :])
     odd = odd_place()
-    halos[:, lanes((1 - odd) * halo, halo)] = near_ref[...]
-    halos[:, lanes(odd * halo, halo)] = far_ref[...]
-    for end in range(2):
-        for g in range(0, channels, group):
-            rows = slice(g, g + group)
-            for s in range(0, halo, unit):
-                inner = (length - 2 * halo) * end + s
-                taps = [
-                    grad_ref[rows, inner:inner + unit],
-                    grad_ref[rows, inner + halo:inner + halo + unit],
-                ]
-                outer = halos[rows, end * halo + s:end * halo + s + unit]
-                taps = taps + [outer] if end else [outer] + taps
-                ends[rows, end * halo + s:end * halo + s + unit] = back(turned_ref, rows, taps)
-        send(
-            ends.at[:, end * halo:(end + 1) * halo],
-            out_ref.at[:, end * (length - halo):end * (length - halo) + halo],
-        )
+    for place, (halo_ref, at_end) in enumerate(((near_ref, 1 - odd), (far_ref, odd))):
+        back_end(halo_ref, ends_ref, turned_ref, at_end, both.at[place])
+        send(both.at[place], end_of(out_ref, at_end))
     for copy in copies:
         copy.wait()
 
 
-def tail(pw_weight, order, partial, active, near, far, grad, turned, grad_inputs):
+def tail(pw_weight, order, partial, active, near, far, ends, turned, grad_inputs):
     channels, halo = near.shape
-    operands = [columns_of(pw_weight, channels, order), partial, *[active[k] for k in order]]
-    operands = [(o, True) for o in (*operands, near, far, grad, turned)] + [(grad_inputs, False)]
+    operands = [near, far, columns_of(pw_weight, channels, order), partial, *[active[k] for k in order]]
+    operands = [(o, True) for o in (*operands, ends, turned)] + [(grad_inputs, False)]
     return kernel_call(
         "tail", functools.partial(tail_kernel, order), operands,
         [(partial.shape, BF16, False), (grad_inputs.shape, BF16, False)],
-        [pltpu.VMEM(partial.shape, BF16)] + [pltpu.VMEM((channels, 2 * halo), BF16)] * 2
-        + [DMA((partial.shape[0] // 512 + 2,))],
+        [
+            pltpu.VMEM(partial.shape, BF16), pltpu.VMEM((2, channels, halo), BF16),
+            DMA((partial.shape[0] // 512 + 2,)),
+        ],
         {len(operands) - 1: 1},
     )
 
@@ -367,29 +380,31 @@
     weight = jnp.swapaxes(conv_weight, 1, 2)
     if channels % 128 != 0:
         weight = lax.dynamic_slice_in_dim(weight, lax.axis_index("ch") * channels, channels, 2)
-    pieces, cot_in, near = upstream(pw_weight, cotangent, inputs, first, True)
+    (near,) = kernel_call(
+        "near_source", near_source_kernel, [(inputs, False)], [((channels, halo), BF16, True)], [DMA]
+    )
     near = swap(near, 0)
+    pieces, cot_in = upstream(pw_weight, cotangent, inputs, first, True)
     ups = {k: exchange(p, k) for k, p in zip(first, pieces)}
     pieces, far = upstream(pw_weight, cot_in, inputs, second + rest, False)
     ups.update({k: exchange(p, k) for k, p in zip(second + rest, pieces)})
     far = swap(far, 1)
 
     active, slope, wide, plain, turned = interior(inputs, weight, n)
-    active, slope, wide = one_end(True, near, plain, active, slope, wide, [])
-    active, slope, wide = one_end(
-        False, far, plain, active, slope, wide, [ups[first[0]]]
-    )
+    active, slope, wide = one_end(True, near, plain, active, slope, wide, [ups[first[0]]])
+    active, slope, wide = one_end(False, far, plain, active, slope, wide, [])
     grad, near_grad, far_grad = grad_conv(slope, order, ups)
     active = {k: exchange(active[k], k) for k in order}
     near_grad, far_grad = swap(near_grad, 0), swap(far_grad, 1)
 
-    (grad_inputs,) = kernel_call(
+    grad_inputs, ends = kernel_call(
         "back_interior", back_interior_kernel, [(grad, True), (turned, True)],
-        [((channels, length), BF16, False)], [pltpu.VMEM((channels, length - 2 * halo), BF16), DMA],
+        [((channels, length), BF16, False), ((channels, 2 * halo), F32, True)],
+        [pltpu.VMEM((channels, length - 2 * halo), BF16), DMA],
     )
     partial = mix("early_mix", pw_weight, first, active, [])
     (partial,) = mix("half_mix", pw_weight, rest, active, partial)
-    return tuple(tail(pw_weight, second, partial, active, near_grad, far_grad, grad, turned, grad_inputs))
+    return tuple(tail(pw_weight, second, partial, active, near_grad, far_grad, ends, turned, grad_inputs))
 
 
 def solution(mesh):

time: 49.2 us -> 48.8 us (level); the launches traced: 48.8 us -> 47.9 us
  starting transfers between devices: 17.1 us -> 11.2 us
  waiting for transfers between devices: 12.6 us -> 16.9 us
  Pallas kernels: 18.2 us -> 18.9 us
    ppermute x4, waiting for transfers between devices: 2.19 us -> 7.68 us  [swap(): return lax.ppermute(values, 'ctx', pairs + [(b, a) for a, b in pairs])]
    ppermute x6, starting transfers between devices: 9.93 us -> 5.43 us  [exchange(): lax.ppermute(piece, 'ch', [(i, i ^ k) for i in range(lax.axis_size('ch'))])]
    ppermute x4, starting transfers between devices: 7.12 us -> 5.74 us  [swap(): return lax.ppermute(values, 'ctx', pairs + [(b, a) for a, b in pairs])]
    ppermute x6, waiting for transfers between devices: 10.5 us -> 9.22 us  [exchange(): lax.ppermute(piece, 'ch', [(i, i ^ k) for i in range(lax.axis_size('ch'))])]
    pallas_call x10 -> x11, Pallas kernels: 18.2 us -> 18.9 us  [kernel_call(): pl.pallas_call(kernel, in_specs=[INSIDE if held else ANY for _, held in o...]
  transfers between devices with their start and end apart: 10 -> 10, of which waited for: 4 -> 4; matrix products, arithmetic and copies ran while one was open for 0% -> 0% of each run, Pallas kernels for 28% -> 33%
where the time goes in v12:
time: 48.8 us; the launch traced here: 47.9 us
  Pallas kernels  18.9 us (39%)
  waiting for transfers between devices  16.9 us (35%)
  starting transfers between devices  11.2 us (23%)
  between operations  0.92 us (2%)
    pallas_call x11, Pallas kernels, kernel_call(): pl.pallas_call(kernel, in_specs=[INSIDE if held else ANY for _, held in o...  18.9 us
    ppermute x6, waiting for transfers between devices, exchange(): lax.ppermute(piece, 'ch', [(i, i ^ k) for i in range(lax.axis_size('ch'))])  9.22 us
    ppermute x4, waiting for transfers between devices, swap(): return lax.ppermute(values, 'ctx', pairs + [(b, a) for a, b in pairs])  7.68 us
    ppermute x4, starting transfers between devices, swap(): return lax.ppermute(values, 'ctx', pairs + [(b, a) for a, b in pairs])  5.74 us
    ppermute x6, starting transfers between devices, exchange(): lax.ppermute(piece, 'ch', [(i, i ^ k) for i in range(lax.axis_size('ch'))])  5.43 us
  transfers between devices with their start and end apart: 10, of which 4 were waited for; matrix products, arithmetic and copies ran while one was open for 0% of the time, Pallas kernels for 33%

profile of v12, /device:TPU:0, one launch (start us, length us, event | category | flops | bytes accessed | tf_op | source)
XLA Modules:
  0.0 47.9 jit_solution(14963404981313113485)
XLA Ops:
  0.6 1.0 %near_source.1 = bf16[384,512]{1,0:T(8,128)(2,1)S(1)} custom-call(bf16[384,2048]{1,0:T(8,128)(2,1)} %x_ref.7), custom_call_target="tpu_custom_call" | custom-call | tf_op jit(solution)/shard_map/near_source/pallas_call | solution.py:19
  1.7 3.0 %collective-permute-start.2 = (bf16[384,512]{1,0:T(8,128)(2,1)S(1)}, bf16[384,512]{1,0:T(8,128)(2,1)S(1)}, u32[]{:S(2)}, u32[]{:S(2)}) collective-permute-start(bf16[384,512]{1,0:T(8,128)(2,1)S(1)} %near_source.1), channel_id=1, source_target_pairs={{0,4},{8,12},{16,20},{24,28},{4,0},{12,8},{20,16},{28,24},{1,5},{9... | collective-permute-start | bytes 1179656 | tf_op jit(solution)/shard_map/ppermute | solution.py:370
  4.7 2.2 %upstream.2 = (bf16[384,512]{1,0:T(8,128)(2,1)S(1)}, bf16[1536,512]{1,0:T(8,128)(2,1)S(1)}) custom-call(bf16[1536,1536]{1,0:T(8,128)(2,1)} %pw_ref.9, bf16[1536,512]{1,0:T(8,128)(2,1)} %cot_ref.1, bf16[384,2048]{1,0:T(8,128)(2,1)} %x_ref.7), custom_call_target="tpu_custom_call" | custom-call | tf_op jit(solution)/shard_map/upstream/pallas_call | solution.py:19
  6.9 0.7 %collective-permute-start.1 = (bf16[384,512]{1,0:T(8,128)(2,1)S(1)}, bf16[384,512]{1,0:T(8,128)(2,1)S(1)}, u32[]{:S(2)}, u32[]{:S(2)}) collective-permute-start(bf16[384,512]{1,0:T(8,128)(2,1)S(1)} %get-tuple-element.35), channel_id=1, source_target_pairs={{0,3},{1,2},{2,1},{3,0},{4,7},{5,6},{6,5},{7,4},{8,11},{9,10},{10,... | collective-permute-start | bytes 1179656 | tf_op jit(solution)/shard_map/ppermute | solution.py:364
  7.6 3.6 %upstream.3 = (bf16[384,512]{1,0:T(8,128)(2,1)S(1)}, bf16[384,512]{1,0:T(8,128)(2,1)S(1)}, bf16[384,512]{1,0:T(8,128)(2,1)S(1)}, bf16[384,512]{1,0:T(8,128)(2,1)S(1)}) custom-call(bf16[1536,1536]{1,0:T(8,128)(2,1)} %pw_ref.9, bf16[1536,512]{1,0:T(8,128)(2,1)S(1)} %get-tuple-element.32.cot_ref, bf16[384,2048]{1,0:T(8,128)(2,1)} %x_ref.7), custom_call_target="tpu_custom_call" | custom-call | tf_op jit(solution)/shard_map/upstream/pallas_call | solution.py:19
  11.3 0.7 %collective-permute-start = (bf16[384,512]{1,0:T(8,128)(2,1)S(1)}, bf16[384,512]{1,0:T(8,128)(2,1)S(1)}, u32[]{:S(2)}, u32[]{:S(2)}) collective-permute-start(bf16[384,512]{1,0:T(8,128)(2,1)S(1)} %get-tuple-element.33), channel_id=1, source_target_pairs={{4,8},{12,16},{20,24},{8,4},{16,12},{24,20},{5,9},{13,17},{21,25},... | collective-permute-start | bytes 1179656 | tf_op jit(solution)/shard_map/ppermute | solution.py:370
  12.0 0.9 %collective-permute-start.3 = (bf16[384,512]{1,0:T(8,128)(2,1)S(1)}, bf16[384,512]{1,0:T(8,128)(2,1)S(1)}, u32[]{:S(2)}, u32[]{:S(2)}) collective-permute-start(bf16[384,512]{1,0:T(8,128)(2,1)S(1)} %get-tuple-element.49), channel_id=1, source_target_pairs={{0,2},{1,3},{2,0},{3,1},{4,6},{5,7},{6,4},{7,5},{8,10},{9,11},{10,... | collective-permute-start | bytes 1179656 | tf_op jit(solution)/shard_map/ppermute | solution.py:364
  12.9 0.3 collective-permute-start.4
  13.2 3.3 %interior.1 = (bf16[384,512]{1,0:T(8,128)(2,1)S(1)}, bf16[384,512]{1,0:T(8,128)(2,1)S(1)}, bf16[384,512]{1,0:T(8,128)(2,1)S(1)}, bf16[384,512]{1,0:T(8,128)(2,1)...) custom-call(bf16[384,2048]{1,0:T(8,128)(2,1)} %x_ref.7, ...), custom_call_target="tpu_custom_call" | custom-call | tf_op jit(solution)/shard_map/interior/pallas_call | solution.py:19
  16.6 0.0 collective-permute-done.2.refs_1_
  16.6 1.7 %collective-permute-done.1.refs_0_.rest_0_ = bf16[384,512]{1,0:T(8,128)(2,1)S(1)} collective-permute-done((bf16[384,512]{1,0:T(8,128)(2,1)S(1)}, bf16[384,512]{1,0:T(8,128)(2,1)S(1)}, u32[]{:S(2)}, u32[]{:S(2)}) %collective-permute-start.1) | collective-permute-done | bytes 393248 | tf_op jit(solution)/shard_map/ppermute | solution.py:364
  18.3 0.8 %near_end.1 = (bf16[384,512]{1,0:T(8,128)(2,1)S(1)}, bf16[384,512]{1,0:T(8,128)(2,1)S(1)}, bf16[384,512]{1,0:T(8,128)(2,1)S(1)}, bf16[384,512]{1,0:T(8,128)(2,1)...) custom-call(bf16[384,512]{1,0:T(8,128)(2,1)S(1)} %collective-permute, ...), custom_call_target="tpu_custom_call", output_to_operand_aliasing={{0}: (3, {}), {1}: (4, {}), {2}: (5, {}), {3}: (6, {}), {4}... | custom-call | tf_op jit(solution)/shard_map/near_end/pallas_call | solution.py:19
  19.0 0.0 collective-permute-done.refs_0_
  19.0 0.0 slice-start
  19.1 0.0 slice-start.1
  19.1 0.8 %far_end.1 = (bf16[384,512]{1,0:T(8,128)(2,1)S(1)}, bf16[384,512]{1,0:T(8,128)(2,1)S(1)}, bf16[384,512]{1,0:T(8,128)(2,1)S(1)}, bf16[384,512]{1,0:T(8,128)(2,1)S...) custom-call(bf16[384,512]{1,0:T(8,128)(2,1)S(1)} %collective-permute, ...), custom_call_target="tpu_custom_call", output_to_operand_aliasing={{0}: (2, {}), {1}: (3, {}), {2}: (4, {}), {3}: (5, {}), {4}... | custom-call | tf_op jit(solution)/shard_map/far_end/pallas_call | solution.py:19
  19.8 0.2 collective-permute-start.7
  20.0 1.6 %collective-permute-start.8 = (bf16[384,512]{1,0:T(8,128)(2,1)S(1)}, bf16[384,512]{1,0:T(8,128)(2,1)S(1)}, u32[]{:S(2)}, u32[]{:S(2)}) collective-permute-start(bf16[384,512]{1,0:T(8,128)(2,1)S(1)} %get-tuple-element.56), channel_id=1, source_target_pairs={{0,3},{1,2},{2,1},{3,0},{4,7},{5,6},{6,5},{7,4},{8,11},{9,10},{10,... | collective-permute-start | bytes 1179656 | tf_op jit(solution)/shard_map/ppermute | solution.py:364
  21.6 5.2 %collective-permute-done.3.rest_1_ = bf16[384,512]{1,0:T(8,128)(2,1)S(1)} collective-permute-done((bf16[384,512]{1,0:T(8,128)(2,1)S(1)}, bf16[384,512]{1,0:T(8,128)(2,1)S(1)}, u32[]{:S(2)}, u32[]{:S(2)}) %collective-permute-start.3) | collective-permute-done | bytes 393248 | tf_op jit(solution)/shard_map/ppermute | solution.py:364
  26.9 0.0 collective-permute-done.4.rest_2_
  26.9 0.6 %grad_conv.1 = (bf16[384,2048]{1,0:T(8,128)(2,1)S(1)}, bf16[384,512]{1,0:T(8,128)(2,1)S(1)}, bf16[384,512]{1,0:T(8,128)(2,1)S(1)}) custom-call(f32[384,2048]{1,0:T(8,128)S(1)} %get-tuple-element.48.slope_ref, bf16[384,512]{1,0:T(8,128)(2,1)S(1)} %collective-permute-done.1.refs_0_.rest_0_, bf16[384,512]{1,0:T(8,128)(2,1)S(1)} %collective-permute-done.3.rest_1_, ...), custom_call_target="tpu_custom_call" | custom-call | tf_op jit(solution)/shard_map/grad_conv/pallas_call | solution.py:19
  27.5 1.2 %collective-permute-start.5 = (bf16[384,512]{1,0:T(8,128)(2,1)S(1)}, bf16[384,512]{1,0:T(8,128)(2,1)S(1)}, u32[]{:S(2)}, u32[]{:S(2)}) collective-permute-start(bf16[384,512]{1,0:T(8,128)(2,1)S(1)} %get-tuple-element.52), channel_id=1, source_target_pairs={{0,4},{8,12},{16,20},{24,28},{4,0},{12,8},{20,16},{28,24},{1,5},{9... | collective-permute-start | bytes 1179656 | tf_op jit(solution)/shard_map/ppermute | solution.py:370
  28.7 0.9 %collective-permute-start.6 = (bf16[384,512]{1,0:T(8,128)(2,1)S(1)}, bf16[384,512]{1,0:T(8,128)(2,1)S(1)}, u32[]{:S(2)}, u32[]{:S(2)}) collective-permute-start(bf16[384,512]{1,0:T(8,128)(2,1)S(1)} %get-tuple-element.53), channel_id=1, source_target_pairs={{4,8},{12,16},{20,24},{8,4},{16,12},{24,20},{5,9},{13,17},{21,25},... | collective-permute-start | bytes 1179656 | tf_op jit(solution)/shard_map/ppermute | solution.py:370
  29.5 1.6 %collective-permute-start.9 = (bf16[384,512]{1,0:T(8,128)(2,1)S(1)}, bf16[384,512]{1,0:T(8,128)(2,1)S(1)}, u32[]{:S(2)}, u32[]{:S(2)}) collective-permute-start(bf16[384,512]{1,0:T(8,128)(2,1)S(1)} %get-tuple-element.57), channel_id=1, source_target_pairs={{0,2},{1,3},{2,0},{3,1},{4,6},{5,7},{6,4},{7,5},{8,10},{9,11},{10,... | collective-permute-start | bytes 1179656 | tf_op jit(solution)/shard_map/ppermute | solution.py:364
  31.2 1.7 %back_interior.1 = (bf16[384,2048]{1,0:T(8,128)(2,1)}, f32[384,1024]{1,0:T(8,128)S(1)}) custom-call(bf16[384,2048]{1,0:T(8,128)(2,1)S(1)} %get-tuple-element.58.grad_ref, bf16[3,384,96]{2,1,0:T(8,128)(2,1)S(1)} %get-tuple-element.59.turned_ref.rest_2_), custom_call_target="tpu_custom_call" | custom-call | tf_op jit(solution)/shard_map/back_interior/pallas_call | solution.py:19
  32.8 2.3 %collective-permute-done.8.rest_0_ = bf16[384,512]{1,0:T(8,128)(2,1)S(1)} collective-permute-done((bf16[384,512]{1,0:T(8,128)(2,1)S(1)}, bf16[384,512]{1,0:T(8,128)(2,1)S(1)}, u32[]{:S(2)}, u32[]{:S(2)}) %collective-permute-start.8) | collective-permute-done | bytes 393248 | tf_op jit(solution)/shard_map/ppermute | solution.py:364
  35.1 1.0 %early_mix.1.rest_2_ = f32[1536,512]{1,0:T(8,128)S(1)} custom-call(bf16[1536,1536]{1,0:T(8,128)(2,1)S(1)} %bitcast.2, bf16[384,512]{1,0:T(8,128)(2,1)S(1)} %collective-permute-done.8.rest_0_), custom_call_target="tpu_custom_call" | custom-call | tf_op jit(solution)/shard_map/early_mix/pallas_call | solution.py:19
  36.1 1.8 %half_mix.1.sum_ref = f32[1536,512]{1,0:T(8,128)S(1)} custom-call(bf16[1536,1536]{1,0:T(8,128)(2,1)S(1)} %bitcast.2, bf16[384,512]{1,0:T(8,128)(2,1)S(1)} %collective-permute-done.7.rest_0_, bf16[384,512]{1,0:T(8,128)(2,1)S(1)} %get-tuple-element.55.rest_1_, f32[1536,512]{1,0:T(8,128)S(1)} %early_mix.1.rest_2_), custom_call_target="tpu_custom_call", output_to_operand_aliasing={{}: (3, {})} | custom-call | tf_op jit(solution)/shard_map/half_mix/pallas_call | solution.py:19
  37.9 7.7 %collective-permute-done.5.near_ref = bf16[384,512]{1,0:T(8,128)(2,1)S(1)} collective-permute-done((bf16[384,512]{1,0:T(8,128)(2,1)S(1)}, bf16[384,512]{1,0:T(8,128)(2,1)S(1)}, u32[]{:S(2)}, u32[]{:S(2)}) %collective-permute-start.5) | collective-permute-done | bytes 393248 | tf_op jit(solution)/shard_map/ppermute | solution.py:370
  45.6 0.0 collective-permute-done.6.far_ref
  45.6 0.0 collective-permute-done.9.rest_0_
  45.6 2.1 %tail.1 = (bf16[1536,512]{1,0:T(8,128)(2,1)}, bf16[384,2048]{1,0:T(8,128)(2,1)}) custom-call(bf16[384,512]{1,0:T(8,128)(2,1)S(1)} %collective-permute-done.5.near_ref, bf16[384,512]{1,0:T(8,128)(2,1)S(1)} %collective-permute-done.6.far_ref, bf16[1536,1536]{1,0:T(8,128)(2,1)S(1)} %bitcast.2, ...), custom_call_target="tpu_custom_call", output_to_operand_aliasing={{1}: (7, {})} | custom-call | tf_op jit(solution)/shard_map/tail/pallas_call | solution.py:19
  (4 shorter events, 0.0 us)
Async XLA Ops:
  1.7 14.9 %collective-permute-start.2 = (bf16[384,512]{1,0:T(8,128)(2,1)S(1)}, bf16[384,512]{1,0:T(8,128)(2,1)S(1)}, u32[]{:S(2)}, u32[]{:S(2)}) collective-permute-start(bf16[384,512]{1,0:T(8,128)(2,1)S(1)} %near_source.1), channel_id=1, source_target_pairs={{0,4},{8,12},{16,20},{24,28},{4,0},{12,8},{20,16},{28,24},{1,5},{9... | collective-permute-start | bytes 1179656 | tf_op jit(solution)/shard_map/ppermute | solution.py:370
  6.9 11.4 %collective-permute-start.1 = (bf16[384,512]{1,0:T(8,128)(2,1)S(1)}, bf16[384,512]{1,0:T(8,128)(2,1)S(1)}, u32[]{:S(2)}, u32[]{:S(2)}) collective-permute-start(bf16[384,512]{1,0:T(8,128)(2,1)S(1)} %get-tuple-element.35), channel_id=1, source_target_pairs={{0,3},{1,2},{2,1},{3,0},{4,7},{5,6},{6,5},{7,4},{8,11},{9,10},{10,... | collective-permute-start | bytes 1179656 | tf_op jit(solution)/shard_map/ppermute | solution.py:364
  11.3 7.8 %collective-permute-start = (bf16[384,512]{1,0:T(8,128)(2,1)S(1)}, bf16[384,512]{1,0:T(8,128)(2,1)S(1)}, u32[]{:S(2)}, u32[]{:S(2)}) collective-permute-start(bf16[384,512]{1,0:T(8,128)(2,1)S(1)} %get-tuple-element.33), channel_id=1, source_target_pairs={{4,8},{12,16},{20,24},{8,4},{16,12},{24,20},{5,9},{13,17},{21,25},... | collective-permute-start | bytes 1179656 | tf_op jit(solution)/shard_map/ppermute | solution.py:370
  12.0 14.9 %collective-permute-start.3 = (bf16[384,512]{1,0:T(8,128)(2,1)S(1)}, bf16[384,512]{1,0:T(8,128)(2,1)S(1)}, u32[]{:S(2)}, u32[]{:S(2)}) collective-permute-start(bf16[384,512]{1,0:T(8,128)(2,1)S(1)} %get-tuple-element.49), channel_id=1, source_target_pairs={{0,2},{1,3},{2,0},{3,1},{4,6},{5,7},{6,4},{7,5},{8,10},{9,11},{10,... | collective-permute-start | bytes 1179656 | tf_op jit(solution)/shard_map/ppermute | solution.py:364
  12.9 14.0 %collective-permute-start.4 = (bf16[384,512]{1,0:T(8,128)(2,1)S(1)}, bf16[384,512]{1,0:T(8,128)(2,1)S(1)}, u32[]{:S(2)}, u32[]{:S(2)}) collective-permute-start(bf16[384,512]{1,0:T(8,128)(2,1)S(1)} %get-tuple-element.50), channel_id=1, source_target_pairs={{0,1},{1,0},{2,3},{3,2},{4,5},{5,4},{6,7},{7,6},{8,9},{9,8},{10,11... | collective-permute-start | bytes 1179656 | tf_op jit(solution)/shard_map/ppermute | solution.py:364
  19.0 16.1 %slice-start = ((s8[4718592]{0:T(1024)(128)(4,1)}), s8[4194304]{0:T(1024)(128)(4,1)S(1)}, s32[]{:S(2)}) async-start(s8[4718592]{0:T(1024)(128)(4,1)} %bitcast.1), calls=%async_computation | async-start | bytes 8388608
  19.1 16.1 %slice-start.1 = ((s8[4718592]{0:T(1024)(128)(4,1)}), s8[524288]{0:T(1024)(128)(4,1)S(1)}, s32[]{:S(2)}) async-start(s8[4718592]{0:T(1024)(128)(4,1)} %bitcast.1), calls=%async_computation.1 | async-start | bytes 1048576
  19.8 16.3 %collective-permute-start.7 = (bf16[384,512]{1,0:T(8,128)(2,1)S(1)}, bf16[384,512]{1,0:T(8,128)(2,1)S(1)}, u32[]{:S(2)}, u32[]{:S(2)}) collective-permute-start(bf16[384,512]{1,0:T(8,128)(2,1)S(1)} %get-tuple-element.54), channel_id=1, source_target_pairs={{0,1},{1,0},{2,3},{3,2},{4,5},{5,4},{6,7},{7,6},{8,9},{9,8},{10,11... | collective-permute-start | bytes 1179656 | tf_op jit(solution)/shard_map/ppermute | solution.py:364
  20.0 15.1 %collective-permute-start.8 = (bf16[384,512]{1,0:T(8,128)(2,1)S(1)}, bf16[384,512]{1,0:T(8,128)(2,1)S(1)}, u32[]{:S(2)}, u32[]{:S(2)}) collective-permute-start(bf16[384,512]{1,0:T(8,128)(2,1)S(1)} %get-tuple-element.56), channel_id=1, source_target_pairs={{0,3},{1,2},{2,1},{3,0},{4,7},{5,6},{6,5},{7,4},{8,11},{9,10},{10,... | collective-permute-start | bytes 1179656 | tf_op jit(solution)/shard_map/ppermute | solution.py:364
  27.5 18.2 %collective-permute-start.5 = (bf16[384,512]{1,0:T(8,128)(2,1)S(1)}, bf16[384,512]{1,0:T(8,128)(2,1)S(1)}, u32[]{:S(2)}, u32[]{:S(2)}) collective-permute-start(bf16[384,512]{1,0:T(8,128)(2,1)S(1)} %get-tuple-element.52), channel_id=1, source_target_pairs={{0,4},{8,12},{16,20},{24,28},{4,0},{12,8},{20,16},{28,24},{1,5},{9... | collective-permute-start | bytes 1179656 | tf_op jit(solution)/shard_map/ppermute | solution.py:370
  28.7 17.0 %collective-permute-start.6 = (bf16[384,512]{1,0:T(8,128)(2,1)S(1)}, bf16[384,512]{1,0:T(8,128)(2,1)S(1)}, u32[]{:S(2)}, u32[]{:S(2)}) collective-permute-start(bf16[384,512]{1,0:T(8,128)(2,1)S(1)} %get-tuple-element.53), channel_id=1, source_target_pairs={{4,8},{12,16},{20,24},{8,4},{16,12},{24,20},{5,9},{13,17},{21,25},... | collective-permute-start | bytes 1179656 | tf_op jit(solution)/shard_map/ppermute | solution.py:370
  29.5 16.1 %collective-permute-start.9 = (bf16[384,512]{1,0:T(8,128)(2,1)S(1)}, bf16[384,512]{1,0:T(8,128)(2,1)S(1)}, u32[]{:S(2)}, u32[]{:S(2)}) collective-permute-start(bf16[384,512]{1,0:T(8,128)(2,1)S(1)} %get-tuple-element.57), channel_id=1, source_target_pairs={{0,2},{1,3},{2,0},{3,1},{4,6},{5,7},{6,4},{7,5},{8,10},{9,11},{10,... | collective-permute-start | bytes 1179656 | tf_op jit(solution)/shard_map/ppermute | solution.py:364

commit v13 on v12

--- a/solution.py
+++ b/solution.py
@@ -72,7 +72,7 @@
     copy.wait()
 
 
-def upstream_kernel(order, channels, first, pw_ref, cot_ref, x_ref, *rest):
+def upstream_kernel(order, channels, first, with_far, pw_ref, cot_ref, x_ref, *rest):
     count = len(order)
     piece_refs, rest = rest[:count], rest[count:]
     columns_ref, total_ref, sems = rest[-3:]
@@ -96,7 +96,7 @@
         for copy in copies:
             copy.start()
         blocks.append((rows, copies))
-    if not first:
+    if with_far:
         end = end_copy(x_ref, rest[-4], odd_place(), sems.at[0, count + 1])
         end.start()
     for step, (rows, copies) in enumerate(blocks):
@@ -111,7 +111,7 @@
                 total_ref[held, :] = part
             else:
                 piece_refs[place][...] = part.astype(BF16)
-    if not first:
+    if with_far:
         end.wait()
 
 
@@ -124,15 +124,15 @@
     )
 
 
-def upstream(pw_weight, cotangent, inputs, order, first):
+def upstream(pw_weight, cotangent, inputs, order, first=False, with_far=False):
     channels = inputs.shape[0]
     total, width = cotangent.shape
     count = len(order)
     outs = [((channels, width), BF16, True)] * count
     outs += [(cotangent.shape, BF16, True)] * first
-    outs += [((channels, DILATION_STEP), BF16, True)] * (not first)
+    outs += [((channels, DILATION_STEP), BF16, True)] * with_far
     results = kernel_call(
-        "upstream", functools.partial(upstream_kernel, order, channels, first),
+        "upstream", functools.partial(upstream_kernel, order, channels, first, with_far),
         [(columns_of(pw_weight, channels, order), False), (cotangent, not first), (inputs, False)], outs,
         [
             pltpu.VMEM((total, count * channels), BF16), pltpu.VMEM((count * channels, width), F32),
@@ -384,16 +384,18 @@
         "near_source", near_source_kernel, [(inputs, False)], [((channels, halo), BF16, True)], [DMA]
     )
     near = swap(near, 0)
-    pieces, cot_in = upstream(pw_weight, cotangent, inputs, first, True)
+    pieces, cot_in = upstream(pw_weight, cotangent, inputs, first, first=True)
     ups = {k: exchange(p, k) for k, p in zip(first, pieces)}
-    pieces, far = upstream(pw_weight, cot_in, inputs, second + rest, False)
-    ups.update({k: exchange(p, k) for k, p in zip(second + rest, pieces)})
+    pieces, far = upstream(pw_weight, cot_in, inputs, second, with_far=True)
     far = swap(far, 1)
+    ups.update({k: exchange(p, k) for k, p in zip(second, pieces)})
+    (pieces,) = upstream(pw_weight, cot_in, inputs, rest)
+    ups.update({k: exchange(p, k) for k, p in zip(rest, pieces)})
 
     active, slope, wide, plain, turned = interior(inputs, weight, n)
     active, slope, wide = one_end(True, near, plain, active, slope, wide, [ups[first[0]]])
     active, slope, wide = one_end(False, far, plain, active, slope, wide, [])
-    grad, near_grad, far_grad = grad_conv(slope, order, ups)
+    grad, near_grad, far_grad = grad_conv(slope, rest + second + first, ups)
     active = {k: exchange(active[k], k) for k in order}
     near_grad, far_grad = swap(near_grad, 0), swap(far_grad, 1)
 

time: 48.8 us -> 48.7 us (level); the launches traced: 47.9 us -> 48.4 us
  waiting for transfers between devices: 16.9 us -> 15.6 us
  Pallas kernels: 18.9 us -> 20.1 us
  starting transfers between devices: 11.2 us -> 11.8 us
    ppermute x6, waiting for transfers between devices: 9.22 us -> 7.39 us  [exchange(): lax.ppermute(piece, 'ch', [(i, i ^ k) for i in range(lax.axis_size('ch'))])]
    ppermute x4, starting transfers between devices: 5.74 us -> 7.37 us  [swap(): return lax.ppermute(values, 'ctx', pairs + [(b, a) for a, b in pairs])]
    pallas_call x11 -> x12, Pallas kernels: 18.9 us -> 20.1 us  [kernel_call(): pl.pallas_call(kernel, in_specs=[INSIDE if held else ANY for _, held in o...]
    ppermute x6, starting transfers between devices: 5.43 us -> 4.4 us  [exchange(): lax.ppermute(piece, 'ch', [(i, i ^ k) for i in range(lax.axis_size('ch'))])]
    ppermute x4, waiting for transfers between devices: 7.68 us -> 8.22 us  [swap(): return lax.ppermute(values, 'ctx', pairs + [(b, a) for a, b in pairs])]
  transfers between devices with their start and end apart: 10 -> 10, of which waited for: 4 -> 4; matrix products, arithmetic and copies ran while one was open for 0% -> 0% of each run, Pallas kernels for 33% -> 35%
where the time goes in v13:
time: 48.7 us; the launch traced here: 48.4 us
  Pallas kernels  20.1 us (41%)
  waiting for transfers between devices  15.6 us (32%)
  starting transfers between devices  11.8 us (24%)
  between operations  0.94 us (2%)
    pallas_call x12, Pallas kernels, kernel_call(): pl.pallas_call(kernel, in_specs=[INSIDE if held else ANY for _, held in o...  20.1 us
    ppermute x4, waiting for transfers between devices, swap(): return lax.ppermute(values, 'ctx', pairs + [(b, a) for a, b in pairs])  8.22 us
    ppermute x6, waiting for transfers between devices, exchange(): lax.ppermute(piece, 'ch', [(i, i ^ k) for i in range(lax.axis_size('ch'))])  7.39 us
    ppermute x4, starting transfers between devices, swap(): return lax.ppermute(values, 'ctx', pairs + [(b, a) for a, b in pairs])  7.37 us
    ppermute x6, starting transfers between devices, exchange(): lax.ppermute(piece, 'ch', [(i, i ^ k) for i in range(lax.axis_size('ch'))])  4.4 us
  transfers between devices with their start and end apart: 10, of which 4 were waited for; matrix products, arithmetic and copies ran while one was open for 0% of the time, Pallas kernels for 35%

profile of v13, /device:TPU:0, one launch (start us, length us, event | category | flops | bytes accessed | tf_op | source)
XLA Modules:
  0.0 48.4 jit_solution(1915983202462467038)
XLA Ops:
  0.6 1.0 %near_source.1 = bf16[384,512]{1,0:T(8,128)(2,1)S(1)} custom-call(bf16[384,2048]{1,0:T(8,128)(2,1)} %x_ref.9), custom_call_target="tpu_custom_call" | custom-call | tf_op jit(solution)/shard_map/near_source/pallas_call | solution.py:19
  1.7 3.0 %collective-permute-start.2 = (bf16[384,512]{1,0:T(8,128)(2,1)S(1)}, bf16[384,512]{1,0:T(8,128)(2,1)S(1)}, u32[]{:S(2)}, u32[]{:S(2)}) collective-permute-start(bf16[384,512]{1,0:T(8,128)(2,1)S(1)} %near_source.1), channel_id=1, source_target_pairs={{0,4},{8,12},{16,20},{24,28},{4,0},{12,8},{20,16},{28,24},{1,5},{9... | collective-permute-start | bytes 1179656 | tf_op jit(solution)/shard_map/ppermute | solution.py:370
  4.7 2.2 %upstream.3 = (bf16[384,512]{1,0:T(8,128)(2,1)S(1)}, bf16[1536,512]{1,0:T(8,128)(2,1)S(1)}) custom-call(bf16[1536,1536]{1,0:T(8,128)(2,1)} %pw_ref.11, bf16[1536,512]{1,0:T(8,128)(2,1)} %cot_ref.1, bf16[384,2048]{1,0:T(8,128)(2,1)} %x_ref.9), custom_call_target="tpu_custom_call" | custom-call | tf_op jit(solution)/shard_map/upstream/pallas_call | solution.py:19
  6.9 0.7 %collective-permute-start.1 = (bf16[384,512]{1,0:T(8,128)(2,1)S(1)}, bf16[384,512]{1,0:T(8,128)(2,1)S(1)}, u32[]{:S(2)}, u32[]{:S(2)}) collective-permute-start(bf16[384,512]{1,0:T(8,128)(2,1)S(1)} %get-tuple-element.35), channel_id=1, source_target_pairs={{0,3},{1,2},{2,1},{3,0},{4,7},{5,6},{6,5},{7,4},{8,11},{9,10},{10,... | collective-permute-start | bytes 1179656 | tf_op jit(solution)/shard_map/ppermute | solution.py:364
  7.6 2.0 %upstream.4 = (bf16[384,512]{1,0:T(8,128)(2,1)S(1)}, bf16[384,512]{1,0:T(8,128)(2,1)S(1)}) custom-call(bf16[1536,1536]{1,0:T(8,128)(2,1)} %pw_ref.11, bf16[1536,512]{1,0:T(8,128)(2,1)S(1)} %get-tuple-element.32.cot_ref, bf16[384,2048]{1,0:T(8,128)(2,1)} %x_ref.9), custom_call_target="tpu_custom_call" | custom-call | tf_op jit(solution)/shard_map/upstream/pallas_call | solution.py:19
  9.7 0.7 %collective-permute-start = (bf16[384,512]{1,0:T(8,128)(2,1)S(1)}, bf16[384,512]{1,0:T(8,128)(2,1)S(1)}, u32[]{:S(2)}, u32[]{:S(2)}) collective-permute-start(bf16[384,512]{1,0:T(8,128)(2,1)S(1)} %get-tuple-element.33), channel_id=1, source_target_pairs={{4,8},{12,16},{20,24},{8,4},{16,12},{24,20},{5,9},{13,17},{21,25},... | collective-permute-start | bytes 1179656 | tf_op jit(solution)/shard_map/ppermute | solution.py:370
  10.4 2.8 %upstream.5 = (bf16[384,512]{1,0:T(8,128)(2,1)S(1)}, bf16[384,512]{1,0:T(8,128)(2,1)S(1)}) custom-call(bf16[1536,1536]{1,0:T(8,128)(2,1)} %pw_ref.11, bf16[1536,512]{1,0:T(8,128)(2,1)S(1)} %get-tuple-element.32.cot_ref, bf16[384,2048]{1,0:T(8,128)(2,1)} %x_ref.9), custom_call_target="tpu_custom_call" | custom-call | tf_op jit(solution)/shard_map/upstream/pallas_call | solution.py:19
  13.2 1.0 %collective-permute-start.3 = (bf16[384,512]{1,0:T(8,128)(2,1)S(1)}, bf16[384,512]{1,0:T(8,128)(2,1)S(1)}, u32[]{:S(2)}, u32[]{:S(2)}) collective-permute-start(bf16[384,512]{1,0:T(8,128)(2,1)S(1)} %get-tuple-element.49), channel_id=1, source_target_pairs={{0,1},{1,0},{2,3},{3,2},{4,5},{5,4},{6,7},{7,6},{8,9},{9,8},{10,11... | collective-permute-start | bytes 1179656 | tf_op jit(solution)/shard_map/ppermute | solution.py:364
  14.2 0.5 %collective-permute-start.4 = (bf16[384,512]{1,0:T(8,128)(2,1)S(1)}, bf16[384,512]{1,0:T(8,128)(2,1)S(1)}, u32[]{:S(2)}, u32[]{:S(2)}) collective-permute-start(bf16[384,512]{1,0:T(8,128)(2,1)S(1)} %get-tuple-element.51), channel_id=1, source_target_pairs={{0,2},{1,3},{2,0},{3,1},{4,6},{5,7},{6,4},{7,5},{8,10},{9,11},{10,... | collective-permute-start | bytes 1179656 | tf_op jit(solution)/shard_map/ppermute | solution.py:364
  14.7 3.3 %interior.1 = (bf16[384,512]{1,0:T(8,128)(2,1)S(1)}, bf16[384,512]{1,0:T(8,128)(2,1)S(1)}, bf16[384,512]{1,0:T(8,128)(2,1)S(1)}, bf16[384,512]{1,0:T(8,128)(2,1)...) custom-call(bf16[384,2048]{1,0:T(8,128)(2,1)} %x_ref.9, ...), custom_call_target="tpu_custom_call" | custom-call | tf_op jit(solution)/shard_map/interior/pallas_call | solution.py:19
  18.1 0.2 collective-permute-done.1.refs_0_.rest_3_
  18.3 0.8 %near_end.1 = (bf16[384,512]{1,0:T(8,128)(2,1)S(1)}, bf16[384,512]{1,0:T(8,128)(2,1)S(1)}, bf16[384,512]{1,0:T(8,128)(2,1)S(1)}, bf16[384,512]{1,0:T(8,128)(2,1)...) custom-call(bf16[384,512]{1,0:T(8,128)(2,1)S(1)} %collective-permute, ...), custom_call_target="tpu_custom_call", output_to_operand_aliasing={{0}: (3, {}), {1}: (4, {}), {2}: (5, {}), {3}: (6, {}), {4}... | custom-call | tf_op jit(solution)/shard_map/near_end/pallas_call | solution.py:19
  19.0 0.0 collective-permute-done.refs_0_
  19.0 0.0 slice-start
  19.1 0.0 slice-start.1
  19.1 0.8 %far_end.1 = (bf16[384,512]{1,0:T(8,128)(2,1)S(1)}, bf16[384,512]{1,0:T(8,128)(2,1)S(1)}, bf16[384,512]{1,0:T(8,128)(2,1)S(1)}, bf16[384,512]{1,0:T(8,128)(2,1)S...) custom-call(bf16[384,512]{1,0:T(8,128)(2,1)S(1)} %collective-permute, ...), custom_call_target="tpu_custom_call", output_to_operand_aliasing={{0}: (2, {}), {1}: (3, {}), {2}: (4, {}), {3}: (5, {}), {4}... | custom-call | tf_op jit(solution)/shard_map/far_end/pallas_call | solution.py:19
  19.8 0.2 collective-permute-start.7
  20.0 1.6 %collective-permute-start.8 = (bf16[384,512]{1,0:T(8,128)(2,1)S(1)}, bf16[384,512]{1,0:T(8,128)(2,1)S(1)}, u32[]{:S(2)}, u32[]{:S(2)}) collective-permute-start(bf16[384,512]{1,0:T(8,128)(2,1)S(1)} %get-tuple-element.56), channel_id=1, source_target_pairs={{0,3},{1,2},{2,1},{3,0},{4,7},{5,6},{6,5},{7,4},{8,11},{9,10},{10,... | collective-permute-start | bytes 1179656 | tf_op jit(solution)/shard_map/ppermute | solution.py:364
  21.6 0.0 collective-permute-done.3.rest_0_
  21.6 5.2 %collective-permute-done.4.rest_2_ = bf16[384,512]{1,0:T(8,128)(2,1)S(1)} collective-permute-done((bf16[384,512]{1,0:T(8,128)(2,1)S(1)}, bf16[384,512]{1,0:T(8,128)(2,1)S(1)}, u32[]{:S(2)}, u32[]{:S(2)}) %collective-permute-start.4) | collective-permute-done | bytes 393248 | tf_op jit(solution)/shard_map/ppermute | solution.py:364
  26.9 0.6 %grad_conv.1 = (bf16[384,2048]{1,0:T(8,128)(2,1)S(1)}, bf16[384,512]{1,0:T(8,128)(2,1)S(1)}, bf16[384,512]{1,0:T(8,128)(2,1)S(1)}) custom-call(f32[384,2048]{1,0:T(8,128)S(1)} %get-tuple-element.48.slope_ref, bf16[384,512]{1,0:T(8,128)(2,1)S(1)} %collective-permute-done.3.rest_0_, bf16[384,512]{1,0:T(8,128)(2,1)S(1)} %get-tuple-element.50.rest_1_, ...), custom_call_target="tpu_custom_call" | custom-call | tf_op jit(solution)/shard_map/grad_conv/pallas_call | solution.py:19
  27.5 2.8 %collective-permute-start.5 = (bf16[384,512]{1,0:T(8,128)(2,1)S(1)}, bf16[384,512]{1,0:T(8,128)(2,1)S(1)}, u32[]{:S(2)}, u32[]{:S(2)}) collective-permute-start(bf16[384,512]{1,0:T(8,128)(2,1)S(1)} %get-tuple-element.52), channel_id=1, source_target_pairs={{0,4},{8,12},{16,20},{24,28},{4,0},{12,8},{20,16},{28,24},{1,5},{9... | collective-permute-start | bytes 1179656 | tf_op jit(solution)/shard_map/ppermute | solution.py:370
  30.3 0.9 %collective-permute-start.6 = (bf16[384,512]{1,0:T(8,128)(2,1)S(1)}, bf16[384,512]{1,0:T(8,128)(2,1)S(1)}, u32[]{:S(2)}, u32[]{:S(2)}) collective-permute-start(bf16[384,512]{1,0:T(8,128)(2,1)S(1)} %get-tuple-element.53), channel_id=1, source_target_pairs={{4,8},{12,16},{20,24},{8,4},{16,12},{24,20},{5,9},{13,17},{21,25},... | collective-permute-start | bytes 1179656 | tf_op jit(solution)/shard_map/ppermute | solution.py:370
  31.2 0.3 collective-permute-start.9
  31.5 1.7 %back_interior.1 = (bf16[384,2048]{1,0:T(8,128)(2,1)}, f32[384,1024]{1,0:T(8,128)S(1)}) custom-call(bf16[384,2048]{1,0:T(8,128)(2,1)S(1)} %get-tuple-element.58.grad_ref, bf16[3,384,96]{2,1,0:T(8,128)(2,1)S(1)} %get-tuple-element.59.turned_ref.rest_2_), custom_call_target="tpu_custom_call" | custom-call | tf_op jit(solution)/shard_map/back_interior/pallas_call | solution.py:19
  33.2 2.0 %collective-permute-done.8.rest_0_ = bf16[384,512]{1,0:T(8,128)(2,1)S(1)} collective-permute-done((bf16[384,512]{1,0:T(8,128)(2,1)S(1)}, bf16[384,512]{1,0:T(8,128)(2,1)S(1)}, u32[]{:S(2)}, u32[]{:S(2)}) %collective-permute-start.8) | collective-permute-done | bytes 393248 | tf_op jit(solution)/shard_map/ppermute | solution.py:364
  35.1 1.0 %early_mix.1.rest_2_ = f32[1536,512]{1,0:T(8,128)S(1)} custom-call(bf16[1536,1536]{1,0:T(8,128)(2,1)S(1)} %bitcast.2, bf16[384,512]{1,0:T(8,128)(2,1)S(1)} %collective-permute-done.8.rest_0_), custom_call_target="tpu_custom_call" | custom-call | tf_op jit(solution)/shard_map/early_mix/pallas_call | solution.py:19
  36.1 0.0 collective-permute-done.7.rest_0_
  36.1 1.8 %half_mix.1.sum_ref = f32[1536,512]{1,0:T(8,128)S(1)} custom-call(bf16[1536,1536]{1,0:T(8,128)(2,1)S(1)} %bitcast.2, bf16[384,512]{1,0:T(8,128)(2,1)S(1)} %collective-permute-done.7.rest_0_, bf16[384,512]{1,0:T(8,128)(2,1)S(1)} %get-tuple-element.55.rest_1_, f32[1536,512]{1,0:T(8,128)S(1)} %early_mix.1.rest_2_), custom_call_target="tpu_custom_call", output_to_operand_aliasing={{}: (3, {})} | custom-call | tf_op jit(solution)/shard_map/half_mix/pallas_call | solution.py:19
  37.9 8.2 %collective-permute-done.5.near_ref = bf16[384,512]{1,0:T(8,128)(2,1)S(1)} collective-permute-done((bf16[384,512]{1,0:T(8,128)(2,1)S(1)}, bf16[384,512]{1,0:T(8,128)(2,1)S(1)}, u32[]{:S(2)}, u32[]{:S(2)}) %collective-permute-start.5) | collective-permute-done | bytes 393248 | tf_op jit(solution)/shard_map/ppermute | solution.py:370
  46.2 0.0 collective-permute-done.6.far_ref
  46.2 2.1 %tail.1 = (bf16[1536,512]{1,0:T(8,128)(2,1)}, bf16[384,2048]{1,0:T(8,128)(2,1)}) custom-call(bf16[384,512]{1,0:T(8,128)(2,1)S(1)} %collective-permute-done.5.near_ref, bf16[384,512]{1,0:T(8,128)(2,1)S(1)} %collective-permute-done.6.far_ref, bf16[1536,1536]{1,0:T(8,128)(2,1)S(1)} %bitcast.2, ...), custom_call_target="tpu_custom_call", output_to_operand_aliasing={{1}: (7, {})} | custom-call | tf_op jit(solution)/shard_map/tail/pallas_call | solution.py:19
  (5 shorter events, 0.0 us)
Async XLA Ops:
  1.7 16.4 %collective-permute-start.2 = (bf16[384,512]{1,0:T(8,128)(2,1)S(1)}, bf16[384,512]{1,0:T(8,128)(2,1)S(1)}, u32[]{:S(2)}, u32[]{:S(2)}) collective-permute-start(bf16[384,512]{1,0:T(8,128)(2,1)S(1)} %near_source.1), channel_id=1, source_target_pairs={{0,4},{8,12},{16,20},{24,28},{4,0},{12,8},{20,16},{28,24},{1,5},{9... | collective-permute-start | bytes 1179656 | tf_op jit(solution)/shard_map/ppermute | solution.py:370
  6.9 11.4 %collective-permute-start.1 = (bf16[384,512]{1,0:T(8,128)(2,1)S(1)}, bf16[384,512]{1,0:T(8,128)(2,1)S(1)}, u32[]{:S(2)}, u32[]{:S(2)}) collective-permute-start(bf16[384,512]{1,0:T(8,128)(2,1)S(1)} %get-tuple-element.35), channel_id=1, source_target_pairs={{0,3},{1,2},{2,1},{3,0},{4,7},{5,6},{6,5},{7,4},{8,11},{9,10},{10,... | collective-permute-start | bytes 1179656 | tf_op jit(solution)/shard_map/ppermute | solution.py:364
  9.7 9.4 %collective-permute-start = (bf16[384,512]{1,0:T(8,128)(2,1)S(1)}, bf16[384,512]{1,0:T(8,128)(2,1)S(1)}, u32[]{:S(2)}, u32[]{:S(2)}) collective-permute-start(bf16[384,512]{1,0:T(8,128)(2,1)S(1)} %get-tuple-element.33), channel_id=1, source_target_pairs={{4,8},{12,16},{20,24},{8,4},{16,12},{24,20},{5,9},{13,17},{21,25},... | collective-permute-start | bytes 1179656 | tf_op jit(solution)/shard_map/ppermute | solution.py:370
  13.2 8.5 %collective-permute-start.3 = (bf16[384,512]{1,0:T(8,128)(2,1)S(1)}, bf16[384,512]{1,0:T(8,128)(2,1)S(1)}, u32[]{:S(2)}, u32[]{:S(2)}) collective-permute-start(bf16[384,512]{1,0:T(8,128)(2,1)S(1)} %get-tuple-element.49), channel_id=1, source_target_pairs={{0,1},{1,0},{2,3},{3,2},{4,5},{5,4},{6,7},{7,6},{8,9},{9,8},{10,11... | collective-permute-start | bytes 1179656 | tf_op jit(solution)/shard_map/ppermute | solution.py:364
  14.2 12.6 %collective-permute-start.4 = (bf16[384,512]{1,0:T(8,128)(2,1)S(1)}, bf16[384,512]{1,0:T(8,128)(2,1)S(1)}, u32[]{:S(2)}, u32[]{:S(2)}) collective-permute-start(bf16[384,512]{1,0:T(8,128)(2,1)S(1)} %get-tuple-element.51), channel_id=1, source_target_pairs={{0,2},{1,3},{2,0},{3,1},{4,6},{5,7},{6,4},{7,5},{8,10},{9,11},{10,... | collective-permute-start | bytes 1179656 | tf_op jit(solution)/shard_map/ppermute | solution.py:364
  19.0 16.1 %slice-start = ((s8[4718592]{0:T(1024)(128)(4,1)}), s8[4194304]{0:T(1024)(128)(4,1)S(1)}, s32[]{:S(2)}) async-start(s8[4718592]{0:T(1024)(128)(4,1)} %bitcast.1), calls=%async_computation | async-start | bytes 8388608
  19.1 16.1 %slice-start.1 = ((s8[4718592]{0:T(1024)(128)(4,1)}), s8[524288]{0:T(1024)(128)(4,1)S(1)}, s32[]{:S(2)}) async-start(s8[4718592]{0:T(1024)(128)(4,1)} %bitcast.1), calls=%async_computation.1 | async-start | bytes 1048576
  19.8 16.3 %collective-permute-start.7 = (bf16[384,512]{1,0:T(8,128)(2,1)S(1)}, bf16[384,512]{1,0:T(8,128)(2,1)S(1)}, u32[]{:S(2)}, u32[]{:S(2)}) collective-permute-start(bf16[384,512]{1,0:T(8,128)(2,1)S(1)} %get-tuple-element.54), channel_id=1, source_target_pairs={{0,1},{1,0},{2,3},{3,2},{4,5},{5,4},{6,7},{7,6},{8,9},{9,8},{10,11... | collective-permute-start | bytes 1179656 | tf_op jit(solution)/shard_map/ppermute | solution.py:364
  20.0 15.1 %collective-permute-start.8 = (bf16[384,512]{1,0:T(8,128)(2,1)S(1)}, bf16[384,512]{1,0:T(8,128)(2,1)S(1)}, u32[]{:S(2)}, u32[]{:S(2)}) collective-permute-start(bf16[384,512]{1,0:T(8,128)(2,1)S(1)} %get-tuple-element.56), channel_id=1, source_target_pairs={{0,3},{1,2},{2,1},{3,0},{4,7},{5,6},{6,5},{7,4},{8,11},{9,10},{10,... | collective-permute-start | bytes 1179656 | tf_op jit(solution)/shard_map/ppermute | solution.py:364
  27.5 18.7 %collective-permute-start.5 = (bf16[384,512]{1,0:T(8,128)(2,1)S(1)}, bf16[384,512]{1,0:T(8,128)(2,1)S(1)}, u32[]{:S(2)}, u32[]{:S(2)}) collective-permute-start(bf16[384,512]{1,0:T(8,128)(2,1)S(1)} %get-tuple-element.52), channel_id=1, source_target_pairs={{0,4},{8,12},{16,20},{24,28},{4,0},{12,8},{20,16},{28,24},{1,5},{9... | collective-permute-start | bytes 1179656 | tf_op jit(solution)/shard_map/ppermute | solution.py:370
  30.3 15.9 %collective-permute-start.6 = (bf16[384,512]{1,0:T(8,128)(2,1)S(1)}, bf16[384,512]{1,0:T(8,128)(2,1)S(1)}, u32[]{:S(2)}, u32[]{:S(2)}) collective-permute-start(bf16[384,512]{1,0:T(8,128)(2,1)S(1)} %get-tuple-element.53), channel_id=1, source_target_pairs={{4,8},{12,16},{20,24},{8,4},{16,12},{24,20},{5,9},{13,17},{21,25},... | collective-permute-start | bytes 1179656 | tf_op jit(solution)/shard_map/ppermute | solution.py:370
  31.2 15.0 %collective-permute-start.9 = (bf16[384,512]{1,0:T(8,128)(2,1)S(1)}, bf16[384,512]{1,0:T(8,128)(2,1)S(1)}, u32[]{:S(2)}, u32[]{:S(2)}) collective-permute-start(bf16[384,512]{1,0:T(8,128)(2,1)S(1)} %get-tuple-element.57), channel_id=1, source_target_pairs={{0,2},{1,3},{2,0},{3,1},{4,6},{5,7},{6,4},{7,5},{8,10},{9,11},{10,... | collective-permute-start | bytes 1179656 | tf_op jit(solution)/shard_map/ppermute | solution.py:364

commit v14 on v13

--- a/solution.py
+++ b/solution.py
@@ -358,6 +358,13 @@
     )
 
 
+def arrived(arrays):
+    return kernel_call(
+        "arrived", lambda *refs: None, [(o, True) for o in arrays], [(o.shape, o.dtype, True) for o in arrays],
+        aliases={i: i for i in range(len(arrays))},
+    )
+
+
 def exchange(piece, k):
     if k == 0:
         return piece
@@ -395,7 +402,8 @@
     active, slope, wide, plain, turned = interior(inputs, weight, n)
     active, slope, wide = one_end(True, near, plain, active, slope, wide, [ups[first[0]]])
     active, slope, wide = one_end(False, far, plain, active, slope, wide, [])
-    grad, near_grad, far_grad = grad_conv(slope, rest + second + first, ups)
+    ups.update(zip(second, arrived([ups[k] for k in second])))
+    grad, near_grad, far_grad = grad_conv(slope, order, ups)
     active = {k: exchange(active[k], k) for k in order}
     near_grad, far_grad = swap(near_grad, 0), swap(far_grad, 1)
 

time: 48.7 us -> 48 us (0.986); the launches traced: 48.4 us -> 47.2 us
  starting transfers between devices: 11.8 us -> 9.97 us
  waiting for transfers between devices: 15.6 us -> 16.2 us
    ppermute x4, starting transfers between devices: 7.37 us -> 5 us  [swap(): return lax.ppermute(values, 'ctx', pairs + [(b, a) for a, b in pairs])]
    ppermute x6, waiting for transfers between devices: 7.39 us -> 9.21 us  [exchange(): lax.ppermute(piece, 'ch', [(i, i ^ k) for i in range(lax.axis_size('ch'))])]
    ppermute x4, waiting for transfers between devices: 8.22 us -> 7.01 us  [swap(): return lax.ppermute(values, 'ctx', pairs + [(b, a) for a, b in pairs])]
    ppermute x6, starting transfers between devices: 4.4 us -> 4.98 us  [exchange(): lax.ppermute(piece, 'ch', [(i, i ^ k) for i in range(lax.axis_size('ch'))])]
    pallas_call x12 -> x13, Pallas kernels: 20.1 us -> 20.1 us  [kernel_call(): pl.pallas_call(kernel, in_specs=[INSIDE if held else ANY for _, held in o...]
  transfers between devices with their start and end apart: 10 -> 10, of which waited for: 4 -> 4; matrix products, arithmetic and copies ran while one was open for 0% -> 0% of each run, Pallas kernels for 35% -> 36%
where the time goes in v14:
time: 48 us; the launch traced here: 47.2 us
  Pallas kernels  20.1 us (42%)
  waiting for transfers between devices  16.2 us (34%)
  starting transfers between devices  9.97 us (21%)
  between operations  0.93 us (2%)
    pallas_call x13, Pallas kernels, kernel_call(): pl.pallas_call(kernel, in_specs=[INSIDE if held else ANY for _, held in o...  20.1 us
    ppermute x6, waiting for transfers between devices, exchange(): lax.ppermute(piece, 'ch', [(i, i ^ k) for i in range(lax.axis_size('ch'))])  9.21 us
    ppermute x4, waiting for transfers between devices, swap(): return lax.ppermute(values, 'ctx', pairs + [(b, a) for a, b in pairs])  7.01 us
    ppermute x4, starting transfers between devices, swap(): return lax.ppermute(values, 'ctx', pairs + [(b, a) for a, b in pairs])  5 us
    ppermute x6, starting transfers between devices, exchange(): lax.ppermute(piece, 'ch', [(i, i ^ k) for i in range(lax.axis_size('ch'))])  4.98 us
  transfers between devices with their start and end apart: 10, of which 4 were waited for; matrix products, arithmetic and copies ran while one was open for 0% of the time, Pallas kernels for 36%

profile of v14, /device:TPU:0, one launch (start us, length us, event | category | flops | bytes accessed | tf_op | source)
XLA Modules:
  0.0 47.2 jit_solution(15621704450027243430)
XLA Ops:
  0.6 1.0 %near_source.1 = bf16[384,512]{1,0:T(8,128)(2,1)S(1)} custom-call(bf16[384,2048]{1,0:T(8,128)(2,1)} %x_ref.9), custom_call_target="tpu_custom_call" | custom-call | tf_op jit(solution)/shard_map/near_source/pallas_call | solution.py:19
  1.7 3.0 %collective-permute-start.2 = (bf16[384,512]{1,0:T(8,128)(2,1)S(1)}, bf16[384,512]{1,0:T(8,128)(2,1)S(1)}, u32[]{:S(2)}, u32[]{:S(2)}) collective-permute-start(bf16[384,512]{1,0:T(8,128)(2,1)S(1)} %near_source.1), channel_id=1, source_target_pairs={{0,4},{8,12},{16,20},{24,28},{4,0},{12,8},{20,16},{28,24},{1,5},{9... | collective-permute-start | bytes 1179656 | tf_op jit(solution)/shard_map/ppermute | solution.py:377
  4.7 2.2 %upstream.3 = (bf16[384,512]{1,0:T(8,128)(2,1)S(1)}, bf16[1536,512]{1,0:T(8,128)(2,1)S(1)}) custom-call(bf16[1536,1536]{1,0:T(8,128)(2,1)} %pw_ref.11, bf16[1536,512]{1,0:T(8,128)(2,1)} %cot_ref.1, bf16[384,2048]{1,0:T(8,128)(2,1)} %x_ref.9), custom_call_target="tpu_custom_call" | custom-call | tf_op jit(solution)/shard_map/upstream/pallas_call | solution.py:19
  6.9 0.7 %collective-permute-start.1 = (bf16[384,512]{1,0:T(8,128)(2,1)S(1)}, bf16[384,512]{1,0:T(8,128)(2,1)S(1)}, u32[]{:S(2)}, u32[]{:S(2)}) collective-permute-start(bf16[384,512]{1,0:T(8,128)(2,1)S(1)} %get-tuple-element.35), channel_id=1, source_target_pairs={{0,3},{1,2},{2,1},{3,0},{4,7},{5,6},{6,5},{7,4},{8,11},{9,10},{10,... | collective-permute-start | bytes 1179656 | tf_op jit(solution)/shard_map/ppermute | solution.py:371
  7.6 2.0 %upstream.4 = (bf16[384,512]{1,0:T(8,128)(2,1)S(1)}, bf16[384,512]{1,0:T(8,128)(2,1)S(1)}) custom-call(bf16[1536,1536]{1,0:T(8,128)(2,1)} %pw_ref.11, bf16[1536,512]{1,0:T(8,128)(2,1)S(1)} %get-tuple-element.32.cot_ref, bf16[384,2048]{1,0:T(8,128)(2,1)} %x_ref.9), custom_call_target="tpu_custom_call" | custom-call | tf_op jit(solution)/shard_map/upstream/pallas_call | solution.py:19
  9.7 0.7 %collective-permute-start = (bf16[384,512]{1,0:T(8,128)(2,1)S(1)}, bf16[384,512]{1,0:T(8,128)(2,1)S(1)}, u32[]{:S(2)}, u32[]{:S(2)}) collective-permute-start(bf16[384,512]{1,0:T(8,128)(2,1)S(1)} %get-tuple-element.33), channel_id=1, source_target_pairs={{4,8},{12,16},{20,24},{8,4},{16,12},{24,20},{5,9},{13,17},{21,25},... | collective-permute-start | bytes 1179656 | tf_op jit(solution)/shard_map/ppermute | solution.py:377
  10.4 0.9 %collective-permute-start.3 = (bf16[384,512]{1,0:T(8,128)(2,1)S(1)}, bf16[384,512]{1,0:T(8,128)(2,1)S(1)}, u32[]{:S(2)}, u32[]{:S(2)}) collective-permute-start(bf16[384,512]{1,0:T(8,128)(2,1)S(1)} %get-tuple-element.49), channel_id=1, source_target_pairs={{0,2},{1,3},{2,0},{3,1},{4,6},{5,7},{6,4},{7,5},{8,10},{9,11},{10,... | collective-permute-start | bytes 1179656 | tf_op jit(solution)/shard_map/ppermute | solution.py:371
  11.3 2.8 %upstream.5 = (bf16[384,512]{1,0:T(8,128)(2,1)S(1)}, bf16[384,512]{1,0:T(8,128)(2,1)S(1)}) custom-call(bf16[1536,1536]{1,0:T(8,128)(2,1)} %pw_ref.11, bf16[1536,512]{1,0:T(8,128)(2,1)S(1)} %get-tuple-element.32.cot_ref, bf16[384,2048]{1,0:T(8,128)(2,1)} %x_ref.9), custom_call_target="tpu_custom_call" | custom-call | tf_op jit(solution)/shard_map/upstream/pallas_call | solution.py:19
  14.1 0.4 collective-permute-start.4
  14.5 3.3 %interior.1 = (bf16[384,512]{1,0:T(8,128)(2,1)S(1)}, bf16[384,512]{1,0:T(8,128)(2,1)S(1)}, bf16[384,512]{1,0:T(8,128)(2,1)S(1)}, bf16[384,512]{1,0:T(8,128)(2,1)...) custom-call(bf16[384,2048]{1,0:T(8,128)(2,1)} %x_ref.9, ...), custom_call_target="tpu_custom_call" | custom-call | tf_op jit(solution)/shard_map/interior/pallas_call | solution.py:19
  17.8 0.0 collective-permute-done.2.refs_1_
  17.8 0.4 collective-permute-done.1.refs_0_.rest_0_
  18.3 0.8 %near_end.1 = (bf16[384,512]{1,0:T(8,128)(2,1)S(1)}, bf16[384,512]{1,0:T(8,128)(2,1)S(1)}, bf16[384,512]{1,0:T(8,128)(2,1)S(1)}, bf16[384,512]{1,0:T(8,128)(2,1)...) custom-call(bf16[384,512]{1,0:T(8,128)(2,1)S(1)} %collective-permute, ...), custom_call_target="tpu_custom_call", output_to_operand_aliasing={{0}: (3, {}), {1}: (4, {}), {2}: (5, {}), {3}: (6, {}), {4}... | custom-call | tf_op jit(solution)/shard_map/near_end/pallas_call | solution.py:19
  19.0 0.0 collective-permute-done.refs_0_
  19.0 0.0 slice-start
  19.1 0.0 slice-start.1
  19.1 0.8 %far_end.1 = (bf16[384,512]{1,0:T(8,128)(2,1)S(1)}, bf16[384,512]{1,0:T(8,128)(2,1)S(1)}, bf16[384,512]{1,0:T(8,128)(2,1)S(1)}, bf16[384,512]{1,0:T(8,128)(2,1)S...) custom-call(bf16[384,512]{1,0:T(8,128)(2,1)S(1)} %collective-permute, ...), custom_call_target="tpu_custom_call", output_to_operand_aliasing={{0}: (2, {}), {1}: (3, {}), {2}: (4, {}), {3}: (5, {}), {4}... | custom-call | tf_op jit(solution)/shard_map/far_end/pallas_call | solution.py:19
  19.8 0.2 collective-permute-start.7
  20.0 1.6 %collective-permute-start.8 = (bf16[384,512]{1,0:T(8,128)(2,1)S(1)}, bf16[384,512]{1,0:T(8,128)(2,1)S(1)}, u32[]{:S(2)}, u32[]{:S(2)}) collective-permute-start(bf16[384,512]{1,0:T(8,128)(2,1)S(1)} %get-tuple-element.56), channel_id=1, source_target_pairs={{0,3},{1,2},{2,1},{3,0},{4,7},{5,6},{6,5},{7,4},{8,11},{9,10},{10,... | collective-permute-start | bytes 1179656 | tf_op jit(solution)/shard_map/ppermute | solution.py:371
  21.6 5.2 %collective-permute-done.3.refs_0_ = bf16[384,512]{1,0:T(8,128)(2,1)S(1)} collective-permute-done((bf16[384,512]{1,0:T(8,128)(2,1)S(1)}, bf16[384,512]{1,0:T(8,128)(2,1)S(1)}, u32[]{:S(2)}, u32[]{:S(2)}) %collective-permute-start.3) | collective-permute-done | bytes 393248 | tf_op jit(solution)/shard_map/ppermute | solution.py:371
  26.9 0.6 %grad_conv.1 = (bf16[384,2048]{1,0:T(8,128)(2,1)S(1)}, bf16[384,512]{1,0:T(8,128)(2,1)S(1)}, bf16[384,512]{1,0:T(8,128)(2,1)S(1)}) custom-call(f32[384,2048]{1,0:T(8,128)S(1)} %get-tuple-element.48.slope_ref, bf16[384,512]{1,0:T(8,128)(2,1)S(1)} %collective-permute-done.1.refs_0_.rest_0_, bf16[384,512]{1,0:T(8,128)(2,1)S(1)} %arrived.1.rest_1_, ...), custom_call_target="tpu_custom_call" | custom-call | tf_op jit(solution)/shard_map/grad_conv/pallas_call | solution.py:19
  27.5 0.5 collective-permute-start.5
  27.9 0.9 %collective-permute-start.6 = (bf16[384,512]{1,0:T(8,128)(2,1)S(1)}, bf16[384,512]{1,0:T(8,128)(2,1)S(1)}, u32[]{:S(2)}, u32[]{:S(2)}) collective-permute-start(bf16[384,512]{1,0:T(8,128)(2,1)S(1)} %get-tuple-element.53), channel_id=1, source_target_pairs={{4,8},{12,16},{20,24},{8,4},{16,12},{24,20},{5,9},{13,17},{21,25},... | collective-permute-start | bytes 1179656 | tf_op jit(solution)/shard_map/ppermute | solution.py:377
  28.8 1.1 %collective-permute-start.9 = (bf16[384,512]{1,0:T(8,128)(2,1)S(1)}, bf16[384,512]{1,0:T(8,128)(2,1)S(1)}, u32[]{:S(2)}, u32[]{:S(2)}) collective-permute-start(bf16[384,512]{1,0:T(8,128)(2,1)S(1)} %get-tuple-element.57), channel_id=1, source_target_pairs={{0,2},{1,3},{2,0},{3,1},{4,6},{5,7},{6,4},{7,5},{8,10},{9,11},{10,... | collective-permute-start | bytes 1179656 | tf_op jit(solution)/shard_map/ppermute | solution.py:371
  29.9 1.7 %back_interior.1 = (bf16[384,2048]{1,0:T(8,128)(2,1)}, f32[384,1024]{1,0:T(8,128)S(1)}) custom-call(bf16[384,2048]{1,0:T(8,128)(2,1)S(1)} %get-tuple-element.58.grad_ref, bf16[3,384,96]{2,1,0:T(8,128)(2,1)S(1)} %get-tuple-element.59.turned_ref.rest_2_), custom_call_target="tpu_custom_call" | custom-call | tf_op jit(solution)/shard_map/back_interior/pallas_call | solution.py:19
  31.6 3.6 %collective-permute-done.8.rest_0_ = bf16[384,512]{1,0:T(8,128)(2,1)S(1)} collective-permute-done((bf16[384,512]{1,0:T(8,128)(2,1)S(1)}, bf16[384,512]{1,0:T(8,128)(2,1)S(1)}, u32[]{:S(2)}, u32[]{:S(2)}) %collective-permute-start.8) | collective-permute-done | bytes 393248 | tf_op jit(solution)/shard_map/ppermute | solution.py:371
  35.1 1.0 %early_mix.1.rest_2_ = f32[1536,512]{1,0:T(8,128)S(1)} custom-call(bf16[1536,1536]{1,0:T(8,128)(2,1)S(1)} %bitcast.2, bf16[384,512]{1,0:T(8,128)(2,1)S(1)} %collective-permute-done.8.rest_0_), custom_call_target="tpu_custom_call" | custom-call | tf_op jit(solution)/shard_map/early_mix/pallas_call | solution.py:19
  36.1 0.0 collective-permute-done.7.rest_0_
  36.1 1.8 %half_mix.1.sum_ref = f32[1536,512]{1,0:T(8,128)S(1)} custom-call(bf16[1536,1536]{1,0:T(8,128)(2,1)S(1)} %bitcast.2, bf16[384,512]{1,0:T(8,128)(2,1)S(1)} %collective-permute-done.7.rest_0_, bf16[384,512]{1,0:T(8,128)(2,1)S(1)} %get-tuple-element.55.rest_1_, f32[1536,512]{1,0:T(8,128)S(1)} %early_mix.1.rest_2_), custom_call_target="tpu_custom_call", output_to_operand_aliasing={{}: (3, {})} | custom-call | tf_op jit(solution)/shard_map/half_mix/pallas_call | solution.py:19
  37.9 7.0 %collective-permute-done.5.near_ref = bf16[384,512]{1,0:T(8,128)(2,1)S(1)} collective-permute-done((bf16[384,512]{1,0:T(8,128)(2,1)S(1)}, bf16[384,512]{1,0:T(8,128)(2,1)S(1)}, u32[]{:S(2)}, u32[]{:S(2)}) %collective-permute-start.5) | collective-permute-done | bytes 393248 | tf_op jit(solution)/shard_map/ppermute | solution.py:377
  44.9 0.0 collective-permute-done.6.far_ref
  45.0 2.1 %tail.1 = (bf16[1536,512]{1,0:T(8,128)(2,1)}, bf16[384,2048]{1,0:T(8,128)(2,1)}) custom-call(bf16[384,512]{1,0:T(8,128)(2,1)S(1)} %collective-permute-done.5.near_ref, bf16[384,512]{1,0:T(8,128)(2,1)S(1)} %collective-permute-done.6.far_ref, bf16[1536,1536]{1,0:T(8,128)(2,1)S(1)} %bitcast.2, ...), custom_call_target="tpu_custom_call", output_to_operand_aliasing={{1}: (7, {})} | custom-call | tf_op jit(solution)/shard_map/tail/pallas_call | solution.py:19
  (6 shorter events, 0.0 us)
Async XLA Ops:
  1.7 16.2 %collective-permute-start.2 = (bf16[384,512]{1,0:T(8,128)(2,1)S(1)}, bf16[384,512]{1,0:T(8,128)(2,1)S(1)}, u32[]{:S(2)}, u32[]{:S(2)}) collective-permute-start(bf16[384,512]{1,0:T(8,128)(2,1)S(1)} %near_source.1), channel_id=1, source_target_pairs={{0,4},{8,12},{16,20},{24,28},{4,0},{12,8},{20,16},{28,24},{1,5},{9... | collective-permute-start | bytes 1179656 | tf_op jit(solution)/shard_map/ppermute | solution.py:377
  6.9 11.4 %collective-permute-start.1 = (bf16[384,512]{1,0:T(8,128)(2,1)S(1)}, bf16[384,512]{1,0:T(8,128)(2,1)S(1)}, u32[]{:S(2)}, u32[]{:S(2)}) collective-permute-start(bf16[384,512]{1,0:T(8,128)(2,1)S(1)} %get-tuple-element.35), channel_id=1, source_target_pairs={{0,3},{1,2},{2,1},{3,0},{4,7},{5,6},{6,5},{7,4},{8,11},{9,10},{10,... | collective-permute-start | bytes 1179656 | tf_op jit(solution)/shard_map/ppermute | solution.py:371
  9.7 9.4 %collective-permute-start = (bf16[384,512]{1,0:T(8,128)(2,1)S(1)}, bf16[384,512]{1,0:T(8,128)(2,1)S(1)}, u32[]{:S(2)}, u32[]{:S(2)}) collective-permute-start(bf16[384,512]{1,0:T(8,128)(2,1)S(1)} %get-tuple-element.33), channel_id=1, source_target_pairs={{4,8},{12,16},{20,24},{8,4},{16,12},{24,20},{5,9},{13,17},{21,25},... | collective-permute-start | bytes 1179656 | tf_op jit(solution)/shard_map/ppermute | solution.py:377
  10.4 16.5 %collective-permute-start.3 = (bf16[384,512]{1,0:T(8,128)(2,1)S(1)}, bf16[384,512]{1,0:T(8,128)(2,1)S(1)}, u32[]{:S(2)}, u32[]{:S(2)}) collective-permute-start(bf16[384,512]{1,0:T(8,128)(2,1)S(1)} %get-tuple-element.49), channel_id=1, source_target_pairs={{0,2},{1,3},{2,0},{3,1},{4,6},{5,7},{6,4},{7,5},{8,10},{9,11},{10,... | collective-permute-start | bytes 1179656 | tf_op jit(solution)/shard_map/ppermute | solution.py:371
  14.1 12.8 %collective-permute-start.4 = (bf16[384,512]{1,0:T(8,128)(2,1)S(1)}, bf16[384,512]{1,0:T(8,128)(2,1)S(1)}, u32[]{:S(2)}, u32[]{:S(2)}) collective-permute-start(bf16[384,512]{1,0:T(8,128)(2,1)S(1)} %get-tuple-element.50), channel_id=1, source_target_pairs={{0,1},{1,0},{2,3},{3,2},{4,5},{5,4},{6,7},{7,6},{8,9},{9,8},{10,11... | collective-permute-start | bytes 1179656 | tf_op jit(solution)/shard_map/ppermute | solution.py:371
  19.0 16.1 %slice-start = ((s8[4718592]{0:T(1024)(128)(4,1)}), s8[4194304]{0:T(1024)(128)(4,1)S(1)}, s32[]{:S(2)}) async-start(s8[4718592]{0:T(1024)(128)(4,1)} %bitcast.1), calls=%async_computation | async-start | bytes 8388608
  19.1 16.1 %slice-start.1 = ((s8[4718592]{0:T(1024)(128)(4,1)}), s8[524288]{0:T(1024)(128)(4,1)S(1)}, s32[]{:S(2)}) async-start(s8[4718592]{0:T(1024)(128)(4,1)} %bitcast.1), calls=%async_computation.1 | async-start | bytes 1048576
  19.8 16.3 %collective-permute-start.7 = (bf16[384,512]{1,0:T(8,128)(2,1)S(1)}, bf16[384,512]{1,0:T(8,128)(2,1)S(1)}, u32[]{:S(2)}, u32[]{:S(2)}) collective-permute-start(bf16[384,512]{1,0:T(8,128)(2,1)S(1)} %get-tuple-element.54), channel_id=1, source_target_pairs={{0,1},{1,0},{2,3},{3,2},{4,5},{5,4},{6,7},{7,6},{8,9},{9,8},{10,11... | collective-permute-start | bytes 1179656 | tf_op jit(solution)/shard_map/ppermute | solution.py:371
  20.0 15.1 %collective-permute-start.8 = (bf16[384,512]{1,0:T(8,128)(2,1)S(1)}, bf16[384,512]{1,0:T(8,128)(2,1)S(1)}, u32[]{:S(2)}, u32[]{:S(2)}) collective-permute-start(bf16[384,512]{1,0:T(8,128)(2,1)S(1)} %get-tuple-element.56), channel_id=1, source_target_pairs={{0,3},{1,2},{2,1},{3,0},{4,7},{5,6},{6,5},{7,4},{8,11},{9,10},{10,... | collective-permute-start | bytes 1179656 | tf_op jit(solution)/shard_map/ppermute | solution.py:371
  27.5 17.5 %collective-permute-start.5 = (bf16[384,512]{1,0:T(8,128)(2,1)S(1)}, bf16[384,512]{1,0:T(8,128)(2,1)S(1)}, u32[]{:S(2)}, u32[]{:S(2)}) collective-permute-start(bf16[384,512]{1,0:T(8,128)(2,1)S(1)} %get-tuple-element.52), channel_id=1, source_target_pairs={{0,4},{8,12},{16,20},{24,28},{4,0},{12,8},{20,16},{28,24},{1,5},{9... | collective-permute-start | bytes 1179656 | tf_op jit(solution)/shard_map/ppermute | solution.py:377
  27.9 17.0 %collective-permute-start.6 = (bf16[384,512]{1,0:T(8,128)(2,1)S(1)}, bf16[384,512]{1,0:T(8,128)(2,1)S(1)}, u32[]{:S(2)}, u32[]{:S(2)}) collective-permute-start(bf16[384,512]{1,0:T(8,128)(2,1)S(1)} %get-tuple-element.53), channel_id=1, source_target_pairs={{4,8},{12,16},{20,24},{8,4},{16,12},{24,20},{5,9},{13,17},{21,25},... | collective-permute-start | bytes 1179656 | tf_op jit(solution)/shard_map/ppermute | solution.py:377
  28.8 16.2 %collective-permute-start.9 = (bf16[384,512]{1,0:T(8,128)(2,1)S(1)}, bf16[384,512]{1,0:T(8,128)(2,1)S(1)}, u32[]{:S(2)}, u32[]{:S(2)}) collective-permute-start(bf16[384,512]{1,0:T(8,128)(2,1)S(1)} %get-tuple-element.57), channel_id=1, source_target_pairs={{0,2},{1,3},{2,0},{3,1},{4,6},{5,7},{6,4},{7,5},{8,10},{9,11},{10,... | collective-permute-start | bytes 1179656 | tf_op jit(solution)/shard_map/ppermute | solution.py:371

commit v15 on v14

--- a/solution.py
+++ b/solution.py
@@ -320,42 +320,49 @@
     return out_ref.at[:, lanes(at_end * (out_ref.shape[1] - DILATION_STEP), DILATION_STEP)]
 
 
-def tail_kernel(order, near_ref, far_ref, pw_ref, sum_ref, *rest):
-    piece_refs, rest = rest[:len(order)], rest[len(order):]
-    ends_ref, turned_ref, _, mixed_ref, out_ref, held, both, sems = rest
+def late_mix_kernel(order, pw_ref, sum_ref, *rest):
+    piece_refs, (out_ref, done_ref, held, sems) = rest[:len(order)], rest[len(order):]
     pieces = jnp.concatenate([p[...] for p in piece_refs], axis=0)
+    step = 512
     copies = []
-
-    def send(source, place):
-        copies.append(pltpu.make_async_copy(source, place, sems.at[len(copies)]))
-        copies[-1].start()
-
-    step = 512
     for m in range(0, sum_ref.shape[0], step):
         rows = slice(m, m + step)
         held[rows, :] = (sum_ref[rows, :] + columns_times(order, pw_ref, rows, pieces)).astype(BF16)
-        send(held.at[rows, :], mixed_ref.at[rows, :])
+        copies.append(pltpu.make_async_copy(held.at[rows, :], out_ref.at[rows, :], sems.at[len(copies)]))
+        copies[-1].start()
+    done_ref[...] = jnp.zeros_like(done_ref)
+    for copy in copies:
+        copy.wait()
+
+
+def late_mix(pw_weight, order, partial, active):
+    channels = active[order[0]].shape[0]
+    operands = [columns_of(pw_weight, channels, order), partial, *[active[k] for k in order]]
+    return kernel_call(
+        "late_mix", functools.partial(late_mix_kernel, order), [(o, True) for o in operands],
+        [(partial.shape, BF16, False), ((8, 128), F32, True)],
+        [pltpu.VMEM(partial.shape, BF16), DMA((partial.shape[0] // 512,))],
+    )
+
+
+def back_ends_kernel(near_ref, far_ref, ends_ref, turned_ref, _, __, out_ref, both, sems):
     odd = odd_place()
+    copies = []
     for place, (halo_ref, at_end) in enumerate(((near_ref, 1 - odd), (far_ref, odd))):
         back_end(halo_ref, ends_ref, turned_ref, at_end, both.at[place])
-        send(both.at[place], end_of(out_ref, at_end))
+        copies.append(pltpu.make_async_copy(both.at[place], end_of(out_ref, at_end), sems.at[place]))
+        copies[-1].start()
     for copy in copies:
         copy.wait()
 
 
-def tail(pw_weight, order, partial, active, near, far, ends, turned, grad_inputs):
-    channels, halo = near.shape
-    operands = [near, far, columns_of(pw_weight, channels, order), partial, *[active[k] for k in order]]
-    operands = [(o, True) for o in (*operands, ends, turned)] + [(grad_inputs, False)]
-    return kernel_call(
-        "tail", functools.partial(tail_kernel, order), operands,
-        [(partial.shape, BF16, False), (grad_inputs.shape, BF16, False)],
-        [
-            pltpu.VMEM(partial.shape, BF16), pltpu.VMEM((2, channels, halo), BF16),
-            DMA((partial.shape[0] // 512 + 2,)),
-        ],
-        {len(operands) - 1: 1},
-    )
+def back_ends(near, far, ends, turned, done, grad_inputs):
+    operands = [(o, True) for o in (near, far, ends, turned, done)] + [(grad_inputs, False)]
+    (result,) = kernel_call(
+        "back_ends", back_ends_kernel, operands, [(grad_inputs.shape, BF16, False)],
+        [pltpu.VMEM((2, *near.shape), BF16), DMA((2,))], {5: 0},
+    )
+    return result
 
 
 def arrived(arrays):
@@ -414,7 +421,8 @@
     )
     partial = mix("early_mix", pw_weight, first, active, [])
     (partial,) = mix("half_mix", pw_weight, rest, active, partial)
-    return tuple(tail(pw_weight, second, partial, active, near_grad, far_grad, ends, turned, grad_inputs))
+    mixed, done = late_mix(pw_weight, second, partial, active)
+    return mixed, back_ends(near_grad, far_grad, ends, turned, done, grad_inputs)
 
 
 def solution(mesh):

time: 48 us -> 47.5 us (0.990)
  waiting for transfers between devices: 16.2 us -> 14.9 us
  Pallas kernels: 20.1 us -> 21 us
    ppermute x4, waiting for transfers between devices: 7.01 us -> 0.01 us  [swap(): return lax.ppermute(values, 'ctx', pairs + [(b, a) for a, b in pairs])]
    ppermute x6, waiting for transfers between devices: 9.21 us -> 14.9 us  [exchange(): lax.ppermute(piece, 'ch', [(i, i ^ k) for i in range(lax.axis_size('ch'))])]
    pallas_call x13 -> x14, Pallas kernels: 20.1 us -> 21 us  [kernel_call(): pl.pallas_call(kernel, in_specs=[INSIDE if held else ANY for _, held in o...]
    ppermute x4, starting transfers between devices: 5 us -> 5.71 us  [swap(): return lax.ppermute(values, 'ctx', pairs + [(b, a) for a, b in pairs])]
    ppermute x6, starting transfers between devices: 4.98 us -> 4.29 us  [exchange(): lax.ppermute(piece, 'ch', [(i, i ^ k) for i in range(lax.axis_size('ch'))])]
  transfers between devices with their start and end apart: 10 -> 10, of which waited for: 4 -> 4; matrix products, arithmetic and copies ran while one was open for 0% -> 0% of each run, Pallas kernels for 36% -> 40%
where the time goes in v15:
time: 47.5 us; the launch traced here: 46.8 us
  Pallas kernels  21 us (44%)
  waiting for transfers between devices  14.9 us (31%)
  starting transfers between devices  10 us (21%)
  between operations  0.95 us (2%)
    pallas_call x14, Pallas kernels, kernel_call(): pl.pallas_call(kernel, in_specs=[INSIDE if held else ANY for _, held in o...  21 us
    ppermute x6, waiting for transfers between devices, exchange(): lax.ppermute(piece, 'ch', [(i, i ^ k) for i in range(lax.axis_size('ch'))])  14.9 us
    ppermute x4, starting transfers between devices, swap(): return lax.ppermute(values, 'ctx', pairs + [(b, a) for a, b in pairs])  5.71 us
    ppermute x6, starting transfers between devices, exchange(): lax.ppermute(piece, 'ch', [(i, i ^ k) for i in range(lax.axis_size('ch'))])  4.29 us
  transfers between devices with their start and end apart: 10, of which 4 were waited for; matrix products, arithmetic and copies ran while one was open for 0% of the time, Pallas kernels for 40%

profile of v15, /device:TPU:0, one launch (start us, length us, event | category | flops | bytes accessed | tf_op | source)
XLA Modules:
  0.0 46.8 jit_solution(8547408356298550645)
XLA Ops:
  0.6 1.0 %near_source.1 = bf16[384,512]{1,0:T(8,128)(2,1)S(1)} custom-call(bf16[384,2048]{1,0:T(8,128)(2,1)} %x_ref.9), custom_call_target="tpu_custom_call" | custom-call | tf_op jit(solution)/shard_map/near_source/pallas_call | solution.py:19
  1.7 3.0 %collective-permute-start.2 = (bf16[384,512]{1,0:T(8,128)(2,1)S(1)}, bf16[384,512]{1,0:T(8,128)(2,1)S(1)}, u32[]{:S(2)}, u32[]{:S(2)}) collective-permute-start(bf16[384,512]{1,0:T(8,128)(2,1)S(1)} %near_source.1), channel_id=1, source_target_pairs={{0,4},{8,12},{16,20},{24,28},{4,0},{12,8},{20,16},{28,24},{1,5},{9... | collective-permute-start | bytes 1179656 | tf_op jit(solution)/shard_map/ppermute | solution.py:384
  4.7 2.2 %upstream.3 = (bf16[384,512]{1,0:T(8,128)(2,1)S(1)}, bf16[1536,512]{1,0:T(8,128)(2,1)S(1)}) custom-call(bf16[1536,1536]{1,0:T(8,128)(2,1)} %pw_ref.11, bf16[1536,512]{1,0:T(8,128)(2,1)} %cot_ref.1, bf16[384,2048]{1,0:T(8,128)(2,1)} %x_ref.9), custom_call_target="tpu_custom_call" | custom-call | tf_op jit(solution)/shard_map/upstream/pallas_call | solution.py:19
  6.9 0.7 %collective-permute-start.1 = (bf16[384,512]{1,0:T(8,128)(2,1)S(1)}, bf16[384,512]{1,0:T(8,128)(2,1)S(1)}, u32[]{:S(2)}, u32[]{:S(2)}) collective-permute-start(bf16[384,512]{1,0:T(8,128)(2,1)S(1)} %get-tuple-element.37), channel_id=1, source_target_pairs={{0,3},{1,2},{2,1},{3,0},{4,7},{5,6},{6,5},{7,4},{8,11},{9,10},{10,... | collective-permute-start | bytes 1179656 | tf_op jit(solution)/shard_map/ppermute | solution.py:378
  7.6 2.0 %upstream.4 = (bf16[384,512]{1,0:T(8,128)(2,1)S(1)}, bf16[384,512]{1,0:T(8,128)(2,1)S(1)}) custom-call(bf16[1536,1536]{1,0:T(8,128)(2,1)} %pw_ref.11, bf16[1536,512]{1,0:T(8,128)(2,1)S(1)} %get-tuple-element.34.cot_ref, bf16[384,2048]{1,0:T(8,128)(2,1)} %x_ref.9), custom_call_target="tpu_custom_call" | custom-call | tf_op jit(solution)/shard_map/upstream/pallas_call | solution.py:19
  9.7 0.7 %collective-permute-start = (bf16[384,512]{1,0:T(8,128)(2,1)S(1)}, bf16[384,512]{1,0:T(8,128)(2,1)S(1)}, u32[]{:S(2)}, u32[]{:S(2)}) collective-permute-start(bf16[384,512]{1,0:T(8,128)(2,1)S(1)} %get-tuple-element.35), channel_id=1, source_target_pairs={{4,8},{12,16},{20,24},{8,4},{16,12},{24,20},{5,9},{13,17},{21,25},... | collective-permute-start | bytes 1179656 | tf_op jit(solution)/shard_map/ppermute | solution.py:384
  10.4 0.9 %collective-permute-start.6 = (bf16[384,512]{1,0:T(8,128)(2,1)S(1)}, bf16[384,512]{1,0:T(8,128)(2,1)S(1)}, u32[]{:S(2)}, u32[]{:S(2)}) collective-permute-start(bf16[384,512]{1,0:T(8,128)(2,1)S(1)} %get-tuple-element.56), channel_id=1, source_target_pairs={{0,2},{1,3},{2,0},{3,1},{4,6},{5,7},{6,4},{7,5},{8,10},{9,11},{10,... | collective-permute-start | bytes 1179656 | tf_op jit(solution)/shard_map/ppermute | solution.py:378
  11.3 2.8 %upstream.5 = (bf16[384,512]{1,0:T(8,128)(2,1)S(1)}, bf16[384,512]{1,0:T(8,128)(2,1)S(1)}) custom-call(bf16[1536,1536]{1,0:T(8,128)(2,1)} %pw_ref.11, bf16[1536,512]{1,0:T(8,128)(2,1)S(1)} %get-tuple-element.34.cot_ref, bf16[384,2048]{1,0:T(8,128)(2,1)} %x_ref.9), custom_call_target="tpu_custom_call" | custom-call | tf_op jit(solution)/shard_map/upstream/pallas_call | solution.py:19
  14.1 0.4 collective-permute-start.7
  14.5 3.3 %interior.1 = (bf16[384,512]{1,0:T(8,128)(2,1)S(1)}, bf16[384,512]{1,0:T(8,128)(2,1)S(1)}, bf16[384,512]{1,0:T(8,128)(2,1)S(1)}, bf16[384,512]{1,0:T(8,128)(2,1)...) custom-call(bf16[384,2048]{1,0:T(8,128)(2,1)} %x_ref.9, ...), custom_call_target="tpu_custom_call" | custom-call | tf_op jit(solution)/shard_map/interior/pallas_call | solution.py:19
  17.8 0.0 collective-permute-done.2.refs_1_
  17.8 0.4 collective-permute-done.1.refs_0_.rest_0_
  18.3 0.8 %near_end.1 = (bf16[384,512]{1,0:T(8,128)(2,1)S(1)}, bf16[384,512]{1,0:T(8,128)(2,1)S(1)}, bf16[384,512]{1,0:T(8,128)(2,1)S(1)}, bf16[384,512]{1,0:T(8,128)(2,1)...) custom-call(bf16[384,512]{1,0:T(8,128)(2,1)S(1)} %collective-permute, ...), custom_call_target="tpu_custom_call", output_to_operand_aliasing={{0}: (3, {}), {1}: (4, {}), {2}: (5, {}), {3}: (6, {}), {4}... | custom-call | tf_op jit(solution)/shard_map/near_end/pallas_call | solution.py:19
  19.1 0.0 slice-start.1
  19.1 0.8 %far_end.1 = (bf16[384,512]{1,0:T(8,128)(2,1)S(1)}, bf16[384,512]{1,0:T(8,128)(2,1)S(1)}, bf16[384,512]{1,0:T(8,128)(2,1)S(1)}, bf16[384,512]{1,0:T(8,128)(2,1)S...) custom-call(bf16[384,512]{1,0:T(8,128)(2,1)S(1)} %collective-permute, ...), custom_call_target="tpu_custom_call", output_to_operand_aliasing={{0}: (2, {}), {1}: (3, {}), {2}: (4, {}), {3}: (5, {}), {4}... | custom-call | tf_op jit(solution)/shard_map/far_end/pallas_call | solution.py:19
  19.9 0.2 collective-permute-start.3
  20.0 1.6 %collective-permute-start.4 = (bf16[384,512]{1,0:T(8,128)(2,1)S(1)}, bf16[384,512]{1,0:T(8,128)(2,1)S(1)}, u32[]{:S(2)}, u32[]{:S(2)}) collective-permute-start(bf16[384,512]{1,0:T(8,128)(2,1)S(1)} %get-tuple-element.52), channel_id=1, source_target_pairs={{0,3},{1,2},{2,1},{3,0},{4,7},{5,6},{6,5},{7,4},{8,11},{9,10},{10,... | collective-permute-start | bytes 1179656 | tf_op jit(solution)/shard_map/ppermute | solution.py:378
  21.6 0.5 collective-permute-start.5
  22.1 4.8 %collective-permute-done.6.refs_0_ = bf16[384,512]{1,0:T(8,128)(2,1)S(1)} collective-permute-done((bf16[384,512]{1,0:T(8,128)(2,1)S(1)}, bf16[384,512]{1,0:T(8,128)(2,1)S(1)}, u32[]{:S(2)}, u32[]{:S(2)}) %collective-permute-start.6) | collective-permute-done | bytes 393248 | tf_op jit(solution)/shard_map/ppermute | solution.py:378
  26.9 0.0 collective-permute-done.7.rest_2_
  26.9 0.6 %grad_conv.1 = (bf16[384,2048]{1,0:T(8,128)(2,1)S(1)}, bf16[384,512]{1,0:T(8,128)(2,1)S(1)}, bf16[384,512]{1,0:T(8,128)(2,1)S(1)}) custom-call(f32[384,2048]{1,0:T(8,128)S(1)} %get-tuple-element.55.slope_ref, bf16[384,512]{1,0:T(8,128)(2,1)S(1)} %collective-permute-done.1.refs_0_.rest_0_, bf16[384,512]{1,0:T(8,128)(2,1)S(1)} %arrived.1.rest_1_, ...), custom_call_target="tpu_custom_call" | custom-call | tf_op jit(solution)/shard_map/grad_conv/pallas_call | solution.py:19
  27.5 1.2 %collective-permute-start.8 = (bf16[384,512]{1,0:T(8,128)(2,1)S(1)}, bf16[384,512]{1,0:T(8,128)(2,1)S(1)}, u32[]{:S(2)}, u32[]{:S(2)}) collective-permute-start(bf16[384,512]{1,0:T(8,128)(2,1)S(1)} %get-tuple-element.59), channel_id=1, source_target_pairs={{0,4},{8,12},{16,20},{24,28},{4,0},{12,8},{20,16},{28,24},{1,5},{9... | collective-permute-start | bytes 1179656 | tf_op jit(solution)/shard_map/ppermute | solution.py:384
  28.6 0.9 %collective-permute-start.9 = (bf16[384,512]{1,0:T(8,128)(2,1)S(1)}, bf16[384,512]{1,0:T(8,128)(2,1)S(1)}, u32[]{:S(2)}, u32[]{:S(2)}) collective-permute-start(bf16[384,512]{1,0:T(8,128)(2,1)S(1)} %get-tuple-element.60), channel_id=1, source_target_pairs={{4,8},{12,16},{20,24},{8,4},{16,12},{24,20},{5,9},{13,17},{21,25},... | collective-permute-start | bytes 1179656 | tf_op jit(solution)/shard_map/ppermute | solution.py:384
  29.5 1.7 %back_interior.1 = (bf16[384,2048]{1,0:T(8,128)(2,1)}, f32[384,1024]{1,0:T(8,128)S(1)}) custom-call(bf16[384,2048]{1,0:T(8,128)(2,1)S(1)} %get-tuple-element.61.grad_ref, bf16[3,384,96]{2,1,0:T(8,128)(2,1)S(1)} %get-tuple-element.62.turned_ref), custom_call_target="tpu_custom_call" | custom-call | tf_op jit(solution)/shard_map/back_interior/pallas_call | solution.py:19
  31.2 4.0 %collective-permute-done.4.rest_0_ = bf16[384,512]{1,0:T(8,128)(2,1)S(1)} collective-permute-done((bf16[384,512]{1,0:T(8,128)(2,1)S(1)}, bf16[384,512]{1,0:T(8,128)(2,1)S(1)}, u32[]{:S(2)}, u32[]{:S(2)}) %collective-permute-start.4) | collective-permute-done | bytes 393248 | tf_op jit(solution)/shard_map/ppermute | solution.py:378
  35.1 1.0 %early_mix.1.rest_2_ = f32[1536,512]{1,0:T(8,128)S(1)} custom-call(bf16[1536,1536]{1,0:T(8,128)(2,1)S(1)} %bitcast.2, bf16[384,512]{1,0:T(8,128)(2,1)S(1)} %collective-permute-done.4.rest_0_), custom_call_target="tpu_custom_call" | custom-call | tf_op jit(solution)/shard_map/early_mix/pallas_call | solution.py:19
  36.1 1.8 %half_mix.1.sum_ref = f32[1536,512]{1,0:T(8,128)S(1)} custom-call(bf16[1536,1536]{1,0:T(8,128)(2,1)S(1)} %bitcast.2, bf16[384,512]{1,0:T(8,128)(2,1)S(1)} %collective-permute-done.3.rest_0_, bf16[384,512]{1,0:T(8,128)(2,1)S(1)} %get-tuple-element.51.rest_1_, f32[1536,512]{1,0:T(8,128)S(1)} %early_mix.1.rest_2_), custom_call_target="tpu_custom_call", output_to_operand_aliasing={{}: (3, {})} | custom-call | tf_op jit(solution)/shard_map/half_mix/pallas_call | solution.py:19
  37.9 5.7 %collective-permute-done.5.rest_0_ = bf16[384,512]{1,0:T(8,128)(2,1)S(1)} collective-permute-done((bf16[384,512]{1,0:T(8,128)(2,1)S(1)}, bf16[384,512]{1,0:T(8,128)(2,1)S(1)}, u32[]{:S(2)}, u32[]{:S(2)}) %collective-permute-start.5) | collective-permute-done | bytes 393248 | tf_op jit(solution)/shard_map/ppermute | solution.py:378
  43.6 1.8 %late_mix.1 = (bf16[1536,512]{1,0:T(8,128)(2,1)}, f32[8,128]{1,0:T(8,128)S(1)}) custom-call(bf16[1536,1536]{1,0:T(8,128)(2,1)S(1)} %bitcast.2, f32[1536,512]{1,0:T(8,128)S(1)} %half_mix.1.sum_ref, bf16[384,512]{1,0:T(8,128)(2,1)S(1)} %collective-permute-done.5.rest_0_), custom_call_target="tpu_custom_call" | custom-call | tf_op jit(solution)/shard_map/late_mix/pallas_call | solution.py:19
  45.5 0.0 collective-permute-done.8.near_ref
  45.5 0.0 collective-permute-done.9.far_ref
  45.5 1.2 %back_ends.1 = bf16[384,2048]{1,0:T(8,128)(2,1)} custom-call(bf16[384,512]{1,0:T(8,128)(2,1)S(1)} %collective-permute-done.8.near_ref, bf16[384,512]{1,0:T(8,128)(2,1)S(1)} %collective-permute-done.9.far_ref, f32[384,1024]{1,0:T(8,128)S(1)} %get-tuple-element.63.ends_ref, ...), custom_call_target="tpu_custom_call", output_to_operand_aliasing={{}: (5, {})} | custom-call | tf_op jit(solution)/shard_map/back_ends/pallas_call | solution.py:19
  (7 shorter events, 0.0 us)
Async XLA Ops:
  1.7 16.2 %collective-permute-start.2 = (bf16[384,512]{1,0:T(8,128)(2,1)S(1)}, bf16[384,512]{1,0:T(8,128)(2,1)S(1)}, u32[]{:S(2)}, u32[]{:S(2)}) collective-permute-start(bf16[384,512]{1,0:T(8,128)(2,1)S(1)} %near_source.1), channel_id=1, source_target_pairs={{0,4},{8,12},{16,20},{24,28},{4,0},{12,8},{20,16},{28,24},{1,5},{9... | collective-permute-start | bytes 1179656 | tf_op jit(solution)/shard_map/ppermute | solution.py:384
  6.9 11.4 %collective-permute-start.1 = (bf16[384,512]{1,0:T(8,128)(2,1)S(1)}, bf16[384,512]{1,0:T(8,128)(2,1)S(1)}, u32[]{:S(2)}, u32[]{:S(2)}) collective-permute-start(bf16[384,512]{1,0:T(8,128)(2,1)S(1)} %get-tuple-element.37), channel_id=1, source_target_pairs={{0,3},{1,2},{2,1},{3,0},{4,7},{5,6},{6,5},{7,4},{8,11},{9,10},{10,... | collective-permute-start | bytes 1179656 | tf_op jit(solution)/shard_map/ppermute | solution.py:378
  9.7 9.4 %collective-permute-start = (bf16[384,512]{1,0:T(8,128)(2,1)S(1)}, bf16[384,512]{1,0:T(8,128)(2,1)S(1)}, u32[]{:S(2)}, u32[]{:S(2)}) collective-permute-start(bf16[384,512]{1,0:T(8,128)(2,1)S(1)} %get-tuple-element.35), channel_id=1, source_target_pairs={{4,8},{12,16},{20,24},{8,4},{16,12},{24,20},{5,9},{13,17},{21,25},... | collective-permute-start | bytes 1179656 | tf_op jit(solution)/shard_map/ppermute | solution.py:384
  10.4 16.5 %collective-permute-start.6 = (bf16[384,512]{1,0:T(8,128)(2,1)S(1)}, bf16[384,512]{1,0:T(8,128)(2,1)S(1)}, u32[]{:S(2)}, u32[]{:S(2)}) collective-permute-start(bf16[384,512]{1,0:T(8,128)(2,1)S(1)} %get-tuple-element.56), channel_id=1, source_target_pairs={{0,2},{1,3},{2,0},{3,1},{4,6},{5,7},{6,4},{7,5},{8,10},{9,11},{10,... | collective-permute-start | bytes 1179656 | tf_op jit(solution)/shard_map/ppermute | solution.py:378
  14.1 12.8 %collective-permute-start.7 = (bf16[384,512]{1,0:T(8,128)(2,1)S(1)}, bf16[384,512]{1,0:T(8,128)(2,1)S(1)}, u32[]{:S(2)}, u32[]{:S(2)}) collective-permute-start(bf16[384,512]{1,0:T(8,128)(2,1)S(1)} %get-tuple-element.57), channel_id=1, source_target_pairs={{0,1},{1,0},{2,3},{3,2},{4,5},{5,4},{6,7},{7,6},{8,9},{9,8},{10,11... | collective-permute-start | bytes 1179656 | tf_op jit(solution)/shard_map/ppermute | solution.py:378
  18.3 16.9 %slice-start = ((s8[4718592]{0:T(1024)(128)(4,1)}), s8[4194304]{0:T(1024)(128)(4,1)S(1)}, s32[]{:S(2)}) async-start(s8[4718592]{0:T(1024)(128)(4,1)} %bitcast.1), calls=%async_computation | async-start | bytes 8388608
  19.1 16.1 %slice-start.1 = ((s8[4718592]{0:T(1024)(128)(4,1)}), s8[524288]{0:T(1024)(128)(4,1)S(1)}, s32[]{:S(2)}) async-start(s8[4718592]{0:T(1024)(128)(4,1)} %bitcast.1), calls=%async_computation.1 | async-start | bytes 1048576
  19.9 16.3 %collective-permute-start.3 = (bf16[384,512]{1,0:T(8,128)(2,1)S(1)}, bf16[384,512]{1,0:T(8,128)(2,1)S(1)}, u32[]{:S(2)}, u32[]{:S(2)}) collective-permute-start(bf16[384,512]{1,0:T(8,128)(2,1)S(1)} %get-tuple-element.50), channel_id=1, source_target_pairs={{0,1},{1,0},{2,3},{3,2},{4,5},{5,4},{6,7},{7,6},{8,9},{9,8},{10,11... | collective-permute-start | bytes 1179656 | tf_op jit(solution)/shard_map/ppermute | solution.py:378
  20.0 15.1 %collective-permute-start.4 = (bf16[384,512]{1,0:T(8,128)(2,1)S(1)}, bf16[384,512]{1,0:T(8,128)(2,1)S(1)}, u32[]{:S(2)}, u32[]{:S(2)}) collective-permute-start(bf16[384,512]{1,0:T(8,128)(2,1)S(1)} %get-tuple-element.52), channel_id=1, source_target_pairs={{0,3},{1,2},{2,1},{3,0},{4,7},{5,6},{6,5},{7,4},{8,11},{9,10},{10,... | collective-permute-start | bytes 1179656 | tf_op jit(solution)/shard_map/ppermute | solution.py:378
  21.6 22.0 %collective-permute-start.5 = (bf16[384,512]{1,0:T(8,128)(2,1)S(1)}, bf16[384,512]{1,0:T(8,128)(2,1)S(1)}, u32[]{:S(2)}, u32[]{:S(2)}) collective-permute-start(bf16[384,512]{1,0:T(8,128)(2,1)S(1)} %get-tuple-element.53), channel_id=1, source_target_pairs={{0,2},{1,3},{2,0},{3,1},{4,6},{5,7},{6,4},{7,5},{8,10},{9,11},{10,... | collective-permute-start | bytes 1179656 | tf_op jit(solution)/shard_map/ppermute | solution.py:378
  27.5 18.0 %collective-permute-start.8 = (bf16[384,512]{1,0:T(8,128)(2,1)S(1)}, bf16[384,512]{1,0:T(8,128)(2,1)S(1)}, u32[]{:S(2)}, u32[]{:S(2)}) collective-permute-start(bf16[384,512]{1,0:T(8,128)(2,1)S(1)} %get-tuple-element.59), channel_id=1, source_target_pairs={{0,4},{8,12},{16,20},{24,28},{4,0},{12,8},{20,16},{28,24},{1,5},{9... | collective-permute-start | bytes 1179656 | tf_op jit(solution)/shard_map/ppermute | solution.py:384
  28.6 16.8 %collective-permute-start.9 = (bf16[384,512]{1,0:T(8,128)(2,1)S(1)}, bf16[384,512]{1,0:T(8,128)(2,1)S(1)}, u32[]{:S(2)}, u32[]{:S(2)}) collective-permute-start(bf16[384,512]{1,0:T(8,128)(2,1)S(1)} %get-tuple-element.60), channel_id=1, source_target_pairs={{4,8},{12,16},{20,24},{8,4},{16,12},{24,20},{5,9},{13,17},{21,25},... | collective-permute-start | bytes 1179656 | tf_op jit(solution)/shard_map/ppermute | solution.py:384

commit v16 on v15

--- a/solution.py
+++ b/solution.py
@@ -321,33 +321,28 @@
 
 
 def late_mix_kernel(order, pw_ref, sum_ref, *rest):
-    piece_refs, (out_ref, done_ref, held, sems) = rest[:len(order)], rest[len(order):]
+    piece_refs, out_ref = rest[:-1], rest[-1]
     pieces = jnp.concatenate([p[...] for p in piece_refs], axis=0)
     step = 512
-    copies = []
     for m in range(0, sum_ref.shape[0], step):
         rows = slice(m, m + step)
-        held[rows, :] = (sum_ref[rows, :] + columns_times(order, pw_ref, rows, pieces)).astype(BF16)
-        copies.append(pltpu.make_async_copy(held.at[rows, :], out_ref.at[rows, :], sems.at[len(copies)]))
-        copies[-1].start()
-    done_ref[...] = jnp.zeros_like(done_ref)
-    for copy in copies:
-        copy.wait()
+        out_ref[rows, :] = (sum_ref[rows, :] + columns_times(order, pw_ref, rows, pieces)).astype(BF16)
 
 
 def late_mix(pw_weight, order, partial, active):
     channels = active[order[0]].shape[0]
     operands = [columns_of(pw_weight, channels, order), partial, *[active[k] for k in order]]
-    return kernel_call(
+    (mixed,) = kernel_call(
         "late_mix", functools.partial(late_mix_kernel, order), [(o, True) for o in operands],
-        [(partial.shape, BF16, False), ((8, 128), F32, True)],
-        [pltpu.VMEM(partial.shape, BF16), DMA((partial.shape[0] // 512,))],
-    )
-
-
-def back_ends_kernel(near_ref, far_ref, ends_ref, turned_ref, _, __, out_ref, both, sems):
+        [(partial.shape, BF16, True)],
+    )
+    return mixed
+
+
+def last_kernel(mixed_ref, near_ref, far_ref, ends_ref, turned_ref, _, mixed_out, out_ref, both, sems):
     odd = odd_place()
-    copies = []
+    copies = [pltpu.make_async_copy(mixed_ref, mixed_out, sems.at[2])]
+    copies[0].start()
     for place, (halo_ref, at_end) in enumerate(((near_ref, 1 - odd), (far_ref, odd))):
         back_end(halo_ref, ends_ref, turned_ref, at_end, both.at[place])
         copies.append(pltpu.make_async_copy(both.at[place], end_of(out_ref, at_end), sems.at[place]))
@@ -356,13 +351,12 @@
         copy.wait()
 
 
-def back_ends(near, far, ends, turned, done, grad_inputs):
-    operands = [(o, True) for o in (near, far, ends, turned, done)] + [(grad_inputs, False)]
-    (result,) = kernel_call(
-        "back_ends", back_ends_kernel, operands, [(grad_inputs.shape, BF16, False)],
-        [pltpu.VMEM((2, *near.shape), BF16), DMA((2,))], {5: 0},
-    )
-    return result
+def last(mixed, near, far, ends, turned, grad_inputs):
+    operands = [(o, True) for o in (mixed, near, far, ends, turned)] + [(grad_inputs, False)]
+    return kernel_call(
+        "last", last_kernel, operands, [(mixed.shape, BF16, False), (grad_inputs.shape, BF16, False)],
+        [pltpu.VMEM((2, *near.shape), BF16), DMA((3,))], {5: 1},
+    )
 
 
 def arrived(arrays):
@@ -421,8 +415,8 @@
     )
     partial = mix("early_mix", pw_weight, first, active, [])
     (partial,) = mix("half_mix", pw_weight, rest, active, partial)
-    mixed, done = late_mix(pw_weight, second, partial, active)
-    return mixed, back_ends(near_grad, far_grad, ends, turned, done, grad_inputs)
+    mixed = late_mix(pw_weight, second, partial, active)
+    return tuple(last(mixed, near_grad, far_grad, ends, turned, grad_inputs))
 
 
 def solution(mesh):

time: 47.5 us -> 47.8 us (level)
  waiting for transfers between devices: 14.9 us -> 15.6 us
  Pallas kernels: 21 us -> 20.4 us
    ppermute x4, waiting for transfers between devices: 0.01 us -> 0.77 us  [swap(): return lax.ppermute(values, 'ctx', pairs + [(b, a) for a, b in pairs])]
    pallas_call x14, Pallas kernels: 21 us -> 20.4 us  [kernel_call(): pl.pallas_call(kernel, in_specs=[INSIDE if held else ANY for _, held in o...]
  transfers between devices with their start and end apart: 10 -> 10, of which waited for: 4 -> 5; matrix products, arithmetic and copies ran while one was open for 0% -> 0% of each run, Pallas kernels for 40% -> 38%
where the time goes in v16:
time: 47.8 us; the launch traced here: 47 us
  Pallas kernels  20.4 us (43%)
  waiting for transfers between devices  15.6 us (33%)
  starting transfers between devices  10 us (21%)
  between operations  0.93 us (2%)
    pallas_call x14, Pallas kernels, kernel_call(): pl.pallas_call(kernel, in_specs=[INSIDE if held else ANY for _, held in o...  20.4 us
    ppermute x6, waiting for transfers between devices, exchange(): lax.ppermute(piece, 'ch', [(i, i ^ k) for i in range(lax.axis_size('ch'))])  14.9 us
    ppermute x4, starting transfers between devices, swap(): return lax.ppermute(values, 'ctx', pairs + [(b, a) for a, b in pairs])  5.71 us
    ppermute x6, starting transfers between devices, exchange(): lax.ppermute(piece, 'ch', [(i, i ^ k) for i in range(lax.axis_size('ch'))])  4.29 us
  transfers between devices with their start and end apart: 10, of which 5 were waited for; matrix products, arithmetic and copies ran while one was open for 0% of the time, Pallas kernels for 38%

profile of v16, /device:TPU:0, one launch (start us, length us, event | category | flops | bytes accessed | tf_op | source)
XLA Modules:
  0.0 47.0 jit_solution(12842390597338379010)
XLA Ops:
  0.6 1.0 %near_source.1 = bf16[384,512]{1,0:T(8,128)(2,1)S(1)} custom-call(bf16[384,2048]{1,0:T(8,128)(2,1)} %x_ref.9), custom_call_target="tpu_custom_call" | custom-call | tf_op jit(solution)/shard_map/near_source/pallas_call | solution.py:19
  1.7 3.0 %collective-permute-start.2 = (bf16[384,512]{1,0:T(8,128)(2,1)S(1)}, bf16[384,512]{1,0:T(8,128)(2,1)S(1)}, u32[]{:S(2)}, u32[]{:S(2)}) collective-permute-start(bf16[384,512]{1,0:T(8,128)(2,1)S(1)} %near_source.1), channel_id=1, source_target_pairs={{0,4},{8,12},{16,20},{24,28},{4,0},{12,8},{20,16},{28,24},{1,5},{9... | collective-permute-start | bytes 1179656 | tf_op jit(solution)/shard_map/ppermute | solution.py:378
  4.7 2.2 %upstream.3 = (bf16[384,512]{1,0:T(8,128)(2,1)S(1)}, bf16[1536,512]{1,0:T(8,128)(2,1)S(1)}) custom-call(bf16[1536,1536]{1,0:T(8,128)(2,1)} %pw_ref.11, bf16[1536,512]{1,0:T(8,128)(2,1)} %cot_ref.1, bf16[384,2048]{1,0:T(8,128)(2,1)} %x_ref.9), custom_call_target="tpu_custom_call" | custom-call | tf_op jit(solution)/shard_map/upstream/pallas_call | solution.py:19
  6.9 0.7 %collective-permute-start.1 = (bf16[384,512]{1,0:T(8,128)(2,1)S(1)}, bf16[384,512]{1,0:T(8,128)(2,1)S(1)}, u32[]{:S(2)}, u32[]{:S(2)}) collective-permute-start(bf16[384,512]{1,0:T(8,128)(2,1)S(1)} %get-tuple-element.35), channel_id=1, source_target_pairs={{0,3},{1,2},{2,1},{3,0},{4,7},{5,6},{6,5},{7,4},{8,11},{9,10},{10,... | collective-permute-start | bytes 1179656 | tf_op jit(solution)/shard_map/ppermute | solution.py:372
  7.6 2.0 %upstream.4 = (bf16[384,512]{1,0:T(8,128)(2,1)S(1)}, bf16[384,512]{1,0:T(8,128)(2,1)S(1)}) custom-call(bf16[1536,1536]{1,0:T(8,128)(2,1)} %pw_ref.11, bf16[1536,512]{1,0:T(8,128)(2,1)S(1)} %get-tuple-element.32.cot_ref, bf16[384,2048]{1,0:T(8,128)(2,1)} %x_ref.9), custom_call_target="tpu_custom_call" | custom-call | tf_op jit(solution)/shard_map/upstream/pallas_call | solution.py:19
  9.7 0.7 %collective-permute-start = (bf16[384,512]{1,0:T(8,128)(2,1)S(1)}, bf16[384,512]{1,0:T(8,128)(2,1)S(1)}, u32[]{:S(2)}, u32[]{:S(2)}) collective-permute-start(bf16[384,512]{1,0:T(8,128)(2,1)S(1)} %get-tuple-element.33), channel_id=1, source_target_pairs={{4,8},{12,16},{20,24},{8,4},{16,12},{24,20},{5,9},{13,17},{21,25},... | collective-permute-start | bytes 1179656 | tf_op jit(solution)/shard_map/ppermute | solution.py:378
  10.4 0.9 %collective-permute-start.6 = (bf16[384,512]{1,0:T(8,128)(2,1)S(1)}, bf16[384,512]{1,0:T(8,128)(2,1)S(1)}, u32[]{:S(2)}, u32[]{:S(2)}) collective-permute-start(bf16[384,512]{1,0:T(8,128)(2,1)S(1)} %get-tuple-element.53), channel_id=1, source_target_pairs={{0,2},{1,3},{2,0},{3,1},{4,6},{5,7},{6,4},{7,5},{8,10},{9,11},{10,... | collective-permute-start | bytes 1179656 | tf_op jit(solution)/shard_map/ppermute | solution.py:372
  11.3 2.8 %upstream.5 = (bf16[384,512]{1,0:T(8,128)(2,1)S(1)}, bf16[384,512]{1,0:T(8,128)(2,1)S(1)}) custom-call(bf16[1536,1536]{1,0:T(8,128)(2,1)} %pw_ref.11, bf16[1536,512]{1,0:T(8,128)(2,1)S(1)} %get-tuple-element.32.cot_ref, bf16[384,2048]{1,0:T(8,128)(2,1)} %x_ref.9), custom_call_target="tpu_custom_call" | custom-call | tf_op jit(solution)/shard_map/upstream/pallas_call | solution.py:19
  14.1 0.4 collective-permute-start.7
  14.5 3.3 %interior.1 = (bf16[384,512]{1,0:T(8,128)(2,1)S(1)}, bf16[384,512]{1,0:T(8,128)(2,1)S(1)}, bf16[384,512]{1,0:T(8,128)(2,1)S(1)}, bf16[384,512]{1,0:T(8,128)(2,1)...) custom-call(bf16[384,2048]{1,0:T(8,128)(2,1)} %x_ref.9, ...), custom_call_target="tpu_custom_call" | custom-call | tf_op jit(solution)/shard_map/interior/pallas_call | solution.py:19
  17.8 0.0 collective-permute-done.2.refs_1_
  17.8 0.4 collective-permute-done.1.refs_0_.rest_0_
  18.3 0.8 %near_end.1 = (bf16[384,512]{1,0:T(8,128)(2,1)S(1)}, bf16[384,512]{1,0:T(8,128)(2,1)S(1)}, bf16[384,512]{1,0:T(8,128)(2,1)S(1)}, bf16[384,512]{1,0:T(8,128)(2,1)...) custom-call(bf16[384,512]{1,0:T(8,128)(2,1)S(1)} %collective-permute, ...), custom_call_target="tpu_custom_call", output_to_operand_aliasing={{0}: (3, {}), {1}: (4, {}), {2}: (5, {}), {3}: (6, {}), {4}... | custom-call | tf_op jit(solution)/shard_map/near_end/pallas_call | solution.py:19
  19.1 0.0 slice-start.1
  19.1 0.8 %far_end.1 = (bf16[384,512]{1,0:T(8,128)(2,1)S(1)}, bf16[384,512]{1,0:T(8,128)(2,1)S(1)}, bf16[384,512]{1,0:T(8,128)(2,1)S(1)}, bf16[384,512]{1,0:T(8,128)(2,1)S...) custom-call(bf16[384,512]{1,0:T(8,128)(2,1)S(1)} %collective-permute, ...), custom_call_target="tpu_custom_call", output_to_operand_aliasing={{0}: (2, {}), {1}: (3, {}), {2}: (4, {}), {3}: (5, {}), {4}... | custom-call | tf_op jit(solution)/shard_map/far_end/pallas_call | solution.py:19
  19.9 0.2 collective-permute-start.3
  20.0 1.6 %collective-permute-start.4 = (bf16[384,512]{1,0:T(8,128)(2,1)S(1)}, bf16[384,512]{1,0:T(8,128)(2,1)S(1)}, u32[]{:S(2)}, u32[]{:S(2)}) collective-permute-start(bf16[384,512]{1,0:T(8,128)(2,1)S(1)} %get-tuple-element.50), channel_id=1, source_target_pairs={{0,3},{1,2},{2,1},{3,0},{4,7},{5,6},{6,5},{7,4},{8,11},{9,10},{10,... | collective-permute-start | bytes 1179656 | tf_op jit(solution)/shard_map/ppermute | solution.py:372
  21.6 0.5 collective-permute-start.5
  22.1 4.8 %collective-permute-done.6.refs_0_ = bf16[384,512]{1,0:T(8,128)(2,1)S(1)} collective-permute-done((bf16[384,512]{1,0:T(8,128)(2,1)S(1)}, bf16[384,512]{1,0:T(8,128)(2,1)S(1)}, u32[]{:S(2)}, u32[]{:S(2)}) %collective-permute-start.6) | collective-permute-done | bytes 393248 | tf_op jit(solution)/shard_map/ppermute | solution.py:372
  26.9 0.0 collective-permute-done.7.rest_2_
  26.9 0.6 %grad_conv.1 = (bf16[384,2048]{1,0:T(8,128)(2,1)S(1)}, bf16[384,512]{1,0:T(8,128)(2,1)S(1)}, bf16[384,512]{1,0:T(8,128)(2,1)S(1)}) custom-call(f32[384,2048]{1,0:T(8,128)S(1)} %get-tuple-element.52.slope_ref, bf16[384,512]{1,0:T(8,128)(2,1)S(1)} %collective-permute-done.1.refs_0_.rest_0_, bf16[384,512]{1,0:T(8,128)(2,1)S(1)} %arrived.1.rest_1_, ...), custom_call_target="tpu_custom_call" | custom-call | tf_op jit(solution)/shard_map/grad_conv/pallas_call | solution.py:19
  27.5 1.2 %collective-permute-start.8 = (bf16[384,512]{1,0:T(8,128)(2,1)S(1)}, bf16[384,512]{1,0:T(8,128)(2,1)S(1)}, u32[]{:S(2)}, u32[]{:S(2)}) collective-permute-start(bf16[384,512]{1,0:T(8,128)(2,1)S(1)} %get-tuple-element.56), channel_id=1, source_target_pairs={{0,4},{8,12},{16,20},{24,28},{4,0},{12,8},{20,16},{28,24},{1,5},{9... | collective-permute-start | bytes 1179656 | tf_op jit(solution)/shard_map/ppermute | solution.py:378
  28.6 0.9 %collective-permute-start.9 = (bf16[384,512]{1,0:T(8,128)(2,1)S(1)}, bf16[384,512]{1,0:T(8,128)(2,1)S(1)}, u32[]{:S(2)}, u32[]{:S(2)}) collective-permute-start(bf16[384,512]{1,0:T(8,128)(2,1)S(1)} %get-tuple-element.57), channel_id=1, source_target_pairs={{4,8},{12,16},{20,24},{8,4},{16,12},{24,20},{5,9},{13,17},{21,25},... | collective-permute-start | bytes 1179656 | tf_op jit(solution)/shard_map/ppermute | solution.py:378
  29.5 1.7 %back_interior.1 = (bf16[384,2048]{1,0:T(8,128)(2,1)}, f32[384,1024]{1,0:T(8,128)S(1)}) custom-call(bf16[384,2048]{1,0:T(8,128)(2,1)S(1)} %get-tuple-element.58.grad_ref, bf16[3,384,96]{2,1,0:T(8,128)(2,1)S(1)} %get-tuple-element.59.turned_ref), custom_call_target="tpu_custom_call" | custom-call | tf_op jit(solution)/shard_map/back_interior/pallas_call | solution.py:19
  31.2 4.0 %collective-permute-done.4.rest_0_ = bf16[384,512]{1,0:T(8,128)(2,1)S(1)} collective-permute-done((bf16[384,512]{1,0:T(8,128)(2,1)S(1)}, bf16[384,512]{1,0:T(8,128)(2,1)S(1)}, u32[]{:S(2)}, u32[]{:S(2)}) %collective-permute-start.4) | collective-permute-done | bytes 393248 | tf_op jit(solution)/shard_map/ppermute | solution.py:372
  35.1 1.0 %early_mix.1.rest_2_ = f32[1536,512]{1,0:T(8,128)S(1)} custom-call(bf16[1536,1536]{1,0:T(8,128)(2,1)S(1)} %bitcast.2, bf16[384,512]{1,0:T(8,128)(2,1)S(1)} %collective-permute-done.4.rest_0_), custom_call_target="tpu_custom_call" | custom-call | tf_op jit(solution)/shard_map/early_mix/pallas_call | solution.py:19
  36.1 1.8 %half_mix.1.sum_ref = f32[1536,512]{1,0:T(8,128)S(1)} custom-call(bf16[1536,1536]{1,0:T(8,128)(2,1)S(1)} %bitcast.2, bf16[384,512]{1,0:T(8,128)(2,1)S(1)} %collective-permute-done.3.rest_0_, bf16[384,512]{1,0:T(8,128)(2,1)S(1)} %get-tuple-element.49.rest_1_, f32[1536,512]{1,0:T(8,128)S(1)} %early_mix.1.rest_2_), custom_call_target="tpu_custom_call", output_to_operand_aliasing={{}: (3, {})} | custom-call | tf_op jit(solution)/shard_map/half_mix/pallas_call | solution.py:19
  37.9 5.7 %collective-permute-done.5.rest_0_ = bf16[384,512]{1,0:T(8,128)(2,1)S(1)} collective-permute-done((bf16[384,512]{1,0:T(8,128)(2,1)S(1)}, bf16[384,512]{1,0:T(8,128)(2,1)S(1)}, u32[]{:S(2)}, u32[]{:S(2)}) %collective-permute-start.5) | collective-permute-done | bytes 393248 | tf_op jit(solution)/shard_map/ppermute | solution.py:372
  43.6 1.0 %late_mix.1.mixed_ref = bf16[1536,512]{1,0:T(8,128)(2,1)S(1)} custom-call(bf16[1536,1536]{1,0:T(8,128)(2,1)S(1)} %bitcast.2, f32[1536,512]{1,0:T(8,128)S(1)} %half_mix.1.sum_ref, bf16[384,512]{1,0:T(8,128)(2,1)S(1)} %collective-permute-done.5.rest_0_), custom_call_target="tpu_custom_call" | custom-call | tf_op jit(solution)/shard_map/late_mix/pallas_call | solution.py:19
  44.6 0.8 %collective-permute-done.8.near_ref = bf16[384,512]{1,0:T(8,128)(2,1)S(1)} collective-permute-done((bf16[384,512]{1,0:T(8,128)(2,1)S(1)}, bf16[384,512]{1,0:T(8,128)(2,1)S(1)}, u32[]{:S(2)}, u32[]{:S(2)}) %collective-permute-start.8) | collective-permute-done | bytes 393248 | tf_op jit(solution)/shard_map/ppermute | solution.py:378
  45.4 0.0 collective-permute-done.9.far_ref
  45.4 1.4 %last.1 = (bf16[1536,512]{1,0:T(8,128)(2,1)}, bf16[384,2048]{1,0:T(8,128)(2,1)}) custom-call(bf16[1536,512]{1,0:T(8,128)(2,1)S(1)} %late_mix.1.mixed_ref, bf16[384,512]{1,0:T(8,128)(2,1)S(1)} %collective-permute-done.8.near_ref, bf16[384,512]{1,0:T(8,128)(2,1)S(1)} %collective-permute-done.9.far_ref, ...), custom_call_target="tpu_custom_call", output_to_operand_aliasing={{1}: (5, {})} | custom-call | tf_op jit(solution)/shard_map/last/pallas_call | solution.py:19
  (7 shorter events, 0.0 us)
Async XLA Ops:
  1.7 16.2 %collective-permute-start.2 = (bf16[384,512]{1,0:T(8,128)(2,1)S(1)}, bf16[384,512]{1,0:T(8,128)(2,1)S(1)}, u32[]{:S(2)}, u32[]{:S(2)}) collective-permute-start(bf16[384,512]{1,0:T(8,128)(2,1)S(1)} %near_source.1), channel_id=1, source_target_pairs={{0,4},{8,12},{16,20},{24,28},{4,0},{12,8},{20,16},{28,24},{1,5},{9... | collective-permute-start | bytes 1179656 | tf_op jit(solution)/shard_map/ppermute | solution.py:378
  6.9 11.4 %collective-permute-start.1 = (bf16[384,512]{1,0:T(8,128)(2,1)S(1)}, bf16[384,512]{1,0:T(8,128)(2,1)S(1)}, u32[]{:S(2)}, u32[]{:S(2)}) collective-permute-start(bf16[384,512]{1,0:T(8,128)(2,1)S(1)} %get-tuple-element.35), channel_id=1, source_target_pairs={{0,3},{1,2},{2,1},{3,0},{4,7},{5,6},{6,5},{7,4},{8,11},{9,10},{10,... | collective-permute-start | bytes 1179656 | tf_op jit(solution)/shard_map/ppermute | solution.py:372
  9.7 9.4 %collective-permute-start = (bf16[384,512]{1,0:T(8,128)(2,1)S(1)}, bf16[384,512]{1,0:T(8,128)(2,1)S(1)}, u32[]{:S(2)}, u32[]{:S(2)}) collective-permute-start(bf16[384,512]{1,0:T(8,128)(2,1)S(1)} %get-tuple-element.33), channel_id=1, source_target_pairs={{4,8},{12,16},{20,24},{8,4},{16,12},{24,20},{5,9},{13,17},{21,25},... | collective-permute-start | bytes 1179656 | tf_op jit(solution)/shard_map/ppermute | solution.py:378
  10.4 16.5 %collective-permute-start.6 = (bf16[384,512]{1,0:T(8,128)(2,1)S(1)}, bf16[384,512]{1,0:T(8,128)(2,1)S(1)}, u32[]{:S(2)}, u32[]{:S(2)}) collective-permute-start(bf16[384,512]{1,0:T(8,128)(2,1)S(1)} %get-tuple-element.53), channel_id=1, source_target_pairs={{0,2},{1,3},{2,0},{3,1},{4,6},{5,7},{6,4},{7,5},{8,10},{9,11},{10,... | collective-permute-start | bytes 1179656 | tf_op jit(solution)/shard_map/ppermute | solution.py:372
  14.1 12.8 %collective-permute-start.7 = (bf16[384,512]{1,0:T(8,128)(2,1)S(1)}, bf16[384,512]{1,0:T(8,128)(2,1)S(1)}, u32[]{:S(2)}, u32[]{:S(2)}) collective-permute-start(bf16[384,512]{1,0:T(8,128)(2,1)S(1)} %get-tuple-element.54), channel_id=1, source_target_pairs={{0,1},{1,0},{2,3},{3,2},{4,5},{5,4},{6,7},{7,6},{8,9},{9,8},{10,11... | collective-permute-start | bytes 1179656 | tf_op jit(solution)/shard_map/ppermute | solution.py:372
  18.3 16.9 %slice-start = ((s8[4718592]{0:T(1024)(128)(4,1)}), s8[4194304]{0:T(1024)(128)(4,1)S(1)}, s32[]{:S(2)}) async-start(s8[4718592]{0:T(1024)(128)(4,1)} %bitcast.1), calls=%async_computation | async-start | bytes 8388608
  19.1 16.1 %slice-start.1 = ((s8[4718592]{0:T(1024)(128)(4,1)}), s8[524288]{0:T(1024)(128)(4,1)S(1)}, s32[]{:S(2)}) async-start(s8[4718592]{0:T(1024)(128)(4,1)} %bitcast.1), calls=%async_computation.1 | async-start | bytes 1048576
  19.9 16.3 %collective-permute-start.3 = (bf16[384,512]{1,0:T(8,128)(2,1)S(1)}, bf16[384,512]{1,0:T(8,128)(2,1)S(1)}, u32[]{:S(2)}, u32[]{:S(2)}) collective-permute-start(bf16[384,512]{1,0:T(8,128)(2,1)S(1)} %get-tuple-element.48), channel_id=1, source_target_pairs={{0,1},{1,0},{2,3},{3,2},{4,5},{5,4},{6,7},{7,6},{8,9},{9,8},{10,11... | collective-permute-start | bytes 1179656 | tf_op jit(solution)/shard_map/ppermute | solution.py:372
  20.0 15.1 %collective-permute-start.4 = (bf16[384,512]{1,0:T(8,128)(2,1)S(1)}, bf16[384,512]{1,0:T(8,128)(2,1)S(1)}, u32[]{:S(2)}, u32[]{:S(2)}) collective-permute-start(bf16[384,512]{1,0:T(8,128)(2,1)S(1)} %get-tuple-element.50), channel_id=1, source_target_pairs={{0,3},{1,2},{2,1},{3,0},{4,7},{5,6},{6,5},{7,4},{8,11},{9,10},{10,... | collective-permute-start | bytes 1179656 | tf_op jit(solution)/shard_map/ppermute | solution.py:372
  21.6 22.0 %collective-permute-start.5 = (bf16[384,512]{1,0:T(8,128)(2,1)S(1)}, bf16[384,512]{1,0:T(8,128)(2,1)S(1)}, u32[]{:S(2)}, u32[]{:S(2)}) collective-permute-start(bf16[384,512]{1,0:T(8,128)(2,1)S(1)} %get-tuple-element.51), channel_id=1, source_target_pairs={{0,2},{1,3},{2,0},{3,1},{4,6},{5,7},{6,4},{7,5},{8,10},{9,11},{10,... | collective-permute-start | bytes 1179656 | tf_op jit(solution)/shard_map/ppermute | solution.py:372
  27.5 17.9 %collective-permute-start.8 = (bf16[384,512]{1,0:T(8,128)(2,1)S(1)}, bf16[384,512]{1,0:T(8,128)(2,1)S(1)}, u32[]{:S(2)}, u32[]{:S(2)}) collective-permute-start(bf16[384,512]{1,0:T(8,128)(2,1)S(1)} %get-tuple-element.56), channel_id=1, source_target_pairs={{0,4},{8,12},{16,20},{24,28},{4,0},{12,8},{20,16},{28,24},{1,5},{9... | collective-permute-start | bytes 1179656 | tf_op jit(solution)/shard_map/ppermute | solution.py:378
  28.6 16.8 %collective-permute-start.9 = (bf16[384,512]{1,0:T(8,128)(2,1)S(1)}, bf16[384,512]{1,0:T(8,128)(2,1)S(1)}, u32[]{:S(2)}, u32[]{:S(2)}) collective-permute-start(bf16[384,512]{1,0:T(8,128)(2,1)S(1)} %get-tuple-element.57), channel_id=1, source_target_pairs={{4,8},{12,16},{20,24},{8,4},{16,12},{24,20},{5,9},{13,17},{21,25},... | collective-permute-start | bytes 1179656 | tf_op jit(solution)/shard_map/ppermute | solution.py:378

commit v17 on v15

--- a/solution.py
+++ b/solution.py
@@ -230,7 +230,8 @@
 
 
 def grad_kernel(order, slope_ref, *rest):
-    up_refs, (grad_ref, near_out, far_out) = rest[:-3], rest[-3:]
+    up_refs, passed = rest[:len(order)], (len(rest) - len(order) - 3) // 2
+    grad_ref, near_out, far_out = rest[len(order) + passed:len(order) + passed + 3]
     ch, odd = lax.axis_index("ch"), odd_place()
     length, halo = grad_ref.shape[1], near_out.shape[1]
     block = up_refs[0].shape[1]
@@ -241,13 +242,15 @@
     far_out[...] = grad_ref[:, lanes(odd * (length - halo), halo)]
 
 
-def grad_conv(slope, order, ups):
-    channels = slope.shape[0]
-    return kernel_call(
+def grad_conv(slope, order, ups, passed):
+    end = (slope.shape[0], DILATION_STEP)
+    grad, near, far, *passed = kernel_call(
         "grad_conv", functools.partial(grad_kernel, order),
-        [(o, True) for o in (slope, *[ups[k] for k in order])],
-        [(slope.shape, BF16, True)] + [((channels, DILATION_STEP), BF16, True)] * 2,
-    )
+        [(o, True) for o in (slope, *[ups[k] for k in order], *passed)],
+        [(slope.shape, BF16, True), (end, BF16, True), (end, BF16, True)] + [(o.shape, BF16, True) for o in passed],
+        aliases={1 + len(order) + i: 3 + i for i in range(len(passed))},
+    )
+    return grad, near, far, passed
 
 
 def columns_times(order, pw_ref, rows, pieces):
@@ -410,8 +413,9 @@
     active, slope, wide = one_end(True, near, plain, active, slope, wide, [ups[first[0]]])
     active, slope, wide = one_end(False, far, plain, active, slope, wide, [])
     ups.update(zip(second, arrived([ups[k] for k in second])))
-    grad, near_grad, far_grad = grad_conv(slope, order, ups)
-    active = {k: exchange(active[k], k) for k in order}
+    grad, near_grad, far_grad, late = grad_conv(slope, order, ups, [active[k] for k in second])
+    late = dict(zip(second, late))
+    active = {k: exchange(late.get(k, active[k]), k) for k in order}
     near_grad, far_grad = swap(near_grad, 0), swap(far_grad, 1)
 
     grad_inputs, ends = kernel_call(

time: 47.5 us -> 47.9 us (level)
    ppermute x4, starting transfers between devices: 5.71 us -> 5.07 us  [swap(): return lax.ppermute(values, 'ctx', pairs + [(b, a) for a, b in pairs])]
    ppermute x6, starting transfers between devices: 4.29 us -> 4.83 us  [exchange(): lax.ppermute(piece, 'ch', [(i, i ^ k) for i in range(lax.axis_size('ch'))])]
  transfers between devices with their start and end apart: 10 -> 10, of which waited for: 4 -> 5; matrix products, arithmetic and copies ran while one was open for 0% -> 0% of each run, Pallas kernels for 40% -> 40%
where the time goes in v17:
time: 47.9 us; the launch traced here: 47.1 us
  Pallas kernels  21 us (44%)
  waiting for transfers between devices  15.3 us (32%)
  starting transfers between devices  9.9 us (21%)
  between operations  0.93 us (2%)
    pallas_call x14, Pallas kernels, kernel_call(): pl.pallas_call(kernel, in_specs=[INSIDE if held else ANY for _, held in o...  21 us
    ppermute x6, waiting for transfers between devices, exchange(): lax.ppermute(piece, 'ch', [(i, i ^ k) for i in range(lax.axis_size('ch'))])  15 us
    ppermute x4, starting transfers between devices, swap(): return lax.ppermute(values, 'ctx', pairs + [(b, a) for a, b in pairs])  5.07 us
    ppermute x6, starting transfers between devices, exchange(): lax.ppermute(piece, 'ch', [(i, i ^ k) for i in range(lax.axis_size('ch'))])  4.83 us
  transfers between devices with their start and end apart: 10, of which 5 were waited for; matrix products, arithmetic and copies ran while one was open for 0% of the time, Pallas kernels for 40%

profile of v17, /device:TPU:0, one launch (start us, length us, event | category | flops | bytes accessed | tf_op | source)
XLA Modules:
  0.0 47.1 jit_solution(7299812784128170536)
XLA Ops:
  0.6 1.0 %near_source.1 = bf16[384,512]{1,0:T(8,128)(2,1)S(1)} custom-call(bf16[384,2048]{1,0:T(8,128)(2,1)} %x_ref.9), custom_call_target="tpu_custom_call" | custom-call | tf_op jit(solution)/shard_map/near_source/pallas_call | solution.py:19
  1.7 3.0 %collective-permute-start.2 = (bf16[384,512]{1,0:T(8,128)(2,1)S(1)}, bf16[384,512]{1,0:T(8,128)(2,1)S(1)}, u32[]{:S(2)}, u32[]{:S(2)}) collective-permute-start(bf16[384,512]{1,0:T(8,128)(2,1)S(1)} %near_source.1), channel_id=1, source_target_pairs={{0,4},{8,12},{16,20},{24,28},{4,0},{12,8},{20,16},{28,24},{1,5},{9... | collective-permute-start | bytes 1179656 | tf_op jit(solution)/shard_map/ppermute | solution.py:387
  4.7 2.2 %upstream.3 = (bf16[384,512]{1,0:T(8,128)(2,1)S(1)}, bf16[1536,512]{1,0:T(8,128)(2,1)S(1)}) custom-call(bf16[1536,1536]{1,0:T(8,128)(2,1)} %pw_ref.11, bf16[1536,512]{1,0:T(8,128)(2,1)} %cot_ref.1, bf16[384,2048]{1,0:T(8,128)(2,1)} %x_ref.9), custom_call_target="tpu_custom_call" | custom-call | tf_op jit(solution)/shard_map/upstream/pallas_call | solution.py:19
  6.9 0.7 %collective-permute-start.1 = (bf16[384,512]{1,0:T(8,128)(2,1)S(1)}, bf16[384,512]{1,0:T(8,128)(2,1)S(1)}, u32[]{:S(2)}, u32[]{:S(2)}) collective-permute-start(bf16[384,512]{1,0:T(8,128)(2,1)S(1)} %get-tuple-element.38), channel_id=1, source_target_pairs={{0,3},{1,2},{2,1},{3,0},{4,7},{5,6},{6,5},{7,4},{8,11},{9,10},{10,... | collective-permute-start | bytes 1179656 | tf_op jit(solution)/shard_map/ppermute | solution.py:381
  7.6 2.0 %upstream.4 = (bf16[384,512]{1,0:T(8,128)(2,1)S(1)}, bf16[384,512]{1,0:T(8,128)(2,1)S(1)}) custom-call(bf16[1536,1536]{1,0:T(8,128)(2,1)} %pw_ref.11, bf16[1536,512]{1,0:T(8,128)(2,1)S(1)} %get-tuple-element.35.cot_ref, bf16[384,2048]{1,0:T(8,128)(2,1)} %x_ref.9), custom_call_target="tpu_custom_call" | custom-call | tf_op jit(solution)/shard_map/upstream/pallas_call | solution.py:19
  9.7 0.7 %collective-permute-start = (bf16[384,512]{1,0:T(8,128)(2,1)S(1)}, bf16[384,512]{1,0:T(8,128)(2,1)S(1)}, u32[]{:S(2)}, u32[]{:S(2)}) collective-permute-start(bf16[384,512]{1,0:T(8,128)(2,1)S(1)} %get-tuple-element.36), channel_id=1, source_target_pairs={{4,8},{12,16},{20,24},{8,4},{16,12},{24,20},{5,9},{13,17},{21,25},... | collective-permute-start | bytes 1179656 | tf_op jit(solution)/shard_map/ppermute | solution.py:387
  10.4 0.9 %collective-permute-start.5 = (bf16[384,512]{1,0:T(8,128)(2,1)S(1)}, bf16[384,512]{1,0:T(8,128)(2,1)S(1)}, u32[]{:S(2)}, u32[]{:S(2)}) collective-permute-start(bf16[384,512]{1,0:T(8,128)(2,1)S(1)} %get-tuple-element.55), channel_id=1, source_target_pairs={{0,2},{1,3},{2,0},{3,1},{4,6},{5,7},{6,4},{7,5},{8,10},{9,11},{10,... | collective-permute-start | bytes 1179656 | tf_op jit(solution)/shard_map/ppermute | solution.py:381
  11.3 2.8 %upstream.5 = (bf16[384,512]{1,0:T(8,128)(2,1)S(1)}, bf16[384,512]{1,0:T(8,128)(2,1)S(1)}) custom-call(bf16[1536,1536]{1,0:T(8,128)(2,1)} %pw_ref.11, bf16[1536,512]{1,0:T(8,128)(2,1)S(1)} %get-tuple-element.35.cot_ref, bf16[384,2048]{1,0:T(8,128)(2,1)} %x_ref.9), custom_call_target="tpu_custom_call" | custom-call | tf_op jit(solution)/shard_map/upstream/pallas_call | solution.py:19
  14.1 0.4 collective-permute-start.6
  14.5 3.3 %interior.1 = (bf16[384,512]{1,0:T(8,128)(2,1)S(1)}, bf16[384,512]{1,0:T(8,128)(2,1)S(1)}, bf16[384,512]{1,0:T(8,128)(2,1)S(1)}, bf16[384,512]{1,0:T(8,128)(2,1)...) custom-call(bf16[384,2048]{1,0:T(8,128)(2,1)} %x_ref.9, ...), custom_call_target="tpu_custom_call" | custom-call | tf_op jit(solution)/shard_map/interior/pallas_call | solution.py:19
  17.8 0.0 collective-permute-done.2.refs_1_
  17.8 0.4 collective-permute-done.1.refs_0_.rest_0_
  18.3 0.8 %near_end.1 = (bf16[384,512]{1,0:T(8,128)(2,1)S(1)}, bf16[384,512]{1,0:T(8,128)(2,1)S(1)}, bf16[384,512]{1,0:T(8,128)(2,1)S(1)}, bf16[384,512]{1,0:T(8,128)(2,1)...) custom-call(bf16[384,512]{1,0:T(8,128)(2,1)S(1)} %collective-permute, ...), custom_call_target="tpu_custom_call", output_to_operand_aliasing={{0}: (3, {}), {1}: (4, {}), {2}: (5, {}), {3}: (6, {}), {4}... | custom-call | tf_op jit(solution)/shard_map/near_end/pallas_call | solution.py:19
  19.0 0.0 collective-permute-done.refs_0_
  19.0 0.0 slice-start
  19.1 0.8 %far_end.1 = (bf16[384,512]{1,0:T(8,128)(2,1)S(1)}, bf16[384,512]{1,0:T(8,128)(2,1)S(1)}, bf16[384,512]{1,0:T(8,128)(2,1)S(1)}, bf16[384,512]{1,0:T(8,128)(2,1)S...) custom-call(bf16[384,512]{1,0:T(8,128)(2,1)S(1)} %collective-permute, ...), custom_call_target="tpu_custom_call", output_to_operand_aliasing={{0}: (2, {}), {1}: (3, {}), {2}: (4, {}), {3}: (5, {}), {4}... | custom-call | tf_op jit(solution)/shard_map/far_end/pallas_call | solution.py:19
  19.8 0.2 collective-permute-start.3
  20.0 1.6 %collective-permute-start.4 = (bf16[384,512]{1,0:T(8,128)(2,1)S(1)}, bf16[384,512]{1,0:T(8,128)(2,1)S(1)}, u32[]{:S(2)}, u32[]{:S(2)}) collective-permute-start(bf16[384,512]{1,0:T(8,128)(2,1)S(1)} %get-tuple-element.53), channel_id=1, source_target_pairs={{0,3},{1,2},{2,1},{3,0},{4,7},{5,6},{6,5},{7,4},{8,11},{9,10},{10,... | collective-permute-start | bytes 1179656 | tf_op jit(solution)/shard_map/ppermute | solution.py:381
  21.6 5.2 %collective-permute-done.5.refs_0_ = bf16[384,512]{1,0:T(8,128)(2,1)S(1)} collective-permute-done((bf16[384,512]{1,0:T(8,128)(2,1)S(1)}, bf16[384,512]{1,0:T(8,128)(2,1)S(1)}, u32[]{:S(2)}, u32[]{:S(2)}) %collective-permute-start.5) | collective-permute-done | bytes 393248 | tf_op jit(solution)/shard_map/ppermute | solution.py:381
  26.9 0.6 %grad_conv.1 = (bf16[384,2048]{1,0:T(8,128)(2,1)S(1)}, bf16[384,512]{1,0:T(8,128)(2,1)S(1)}, bf16[384,512]{1,0:T(8,128)(2,1)S(1)}, bf16[384,512]{1,0:T(8,128)(2,1)S(1)}) custom-call(f32[384,2048]{1,0:T(8,128)S(1)} %get-tuple-element.54.slope_ref, bf16[384,512]{1,0:T(8,128)(2,1)S(1)} %collective-permute-done.1.refs_0_.rest_0_, ...), custom_call_target="tpu_custom_call", output_to_operand_aliasing={{3}: (5, {})} | custom-call | tf_op jit(solution)/shard_map/grad_conv/pallas_call | solution.py:19
  27.5 1.0 %collective-permute-start.7 = (bf16[384,512]{1,0:T(8,128)(2,1)S(1)}, bf16[384,512]{1,0:T(8,128)(2,1)S(1)}, u32[]{:S(2)}, u32[]{:S(2)}) collective-permute-start(bf16[384,512]{1,0:T(8,128)(2,1)S(1)} %get-tuple-element.59), channel_id=1, source_target_pairs={{0,2},{1,3},{2,0},{3,1},{4,6},{5,7},{6,4},{7,5},{8,10},{9,11},{10,... | collective-permute-start | bytes 1179656 | tf_op jit(solution)/shard_map/ppermute | solution.py:381
  28.4 0.5 %collective-permute-start.8 = (bf16[384,512]{1,0:T(8,128)(2,1)S(1)}, bf16[384,512]{1,0:T(8,128)(2,1)S(1)}, u32[]{:S(2)}, u32[]{:S(2)}) collective-permute-start(bf16[384,512]{1,0:T(8,128)(2,1)S(1)} %get-tuple-element.61), channel_id=1, source_target_pairs={{0,4},{8,12},{16,20},{24,28},{4,0},{12,8},{20,16},{28,24},{1,5},{9... | collective-permute-start | bytes 1179656 | tf_op jit(solution)/shard_map/ppermute | solution.py:387
  29.0 0.9 %collective-permute-start.9 = (bf16[384,512]{1,0:T(8,128)(2,1)S(1)}, bf16[384,512]{1,0:T(8,128)(2,1)S(1)}, u32[]{:S(2)}, u32[]{:S(2)}) collective-permute-start(bf16[384,512]{1,0:T(8,128)(2,1)S(1)} %get-tuple-element.62), channel_id=1, source_target_pairs={{4,8},{12,16},{20,24},{8,4},{16,12},{24,20},{5,9},{13,17},{21,25},... | collective-permute-start | bytes 1179656 | tf_op jit(solution)/shard_map/ppermute | solution.py:387
  29.8 1.7 %back_interior.1 = (bf16[384,2048]{1,0:T(8,128)(2,1)}, f32[384,1024]{1,0:T(8,128)S(1)}) custom-call(bf16[384,2048]{1,0:T(8,128)(2,1)S(1)} %get-tuple-element.63.grad_ref, bf16[3,384,96]{2,1,0:T(8,128)(2,1)S(1)} %get-tuple-element.64.turned_ref), custom_call_target="tpu_custom_call" | custom-call | tf_op jit(solution)/shard_map/back_interior/pallas_call | solution.py:19
  31.5 3.6 %collective-permute-done.4.rest_0_ = bf16[384,512]{1,0:T(8,128)(2,1)S(1)} collective-permute-done((bf16[384,512]{1,0:T(8,128)(2,1)S(1)}, bf16[384,512]{1,0:T(8,128)(2,1)S(1)}, u32[]{:S(2)}, u32[]{:S(2)}) %collective-permute-start.4) | collective-permute-done | bytes 393248 | tf_op jit(solution)/shard_map/ppermute | solution.py:381
  35.1 1.0 %early_mix.1.rest_2_ = f32[1536,512]{1,0:T(8,128)S(1)} custom-call(bf16[1536,1536]{1,0:T(8,128)(2,1)S(1)} %bitcast.2, bf16[384,512]{1,0:T(8,128)(2,1)S(1)} %collective-permute-done.4.rest_0_), custom_call_target="tpu_custom_call" | custom-call | tf_op jit(solution)/shard_map/early_mix/pallas_call | solution.py:19
  36.1 0.0 collective-permute-done.3.rest_0_
  36.1 1.8 %half_mix.1.sum_ref = f32[1536,512]{1,0:T(8,128)S(1)} custom-call(bf16[1536,1536]{1,0:T(8,128)(2,1)S(1)} %bitcast.2, bf16[384,512]{1,0:T(8,128)(2,1)S(1)} %collective-permute-done.3.rest_0_, bf16[384,512]{1,0:T(8,128)(2,1)S(1)} %get-tuple-element.52.rest_1_, f32[1536,512]{1,0:T(8,128)S(1)} %early_mix.1.rest_2_), custom_call_target="tpu_custom_call", output_to_operand_aliasing={{}: (3, {})} | custom-call | tf_op jit(solution)/shard_map/half_mix/pallas_call | solution.py:19
  37.9 5.7 %collective-permute-done.7.rest_0_ = bf16[384,512]{1,0:T(8,128)(2,1)S(1)} collective-permute-done((bf16[384,512]{1,0:T(8,128)(2,1)S(1)}, bf16[384,512]{1,0:T(8,128)(2,1)S(1)}, u32[]{:S(2)}, u32[]{:S(2)}) %collective-permute-start.7) | collective-permute-done | bytes 393248 | tf_op jit(solution)/shard_map/ppermute | solution.py:381
  43.6 1.8 %late_mix.1 = (bf16[1536,512]{1,0:T(8,128)(2,1)}, f32[8,128]{1,0:T(8,128)S(1)}) custom-call(bf16[1536,1536]{1,0:T(8,128)(2,1)S(1)} %bitcast.2, f32[1536,512]{1,0:T(8,128)S(1)} %half_mix.1.sum_ref, bf16[384,512]{1,0:T(8,128)(2,1)S(1)} %collective-permute-done.7.rest_0_), custom_call_target="tpu_custom_call" | custom-call | tf_op jit(solution)/shard_map/late_mix/pallas_call | solution.py:19
  45.5 0.3 collective-permute-done.8.near_ref
  45.8 1.2 %back_ends.1 = bf16[384,2048]{1,0:T(8,128)(2,1)} custom-call(bf16[384,512]{1,0:T(8,128)(2,1)S(1)} %collective-permute-done.8.near_ref, bf16[384,512]{1,0:T(8,128)(2,1)S(1)} %collective-permute-done.9.far_ref, f32[384,1024]{1,0:T(8,128)S(1)} %get-tuple-element.65.ends_ref, ...), custom_call_target="tpu_custom_call", output_to_operand_aliasing={{}: (5, {})} | custom-call | tf_op jit(solution)/shard_map/back_ends/pallas_call | solution.py:19
  (7 shorter events, 0.0 us)
Async XLA Ops:
  1.7 16.2 %collective-permute-start.2 = (bf16[384,512]{1,0:T(8,128)(2,1)S(1)}, bf16[384,512]{1,0:T(8,128)(2,1)S(1)}, u32[]{:S(2)}, u32[]{:S(2)}) collective-permute-start(bf16[384,512]{1,0:T(8,128)(2,1)S(1)} %near_source.1), channel_id=1, source_target_pairs={{0,4},{8,12},{16,20},{24,28},{4,0},{12,8},{20,16},{28,24},{1,5},{9... | collective-permute-start | bytes 1179656 | tf_op jit(solution)/shard_map/ppermute | solution.py:387
  6.9 11.4 %collective-permute-start.1 = (bf16[384,512]{1,0:T(8,128)(2,1)S(1)}, bf16[384,512]{1,0:T(8,128)(2,1)S(1)}, u32[]{:S(2)}, u32[]{:S(2)}) collective-permute-start(bf16[384,512]{1,0:T(8,128)(2,1)S(1)} %get-tuple-element.38), channel_id=1, source_target_pairs={{0,3},{1,2},{2,1},{3,0},{4,7},{5,6},{6,5},{7,4},{8,11},{9,10},{10,... | collective-permute-start | bytes 1179656 | tf_op jit(solution)/shard_map/ppermute | solution.py:381
  9.7 9.4 %collective-permute-start = (bf16[384,512]{1,0:T(8,128)(2,1)S(1)}, bf16[384,512]{1,0:T(8,128)(2,1)S(1)}, u32[]{:S(2)}, u32[]{:S(2)}) collective-permute-start(bf16[384,512]{1,0:T(8,128)(2,1)S(1)} %get-tuple-element.36), channel_id=1, source_target_pairs={{4,8},{12,16},{20,24},{8,4},{16,12},{24,20},{5,9},{13,17},{21,25},... | collective-permute-start | bytes 1179656 | tf_op jit(solution)/shard_map/ppermute | solution.py:387
  10.4 16.5 %collective-permute-start.5 = (bf16[384,512]{1,0:T(8,128)(2,1)S(1)}, bf16[384,512]{1,0:T(8,128)(2,1)S(1)}, u32[]{:S(2)}, u32[]{:S(2)}) collective-permute-start(bf16[384,512]{1,0:T(8,128)(2,1)S(1)} %get-tuple-element.55), channel_id=1, source_target_pairs={{0,2},{1,3},{2,0},{3,1},{4,6},{5,7},{6,4},{7,5},{8,10},{9,11},{10,... | collective-permute-start | bytes 1179656 | tf_op jit(solution)/shard_map/ppermute | solution.py:381
  14.1 12.8 %collective-permute-start.6 = (bf16[384,512]{1,0:T(8,128)(2,1)S(1)}, bf16[384,512]{1,0:T(8,128)(2,1)S(1)}, u32[]{:S(2)}, u32[]{:S(2)}) collective-permute-start(bf16[384,512]{1,0:T(8,128)(2,1)S(1)} %get-tuple-element.56), channel_id=1, source_target_pairs={{0,1},{1,0},{2,3},{3,2},{4,5},{5,4},{6,7},{7,6},{8,9},{9,8},{10,11... | collective-permute-start | bytes 1179656 | tf_op jit(solution)/shard_map/ppermute | solution.py:381
  19.0 16.1 %slice-start = ((s8[4718592]{0:T(1024)(128)(4,1)}), s8[4194304]{0:T(1024)(128)(4,1)S(1)}, s32[]{:S(2)}) async-start(s8[4718592]{0:T(1024)(128)(4,1)} %bitcast.1), calls=%async_computation | async-start | bytes 8388608
  19.8 16.3 %collective-permute-start.3 = (bf16[384,512]{1,0:T(8,128)(2,1)S(1)}, bf16[384,512]{1,0:T(8,128)(2,1)S(1)}, u32[]{:S(2)}, u32[]{:S(2)}) collective-permute-start(bf16[384,512]{1,0:T(8,128)(2,1)S(1)} %get-tuple-element.51), channel_id=1, source_target_pairs={{0,1},{1,0},{2,3},{3,2},{4,5},{5,4},{6,7},{7,6},{8,9},{9,8},{10,11... | collective-permute-start | bytes 1179656 | tf_op jit(solution)/shard_map/ppermute | solution.py:381
  20.0 15.1 %slice-start.1 = ((s8[4718592]{0:T(1024)(128)(4,1)}), s8[524288]{0:T(1024)(128)(4,1)S(1)}, s32[]{:S(2)}) async-start(s8[4718592]{0:T(1024)(128)(4,1)} %bitcast.1), calls=%async_computation.1 | async-start | bytes 1048576
  20.0 15.1 %collective-permute-start.4 = (bf16[384,512]{1,0:T(8,128)(2,1)S(1)}, bf16[384,512]{1,0:T(8,128)(2,1)S(1)}, u32[]{:S(2)}, u32[]{:S(2)}) collective-permute-start(bf16[384,512]{1,0:T(8,128)(2,1)S(1)} %get-tuple-element.53), channel_id=1, source_target_pairs={{0,3},{1,2},{2,1},{3,0},{4,7},{5,6},{6,5},{7,4},{8,11},{9,10},{10,... | collective-permute-start | bytes 1179656 | tf_op jit(solution)/shard_map/ppermute | solution.py:381
  27.5 16.2 %collective-permute-start.7 = (bf16[384,512]{1,0:T(8,128)(2,1)S(1)}, bf16[384,512]{1,0:T(8,128)(2,1)S(1)}, u32[]{:S(2)}, u32[]{:S(2)}) collective-permute-start(bf16[384,512]{1,0:T(8,128)(2,1)S(1)} %get-tuple-element.59), channel_id=1, source_target_pairs={{0,2},{1,3},{2,0},{3,1},{4,6},{5,7},{6,4},{7,5},{8,10},{9,11},{10,... | collective-permute-start | bytes 1179656 | tf_op jit(solution)/shard_map/ppermute | solution.py:381
  28.4 17.3 %collective-permute-start.8 = (bf16[384,512]{1,0:T(8,128)(2,1)S(1)}, bf16[384,512]{1,0:T(8,128)(2,1)S(1)}, u32[]{:S(2)}, u32[]{:S(2)}) collective-permute-start(bf16[384,512]{1,0:T(8,128)(2,1)S(1)} %get-tuple-element.61), channel_id=1, source_target_pairs={{0,4},{8,12},{16,20},{24,28},{4,0},{12,8},{20,16},{28,24},{1,5},{9... | collective-permute-start | bytes 1179656 | tf_op jit(solution)/shard_map/ppermute | solution.py:387
  29.0 16.8 %collective-permute-start.9 = (bf16[384,512]{1,0:T(8,128)(2,1)S(1)}, bf16[384,512]{1,0:T(8,128)(2,1)S(1)}, u32[]{:S(2)}, u32[]{:S(2)}) collective-permute-start(bf16[384,512]{1,0:T(8,128)(2,1)S(1)} %get-tuple-element.62), channel_id=1, source_target_pairs={{4,8},{12,16},{20,24},{8,4},{16,12},{24,20},{5,9},{13,17},{21,25},... | collective-permute-start | bytes 1179656 | tf_op jit(solution)/shard_map/ppermute | solution.py:387

commit v18 on v15

--- a/solution.py
+++ b/solution.py
@@ -388,7 +388,7 @@
     n = lax.axis_size("ch")
     channels, length = inputs.shape
     halo = DILATION_STEP
-    order = list(range(n - 1, -1, -1))
+    order = [*range(n // 2, n), *range(n // 2 - 1, -1, -1)]
     first, second, rest = order[:n // 4], order[n // 4:n // 2], order[n // 2:]
 
     weight = jnp.swapaxes(conv_weight, 1, 2)

time: 47.5 us -> 46.9 us (0.987)
  waiting for transfers between devices: 14.9 us -> 11 us
  starting transfers between devices: 10 us -> 13.4 us
    ppermute x6, waiting for transfers between devices: 14.9 us -> 10.4 us  [exchange(): lax.ppermute(piece, 'ch', [(i, i ^ k) for i in range(lax.axis_size('ch'))])]
    ppermute x6, starting transfers between devices: 4.29 us -> 6.54 us  [exchange(): lax.ppermute(piece, 'ch', [(i, i ^ k) for i in range(lax.axis_size('ch'))])]
    ppermute x4, starting transfers between devices: 5.71 us -> 6.88 us  [swap(): return lax.ppermute(values, 'ctx', pairs + [(b, a) for a, b in pairs])]
    ppermute x4, waiting for transfers between devices: 0.01 us -> 0.66 us  [swap(): return lax.ppermute(values, 'ctx', pairs + [(b, a) for a, b in pairs])]
  transfers between devices with their start and end apart: 10 -> 10, of which waited for: 4 -> 5; matrix products, arithmetic and copies ran while one was open for 0% -> 0% of each run, Pallas kernels for 40% -> 41%
where the time goes in v18:
time: 46.9 us; the launch traced here: 46.3 us
  Pallas kernels  20.9 us (45%)
  starting transfers between devices  13.4 us (29%)
  waiting for transfers between devices  11 us (23%)
  between operations  0.95 us (2%)
    pallas_call x14, Pallas kernels, kernel_call(): pl.pallas_call(kernel, in_specs=[INSIDE if held else ANY for _, held in o...  20.9 us
    ppermute x6, waiting for transfers between devices, exchange(): lax.ppermute(piece, 'ch', [(i, i ^ k) for i in range(lax.axis_size('ch'))])  10.4 us
    ppermute x4, starting transfers between devices, swap(): return lax.ppermute(values, 'ctx', pairs + [(b, a) for a, b in pairs])  6.88 us
    ppermute x6, starting transfers between devices, exchange(): lax.ppermute(piece, 'ch', [(i, i ^ k) for i in range(lax.axis_size('ch'))])  6.54 us
  transfers between devices with their start and end apart: 10, of which 5 were waited for; matrix products, arithmetic and copies ran while one was open for 0% of the time, Pallas kernels for 41%

profile of v18, /device:TPU:0, one launch (start us, length us, event | category | flops | bytes accessed | tf_op | source)
XLA Modules:
  0.0 46.3 jit_solution(8065957117946935296)
XLA Ops:
  0.6 1.0 %near_source.1 = bf16[384,512]{1,0:T(8,128)(2,1)S(1)} custom-call(bf16[384,2048]{1,0:T(8,128)(2,1)} %x_ref.9), custom_call_target="tpu_custom_call" | custom-call | tf_op jit(solution)/shard_map/near_source/pallas_call | solution.py:19
  1.7 3.0 %collective-permute-start.2 = (bf16[384,512]{1,0:T(8,128)(2,1)S(1)}, bf16[384,512]{1,0:T(8,128)(2,1)S(1)}, u32[]{:S(2)}, u32[]{:S(2)}) collective-permute-start(bf16[384,512]{1,0:T(8,128)(2,1)S(1)} %near_source.1), channel_id=1, source_target_pairs={{0,4},{8,12},{16,20},{24,28},{4,0},{12,8},{20,16},{28,24},{1,5},{9... | collective-permute-start | bytes 1179656 | tf_op jit(solution)/shard_map/ppermute | solution.py:384
  4.7 2.2 %upstream.3 = (bf16[384,512]{1,0:T(8,128)(2,1)S(1)}, bf16[1536,512]{1,0:T(8,128)(2,1)S(1)}) custom-call(bf16[1536,1536]{1,0:T(8,128)(2,1)} %pw_ref.11, bf16[1536,512]{1,0:T(8,128)(2,1)} %cot_ref.1, bf16[384,2048]{1,0:T(8,128)(2,1)} %x_ref.9), custom_call_target="tpu_custom_call" | custom-call | tf_op jit(solution)/shard_map/upstream/pallas_call | solution.py:19
  6.9 1.6 %collective-permute-start.1 = (bf16[384,512]{1,0:T(8,128)(2,1)S(1)}, bf16[384,512]{1,0:T(8,128)(2,1)S(1)}, u32[]{:S(2)}, u32[]{:S(2)}) collective-permute-start(bf16[384,512]{1,0:T(8,128)(2,1)S(1)} %get-tuple-element.37), channel_id=1, source_target_pairs={{0,2},{1,3},{2,0},{3,1},{4,6},{5,7},{6,4},{7,5},{8,10},{9,11},{10,... | collective-permute-start | bytes 1179656 | tf_op jit(solution)/shard_map/ppermute | solution.py:378
  8.5 2.0 %upstream.4 = (bf16[384,512]{1,0:T(8,128)(2,1)S(1)}, bf16[384,512]{1,0:T(8,128)(2,1)S(1)}) custom-call(bf16[1536,1536]{1,0:T(8,128)(2,1)} %pw_ref.11, bf16[1536,512]{1,0:T(8,128)(2,1)S(1)} %get-tuple-element.34.cot_ref, bf16[384,2048]{1,0:T(8,128)(2,1)} %x_ref.9), custom_call_target="tpu_custom_call" | custom-call | tf_op jit(solution)/shard_map/upstream/pallas_call | solution.py:19
  10.5 0.7 %collective-permute-start = (bf16[384,512]{1,0:T(8,128)(2,1)S(1)}, bf16[384,512]{1,0:T(8,128)(2,1)S(1)}, u32[]{:S(2)}, u32[]{:S(2)}) collective-permute-start(bf16[384,512]{1,0:T(8,128)(2,1)S(1)} %get-tuple-element.35), channel_id=1, source_target_pairs={{4,8},{12,16},{20,24},{8,4},{16,12},{24,20},{5,9},{13,17},{21,25},... | collective-permute-start | bytes 1179656 | tf_op jit(solution)/shard_map/ppermute | solution.py:384
  11.2 0.1 collective-permute-start.6
  11.3 2.8 %upstream.5 = (bf16[384,512]{1,0:T(8,128)(2,1)S(1)}, bf16[384,512]{1,0:T(8,128)(2,1)S(1)}) custom-call(bf16[1536,1536]{1,0:T(8,128)(2,1)} %pw_ref.11, bf16[1536,512]{1,0:T(8,128)(2,1)S(1)} %get-tuple-element.34.cot_ref, bf16[384,2048]{1,0:T(8,128)(2,1)} %x_ref.9), custom_call_target="tpu_custom_call" | custom-call | tf_op jit(solution)/shard_map/upstream/pallas_call | solution.py:19
  14.1 0.7 %collective-permute-start.7 = (bf16[384,512]{1,0:T(8,128)(2,1)S(1)}, bf16[384,512]{1,0:T(8,128)(2,1)S(1)}, u32[]{:S(2)}, u32[]{:S(2)}) collective-permute-start(bf16[384,512]{1,0:T(8,128)(2,1)S(1)} %get-tuple-element.57), channel_id=1, source_target_pairs={{0,1},{1,0},{2,3},{3,2},{4,5},{5,4},{6,7},{7,6},{8,9},{9,8},{10,11... | collective-permute-start | bytes 1179656 | tf_op jit(solution)/shard_map/ppermute | solution.py:378
  14.8 3.3 %interior.1 = (bf16[384,512]{1,0:T(8,128)(2,1)S(1)}, bf16[384,512]{1,0:T(8,128)(2,1)S(1)}, bf16[384,512]{1,0:T(8,128)(2,1)S(1)}, bf16[384,512]{1,0:T(8,128)(2,1)...) custom-call(bf16[384,2048]{1,0:T(8,128)(2,1)} %x_ref.9, ...), custom_call_target="tpu_custom_call" | custom-call | tf_op jit(solution)/shard_map/interior/pallas_call | solution.py:19
  18.1 0.0 collective-permute-done.2.refs_1_
  18.1 0.9 %collective-permute-done.1.refs_0_.rest_0_ = bf16[384,512]{1,0:T(8,128)(2,1)S(1)} collective-permute-done((bf16[384,512]{1,0:T(8,128)(2,1)S(1)}, bf16[384,512]{1,0:T(8,128)(2,1)S(1)}, u32[]{:S(2)}, u32[]{:S(2)}) %collective-permute-start.1) | collective-permute-done | bytes 393248 | tf_op jit(solution)/shard_map/ppermute | solution.py:378
  19.0 0.8 %near_end.1 = (bf16[384,512]{1,0:T(8,128)(2,1)S(1)}, bf16[384,512]{1,0:T(8,128)(2,1)S(1)}, bf16[384,512]{1,0:T(8,128)(2,1)S(1)}, bf16[384,512]{1,0:T(8,128)(2,1)...) custom-call(bf16[384,512]{1,0:T(8,128)(2,1)S(1)} %collective-permute, ...), custom_call_target="tpu_custom_call", output_to_operand_aliasing={{0}: (3, {}), {1}: (4, {}), {2}: (5, {}), {3}: (6, {}), {4}... | custom-call | tf_op jit(solution)/shard_map/near_end/pallas_call | solution.py:19
  19.7 0.0 collective-permute-done.refs_0_
  19.8 0.0 slice-start.1
  19.8 0.8 %far_end.1 = (bf16[384,512]{1,0:T(8,128)(2,1)S(1)}, bf16[384,512]{1,0:T(8,128)(2,1)S(1)}, bf16[384,512]{1,0:T(8,128)(2,1)S(1)}, bf16[384,512]{1,0:T(8,128)(2,1)S...) custom-call(bf16[384,512]{1,0:T(8,128)(2,1)S(1)} %collective-permute, ...), custom_call_target="tpu_custom_call", output_to_operand_aliasing={{0}: (2, {}), {1}: (3, {}), {2}: (4, {}), {3}: (5, {}), {4}... | custom-call | tf_op jit(solution)/shard_map/far_end/pallas_call | solution.py:19
  20.6 0.1 collective-permute-start.3
  20.6 4.1 %collective-permute-start.4 = (bf16[384,512]{1,0:T(8,128)(2,1)S(1)}, bf16[384,512]{1,0:T(8,128)(2,1)S(1)}, u32[]{:S(2)}, u32[]{:S(2)}) collective-permute-start(bf16[384,512]{1,0:T(8,128)(2,1)S(1)} %get-tuple-element.52), channel_id=1, source_target_pairs={{0,2},{1,3},{2,0},{3,1},{4,6},{5,7},{6,4},{7,5},{8,10},{9,11},{10,... | collective-permute-start | bytes 1179656 | tf_op jit(solution)/shard_map/ppermute | solution.py:378
  24.7 0.1 collective-permute-start.5
  24.8 0.2 collective-permute-done.6.refs_0_
  25.0 0.0 collective-permute-done.7.rest_2_
  25.0 0.6 %grad_conv.1 = (bf16[384,2048]{1,0:T(8,128)(2,1)S(1)}, bf16[384,512]{1,0:T(8,128)(2,1)S(1)}, bf16[384,512]{1,0:T(8,128)(2,1)S(1)}) custom-call(f32[384,2048]{1,0:T(8,128)S(1)} %get-tuple-element.55.slope_ref, bf16[384,512]{1,0:T(8,128)(2,1)S(1)} %collective-permute-done.1.refs_0_.rest_0_, bf16[384,512]{1,0:T(8,128)(2,1)S(1)} %arrived.1.rest_1_, ...), custom_call_target="tpu_custom_call" | custom-call | tf_op jit(solution)/shard_map/grad_conv/pallas_call | solution.py:19
  25.6 2.3 %collective-permute-start.8 = (bf16[384,512]{1,0:T(8,128)(2,1)S(1)}, bf16[384,512]{1,0:T(8,128)(2,1)S(1)}, u32[]{:S(2)}, u32[]{:S(2)}) collective-permute-start(bf16[384,512]{1,0:T(8,128)(2,1)S(1)} %get-tuple-element.59), channel_id=1, source_target_pairs={{0,4},{8,12},{16,20},{24,28},{4,0},{12,8},{20,16},{28,24},{1,5},{9... | collective-permute-start | bytes 1179656 | tf_op jit(solution)/shard_map/ppermute | solution.py:384
  27.9 0.9 %collective-permute-start.9 = (bf16[384,512]{1,0:T(8,128)(2,1)S(1)}, bf16[384,512]{1,0:T(8,128)(2,1)S(1)}, u32[]{:S(2)}, u32[]{:S(2)}) collective-permute-start(bf16[384,512]{1,0:T(8,128)(2,1)S(1)} %get-tuple-element.60), channel_id=1, source_target_pairs={{4,8},{12,16},{20,24},{8,4},{16,12},{24,20},{5,9},{13,17},{21,25},... | collective-permute-start | bytes 1179656 | tf_op jit(solution)/shard_map/ppermute | solution.py:384
  28.8 1.7 %back_interior.1 = (bf16[384,2048]{1,0:T(8,128)(2,1)}, f32[384,1024]{1,0:T(8,128)S(1)}) custom-call(bf16[384,2048]{1,0:T(8,128)(2,1)S(1)} %get-tuple-element.61.grad_ref, bf16[3,384,96]{2,1,0:T(8,128)(2,1)S(1)} %get-tuple-element.62.turned_ref), custom_call_target="tpu_custom_call" | custom-call | tf_op jit(solution)/shard_map/back_interior/pallas_call | solution.py:19
  30.5 4.2 %collective-permute-done.4.rest_0_ = bf16[384,512]{1,0:T(8,128)(2,1)S(1)} collective-permute-done((bf16[384,512]{1,0:T(8,128)(2,1)S(1)}, bf16[384,512]{1,0:T(8,128)(2,1)S(1)}, u32[]{:S(2)}, u32[]{:S(2)}) %collective-permute-start.4) | collective-permute-done | bytes 393248 | tf_op jit(solution)/shard_map/ppermute | solution.py:378
  34.7 1.0 %early_mix.1.rest_2_ = f32[1536,512]{1,0:T(8,128)S(1)} custom-call(bf16[1536,1536]{1,0:T(8,128)(2,1)S(1)} %bitcast.2, bf16[384,512]{1,0:T(8,128)(2,1)S(1)} %collective-permute-done.4.rest_0_), custom_call_target="tpu_custom_call" | custom-call | tf_op jit(solution)/shard_map/early_mix/pallas_call | solution.py:19
  35.7 1.8 %half_mix.1.sum_ref = f32[1536,512]{1,0:T(8,128)S(1)} custom-call(bf16[1536,1536]{1,0:T(8,128)(2,1)S(1)} %bitcast.2, bf16[384,512]{1,0:T(8,128)(2,1)S(1)} %collective-permute-done.3.rest_0_, bf16[384,512]{1,0:T(8,128)(2,1)S(1)} %get-tuple-element.51.rest_1_, f32[1536,512]{1,0:T(8,128)S(1)} %early_mix.1.rest_2_), custom_call_target="tpu_custom_call", output_to_operand_aliasing={{}: (3, {})} | custom-call | tf_op jit(solution)/shard_map/half_mix/pallas_call | solution.py:19
  37.5 5.1 %collective-permute-done.5.rest_0_ = bf16[384,512]{1,0:T(8,128)(2,1)S(1)} collective-permute-done((bf16[384,512]{1,0:T(8,128)(2,1)S(1)}, bf16[384,512]{1,0:T(8,128)(2,1)S(1)}, u32[]{:S(2)}, u32[]{:S(2)}) %collective-permute-start.5) | collective-permute-done | bytes 393248 | tf_op jit(solution)/shard_map/ppermute | solution.py:378
  42.6 1.8 %late_mix.1 = (bf16[1536,512]{1,0:T(8,128)(2,1)}, f32[8,128]{1,0:T(8,128)S(1)}) custom-call(bf16[1536,1536]{1,0:T(8,128)(2,1)S(1)} %bitcast.2, f32[1536,512]{1,0:T(8,128)S(1)} %half_mix.1.sum_ref, bf16[384,512]{1,0:T(8,128)(2,1)S(1)} %collective-permute-done.5.rest_0_), custom_call_target="tpu_custom_call" | custom-call | tf_op jit(solution)/shard_map/late_mix/pallas_call | solution.py:19
  44.4 0.7 %collective-permute-done.8.near_ref = bf16[384,512]{1,0:T(8,128)(2,1)S(1)} collective-permute-done((bf16[384,512]{1,0:T(8,128)(2,1)S(1)}, bf16[384,512]{1,0:T(8,128)(2,1)S(1)}, u32[]{:S(2)}, u32[]{:S(2)}) %collective-permute-start.8) | collective-permute-done | bytes 393248 | tf_op jit(solution)/shard_map/ppermute | solution.py:384
  45.0 1.2 %back_ends.1 = bf16[384,2048]{1,0:T(8,128)(2,1)} custom-call(bf16[384,512]{1,0:T(8,128)(2,1)S(1)} %collective-permute-done.8.near_ref, bf16[384,512]{1,0:T(8,128)(2,1)S(1)} %collective-permute-done.9.far_ref, f32[384,1024]{1,0:T(8,128)S(1)} %get-tuple-element.63.ends_ref, ...), custom_call_target="tpu_custom_call", output_to_operand_aliasing={{}: (5, {})} | custom-call | tf_op jit(solution)/shard_map/back_ends/pallas_call | solution.py:19
  (7 shorter events, 0.0 us)
Async XLA Ops:
  1.7 16.5 %collective-permute-start.2 = (bf16[384,512]{1,0:T(8,128)(2,1)S(1)}, bf16[384,512]{1,0:T(8,128)(2,1)S(1)}, u32[]{:S(2)}, u32[]{:S(2)}) collective-permute-start(bf16[384,512]{1,0:T(8,128)(2,1)S(1)} %near_source.1), channel_id=1, source_target_pairs={{0,4},{8,12},{16,20},{24,28},{4,0},{12,8},{20,16},{28,24},{1,5},{9... | collective-permute-start | bytes 1179656 | tf_op jit(solution)/shard_map/ppermute | solution.py:384
  6.9 12.1 %collective-permute-start.1 = (bf16[384,512]{1,0:T(8,128)(2,1)S(1)}, bf16[384,512]{1,0:T(8,128)(2,1)S(1)}, u32[]{:S(2)}, u32[]{:S(2)}) collective-permute-start(bf16[384,512]{1,0:T(8,128)(2,1)S(1)} %get-tuple-element.37), channel_id=1, source_target_pairs={{0,2},{1,3},{2,0},{3,1},{4,6},{5,7},{6,4},{7,5},{8,10},{9,11},{10,... | collective-permute-start | bytes 1179656 | tf_op jit(solution)/shard_map/ppermute | solution.py:378
  10.5 9.2 %collective-permute-start = (bf16[384,512]{1,0:T(8,128)(2,1)S(1)}, bf16[384,512]{1,0:T(8,128)(2,1)S(1)}, u32[]{:S(2)}, u32[]{:S(2)}) collective-permute-start(bf16[384,512]{1,0:T(8,128)(2,1)S(1)} %get-tuple-element.35), channel_id=1, source_target_pairs={{4,8},{12,16},{20,24},{8,4},{16,12},{24,20},{5,9},{13,17},{21,25},... | collective-permute-start | bytes 1179656 | tf_op jit(solution)/shard_map/ppermute | solution.py:384
  11.2 13.8 %collective-permute-start.6 = (bf16[384,512]{1,0:T(8,128)(2,1)S(1)}, bf16[384,512]{1,0:T(8,128)(2,1)S(1)}, u32[]{:S(2)}, u32[]{:S(2)}) collective-permute-start(bf16[384,512]{1,0:T(8,128)(2,1)S(1)} %get-tuple-element.56), channel_id=1, source_target_pairs={{0,3},{1,2},{2,1},{3,0},{4,7},{5,6},{6,5},{7,4},{8,11},{9,10},{10,... | collective-permute-start | bytes 1179656 | tf_op jit(solution)/shard_map/ppermute | solution.py:378
  14.1 10.9 %collective-permute-start.7 = (bf16[384,512]{1,0:T(8,128)(2,1)S(1)}, bf16[384,512]{1,0:T(8,128)(2,1)S(1)}, u32[]{:S(2)}, u32[]{:S(2)}) collective-permute-start(bf16[384,512]{1,0:T(8,128)(2,1)S(1)} %get-tuple-element.57), channel_id=1, source_target_pairs={{0,1},{1,0},{2,3},{3,2},{4,5},{5,4},{6,7},{7,6},{8,9},{9,8},{10,11... | collective-permute-start | bytes 1179656 | tf_op jit(solution)/shard_map/ppermute | solution.py:378
  19.0 15.7 %slice-start = ((s8[4718592]{0:T(1024)(128)(4,1)}), s8[4194304]{0:T(1024)(128)(4,1)S(1)}, s32[]{:S(2)}) async-start(s8[4718592]{0:T(1024)(128)(4,1)} %bitcast.1), calls=%async_computation | async-start | bytes 8388608
  19.8 14.9 %slice-start.1 = ((s8[4718592]{0:T(1024)(128)(4,1)}), s8[524288]{0:T(1024)(128)(4,1)S(1)}, s32[]{:S(2)}) async-start(s8[4718592]{0:T(1024)(128)(4,1)} %bitcast.1), calls=%async_computation.1 | async-start | bytes 1048576
  20.6 15.1 %collective-permute-start.3 = (bf16[384,512]{1,0:T(8,128)(2,1)S(1)}, bf16[384,512]{1,0:T(8,128)(2,1)S(1)}, u32[]{:S(2)}, u32[]{:S(2)}) collective-permute-start(bf16[384,512]{1,0:T(8,128)(2,1)S(1)} %get-tuple-element.50), channel_id=1, source_target_pairs={{0,1},{1,0},{2,3},{3,2},{4,5},{5,4},{6,7},{7,6},{8,9},{9,8},{10,11... | collective-permute-start | bytes 1179656 | tf_op jit(solution)/shard_map/ppermute | solution.py:378
  20.6 14.0 %collective-permute-start.4 = (bf16[384,512]{1,0:T(8,128)(2,1)S(1)}, bf16[384,512]{1,0:T(8,128)(2,1)S(1)}, u32[]{:S(2)}, u32[]{:S(2)}) collective-permute-start(bf16[384,512]{1,0:T(8,128)(2,1)S(1)} %get-tuple-element.52), channel_id=1, source_target_pairs={{0,2},{1,3},{2,0},{3,1},{4,6},{5,7},{6,4},{7,5},{8,10},{9,11},{10,... | collective-permute-start | bytes 1179656 | tf_op jit(solution)/shard_map/ppermute | solution.py:378
  24.7 17.9 %collective-permute-start.5 = (bf16[384,512]{1,0:T(8,128)(2,1)S(1)}, bf16[384,512]{1,0:T(8,128)(2,1)S(1)}, u32[]{:S(2)}, u32[]{:S(2)}) collective-permute-start(bf16[384,512]{1,0:T(8,128)(2,1)S(1)} %get-tuple-element.53), channel_id=1, source_target_pairs={{0,3},{1,2},{2,1},{3,0},{4,7},{5,6},{6,5},{7,4},{8,11},{9,10},{10,... | collective-permute-start | bytes 1179656 | tf_op jit(solution)/shard_map/ppermute | solution.py:378
  25.6 19.4 %collective-permute-start.8 = (bf16[384,512]{1,0:T(8,128)(2,1)S(1)}, bf16[384,512]{1,0:T(8,128)(2,1)S(1)}, u32[]{:S(2)}, u32[]{:S(2)}) collective-permute-start(bf16[384,512]{1,0:T(8,128)(2,1)S(1)} %get-tuple-element.59), channel_id=1, source_target_pairs={{0,4},{8,12},{16,20},{24,28},{4,0},{12,8},{20,16},{28,24},{1,5},{9... | collective-permute-start | bytes 1179656 | tf_op jit(solution)/shard_map/ppermute | solution.py:384
  27.9 17.1 %collective-permute-start.9 = (bf16[384,512]{1,0:T(8,128)(2,1)S(1)}, bf16[384,512]{1,0:T(8,128)(2,1)S(1)}, u32[]{:S(2)}, u32[]{:S(2)}) collective-permute-start(bf16[384,512]{1,0:T(8,128)(2,1)S(1)} %get-tuple-element.60), channel_id=1, source_target_pairs={{4,8},{12,16},{20,24},{8,4},{16,12},{24,20},{5,9},{13,17},{21,25},... | collective-permute-start | bytes 1179656 | tf_op jit(solution)/shard_map/ppermute | solution.py:384

commit v19 on v18

--- a/solution.py
+++ b/solution.py
@@ -176,7 +176,7 @@
                 for rows in groups:
                     active, slope = gelu_and_slope(convolve(plain_ref, rows, wide, base + s, halo, unit))
                     active_refs[k][rows, s:s + unit] = active.astype(BF16)
-                    slope_ref[rows, lanes(base + s, unit)] = slope
+                    slope_ref[rows, lanes(base + s, unit)] = slope.astype(BF16)
 
 
 def interior(inputs, weight, n):
@@ -184,7 +184,7 @@
     group = weight.shape[1]
     block = length // n
     outs = [((channels, block), BF16, True)] * n
-    outs += [((channels, length), F32, True), ((channels, length + 2 * DILATION_STEP), BF16, True)]
+    outs += [((channels, length), BF16, True), ((channels, length + 2 * DILATION_STEP), BF16, True)]
     outs += [((3, channels, group), BF16, True)] * 2
     results = kernel_call(
         "interior", functools.partial(interior_kernel, n), [(inputs, False), (weight, False)], outs,
@@ -215,7 +215,7 @@
                 for rows in groups:
                     active, slope = gelu_and_slope(convolve(plain_ref, rows, wide, base + s, halo, unit))
                     active_refs[k][rows, s:s + unit] = active.astype(BF16)
-                    slope_ref[rows, lanes(base + s, unit)] = slope
+                    slope_ref[rows, lanes(base + s, unit)] = slope.astype(BF16)
 
 
 def one_end(near, halo, plain, active, slope, wide, waited):
@@ -235,10 +235,20 @@
     length, halo = grad_ref.shape[1], near_out.shape[1]
     block = up_refs[0].shape[1]
     for k, up_ref in zip(order, up_refs):
-        here = lanes((ch ^ k) * block, block)
-        grad_ref[:, here] = (up_ref[...].astype(F32) * slope_ref[:, here]).astype(BF16)
-    near_out[...] = grad_ref[:, lanes((1 - odd) * (length - halo), halo)]
-    far_out[...] = grad_ref[:, lanes(odd * (length - halo), halo)]
+        base = (ch ^ k) * block
+
+        def product(end_ref=None, first=0, base=base, up_ref=up_ref):
+            for g in range(0, up_ref.shape[0], 16):
+                rows = slice(g, g + 16)
+                value = up_ref[rows, :].astype(F32) * slope_ref[rows, lanes(base, block)].astype(F32)
+                grad_ref[rows, lanes(base, block)] = value.astype(BF16)
+                if end_ref is not None:
+                    end_ref[rows, lanes(base - first, block)] = value.astype(BF16)
+
+        inside = (base >= halo) & (base < length - halo)
+        pl.when(inside)(product)
+        for end_ref, first in ((near_out, (1 - odd) * (length - halo)), (far_out, odd * (length - halo))):
+            pl.when((base >= first) & (base < first + halo))(functools.partial(product, end_ref, first))
 
 
 def grad_conv(slope, order, ups):

time: 46.9 us -> 47 us (level)
  no operation moved by 1% of the time
where the time goes in v19:
time: 47 us; the launch traced here: 46.4 us
  Pallas kernels  21 us (45%)
  starting transfers between devices  13.3 us (28%)
  waiting for transfers between devices  11.1 us (24%)
  between operations  0.95 us (2%)
    pallas_call x14, Pallas kernels, kernel_call(): pl.pallas_call(kernel, in_specs=[INSIDE if held else ANY for _, held in o...  21 us
    ppermute x6, waiting for transfers between devices, exchange(): lax.ppermute(piece, 'ch', [(i, i ^ k) for i in range(lax.axis_size('ch'))])  10.5 us
    ppermute x4, starting transfers between devices, swap(): return lax.ppermute(values, 'ctx', pairs + [(b, a) for a, b in pairs])  6.73 us
    ppermute x6, starting transfers between devices, exchange(): lax.ppermute(piece, 'ch', [(i, i ^ k) for i in range(lax.axis_size('ch'))])  6.54 us
  transfers between devices with their start and end apart: 10, of which 5 were waited for; matrix products, arithmetic and copies ran while one was open for 0% of the time, Pallas kernels for 41%

profile of v19, /device:TPU:0, one launch (start us, length us, event | category | flops | bytes accessed | tf_op | source)
XLA Modules:
  0.0 46.4 jit_solution(4865324973346136123)
XLA Ops:
  0.6 1.0 %near_source.1 = bf16[384,512]{1,0:T(8,128)(2,1)S(1)} custom-call(bf16[384,2048]{1,0:T(8,128)(2,1)} %x_ref.9), custom_call_target="tpu_custom_call" | custom-call | tf_op jit(solution)/shard_map/near_source/pallas_call | solution.py:19
  1.7 3.0 %collective-permute-start.2 = (bf16[384,512]{1,0:T(8,128)(2,1)S(1)}, bf16[384,512]{1,0:T(8,128)(2,1)S(1)}, u32[]{:S(2)}, u32[]{:S(2)}) collective-permute-start(bf16[384,512]{1,0:T(8,128)(2,1)S(1)} %near_source.1), channel_id=1, source_target_pairs={{0,4},{8,12},{16,20},{24,28},{4,0},{12,8},{20,16},{28,24},{1,5},{9... | collective-permute-start | bytes 1179656 | tf_op jit(solution)/shard_map/ppermute | solution.py:394
  4.7 2.2 %upstream.3 = (bf16[384,512]{1,0:T(8,128)(2,1)S(1)}, bf16[1536,512]{1,0:T(8,128)(2,1)S(1)}) custom-call(bf16[1536,1536]{1,0:T(8,128)(2,1)} %pw_ref.11, bf16[1536,512]{1,0:T(8,128)(2,1)} %cot_ref.1, bf16[384,2048]{1,0:T(8,128)(2,1)} %x_ref.9), custom_call_target="tpu_custom_call" | custom-call | tf_op jit(solution)/shard_map/upstream/pallas_call | solution.py:19
  6.9 1.6 %collective-permute-start.1 = (bf16[384,512]{1,0:T(8,128)(2,1)S(1)}, bf16[384,512]{1,0:T(8,128)(2,1)S(1)}, u32[]{:S(2)}, u32[]{:S(2)}) collective-permute-start(bf16[384,512]{1,0:T(8,128)(2,1)S(1)} %get-tuple-element.37), channel_id=1, source_target_pairs={{0,2},{1,3},{2,0},{3,1},{4,6},{5,7},{6,4},{7,5},{8,10},{9,11},{10,... | collective-permute-start | bytes 1179656 | tf_op jit(solution)/shard_map/ppermute | solution.py:388
  8.5 2.0 %upstream.4 = (bf16[384,512]{1,0:T(8,128)(2,1)S(1)}, bf16[384,512]{1,0:T(8,128)(2,1)S(1)}) custom-call(bf16[1536,1536]{1,0:T(8,128)(2,1)} %pw_ref.11, bf16[1536,512]{1,0:T(8,128)(2,1)S(1)} %get-tuple-element.34.cot_ref, bf16[384,2048]{1,0:T(8,128)(2,1)} %x_ref.9), custom_call_target="tpu_custom_call" | custom-call | tf_op jit(solution)/shard_map/upstream/pallas_call | solution.py:19
  10.5 0.7 %collective-permute-start = (bf16[384,512]{1,0:T(8,128)(2,1)S(1)}, bf16[384,512]{1,0:T(8,128)(2,1)S(1)}, u32[]{:S(2)}, u32[]{:S(2)}) collective-permute-start(bf16[384,512]{1,0:T(8,128)(2,1)S(1)} %get-tuple-element.35), channel_id=1, source_target_pairs={{4,8},{12,16},{20,24},{8,4},{16,12},{24,20},{5,9},{13,17},{21,25},... | collective-permute-start | bytes 1179656 | tf_op jit(solution)/shard_map/ppermute | solution.py:394
  11.2 0.1 collective-permute-start.6
  11.3 2.8 %upstream.5 = (bf16[384,512]{1,0:T(8,128)(2,1)S(1)}, bf16[384,512]{1,0:T(8,128)(2,1)S(1)}) custom-call(bf16[1536,1536]{1,0:T(8,128)(2,1)} %pw_ref.11, bf16[1536,512]{1,0:T(8,128)(2,1)S(1)} %get-tuple-element.34.cot_ref, bf16[384,2048]{1,0:T(8,128)(2,1)} %x_ref.9), custom_call_target="tpu_custom_call" | custom-call | tf_op jit(solution)/shard_map/upstream/pallas_call | solution.py:19
  14.1 0.7 %collective-permute-start.7 = (bf16[384,512]{1,0:T(8,128)(2,1)S(1)}, bf16[384,512]{1,0:T(8,128)(2,1)S(1)}, u32[]{:S(2)}, u32[]{:S(2)}) collective-permute-start(bf16[384,512]{1,0:T(8,128)(2,1)S(1)} %get-tuple-element.57), channel_id=1, source_target_pairs={{0,1},{1,0},{2,3},{3,2},{4,5},{5,4},{6,7},{7,6},{8,9},{9,8},{10,11... | collective-permute-start | bytes 1179656 | tf_op jit(solution)/shard_map/ppermute | solution.py:388
  14.8 3.4 %interior.1 = (bf16[384,512]{1,0:T(8,128)(2,1)S(1)}, bf16[384,512]{1,0:T(8,128)(2,1)S(1)}, bf16[384,512]{1,0:T(8,128)(2,1)S(1)}, bf16[384,512]{1,0:T(8,128)(2,1)...) custom-call(bf16[384,2048]{1,0:T(8,128)(2,1)} %x_ref.9, ...), custom_call_target="tpu_custom_call" | custom-call | tf_op jit(solution)/shard_map/interior/pallas_call | solution.py:19
  18.2 0.0 collective-permute-done.2.refs_1_
  18.2 0.8 %collective-permute-done.1.refs_0_.rest_0_ = bf16[384,512]{1,0:T(8,128)(2,1)S(1)} collective-permute-done((bf16[384,512]{1,0:T(8,128)(2,1)S(1)}, bf16[384,512]{1,0:T(8,128)(2,1)S(1)}, u32[]{:S(2)}, u32[]{:S(2)}) %collective-permute-start.1) | collective-permute-done | bytes 393248 | tf_op jit(solution)/shard_map/ppermute | solution.py:388
  19.0 0.8 %near_end.1 = (bf16[384,512]{1,0:T(8,128)(2,1)S(1)}, bf16[384,512]{1,0:T(8,128)(2,1)S(1)}, bf16[384,512]{1,0:T(8,128)(2,1)S(1)}, bf16[384,512]{1,0:T(8,128)(2,1)...) custom-call(bf16[384,512]{1,0:T(8,128)(2,1)S(1)} %collective-permute, ...), custom_call_target="tpu_custom_call", output_to_operand_aliasing={{0}: (3, {}), {1}: (4, {}), {2}: (5, {}), {3}: (6, {}), {4}... | custom-call | tf_op jit(solution)/shard_map/near_end/pallas_call | solution.py:19
  19.8 0.0 collective-permute-done.refs_0_
  19.8 0.0 slice-start.1
  19.8 0.8 %far_end.1 = (bf16[384,512]{1,0:T(8,128)(2,1)S(1)}, bf16[384,512]{1,0:T(8,128)(2,1)S(1)}, bf16[384,512]{1,0:T(8,128)(2,1)S(1)}, bf16[384,512]{1,0:T(8,128)(2,1)S...) custom-call(bf16[384,512]{1,0:T(8,128)(2,1)S(1)} %collective-permute, ...), custom_call_target="tpu_custom_call", output_to_operand_aliasing={{0}: (2, {}), {1}: (3, {}), {2}: (4, {}), {3}: (5, {}), {4}... | custom-call | tf_op jit(solution)/shard_map/far_end/pallas_call | solution.py:19
  20.6 0.1 collective-permute-start.3
  20.7 4.1 %collective-permute-start.4 = (bf16[384,512]{1,0:T(8,128)(2,1)S(1)}, bf16[384,512]{1,0:T(8,128)(2,1)S(1)}, u32[]{:S(2)}, u32[]{:S(2)}) collective-permute-start(bf16[384,512]{1,0:T(8,128)(2,1)S(1)} %get-tuple-element.52), channel_id=1, source_target_pairs={{0,2},{1,3},{2,0},{3,1},{4,6},{5,7},{6,4},{7,5},{8,10},{9,11},{10,... | collective-permute-start | bytes 1179656 | tf_op jit(solution)/shard_map/ppermute | solution.py:388
  24.7 0.1 collective-permute-start.5
  24.8 0.2 collective-permute-done.6.refs_0_
  25.0 0.0 collective-permute-done.7.rest_2_
  25.0 0.6 %grad_conv.1 = (bf16[384,2048]{1,0:T(8,128)(2,1)S(1)}, bf16[384,512]{1,0:T(8,128)(2,1)S(1)}, bf16[384,512]{1,0:T(8,128)(2,1)S(1)}) custom-call(bf16[384,2048]{1,0:T(8,128)(2,1)S(1)} %get-tuple-element.55.slope_ref, bf16[384,512]{1,0:T(8,128)(2,1)S(1)} %collective-permute-done.1.refs_0_.rest_0_, bf16[384,512]{1,0:T(8,128)(2,1)S(1)} %arrived.1.rest_1_, ...), custom_call_target="tpu_custom_call" | custom-call | tf_op jit(solution)/shard_map/grad_conv/pallas_call | solution.py:19
  25.6 2.4 %collective-permute-start.8 = (bf16[384,512]{1,0:T(8,128)(2,1)S(1)}, bf16[384,512]{1,0:T(8,128)(2,1)S(1)}, u32[]{:S(2)}, u32[]{:S(2)}) collective-permute-start(bf16[384,512]{1,0:T(8,128)(2,1)S(1)} %get-tuple-element.59), channel_id=1, source_target_pairs={{0,4},{8,12},{16,20},{24,28},{4,0},{12,8},{20,16},{28,24},{1,5},{9... | collective-permute-start | bytes 1179656 | tf_op jit(solution)/shard_map/ppermute | solution.py:394
  28.0 0.7 %collective-permute-start.9 = (bf16[384,512]{1,0:T(8,128)(2,1)S(1)}, bf16[384,512]{1,0:T(8,128)(2,1)S(1)}, u32[]{:S(2)}, u32[]{:S(2)}) collective-permute-start(bf16[384,512]{1,0:T(8,128)(2,1)S(1)} %get-tuple-element.60), channel_id=1, source_target_pairs={{4,8},{12,16},{20,24},{8,4},{16,12},{24,20},{5,9},{13,17},{21,25},... | collective-permute-start | bytes 1179656 | tf_op jit(solution)/shard_map/ppermute | solution.py:394
  28.6 1.7 %back_interior.1 = (bf16[384,2048]{1,0:T(8,128)(2,1)}, f32[384,1024]{1,0:T(8,128)S(1)}) custom-call(bf16[384,2048]{1,0:T(8,128)(2,1)S(1)} %get-tuple-element.61.grad_ref, bf16[3,384,96]{2,1,0:T(8,128)(2,1)S(1)} %get-tuple-element.62.turned_ref), custom_call_target="tpu_custom_call" | custom-call | tf_op jit(solution)/shard_map/back_interior/pallas_call | solution.py:19
  30.3 4.4 %collective-permute-done.4.rest_0_ = bf16[384,512]{1,0:T(8,128)(2,1)S(1)} collective-permute-done((bf16[384,512]{1,0:T(8,128)(2,1)S(1)}, bf16[384,512]{1,0:T(8,128)(2,1)S(1)}, u32[]{:S(2)}, u32[]{:S(2)}) %collective-permute-start.4) | collective-permute-done | bytes 393248 | tf_op jit(solution)/shard_map/ppermute | solution.py:388
  34.7 1.0 %early_mix.1.rest_2_ = f32[1536,512]{1,0:T(8,128)S(1)} custom-call(bf16[1536,1536]{1,0:T(8,128)(2,1)S(1)} %bitcast.2, bf16[384,512]{1,0:T(8,128)(2,1)S(1)} %collective-permute-done.4.rest_0_), custom_call_target="tpu_custom_call" | custom-call | tf_op jit(solution)/shard_map/early_mix/pallas_call | solution.py:19
  35.7 1.8 %half_mix.1.sum_ref = f32[1536,512]{1,0:T(8,128)S(1)} custom-call(bf16[1536,1536]{1,0:T(8,128)(2,1)S(1)} %bitcast.2, bf16[384,512]{1,0:T(8,128)(2,1)S(1)} %collective-permute-done.3.rest_0_, bf16[384,512]{1,0:T(8,128)(2,1)S(1)} %get-tuple-element.51.rest_1_, f32[1536,512]{1,0:T(8,128)S(1)} %early_mix.1.rest_2_), custom_call_target="tpu_custom_call", output_to_operand_aliasing={{}: (3, {})} | custom-call | tf_op jit(solution)/shard_map/half_mix/pallas_call | solution.py:19
  37.5 5.1 %collective-permute-done.5.rest_0_ = bf16[384,512]{1,0:T(8,128)(2,1)S(1)} collective-permute-done((bf16[384,512]{1,0:T(8,128)(2,1)S(1)}, bf16[384,512]{1,0:T(8,128)(2,1)S(1)}, u32[]{:S(2)}, u32[]{:S(2)}) %collective-permute-start.5) | collective-permute-done | bytes 393248 | tf_op jit(solution)/shard_map/ppermute | solution.py:388
  42.6 1.8 %late_mix.1 = (bf16[1536,512]{1,0:T(8,128)(2,1)}, f32[8,128]{1,0:T(8,128)S(1)}) custom-call(bf16[1536,1536]{1,0:T(8,128)(2,1)S(1)} %bitcast.2, f32[1536,512]{1,0:T(8,128)S(1)} %half_mix.1.sum_ref, bf16[384,512]{1,0:T(8,128)(2,1)S(1)} %collective-permute-done.5.rest_0_), custom_call_target="tpu_custom_call" | custom-call | tf_op jit(solution)/shard_map/late_mix/pallas_call | solution.py:19
  44.4 0.7 %collective-permute-done.8.near_ref = bf16[384,512]{1,0:T(8,128)(2,1)S(1)} collective-permute-done((bf16[384,512]{1,0:T(8,128)(2,1)S(1)}, bf16[384,512]{1,0:T(8,128)(2,1)S(1)}, u32[]{:S(2)}, u32[]{:S(2)}) %collective-permute-start.8) | collective-permute-done | bytes 393248 | tf_op jit(solution)/shard_map/ppermute | solution.py:394
  45.1 1.2 %back_ends.1 = bf16[384,2048]{1,0:T(8,128)(2,1)} custom-call(bf16[384,512]{1,0:T(8,128)(2,1)S(1)} %collective-permute-done.8.near_ref, bf16[384,512]{1,0:T(8,128)(2,1)S(1)} %collective-permute-done.9.far_ref, f32[384,1024]{1,0:T(8,128)S(1)} %get-tuple-element.63.ends_ref, ...), custom_call_target="tpu_custom_call", output_to_operand_aliasing={{}: (5, {})} | custom-call | tf_op jit(solution)/shard_map/back_ends/pallas_call | solution.py:19
  (7 shorter events, 0.0 us)
Async XLA Ops:
  1.7 16.5 %collective-permute-start.2 = (bf16[384,512]{1,0:T(8,128)(2,1)S(1)}, bf16[384,512]{1,0:T(8,128)(2,1)S(1)}, u32[]{:S(2)}, u32[]{:S(2)}) collective-permute-start(bf16[384,512]{1,0:T(8,128)(2,1)S(1)} %near_source.1), channel_id=1, source_target_pairs={{0,4},{8,12},{16,20},{24,28},{4,0},{12,8},{20,16},{28,24},{1,5},{9... | collective-permute-start | bytes 1179656 | tf_op jit(solution)/shard_map/ppermute | solution.py:394
  6.9 12.1 %collective-permute-start.1 = (bf16[384,512]{1,0:T(8,128)(2,1)S(1)}, bf16[384,512]{1,0:T(8,128)(2,1)S(1)}, u32[]{:S(2)}, u32[]{:S(2)}) collective-permute-start(bf16[384,512]{1,0:T(8,128)(2,1)S(1)} %get-tuple-element.37), channel_id=1, source_target_pairs={{0,2},{1,3},{2,0},{3,1},{4,6},{5,7},{6,4},{7,5},{8,10},{9,11},{10,... | collective-permute-start | bytes 1179656 | tf_op jit(solution)/shard_map/ppermute | solution.py:388
  10.5 9.3 %collective-permute-start = (bf16[384,512]{1,0:T(8,128)(2,1)S(1)}, bf16[384,512]{1,0:T(8,128)(2,1)S(1)}, u32[]{:S(2)}, u32[]{:S(2)}) collective-permute-start(bf16[384,512]{1,0:T(8,128)(2,1)S(1)} %get-tuple-element.35), channel_id=1, source_target_pairs={{4,8},{12,16},{20,24},{8,4},{16,12},{24,20},{5,9},{13,17},{21,25},... | collective-permute-start | bytes 1179656 | tf_op jit(solution)/shard_map/ppermute | solution.py:394
  11.2 13.8 %collective-permute-start.6 = (bf16[384,512]{1,0:T(8,128)(2,1)S(1)}, bf16[384,512]{1,0:T(8,128)(2,1)S(1)}, u32[]{:S(2)}, u32[]{:S(2)}) collective-permute-start(bf16[384,512]{1,0:T(8,128)(2,1)S(1)} %get-tuple-element.56), channel_id=1, source_target_pairs={{0,3},{1,2},{2,1},{3,0},{4,7},{5,6},{6,5},{7,4},{8,11},{9,10},{10,... | collective-permute-start | bytes 1179656 | tf_op jit(solution)/shard_map/ppermute | solution.py:388
  14.1 10.9 %collective-permute-start.7 = (bf16[384,512]{1,0:T(8,128)(2,1)S(1)}, bf16[384,512]{1,0:T(8,128)(2,1)S(1)}, u32[]{:S(2)}, u32[]{:S(2)}) collective-permute-start(bf16[384,512]{1,0:T(8,128)(2,1)S(1)} %get-tuple-element.57), channel_id=1, source_target_pairs={{0,1},{1,0},{2,3},{3,2},{4,5},{5,4},{6,7},{7,6},{8,9},{9,8},{10,11... | collective-permute-start | bytes 1179656 | tf_op jit(solution)/shard_map/ppermute | solution.py:388
  19.0 15.7 %slice-start = ((s8[4718592]{0:T(1024)(128)(4,1)}), s8[4194304]{0:T(1024)(128)(4,1)S(1)}, s32[]{:S(2)}) async-start(s8[4718592]{0:T(1024)(128)(4,1)} %bitcast.1), calls=%async_computation | async-start | bytes 8388608
  19.8 14.9 %slice-start.1 = ((s8[4718592]{0:T(1024)(128)(4,1)}), s8[524288]{0:T(1024)(128)(4,1)S(1)}, s32[]{:S(2)}) async-start(s8[4718592]{0:T(1024)(128)(4,1)} %bitcast.1), calls=%async_computation.1 | async-start | bytes 1048576
  20.6 15.1 %collective-permute-start.3 = (bf16[384,512]{1,0:T(8,128)(2,1)S(1)}, bf16[384,512]{1,0:T(8,128)(2,1)S(1)}, u32[]{:S(2)}, u32[]{:S(2)}) collective-permute-start(bf16[384,512]{1,0:T(8,128)(2,1)S(1)} %get-tuple-element.50), channel_id=1, source_target_pairs={{0,1},{1,0},{2,3},{3,2},{4,5},{5,4},{6,7},{7,6},{8,9},{9,8},{10,11... | collective-permute-start | bytes 1179656 | tf_op jit(solution)/shard_map/ppermute | solution.py:388
  20.7 14.0 %collective-permute-start.4 = (bf16[384,512]{1,0:T(8,128)(2,1)S(1)}, bf16[384,512]{1,0:T(8,128)(2,1)S(1)}, u32[]{:S(2)}, u32[]{:S(2)}) collective-permute-start(bf16[384,512]{1,0:T(8,128)(2,1)S(1)} %get-tuple-element.52), channel_id=1, source_target_pairs={{0,2},{1,3},{2,0},{3,1},{4,6},{5,7},{6,4},{7,5},{8,10},{9,11},{10,... | collective-permute-start | bytes 1179656 | tf_op jit(solution)/shard_map/ppermute | solution.py:388
  24.7 17.9 %collective-permute-start.5 = (bf16[384,512]{1,0:T(8,128)(2,1)S(1)}, bf16[384,512]{1,0:T(8,128)(2,1)S(1)}, u32[]{:S(2)}, u32[]{:S(2)}) collective-permute-start(bf16[384,512]{1,0:T(8,128)(2,1)S(1)} %get-tuple-element.53), channel_id=1, source_target_pairs={{0,3},{1,2},{2,1},{3,0},{4,7},{5,6},{6,5},{7,4},{8,11},{9,10},{10,... | collective-permute-start | bytes 1179656 | tf_op jit(solution)/shard_map/ppermute | solution.py:388
  25.6 19.5 %collective-permute-start.8 = (bf16[384,512]{1,0:T(8,128)(2,1)S(1)}, bf16[384,512]{1,0:T(8,128)(2,1)S(1)}, u32[]{:S(2)}, u32[]{:S(2)}) collective-permute-start(bf16[384,512]{1,0:T(8,128)(2,1)S(1)} %get-tuple-element.59), channel_id=1, source_target_pairs={{0,4},{8,12},{16,20},{24,28},{4,0},{12,8},{20,16},{28,24},{1,5},{9... | collective-permute-start | bytes 1179656 | tf_op jit(solution)/shard_map/ppermute | solution.py:394
  28.0 17.1 %collective-permute-start.9 = (bf16[384,512]{1,0:T(8,128)(2,1)S(1)}, bf16[384,512]{1,0:T(8,128)(2,1)S(1)}, u32[]{:S(2)}, u32[]{:S(2)}) collective-permute-start(bf16[384,512]{1,0:T(8,128)(2,1)S(1)} %get-tuple-element.60), channel_id=1, source_target_pairs={{4,8},{12,16},{20,24},{8,4},{16,12},{24,20},{5,9},{13,17},{21,25},... | collective-permute-start | bytes 1179656 | tf_op jit(solution)/shard_map/ppermute | solution.py:394

commit v20 on v18

--- a/solution.py
+++ b/solution.py
@@ -234,11 +234,16 @@
     ch, odd = lax.axis_index("ch"), odd_place()
     length, halo = grad_ref.shape[1], near_out.shape[1]
     block = up_refs[0].shape[1]
-    for k, up_ref in zip(order, up_refs):
-        here = lanes((ch ^ k) * block, block)
-        grad_ref[:, here] = (up_ref[...].astype(F32) * slope_ref[:, here]).astype(BF16)
-    near_out[...] = grad_ref[:, lanes((1 - odd) * (length - halo), halo)]
-    far_out[...] = grad_ref[:, lanes(odd * (length - halo), halo)]
+    step = 32
+
+    @pl.loop(0, grad_ref.shape[0] // step)
+    def _(i):
+        rows = pl.ds(pl.multiple_of(i * step, step), step)
+        for k, up_ref in zip(order, up_refs):
+            here = lanes((ch ^ k) * block, block)
+            grad_ref[rows, here] = (up_ref[rows, :].astype(F32) * slope_ref[rows, here]).astype(BF16)
+        near_out[rows, :] = grad_ref[rows, lanes((1 - odd) * (length - halo), halo)]
+        far_out[rows, :] = grad_ref[rows, lanes(odd * (length - halo), halo)]
 
 
 def grad_conv(slope, order, ups):
@@ -309,8 +314,10 @@
 def back_end(halo_ref, ends_ref, turned_ref, at_end, held):
     channels, halo = halo_ref.shape
     group, unit = turned_ref.shape[2], 256
-    for g in range(0, channels, group):
-        rows = slice(g, g + group)
+
+    @pl.loop(0, channels // group)
+    def _(g):
+        rows = pl.ds(pl.multiple_of(g * group, 16), group)
         for s in range(0, halo, unit):
             outer = dot(turned_ref[2 * at_end, rows, :], halo_ref[rows, s:s + unit])
             held[rows, s:s + unit] = (ends_ref[rows, lanes(at_end * halo + s, unit)] + outer).astype(BF16)

time: 46.9 us -> 47.6 us (1.015)
  Pallas kernels: 20.9 us -> 21.6 us
    pallas_call x14, Pallas kernels: 20.9 us -> 21.6 us  [kernel_call(): pl.pallas_call(kernel, in_specs=[INSIDE if held else ANY for _, held in o...]
  transfers between devices with their start and end apart: 10 -> 10, of which waited for: 5 -> 5; matrix products, arithmetic and copies ran while one was open for 0% -> 0% of each run, Pallas kernels for 41% -> 39%
where the time goes in v20:
time: 47.6 us; the launch traced here: 47 us
  Pallas kernels  21.6 us (45%)
  starting transfers between devices  13.4 us (28%)
  waiting for transfers between devices  11 us (23%)
  between operations  0.95 us (2%)
    pallas_call x14, Pallas kernels, kernel_call(): pl.pallas_call(kernel, in_specs=[INSIDE if held else ANY for _, held in o...  21.6 us
    ppermute x6, waiting for transfers between devices, exchange(): lax.ppermute(piece, 'ch', [(i, i ^ k) for i in range(lax.axis_size('ch'))])  10.6 us
    ppermute x4, starting transfers between devices, swap(): return lax.ppermute(values, 'ctx', pairs + [(b, a) for a, b in pairs])  6.91 us
    ppermute x6, starting transfers between devices, exchange(): lax.ppermute(piece, 'ch', [(i, i ^ k) for i in range(lax.axis_size('ch'))])  6.54 us
  transfers between devices with their start and end apart: 10, of which 5 were waited for; matrix products, arithmetic and copies ran while one was open for 0% of the time, Pallas kernels for 39%

profile of v20, /device:TPU:0, one launch (start us, length us, event | category | flops | bytes accessed | tf_op | source)
XLA Modules:
  0.0 47.0 jit_solution(9699888852484183442)
XLA Ops:
  0.6 1.0 %near_source.1 = bf16[384,512]{1,0:T(8,128)(2,1)S(1)} custom-call(bf16[384,2048]{1,0:T(8,128)(2,1)} %x_ref.9), custom_call_target="tpu_custom_call" | custom-call | tf_op jit(solution)/shard_map/near_source/pallas_call | solution.py:19
  1.7 3.0 %collective-permute-start.2 = (bf16[384,512]{1,0:T(8,128)(2,1)S(1)}, bf16[384,512]{1,0:T(8,128)(2,1)S(1)}, u32[]{:S(2)}, u32[]{:S(2)}) collective-permute-start(bf16[384,512]{1,0:T(8,128)(2,1)S(1)} %near_source.1), channel_id=1, source_target_pairs={{0,4},{8,12},{16,20},{24,28},{4,0},{12,8},{20,16},{28,24},{1,5},{9... | collective-permute-start | bytes 1179656 | tf_op jit(solution)/shard_map/ppermute | solution.py:391
  4.7 2.2 %upstream.3 = (bf16[384,512]{1,0:T(8,128)(2,1)S(1)}, bf16[1536,512]{1,0:T(8,128)(2,1)S(1)}) custom-call(bf16[1536,1536]{1,0:T(8,128)(2,1)} %pw_ref.11, bf16[1536,512]{1,0:T(8,128)(2,1)} %cot_ref.1, bf16[384,2048]{1,0:T(8,128)(2,1)} %x_ref.9), custom_call_target="tpu_custom_call" | custom-call | tf_op jit(solution)/shard_map/upstream/pallas_call | solution.py:19
  6.9 1.6 %collective-permute-start.1 = (bf16[384,512]{1,0:T(8,128)(2,1)S(1)}, bf16[384,512]{1,0:T(8,128)(2,1)S(1)}, u32[]{:S(2)}, u32[]{:S(2)}) collective-permute-start(bf16[384,512]{1,0:T(8,128)(2,1)S(1)} %get-tuple-element.37), channel_id=1, source_target_pairs={{0,2},{1,3},{2,0},{3,1},{4,6},{5,7},{6,4},{7,5},{8,10},{9,11},{10,... | collective-permute-start | bytes 1179656 | tf_op jit(solution)/shard_map/ppermute | solution.py:385
  8.5 2.0 %upstream.4 = (bf16[384,512]{1,0:T(8,128)(2,1)S(1)}, bf16[384,512]{1,0:T(8,128)(2,1)S(1)}) custom-call(bf16[1536,1536]{1,0:T(8,128)(2,1)} %pw_ref.11, bf16[1536,512]{1,0:T(8,128)(2,1)S(1)} %get-tuple-element.34.cot_ref, bf16[384,2048]{1,0:T(8,128)(2,1)} %x_ref.9), custom_call_target="tpu_custom_call" | custom-call | tf_op jit(solution)/shard_map/upstream/pallas_call | solution.py:19
  10.5 0.7 %collective-permute-start = (bf16[384,512]{1,0:T(8,128)(2,1)S(1)}, bf16[384,512]{1,0:T(8,128)(2,1)S(1)}, u32[]{:S(2)}, u32[]{:S(2)}) collective-permute-start(bf16[384,512]{1,0:T(8,128)(2,1)S(1)} %get-tuple-element.35), channel_id=1, source_target_pairs={{4,8},{12,16},{20,24},{8,4},{16,12},{24,20},{5,9},{13,17},{21,25},... | collective-permute-start | bytes 1179656 | tf_op jit(solution)/shard_map/ppermute | solution.py:391
  11.2 0.1 collective-permute-start.6
  11.3 2.8 %upstream.5 = (bf16[384,512]{1,0:T(8,128)(2,1)S(1)}, bf16[384,512]{1,0:T(8,128)(2,1)S(1)}) custom-call(bf16[1536,1536]{1,0:T(8,128)(2,1)} %pw_ref.11, bf16[1536,512]{1,0:T(8,128)(2,1)S(1)} %get-tuple-element.34.cot_ref, bf16[384,2048]{1,0:T(8,128)(2,1)} %x_ref.9), custom_call_target="tpu_custom_call" | custom-call | tf_op jit(solution)/shard_map/upstream/pallas_call | solution.py:19
  14.1 0.7 %collective-permute-start.7 = (bf16[384,512]{1,0:T(8,128)(2,1)S(1)}, bf16[384,512]{1,0:T(8,128)(2,1)S(1)}, u32[]{:S(2)}, u32[]{:S(2)}) collective-permute-start(bf16[384,512]{1,0:T(8,128)(2,1)S(1)} %get-tuple-element.57), channel_id=1, source_target_pairs={{0,1},{1,0},{2,3},{3,2},{4,5},{5,4},{6,7},{7,6},{8,9},{9,8},{10,11... | collective-permute-start | bytes 1179656 | tf_op jit(solution)/shard_map/ppermute | solution.py:385
  14.8 3.3 %interior.1 = (bf16[384,512]{1,0:T(8,128)(2,1)S(1)}, bf16[384,512]{1,0:T(8,128)(2,1)S(1)}, bf16[384,512]{1,0:T(8,128)(2,1)S(1)}, bf16[384,512]{1,0:T(8,128)(2,1)...) custom-call(bf16[384,2048]{1,0:T(8,128)(2,1)} %x_ref.9, ...), custom_call_target="tpu_custom_call" | custom-call | tf_op jit(solution)/shard_map/interior/pallas_call | solution.py:19
  18.1 0.0 collective-permute-done.2.refs_1_
  18.1 0.9 %collective-permute-done.1.refs_0_.rest_0_ = bf16[384,512]{1,0:T(8,128)(2,1)S(1)} collective-permute-done((bf16[384,512]{1,0:T(8,128)(2,1)S(1)}, bf16[384,512]{1,0:T(8,128)(2,1)S(1)}, u32[]{:S(2)}, u32[]{:S(2)}) %collective-permute-start.1) | collective-permute-done | bytes 393248 | tf_op jit(solution)/shard_map/ppermute | solution.py:385
  19.0 0.8 %near_end.1 = (bf16[384,512]{1,0:T(8,128)(2,1)S(1)}, bf16[384,512]{1,0:T(8,128)(2,1)S(1)}, bf16[384,512]{1,0:T(8,128)(2,1)S(1)}, bf16[384,512]{1,0:T(8,128)(2,1)...) custom-call(bf16[384,512]{1,0:T(8,128)(2,1)S(1)} %collective-permute, ...), custom_call_target="tpu_custom_call", output_to_operand_aliasing={{0}: (3, {}), {1}: (4, {}), {2}: (5, {}), {3}: (6, {}), {4}... | custom-call | tf_op jit(solution)/shard_map/near_end/pallas_call | solution.py:19
  19.7 0.0 collective-permute-done.refs_0_
  19.8 0.0 slice-start.1
  19.8 0.8 %far_end.1 = (bf16[384,512]{1,0:T(8,128)(2,1)S(1)}, bf16[384,512]{1,0:T(8,128)(2,1)S(1)}, bf16[384,512]{1,0:T(8,128)(2,1)S(1)}, bf16[384,512]{1,0:T(8,128)(2,1)S...) custom-call(bf16[384,512]{1,0:T(8,128)(2,1)S(1)} %collective-permute, ...), custom_call_target="tpu_custom_call", output_to_operand_aliasing={{0}: (2, {}), {1}: (3, {}), {2}: (4, {}), {3}: (5, {}), {4}... | custom-call | tf_op jit(solution)/shard_map/far_end/pallas_call | solution.py:19
  20.6 0.1 collective-permute-start.3
  20.6 4.1 %collective-permute-start.4 = (bf16[384,512]{1,0:T(8,128)(2,1)S(1)}, bf16[384,512]{1,0:T(8,128)(2,1)S(1)}, u32[]{:S(2)}, u32[]{:S(2)}) collective-permute-start(bf16[384,512]{1,0:T(8,128)(2,1)S(1)} %get-tuple-element.52), channel_id=1, source_target_pairs={{0,2},{1,3},{2,0},{3,1},{4,6},{5,7},{6,4},{7,5},{8,10},{9,11},{10,... | collective-permute-start | bytes 1179656 | tf_op jit(solution)/shard_map/ppermute | solution.py:385
  24.7 0.1 collective-permute-start.5
  24.8 0.2 collective-permute-done.6.refs_0_
  25.0 0.4 grad_conv.1
  25.4 2.4 %collective-permute-start.8 = (bf16[384,512]{1,0:T(8,128)(2,1)S(1)}, bf16[384,512]{1,0:T(8,128)(2,1)S(1)}, u32[]{:S(2)}, u32[]{:S(2)}) collective-permute-start(bf16[384,512]{1,0:T(8,128)(2,1)S(1)} %get-tuple-element.59), channel_id=1, source_target_pairs={{0,4},{8,12},{16,20},{24,28},{4,0},{12,8},{20,16},{28,24},{1,5},{9... | collective-permute-start | bytes 1179656 | tf_op jit(solution)/shard_map/ppermute | solution.py:391
  27.7 0.9 %collective-permute-start.9 = (bf16[384,512]{1,0:T(8,128)(2,1)S(1)}, bf16[384,512]{1,0:T(8,128)(2,1)S(1)}, u32[]{:S(2)}, u32[]{:S(2)}) collective-permute-start(bf16[384,512]{1,0:T(8,128)(2,1)S(1)} %get-tuple-element.60), channel_id=1, source_target_pairs={{4,8},{12,16},{20,24},{8,4},{16,12},{24,20},{5,9},{13,17},{21,25},... | collective-permute-start | bytes 1179656 | tf_op jit(solution)/shard_map/ppermute | solution.py:391
  28.6 1.7 %back_interior.1 = (bf16[384,2048]{1,0:T(8,128)(2,1)}, f32[384,1024]{1,0:T(8,128)S(1)}) custom-call(bf16[384,2048]{1,0:T(8,128)(2,1)S(1)} %get-tuple-element.61.grad_ref, bf16[3,384,96]{2,1,0:T(8,128)(2,1)S(1)} %get-tuple-element.62.turned_ref), custom_call_target="tpu_custom_call" | custom-call | tf_op jit(solution)/shard_map/back_interior/pallas_call | solution.py:19
  30.3 4.4 %collective-permute-done.4.rest_0_ = bf16[384,512]{1,0:T(8,128)(2,1)S(1)} collective-permute-done((bf16[384,512]{1,0:T(8,128)(2,1)S(1)}, bf16[384,512]{1,0:T(8,128)(2,1)S(1)}, u32[]{:S(2)}, u32[]{:S(2)}) %collective-permute-start.4) | collective-permute-done | bytes 393248 | tf_op jit(solution)/shard_map/ppermute | solution.py:385
  34.7 1.0 %early_mix.1.rest_2_ = f32[1536,512]{1,0:T(8,128)S(1)} custom-call(bf16[1536,1536]{1,0:T(8,128)(2,1)S(1)} %bitcast.2, bf16[384,512]{1,0:T(8,128)(2,1)S(1)} %collective-permute-done.4.rest_0_), custom_call_target="tpu_custom_call" | custom-call | tf_op jit(solution)/shard_map/early_mix/pallas_call | solution.py:19
  35.7 1.8 %half_mix.1.sum_ref = f32[1536,512]{1,0:T(8,128)S(1)} custom-call(bf16[1536,1536]{1,0:T(8,128)(2,1)S(1)} %bitcast.2, bf16[384,512]{1,0:T(8,128)(2,1)S(1)} %collective-permute-done.3.rest_0_, bf16[384,512]{1,0:T(8,128)(2,1)S(1)} %get-tuple-element.51.rest_1_, f32[1536,512]{1,0:T(8,128)S(1)} %early_mix.1.rest_2_), custom_call_target="tpu_custom_call", output_to_operand_aliasing={{}: (3, {})} | custom-call | tf_op jit(solution)/shard_map/half_mix/pallas_call | solution.py:19
  37.5 5.1 %collective-permute-done.5.rest_0_ = bf16[384,512]{1,0:T(8,128)(2,1)S(1)} collective-permute-done((bf16[384,512]{1,0:T(8,128)(2,1)S(1)}, bf16[384,512]{1,0:T(8,128)(2,1)S(1)}, u32[]{:S(2)}, u32[]{:S(2)}) %collective-permute-start.5) | collective-permute-done | bytes 393248 | tf_op jit(solution)/shard_map/ppermute | solution.py:385
  42.6 1.8 %late_mix.1 = (bf16[1536,512]{1,0:T(8,128)(2,1)}, f32[8,128]{1,0:T(8,128)S(1)}) custom-call(bf16[1536,1536]{1,0:T(8,128)(2,1)S(1)} %bitcast.2, f32[1536,512]{1,0:T(8,128)S(1)} %half_mix.1.sum_ref, bf16[384,512]{1,0:T(8,128)(2,1)S(1)} %collective-permute-done.5.rest_0_), custom_call_target="tpu_custom_call" | custom-call | tf_op jit(solution)/shard_map/late_mix/pallas_call | solution.py:19
  44.4 0.4 collective-permute-done.8.near_ref
  44.8 0.0 collective-permute-done.9.far_ref
  44.8 2.0 %back_ends.1 = bf16[384,2048]{1,0:T(8,128)(2,1)} custom-call(bf16[384,512]{1,0:T(8,128)(2,1)S(1)} %collective-permute-done.8.near_ref, bf16[384,512]{1,0:T(8,128)(2,1)S(1)} %collective-permute-done.9.far_ref, f32[384,1024]{1,0:T(8,128)S(1)} %get-tuple-element.63.ends_ref, ...), custom_call_target="tpu_custom_call", output_to_operand_aliasing={{}: (5, {})} | custom-call | tf_op jit(solution)/shard_map/back_ends/pallas_call | solution.py:19
  (7 shorter events, 0.0 us)
Async XLA Ops:
  1.7 16.5 %collective-permute-start.2 = (bf16[384,512]{1,0:T(8,128)(2,1)S(1)}, bf16[384,512]{1,0:T(8,128)(2,1)S(1)}, u32[]{:S(2)}, u32[]{:S(2)}) collective-permute-start(bf16[384,512]{1,0:T(8,128)(2,1)S(1)} %near_source.1), channel_id=1, source_target_pairs={{0,4},{8,12},{16,20},{24,28},{4,0},{12,8},{20,16},{28,24},{1,5},{9... | collective-permute-start | bytes 1179656 | tf_op jit(solution)/shard_map/ppermute | solution.py:391
  6.9 12.1 %collective-permute-start.1 = (bf16[384,512]{1,0:T(8,128)(2,1)S(1)}, bf16[384,512]{1,0:T(8,128)(2,1)S(1)}, u32[]{:S(2)}, u32[]{:S(2)}) collective-permute-start(bf16[384,512]{1,0:T(8,128)(2,1)S(1)} %get-tuple-element.37), channel_id=1, source_target_pairs={{0,2},{1,3},{2,0},{3,1},{4,6},{5,7},{6,4},{7,5},{8,10},{9,11},{10,... | collective-permute-start | bytes 1179656 | tf_op jit(solution)/shard_map/ppermute | solution.py:385
  10.5 9.2 %collective-permute-start = (bf16[384,512]{1,0:T(8,128)(2,1)S(1)}, bf16[384,512]{1,0:T(8,128)(2,1)S(1)}, u32[]{:S(2)}, u32[]{:S(2)}) collective-permute-start(bf16[384,512]{1,0:T(8,128)(2,1)S(1)} %get-tuple-element.35), channel_id=1, source_target_pairs={{4,8},{12,16},{20,24},{8,4},{16,12},{24,20},{5,9},{13,17},{21,25},... | collective-permute-start | bytes 1179656 | tf_op jit(solution)/shard_map/ppermute | solution.py:391
  11.2 13.8 %collective-permute-start.6 = (bf16[384,512]{1,0:T(8,128)(2,1)S(1)}, bf16[384,512]{1,0:T(8,128)(2,1)S(1)}, u32[]{:S(2)}, u32[]{:S(2)}) collective-permute-start(bf16[384,512]{1,0:T(8,128)(2,1)S(1)} %get-tuple-element.56), channel_id=1, source_target_pairs={{0,3},{1,2},{2,1},{3,0},{4,7},{5,6},{6,5},{7,4},{8,11},{9,10},{10,... | collective-permute-start | bytes 1179656 | tf_op jit(solution)/shard_map/ppermute | solution.py:385
  14.1 10.9 %collective-permute-start.7 = (bf16[384,512]{1,0:T(8,128)(2,1)S(1)}, bf16[384,512]{1,0:T(8,128)(2,1)S(1)}, u32[]{:S(2)}, u32[]{:S(2)}) collective-permute-start(bf16[384,512]{1,0:T(8,128)(2,1)S(1)} %get-tuple-element.57), channel_id=1, source_target_pairs={{0,1},{1,0},{2,3},{3,2},{4,5},{5,4},{6,7},{7,6},{8,9},{9,8},{10,11... | collective-permute-start | bytes 1179656 | tf_op jit(solution)/shard_map/ppermute | solution.py:385
  19.0 15.7 %slice-start = ((s8[4718592]{0:T(1024)(128)(4,1)}), s8[4194304]{0:T(1024)(128)(4,1)S(1)}, s32[]{:S(2)}) async-start(s8[4718592]{0:T(1024)(128)(4,1)} %bitcast.1), calls=%async_computation | async-start | bytes 8388608
  19.8 14.9 %slice-start.1 = ((s8[4718592]{0:T(1024)(128)(4,1)}), s8[524288]{0:T(1024)(128)(4,1)S(1)}, s32[]{:S(2)}) async-start(s8[4718592]{0:T(1024)(128)(4,1)} %bitcast.1), calls=%async_computation.1 | async-start | bytes 1048576
  20.6 15.1 %collective-permute-start.3 = (bf16[384,512]{1,0:T(8,128)(2,1)S(1)}, bf16[384,512]{1,0:T(8,128)(2,1)S(1)}, u32[]{:S(2)}, u32[]{:S(2)}) collective-permute-start(bf16[384,512]{1,0:T(8,128)(2,1)S(1)} %get-tuple-element.50), channel_id=1, source_target_pairs={{0,1},{1,0},{2,3},{3,2},{4,5},{5,4},{6,7},{7,6},{8,9},{9,8},{10,11... | collective-permute-start | bytes 1179656 | tf_op jit(solution)/shard_map/ppermute | solution.py:385
  20.6 14.0 %collective-permute-start.4 = (bf16[384,512]{1,0:T(8,128)(2,1)S(1)}, bf16[384,512]{1,0:T(8,128)(2,1)S(1)}, u32[]{:S(2)}, u32[]{:S(2)}) collective-permute-start(bf16[384,512]{1,0:T(8,128)(2,1)S(1)} %get-tuple-element.52), channel_id=1, source_target_pairs={{0,2},{1,3},{2,0},{3,1},{4,6},{5,7},{6,4},{7,5},{8,10},{9,11},{10,... | collective-permute-start | bytes 1179656 | tf_op jit(solution)/shard_map/ppermute | solution.py:385
  24.7 17.9 %collective-permute-start.5 = (bf16[384,512]{1,0:T(8,128)(2,1)S(1)}, bf16[384,512]{1,0:T(8,128)(2,1)S(1)}, u32[]{:S(2)}, u32[]{:S(2)}) collective-permute-start(bf16[384,512]{1,0:T(8,128)(2,1)S(1)} %get-tuple-element.53), channel_id=1, source_target_pairs={{0,3},{1,2},{2,1},{3,0},{4,7},{5,6},{6,5},{7,4},{8,11},{9,10},{10,... | collective-permute-start | bytes 1179656 | tf_op jit(solution)/shard_map/ppermute | solution.py:385
  25.4 19.5 %collective-permute-start.8 = (bf16[384,512]{1,0:T(8,128)(2,1)S(1)}, bf16[384,512]{1,0:T(8,128)(2,1)S(1)}, u32[]{:S(2)}, u32[]{:S(2)}) collective-permute-start(bf16[384,512]{1,0:T(8,128)(2,1)S(1)} %get-tuple-element.59), channel_id=1, source_target_pairs={{0,4},{8,12},{16,20},{24,28},{4,0},{12,8},{20,16},{28,24},{1,5},{9... | collective-permute-start | bytes 1179656 | tf_op jit(solution)/shard_map/ppermute | solution.py:391
  27.7 17.1 %collective-permute-start.9 = (bf16[384,512]{1,0:T(8,128)(2,1)S(1)}, bf16[384,512]{1,0:T(8,128)(2,1)S(1)}, u32[]{:S(2)}, u32[]{:S(2)}) collective-permute-start(bf16[384,512]{1,0:T(8,128)(2,1)S(1)} %get-tuple-element.60), channel_id=1, source_target_pairs={{4,8},{12,16},{20,24},{8,4},{16,12},{24,20},{5,9},{13,17},{21,25},... | collective-permute-start | bytes 1179656 | tf_op jit(solution)/shard_map/ppermute | solution.py:391

commit v21 on v20

--- a/solution.py
+++ b/solution.py
@@ -314,10 +314,8 @@
 def back_end(halo_ref, ends_ref, turned_ref, at_end, held):
     channels, halo = halo_ref.shape
     group, unit = turned_ref.shape[2], 256
-
-    @pl.loop(0, channels // group)
-    def _(g):
-        rows = pl.ds(pl.multiple_of(g * group, 16), group)
+    for g in range(0, channels, group):
+        rows = slice(g, g + group)
         for s in range(0, halo, unit):
             outer = dot(turned_ref[2 * at_end, rows, :], halo_ref[rows, s:s + unit])
             held[rows, s:s + unit] = (ends_ref[rows, lanes(at_end * halo + s, unit)] + outer).astype(BF16)

time: 47.6 us -> 46.7 us (0.981)
  Pallas kernels: 21.6 us -> 20.7 us
    pallas_call x14, Pallas kernels: 21.6 us -> 20.7 us  [kernel_call(): pl.pallas_call(kernel, in_specs=[INSIDE if held else ANY for _, held in o...]
  transfers between devices with their start and end apart: 10 -> 10, of which waited for: 5 -> 5; matrix products, arithmetic and copies ran while one was open for 0% -> 0% of each run, Pallas kernels for 39% -> 40%
where the time goes in v21:
time: 46.7 us; the launch traced here: 46.1 us
  Pallas kernels  20.7 us (44%)
  starting transfers between devices  13.4 us (29%)
  waiting for transfers between devices  11 us (24%)
  between operations  0.95 us (2%)
    pallas_call x14, Pallas kernels, kernel_call(): pl.pallas_call(kernel, in_specs=[INSIDE if held else ANY for _, held in o...  20.7 us
    ppermute x6, waiting for transfers between devices, exchange(): lax.ppermute(piece, 'ch', [(i, i ^ k) for i in range(lax.axis_size('ch'))])  10.6 us
    ppermute x4, starting transfers between devices, swap(): return lax.ppermute(values, 'ctx', pairs + [(b, a) for a, b in pairs])  6.91 us
    ppermute x6, starting transfers between devices, exchange(): lax.ppermute(piece, 'ch', [(i, i ^ k) for i in range(lax.axis_size('ch'))])  6.54 us
  transfers between devices with their start and end apart: 10, of which 5 were waited for; matrix products, arithmetic and copies ran while one was open for 0% of the time, Pallas kernels for 40%

profile of v21, /device:TPU:0, one launch (start us, length us, event | category | flops | bytes accessed | tf_op | source)
XLA Modules:
  0.0 46.1 jit_solution(3747599544039363940)
XLA Ops:
  0.6 1.0 %near_source.1 = bf16[384,512]{1,0:T(8,128)(2,1)S(1)} custom-call(bf16[384,2048]{1,0:T(8,128)(2,1)} %x_ref.9), custom_call_target="tpu_custom_call" | custom-call | tf_op jit(solution)/shard_map/near_source/pallas_call | solution.py:19
  1.7 3.0 %collective-permute-start.2 = (bf16[384,512]{1,0:T(8,128)(2,1)S(1)}, bf16[384,512]{1,0:T(8,128)(2,1)S(1)}, u32[]{:S(2)}, u32[]{:S(2)}) collective-permute-start(bf16[384,512]{1,0:T(8,128)(2,1)S(1)} %near_source.1), channel_id=1, source_target_pairs={{0,4},{8,12},{16,20},{24,28},{4,0},{12,8},{20,16},{28,24},{1,5},{9... | collective-permute-start | bytes 1179656 | tf_op jit(solution)/shard_map/ppermute | solution.py:389
  4.7 2.2 %upstream.3 = (bf16[384,512]{1,0:T(8,128)(2,1)S(1)}, bf16[1536,512]{1,0:T(8,128)(2,1)S(1)}) custom-call(bf16[1536,1536]{1,0:T(8,128)(2,1)} %pw_ref.11, bf16[1536,512]{1,0:T(8,128)(2,1)} %cot_ref.1, bf16[384,2048]{1,0:T(8,128)(2,1)} %x_ref.9), custom_call_target="tpu_custom_call" | custom-call | tf_op jit(solution)/shard_map/upstream/pallas_call | solution.py:19
  6.9 1.6 %collective-permute-start.1 = (bf16[384,512]{1,0:T(8,128)(2,1)S(1)}, bf16[384,512]{1,0:T(8,128)(2,1)S(1)}, u32[]{:S(2)}, u32[]{:S(2)}) collective-permute-start(bf16[384,512]{1,0:T(8,128)(2,1)S(1)} %get-tuple-element.37), channel_id=1, source_target_pairs={{0,2},{1,3},{2,0},{3,1},{4,6},{5,7},{6,4},{7,5},{8,10},{9,11},{10,... | collective-permute-start | bytes 1179656 | tf_op jit(solution)/shard_map/ppermute | solution.py:383
  8.5 2.0 %upstream.4 = (bf16[384,512]{1,0:T(8,128)(2,1)S(1)}, bf16[384,512]{1,0:T(8,128)(2,1)S(1)}) custom-call(bf16[1536,1536]{1,0:T(8,128)(2,1)} %pw_ref.11, bf16[1536,512]{1,0:T(8,128)(2,1)S(1)} %get-tuple-element.34.cot_ref, bf16[384,2048]{1,0:T(8,128)(2,1)} %x_ref.9), custom_call_target="tpu_custom_call" | custom-call | tf_op jit(solution)/shard_map/upstream/pallas_call | solution.py:19
  10.5 0.7 %collective-permute-start = (bf16[384,512]{1,0:T(8,128)(2,1)S(1)}, bf16[384,512]{1,0:T(8,128)(2,1)S(1)}, u32[]{:S(2)}, u32[]{:S(2)}) collective-permute-start(bf16[384,512]{1,0:T(8,128)(2,1)S(1)} %get-tuple-element.35), channel_id=1, source_target_pairs={{4,8},{12,16},{20,24},{8,4},{16,12},{24,20},{5,9},{13,17},{21,25},... | collective-permute-start | bytes 1179656 | tf_op jit(solution)/shard_map/ppermute | solution.py:389
  11.2 0.1 collective-permute-start.6
  11.3 2.8 %upstream.5 = (bf16[384,512]{1,0:T(8,128)(2,1)S(1)}, bf16[384,512]{1,0:T(8,128)(2,1)S(1)}) custom-call(bf16[1536,1536]{1,0:T(8,128)(2,1)} %pw_ref.11, bf16[1536,512]{1,0:T(8,128)(2,1)S(1)} %get-tuple-element.34.cot_ref, bf16[384,2048]{1,0:T(8,128)(2,1)} %x_ref.9), custom_call_target="tpu_custom_call" | custom-call | tf_op jit(solution)/shard_map/upstream/pallas_call | solution.py:19
  14.1 0.7 %collective-permute-start.7 = (bf16[384,512]{1,0:T(8,128)(2,1)S(1)}, bf16[384,512]{1,0:T(8,128)(2,1)S(1)}, u32[]{:S(2)}, u32[]{:S(2)}) collective-permute-start(bf16[384,512]{1,0:T(8,128)(2,1)S(1)} %get-tuple-element.57), channel_id=1, source_target_pairs={{0,1},{1,0},{2,3},{3,2},{4,5},{5,4},{6,7},{7,6},{8,9},{9,8},{10,11... | collective-permute-start | bytes 1179656 | tf_op jit(solution)/shard_map/ppermute | solution.py:383
  14.8 3.3 %interior.1 = (bf16[384,512]{1,0:T(8,128)(2,1)S(1)}, bf16[384,512]{1,0:T(8,128)(2,1)S(1)}, bf16[384,512]{1,0:T(8,128)(2,1)S(1)}, bf16[384,512]{1,0:T(8,128)(2,1)...) custom-call(bf16[384,2048]{1,0:T(8,128)(2,1)} %x_ref.9, ...), custom_call_target="tpu_custom_call" | custom-call | tf_op jit(solution)/shard_map/interior/pallas_call | solution.py:19
  18.1 0.0 collective-permute-done.2.refs_1_
  18.1 0.9 %collective-permute-done.1.refs_0_.rest_0_ = bf16[384,512]{1,0:T(8,128)(2,1)S(1)} collective-permute-done((bf16[384,512]{1,0:T(8,128)(2,1)S(1)}, bf16[384,512]{1,0:T(8,128)(2,1)S(1)}, u32[]{:S(2)}, u32[]{:S(2)}) %collective-permute-start.1) | collective-permute-done | bytes 393248 | tf_op jit(solution)/shard_map/ppermute | solution.py:383
  19.0 0.8 %near_end.1 = (bf16[384,512]{1,0:T(8,128)(2,1)S(1)}, bf16[384,512]{1,0:T(8,128)(2,1)S(1)}, bf16[384,512]{1,0:T(8,128)(2,1)S(1)}, bf16[384,512]{1,0:T(8,128)(2,1)...) custom-call(bf16[384,512]{1,0:T(8,128)(2,1)S(1)} %collective-permute, ...), custom_call_target="tpu_custom_call", output_to_operand_aliasing={{0}: (3, {}), {1}: (4, {}), {2}: (5, {}), {3}: (6, {}), {4}... | custom-call | tf_op jit(solution)/shard_map/near_end/pallas_call | solution.py:19
  19.7 0.0 collective-permute-done.refs_0_
  19.8 0.0 slice-start.1
  19.8 0.8 %far_end.1 = (bf16[384,512]{1,0:T(8,128)(2,1)S(1)}, bf16[384,512]{1,0:T(8,128)(2,1)S(1)}, bf16[384,512]{1,0:T(8,128)(2,1)S(1)}, bf16[384,512]{1,0:T(8,128)(2,1)S...) custom-call(bf16[384,512]{1,0:T(8,128)(2,1)S(1)} %collective-permute, ...), custom_call_target="tpu_custom_call", output_to_operand_aliasing={{0}: (2, {}), {1}: (3, {}), {2}: (4, {}), {3}: (5, {}), {4}... | custom-call | tf_op jit(solution)/shard_map/far_end/pallas_call | solution.py:19
  20.6 0.1 collective-permute-start.3
  20.6 4.1 %collective-permute-start.4 = (bf16[384,512]{1,0:T(8,128)(2,1)S(1)}, bf16[384,512]{1,0:T(8,128)(2,1)S(1)}, u32[]{:S(2)}, u32[]{:S(2)}) collective-permute-start(bf16[384,512]{1,0:T(8,128)(2,1)S(1)} %get-tuple-element.52), channel_id=1, source_target_pairs={{0,2},{1,3},{2,0},{3,1},{4,6},{5,7},{6,4},{7,5},{8,10},{9,11},{10,... | collective-permute-start | bytes 1179656 | tf_op jit(solution)/shard_map/ppermute | solution.py:383
  24.7 0.1 collective-permute-start.5
  24.8 0.2 collective-permute-done.6.refs_0_
  25.0 0.4 grad_conv.1
  25.4 2.4 %collective-permute-start.8 = (bf16[384,512]{1,0:T(8,128)(2,1)S(1)}, bf16[384,512]{1,0:T(8,128)(2,1)S(1)}, u32[]{:S(2)}, u32[]{:S(2)}) collective-permute-start(bf16[384,512]{1,0:T(8,128)(2,1)S(1)} %get-tuple-element.59), channel_id=1, source_target_pairs={{0,4},{8,12},{16,20},{24,28},{4,0},{12,8},{20,16},{28,24},{1,5},{9... | collective-permute-start | bytes 1179656 | tf_op jit(solution)/shard_map/ppermute | solution.py:389
  27.7 0.9 %collective-permute-start.9 = (bf16[384,512]{1,0:T(8,128)(2,1)S(1)}, bf16[384,512]{1,0:T(8,128)(2,1)S(1)}, u32[]{:S(2)}, u32[]{:S(2)}) collective-permute-start(bf16[384,512]{1,0:T(8,128)(2,1)S(1)} %get-tuple-element.60), channel_id=1, source_target_pairs={{4,8},{12,16},{20,24},{8,4},{16,12},{24,20},{5,9},{13,17},{21,25},... | collective-permute-start | bytes 1179656 | tf_op jit(solution)/shard_map/ppermute | solution.py:389
  28.6 1.7 %back_interior.1 = (bf16[384,2048]{1,0:T(8,128)(2,1)}, f32[384,1024]{1,0:T(8,128)S(1)}) custom-call(bf16[384,2048]{1,0:T(8,128)(2,1)S(1)} %get-tuple-element.61.grad_ref, bf16[3,384,96]{2,1,0:T(8,128)(2,1)S(1)} %get-tuple-element.62.turned_ref), custom_call_target="tpu_custom_call" | custom-call | tf_op jit(solution)/shard_map/back_interior/pallas_call | solution.py:19
  30.3 4.4 %collective-permute-done.4.rest_0_ = bf16[384,512]{1,0:T(8,128)(2,1)S(1)} collective-permute-done((bf16[384,512]{1,0:T(8,128)(2,1)S(1)}, bf16[384,512]{1,0:T(8,128)(2,1)S(1)}, u32[]{:S(2)}, u32[]{:S(2)}) %collective-permute-start.4) | collective-permute-done | bytes 393248 | tf_op jit(solution)/shard_map/ppermute | solution.py:383
  34.7 1.0 %early_mix.1.rest_2_ = f32[1536,512]{1,0:T(8,128)S(1)} custom-call(bf16[1536,1536]{1,0:T(8,128)(2,1)S(1)} %bitcast.2, bf16[384,512]{1,0:T(8,128)(2,1)S(1)} %collective-permute-done.4.rest_0_), custom_call_target="tpu_custom_call" | custom-call | tf_op jit(solution)/shard_map/early_mix/pallas_call | solution.py:19
  35.7 1.8 %half_mix.1.sum_ref = f32[1536,512]{1,0:T(8,128)S(1)} custom-call(bf16[1536,1536]{1,0:T(8,128)(2,1)S(1)} %bitcast.2, bf16[384,512]{1,0:T(8,128)(2,1)S(1)} %collective-permute-done.3.rest_0_, bf16[384,512]{1,0:T(8,128)(2,1)S(1)} %get-tuple-element.51.rest_1_, f32[1536,512]{1,0:T(8,128)S(1)} %early_mix.1.rest_2_), custom_call_target="tpu_custom_call", output_to_operand_aliasing={{}: (3, {})} | custom-call | tf_op jit(solution)/shard_map/half_mix/pallas_call | solution.py:19
  37.5 5.1 %collective-permute-done.5.rest_0_ = bf16[384,512]{1,0:T(8,128)(2,1)S(1)} collective-permute-done((bf16[384,512]{1,0:T(8,128)(2,1)S(1)}, bf16[384,512]{1,0:T(8,128)(2,1)S(1)}, u32[]{:S(2)}, u32[]{:S(2)}) %collective-permute-start.5) | collective-permute-done | bytes 393248 | tf_op jit(solution)/shard_map/ppermute | solution.py:383
  42.6 1.8 %late_mix.1 = (bf16[1536,512]{1,0:T(8,128)(2,1)}, f32[8,128]{1,0:T(8,128)S(1)}) custom-call(bf16[1536,1536]{1,0:T(8,128)(2,1)S(1)} %bitcast.2, f32[1536,512]{1,0:T(8,128)S(1)} %half_mix.1.sum_ref, bf16[384,512]{1,0:T(8,128)(2,1)S(1)} %collective-permute-done.5.rest_0_), custom_call_target="tpu_custom_call" | custom-call | tf_op jit(solution)/shard_map/late_mix/pallas_call | solution.py:19
  44.4 0.4 collective-permute-done.8.near_ref
  44.8 0.0 collective-permute-done.9.far_ref
  44.8 1.2 %back_ends.1 = bf16[384,2048]{1,0:T(8,128)(2,1)} custom-call(bf16[384,512]{1,0:T(8,128)(2,1)S(1)} %collective-permute-done.8.near_ref, bf16[384,512]{1,0:T(8,128)(2,1)S(1)} %collective-permute-done.9.far_ref, f32[384,1024]{1,0:T(8,128)S(1)} %get-tuple-element.63.ends_ref, ...), custom_call_target="tpu_custom_call", output_to_operand_aliasing={{}: (5, {})} | custom-call | tf_op jit(solution)/shard_map/back_ends/pallas_call | solution.py:19
  (7 shorter events, 0.0 us)
Async XLA Ops:
  1.7 16.5 %collective-permute-start.2 = (bf16[384,512]{1,0:T(8,128)(2,1)S(1)}, bf16[384,512]{1,0:T(8,128)(2,1)S(1)}, u32[]{:S(2)}, u32[]{:S(2)}) collective-permute-start(bf16[384,512]{1,0:T(8,128)(2,1)S(1)} %near_source.1), channel_id=1, source_target_pairs={{0,4},{8,12},{16,20},{24,28},{4,0},{12,8},{20,16},{28,24},{1,5},{9... | collective-permute-start | bytes 1179656 | tf_op jit(solution)/shard_map/ppermute | solution.py:389
  6.9 12.1 %collective-permute-start.1 = (bf16[384,512]{1,0:T(8,128)(2,1)S(1)}, bf16[384,512]{1,0:T(8,128)(2,1)S(1)}, u32[]{:S(2)}, u32[]{:S(2)}) collective-permute-start(bf16[384,512]{1,0:T(8,128)(2,1)S(1)} %get-tuple-element.37), channel_id=1, source_target_pairs={{0,2},{1,3},{2,0},{3,1},{4,6},{5,7},{6,4},{7,5},{8,10},{9,11},{10,... | collective-permute-start | bytes 1179656 | tf_op jit(solution)/shard_map/ppermute | solution.py:383
  10.5 9.2 %collective-permute-start = (bf16[384,512]{1,0:T(8,128)(2,1)S(1)}, bf16[384,512]{1,0:T(8,128)(2,1)S(1)}, u32[]{:S(2)}, u32[]{:S(2)}) collective-permute-start(bf16[384,512]{1,0:T(8,128)(2,1)S(1)} %get-tuple-element.35), channel_id=1, source_target_pairs={{4,8},{12,16},{20,24},{8,4},{16,12},{24,20},{5,9},{13,17},{21,25},... | collective-permute-start | bytes 1179656 | tf_op jit(solution)/shard_map/ppermute | solution.py:389
  11.2 13.8 %collective-permute-start.6 = (bf16[384,512]{1,0:T(8,128)(2,1)S(1)}, bf16[384,512]{1,0:T(8,128)(2,1)S(1)}, u32[]{:S(2)}, u32[]{:S(2)}) collective-permute-start(bf16[384,512]{1,0:T(8,128)(2,1)S(1)} %get-tuple-element.56), channel_id=1, source_target_pairs={{0,3},{1,2},{2,1},{3,0},{4,7},{5,6},{6,5},{7,4},{8,11},{9,10},{10,... | collective-permute-start | bytes 1179656 | tf_op jit(solution)/shard_map/ppermute | solution.py:383
  14.1 10.9 %collective-permute-start.7 = (bf16[384,512]{1,0:T(8,128)(2,1)S(1)}, bf16[384,512]{1,0:T(8,128)(2,1)S(1)}, u32[]{:S(2)}, u32[]{:S(2)}) collective-permute-start(bf16[384,512]{1,0:T(8,128)(2,1)S(1)} %get-tuple-element.57), channel_id=1, source_target_pairs={{0,1},{1,0},{2,3},{3,2},{4,5},{5,4},{6,7},{7,6},{8,9},{9,8},{10,11... | collective-permute-start | bytes 1179656 | tf_op jit(solution)/shard_map/ppermute | solution.py:383
  19.0 15.7 %slice-start = ((s8[4718592]{0:T(1024)(128)(4,1)}), s8[4194304]{0:T(1024)(128)(4,1)S(1)}, s32[]{:S(2)}) async-start(s8[4718592]{0:T(1024)(128)(4,1)} %bitcast.1), calls=%async_computation | async-start | bytes 8388608
  19.8 14.9 %slice-start.1 = ((s8[4718592]{0:T(1024)(128)(4,1)}), s8[524288]{0:T(1024)(128)(4,1)S(1)}, s32[]{:S(2)}) async-start(s8[4718592]{0:T(1024)(128)(4,1)} %bitcast.1), calls=%async_computation.1 | async-start | bytes 1048576
  20.6 15.1 %collective-permute-start.3 = (bf16[384,512]{1,0:T(8,128)(2,1)S(1)}, bf16[384,512]{1,0:T(8,128)(2,1)S(1)}, u32[]{:S(2)}, u32[]{:S(2)}) collective-permute-start(bf16[384,512]{1,0:T(8,128)(2,1)S(1)} %get-tuple-element.50), channel_id=1, source_target_pairs={{0,1},{1,0},{2,3},{3,2},{4,5},{5,4},{6,7},{7,6},{8,9},{9,8},{10,11... | collective-permute-start | bytes 1179656 | tf_op jit(solution)/shard_map/ppermute | solution.py:383
  20.6 14.0 %collective-permute-start.4 = (bf16[384,512]{1,0:T(8,128)(2,1)S(1)}, bf16[384,512]{1,0:T(8,128)(2,1)S(1)}, u32[]{:S(2)}, u32[]{:S(2)}) collective-permute-start(bf16[384,512]{1,0:T(8,128)(2,1)S(1)} %get-tuple-element.52), channel_id=1, source_target_pairs={{0,2},{1,3},{2,0},{3,1},{4,6},{5,7},{6,4},{7,5},{8,10},{9,11},{10,... | collective-permute-start | bytes 1179656 | tf_op jit(solution)/shard_map/ppermute | solution.py:383
  24.7 17.9 %collective-permute-start.5 = (bf16[384,512]{1,0:T(8,128)(2,1)S(1)}, bf16[384,512]{1,0:T(8,128)(2,1)S(1)}, u32[]{:S(2)}, u32[]{:S(2)}) collective-permute-start(bf16[384,512]{1,0:T(8,128)(2,1)S(1)} %get-tuple-element.53), channel_id=1, source_target_pairs={{0,3},{1,2},{2,1},{3,0},{4,7},{5,6},{6,5},{7,4},{8,11},{9,10},{10,... | collective-permute-start | bytes 1179656 | tf_op jit(solution)/shard_map/ppermute | solution.py:383
  25.4 19.5 %collective-permute-start.8 = (bf16[384,512]{1,0:T(8,128)(2,1)S(1)}, bf16[384,512]{1,0:T(8,128)(2,1)S(1)}, u32[]{:S(2)}, u32[]{:S(2)}) collective-permute-start(bf16[384,512]{1,0:T(8,128)(2,1)S(1)} %get-tuple-element.59), channel_id=1, source_target_pairs={{0,4},{8,12},{16,20},{24,28},{4,0},{12,8},{20,16},{28,24},{1,5},{9... | collective-permute-start | bytes 1179656 | tf_op jit(solution)/shard_map/ppermute | solution.py:389
  27.7 17.1 %collective-permute-start.9 = (bf16[384,512]{1,0:T(8,128)(2,1)S(1)}, bf16[384,512]{1,0:T(8,128)(2,1)S(1)}, u32[]{:S(2)}, u32[]{:S(2)}) collective-permute-start(bf16[384,512]{1,0:T(8,128)(2,1)S(1)} %get-tuple-element.60), channel_id=1, source_target_pairs={{4,8},{12,16},{20,24},{8,4},{16,12},{24,20},{5,9},{13,17},{21,25},... | collective-permute-start | bytes 1179656 | tf_op jit(solution)/shard_map/ppermute | solution.py:389

commit v22 on v21

--- a/solution.py
+++ b/solution.py
@@ -64,12 +64,6 @@
 def end_copy(x_ref, end_ref, at_end, sem):
     length, halo = x_ref.shape[1], end_ref.shape[1]
     return pltpu.make_async_copy(x_ref.at[:, lanes(at_end * (length - halo), halo)], end_ref, sem)
-
-
-def near_source_kernel(x_ref, near_ref, sem):
-    copy = end_copy(x_ref, near_ref, 1 - odd_place(), sem)
-    copy.start()
-    copy.wait()
 
 
 def upstream_kernel(order, channels, first, with_far, pw_ref, cot_ref, x_ref, *rest):
@@ -96,8 +90,9 @@
         for copy in copies:
             copy.start()
         blocks.append((rows, copies))
-    if with_far:
-        end = end_copy(x_ref, rest[-4], odd_place(), sems.at[0, count + 1])
+    if first or with_far:
+        at_end = 1 - odd_place() if first else odd_place()
+        end = end_copy(x_ref, rest[-4], at_end, sems.at[0, count + 1])
         end.start()
     for step, (rows, copies) in enumerate(blocks):
         for copy in copies:
@@ -111,7 +106,7 @@
                 total_ref[held, :] = part
             else:
                 piece_refs[place][...] = part.astype(BF16)
-    if with_far:
+    if first or with_far:
         end.wait()
 
 
@@ -130,7 +125,7 @@
     count = len(order)
     outs = [((channels, width), BF16, True)] * count
     outs += [(cotangent.shape, BF16, True)] * first
-    outs += [((channels, DILATION_STEP), BF16, True)] * with_far
+    outs += [((channels, DILATION_STEP), BF16, True)] * (first or with_far)
     results = kernel_call(
         "upstream", functools.partial(upstream_kernel, order, channels, first, with_far),
         [(columns_of(pw_weight, channels, order), False), (cotangent, not first), (inputs, False)], outs,
@@ -399,11 +394,8 @@
     weight = jnp.swapaxes(conv_weight, 1, 2)
     if channels % 128 != 0:
         weight = lax.dynamic_slice_in_dim(weight, lax.axis_index("ch") * channels, channels, 2)
-    (near,) = kernel_call(
-        "near_source", near_source_kernel, [(inputs, False)], [((channels, halo), BF16, True)], [DMA]
-    )
+    pieces, cot_in, near = upstream(pw_weight, cotangent, inputs, first, first=True)
     near = swap(near, 0)
-    pieces, cot_in = upstream(pw_weight, cotangent, inputs, first, first=True)
     ups = {k: exchange(p, k) for k, p in zip(first, pieces)}
     pieces, far = upstream(pw_weight, cot_in, inputs, second, with_far=True)
     far = swap(far, 1)

time: 46.7 us -> 49.2 us (1.054)
  waiting for transfers between devices: 11 us -> 17 us
  starting transfers between devices: 13.4 us -> 11.3 us
  Pallas kernels: 20.7 us -> 19.7 us
    ppermute x4, waiting for transfers between devices: 0.44 us -> 7.64 us  [swap(): return lax.ppermute(values, 'ctx', pairs + [(b, a) for a, b in pairs])]
    ppermute x4, starting transfers between devices: 6.91 us -> 5.59 us  [swap(): return lax.ppermute(values, 'ctx', pairs + [(b, a) for a, b in pairs])]
    ppermute x6, waiting for transfers between devices: 10.6 us -> 9.36 us  [exchange(): lax.ppermute(piece, 'ch', [(i, i ^ k) for i in range(lax.axis_size('ch'))])]
    pallas_call x14 -> x13, Pallas kernels: 20.7 us -> 19.7 us  [kernel_call(): pl.pallas_call(kernel, in_specs=[INSIDE if held else ANY for _, held in o...]
    ppermute x6, starting transfers between devices: 6.54 us -> 5.7 us  [exchange(): lax.ppermute(piece, 'ch', [(i, i ^ k) for i in range(lax.axis_size('ch'))])]
  transfers between devices with their start and end apart: 10 -> 10, of which waited for: 5 -> 4; matrix products, arithmetic and copies ran while one was open for 0% -> 0% of each run, Pallas kernels for 40% -> 33%
where the time goes in v22:
time: 49.2 us; the launch traced here: 49 us
  Pallas kernels  19.7 us (40%)
  waiting for transfers between devices  17 us (35%)
  starting transfers between devices  11.3 us (23%)
  between operations  0.94 us (2%)
    pallas_call x13, Pallas kernels, kernel_call(): pl.pallas_call(kernel, in_specs=[INSIDE if held else ANY for _, held in o...  19.7 us
    ppermute x6, waiting for transfers between devices, exchange(): lax.ppermute(piece, 'ch', [(i, i ^ k) for i in range(lax.axis_size('ch'))])  9.36 us
    ppermute x4, waiting for transfers between devices, swap(): return lax.ppermute(values, 'ctx', pairs + [(b, a) for a, b in pairs])  7.64 us
    ppermute x6, starting transfers between devices, exchange(): lax.ppermute(piece, 'ch', [(i, i ^ k) for i in range(lax.axis_size('ch'))])  5.7 us
    ppermute x4, starting transfers between devices, swap(): return lax.ppermute(values, 'ctx', pairs + [(b, a) for a, b in pairs])  5.59 us
  transfers between devices with their start and end apart: 10, of which 4 were waited for; matrix products, arithmetic and copies ran while one was open for 0% of the time, Pallas kernels for 33%

profile of v22, /device:TPU:0, one launch (start us, length us, event | category | flops | bytes accessed | tf_op | source)
XLA Modules:
  0.0 49.0 jit_solution(13815153367735538030)
XLA Ops:
  0.6 2.2 %upstream.3 = (bf16[384,512]{1,0:T(8,128)(2,1)S(1)}, bf16[1536,512]{1,0:T(8,128)(2,1)S(1)}, bf16[384,512]{1,0:T(8,128)(2,1)S(1)}) custom-call(bf16[1536,1536]{1,0:T(8,128)(2,1)} %pw_ref.11, bf16[1536,512]{1,0:T(8,128)(2,1)} %cot_ref.1, bf16[384,2048]{1,0:T(8,128)(2,1)} %x_ref.7), custom_call_target="tpu_custom_call" | custom-call | tf_op jit(solution)/shard_map/upstream/pallas_call | solution.py:19
  2.8 3.0 %collective-permute-start.1 = (bf16[384,512]{1,0:T(8,128)(2,1)S(1)}, bf16[384,512]{1,0:T(8,128)(2,1)S(1)}, u32[]{:S(2)}, u32[]{:S(2)}) collective-permute-start(bf16[384,512]{1,0:T(8,128)(2,1)S(1)} %get-tuple-element.38), channel_id=1, source_target_pairs={{0,2},{1,3},{2,0},{3,1},{4,6},{5,7},{6,4},{7,5},{8,10},{9,11},{10,... | collective-permute-start | bytes 1179656 | tf_op jit(solution)/shard_map/ppermute | solution.py:378
  5.9 1.5 %collective-permute-start.2 = (bf16[384,512]{1,0:T(8,128)(2,1)S(1)}, bf16[384,512]{1,0:T(8,128)(2,1)S(1)}, u32[]{:S(2)}, u32[]{:S(2)}) collective-permute-start(bf16[384,512]{1,0:T(8,128)(2,1)S(1)} %get-tuple-element.39), channel_id=1, source_target_pairs={{0,4},{8,12},{16,20},{24,28},{4,0},{12,8},{20,16},{28,24},{1,5},{9... | collective-permute-start | bytes 1179656 | tf_op jit(solution)/shard_map/ppermute | solution.py:384
  7.4 2.0 %upstream.4 = (bf16[384,512]{1,0:T(8,128)(2,1)S(1)}, bf16[384,512]{1,0:T(8,128)(2,1)S(1)}) custom-call(bf16[1536,1536]{1,0:T(8,128)(2,1)} %pw_ref.11, bf16[1536,512]{1,0:T(8,128)(2,1)S(1)} %get-tuple-element.35.cot_ref, bf16[384,2048]{1,0:T(8,128)(2,1)} %x_ref.7), custom_call_target="tpu_custom_call" | custom-call | tf_op jit(solution)/shard_map/upstream/pallas_call | solution.py:19
  9.4 0.7 %collective-permute-start = (bf16[384,512]{1,0:T(8,128)(2,1)S(1)}, bf16[384,512]{1,0:T(8,128)(2,1)S(1)}, u32[]{:S(2)}, u32[]{:S(2)}) collective-permute-start(bf16[384,512]{1,0:T(8,128)(2,1)S(1)} %get-tuple-element.36), channel_id=1, source_target_pairs={{4,8},{12,16},{20,24},{8,4},{16,12},{24,20},{5,9},{13,17},{21,25},... | collective-permute-start | bytes 1179656 | tf_op jit(solution)/shard_map/ppermute | solution.py:384
  10.1 0.1 collective-permute-start.6
  10.2 2.8 %upstream.5 = (bf16[384,512]{1,0:T(8,128)(2,1)S(1)}, bf16[384,512]{1,0:T(8,128)(2,1)S(1)}) custom-call(bf16[1536,1536]{1,0:T(8,128)(2,1)} %pw_ref.11, bf16[1536,512]{1,0:T(8,128)(2,1)S(1)} %get-tuple-element.35.cot_ref, bf16[384,2048]{1,0:T(8,128)(2,1)} %x_ref.7), custom_call_target="tpu_custom_call" | custom-call | tf_op jit(solution)/shard_map/upstream/pallas_call | solution.py:19
  13.0 0.7 %collective-permute-start.7 = (bf16[384,512]{1,0:T(8,128)(2,1)S(1)}, bf16[384,512]{1,0:T(8,128)(2,1)S(1)}, u32[]{:S(2)}, u32[]{:S(2)}) collective-permute-start(bf16[384,512]{1,0:T(8,128)(2,1)S(1)} %get-tuple-element.59), channel_id=1, source_target_pairs={{0,1},{1,0},{2,3},{3,2},{4,5},{5,4},{6,7},{7,6},{8,9},{9,8},{10,11... | collective-permute-start | bytes 1179656 | tf_op jit(solution)/shard_map/ppermute | solution.py:378
  13.7 3.3 %interior.1 = (bf16[384,512]{1,0:T(8,128)(2,1)S(1)}, bf16[384,512]{1,0:T(8,128)(2,1)S(1)}, bf16[384,512]{1,0:T(8,128)(2,1)S(1)}, bf16[384,512]{1,0:T(8,128)(2,1)...) custom-call(bf16[384,2048]{1,0:T(8,128)(2,1)} %x_ref.7, ...), custom_call_target="tpu_custom_call" | custom-call | tf_op jit(solution)/shard_map/interior/pallas_call | solution.py:19
  17.0 0.0 collective-permute-done.1.refs_0_.rest_0_
  17.0 6.9 %collective-permute-done.2.refs_1_ = bf16[384,512]{1,0:T(8,128)(2,1)S(1)} collective-permute-done((bf16[384,512]{1,0:T(8,128)(2,1)S(1)}, bf16[384,512]{1,0:T(8,128)(2,1)S(1)}, u32[]{:S(2)}, u32[]{:S(2)}) %collective-permute-start.2) | collective-permute-done | bytes 393248 | tf_op jit(solution)/shard_map/ppermute | solution.py:384
  23.9 0.8 %near_end.1 = (bf16[384,512]{1,0:T(8,128)(2,1)S(1)}, bf16[384,512]{1,0:T(8,128)(2,1)S(1)}, bf16[384,512]{1,0:T(8,128)(2,1)S(1)}, bf16[384,512]{1,0:T(8,128)(2,1)...) custom-call(bf16[384,512]{1,0:T(8,128)(2,1)S(1)} %collective-permute, ...), custom_call_target="tpu_custom_call", output_to_operand_aliasing={{0}: (3, {}), {1}: (4, {}), {2}: (5, {}), {3}: (6, {}), {4}... | custom-call | tf_op jit(solution)/shard_map/near_end/pallas_call | solution.py:19
  24.7 0.0 collective-permute-done.refs_0_
  24.7 0.0 slice-start.1
  24.7 0.8 %far_end.1 = (bf16[384,512]{1,0:T(8,128)(2,1)S(1)}, bf16[384,512]{1,0:T(8,128)(2,1)S(1)}, bf16[384,512]{1,0:T(8,128)(2,1)S(1)}, bf16[384,512]{1,0:T(8,128)(2,1)S...) custom-call(bf16[384,512]{1,0:T(8,128)(2,1)S(1)} %collective-permute, ...), custom_call_target="tpu_custom_call", output_to_operand_aliasing={{0}: (2, {}), {1}: (3, {}), {2}: (4, {}), {3}: (5, {}), {4}... | custom-call | tf_op jit(solution)/shard_map/far_end/pallas_call | solution.py:19
  25.5 0.1 collective-permute-start.3
  25.5 0.6 %collective-permute-start.4 = (bf16[384,512]{1,0:T(8,128)(2,1)S(1)}, bf16[384,512]{1,0:T(8,128)(2,1)S(1)}, u32[]{:S(2)}, u32[]{:S(2)}) collective-permute-start(bf16[384,512]{1,0:T(8,128)(2,1)S(1)} %get-tuple-element.54), channel_id=1, source_target_pairs={{0,2},{1,3},{2,0},{3,1},{4,6},{5,7},{6,4},{7,5},{8,10},{9,11},{10,... | collective-permute-start | bytes 1179656 | tf_op jit(solution)/shard_map/ppermute | solution.py:378
  26.1 1.3 %collective-permute-start.5 = (bf16[384,512]{1,0:T(8,128)(2,1)S(1)}, bf16[384,512]{1,0:T(8,128)(2,1)S(1)}, u32[]{:S(2)}, u32[]{:S(2)}) collective-permute-start(bf16[384,512]{1,0:T(8,128)(2,1)S(1)} %get-tuple-element.55), channel_id=1, source_target_pairs={{0,3},{1,2},{2,1},{3,0},{4,7},{5,6},{6,5},{7,4},{8,11},{9,10},{10,... | collective-permute-start | bytes 1179656 | tf_op jit(solution)/shard_map/ppermute | solution.py:378
  27.4 0.0 collective-permute-done.6.refs_0_
  27.4 0.0 collective-permute-done.7.rest_2_
  27.4 0.4 grad_conv.1
  27.8 2.6 %collective-permute-start.8 = (bf16[384,512]{1,0:T(8,128)(2,1)S(1)}, bf16[384,512]{1,0:T(8,128)(2,1)S(1)}, u32[]{:S(2)}, u32[]{:S(2)}) collective-permute-start(bf16[384,512]{1,0:T(8,128)(2,1)S(1)} %get-tuple-element.61), channel_id=1, source_target_pairs={{0,4},{8,12},{16,20},{24,28},{4,0},{12,8},{20,16},{28,24},{1,5},{9... | collective-permute-start | bytes 1179656 | tf_op jit(solution)/shard_map/ppermute | solution.py:384
  30.3 0.9 %collective-permute-start.9 = (bf16[384,512]{1,0:T(8,128)(2,1)S(1)}, bf16[384,512]{1,0:T(8,128)(2,1)S(1)}, u32[]{:S(2)}, u32[]{:S(2)}) collective-permute-start(bf16[384,512]{1,0:T(8,128)(2,1)S(1)} %get-tuple-element.62), channel_id=1, source_target_pairs={{4,8},{12,16},{20,24},{8,4},{16,12},{24,20},{5,9},{13,17},{21,25},... | collective-permute-start | bytes 1179656 | tf_op jit(solution)/shard_map/ppermute | solution.py:384
  31.2 1.7 %back_interior.1 = (bf16[384,2048]{1,0:T(8,128)(2,1)}, f32[384,1024]{1,0:T(8,128)S(1)}) custom-call(bf16[384,2048]{1,0:T(8,128)(2,1)S(1)} %get-tuple-element.63.grad_ref, bf16[3,384,96]{2,1,0:T(8,128)(2,1)S(1)} %get-tuple-element.64.turned_ref), custom_call_target="tpu_custom_call" | custom-call | tf_op jit(solution)/shard_map/back_interior/pallas_call | solution.py:19
  32.9 4.6 %collective-permute-done.4.rest_0_ = bf16[384,512]{1,0:T(8,128)(2,1)S(1)} collective-permute-done((bf16[384,512]{1,0:T(8,128)(2,1)S(1)}, bf16[384,512]{1,0:T(8,128)(2,1)S(1)}, u32[]{:S(2)}, u32[]{:S(2)}) %collective-permute-start.4) | collective-permute-done | bytes 393248 | tf_op jit(solution)/shard_map/ppermute | solution.py:378
  37.5 1.0 %early_mix.1.rest_2_ = f32[1536,512]{1,0:T(8,128)S(1)} custom-call(bf16[1536,1536]{1,0:T(8,128)(2,1)S(1)} %bitcast.2, bf16[384,512]{1,0:T(8,128)(2,1)S(1)} %collective-permute-done.4.rest_0_), custom_call_target="tpu_custom_call" | custom-call | tf_op jit(solution)/shard_map/early_mix/pallas_call | solution.py:19
  38.5 0.0 collective-permute-done.3.rest_0_
  38.5 1.8 %half_mix.1.sum_ref = f32[1536,512]{1,0:T(8,128)S(1)} custom-call(bf16[1536,1536]{1,0:T(8,128)(2,1)S(1)} %bitcast.2, bf16[384,512]{1,0:T(8,128)(2,1)S(1)} %collective-permute-done.3.rest_0_, bf16[384,512]{1,0:T(8,128)(2,1)S(1)} %get-tuple-element.53.rest_1_, f32[1536,512]{1,0:T(8,128)S(1)} %early_mix.1.rest_2_), custom_call_target="tpu_custom_call", output_to_operand_aliasing={{}: (3, {})} | custom-call | tf_op jit(solution)/shard_map/half_mix/pallas_call | solution.py:19
  40.3 4.7 %collective-permute-done.5.rest_0_ = bf16[384,512]{1,0:T(8,128)(2,1)S(1)} collective-permute-done((bf16[384,512]{1,0:T(8,128)(2,1)S(1)}, bf16[384,512]{1,0:T(8,128)(2,1)S(1)}, u32[]{:S(2)}, u32[]{:S(2)}) %collective-permute-start.5) | collective-permute-done | bytes 393248 | tf_op jit(solution)/shard_map/ppermute | solution.py:378
  45.0 1.8 %late_mix.1 = (bf16[1536,512]{1,0:T(8,128)(2,1)}, f32[8,128]{1,0:T(8,128)S(1)}) custom-call(bf16[1536,1536]{1,0:T(8,128)(2,1)S(1)} %bitcast.2, f32[1536,512]{1,0:T(8,128)S(1)} %half_mix.1.sum_ref, bf16[384,512]{1,0:T(8,128)(2,1)S(1)} %collective-permute-done.5.rest_0_), custom_call_target="tpu_custom_call" | custom-call | tf_op jit(solution)/shard_map/late_mix/pallas_call | solution.py:19
  46.9 0.8 %collective-permute-done.8.near_ref = bf16[384,512]{1,0:T(8,128)(2,1)S(1)} collective-permute-done((bf16[384,512]{1,0:T(8,128)(2,1)S(1)}, bf16[384,512]{1,0:T(8,128)(2,1)S(1)}, u32[]{:S(2)}, u32[]{:S(2)}) %collective-permute-start.8) | collective-permute-done | bytes 393248 | tf_op jit(solution)/shard_map/ppermute | solution.py:384
  47.6 1.2 %back_ends.1 = bf16[384,2048]{1,0:T(8,128)(2,1)} custom-call(bf16[384,512]{1,0:T(8,128)(2,1)S(1)} %collective-permute-done.8.near_ref, bf16[384,512]{1,0:T(8,128)(2,1)S(1)} %collective-permute-done.9.far_ref, f32[384,1024]{1,0:T(8,128)S(1)} %get-tuple-element.65.ends_ref, ...), custom_call_target="tpu_custom_call", output_to_operand_aliasing={{}: (5, {})} | custom-call | tf_op jit(solution)/shard_map/back_ends/pallas_call | solution.py:19
  (6 shorter events, 0.0 us)
Async XLA Ops:
  2.8 14.2 %collective-permute-start.1 = (bf16[384,512]{1,0:T(8,128)(2,1)S(1)}, bf16[384,512]{1,0:T(8,128)(2,1)S(1)}, u32[]{:S(2)}, u32[]{:S(2)}) collective-permute-start(bf16[384,512]{1,0:T(8,128)(2,1)S(1)} %get-tuple-element.38), channel_id=1, source_target_pairs={{0,2},{1,3},{2,0},{3,1},{4,6},{5,7},{6,4},{7,5},{8,10},{9,11},{10,... | collective-permute-start | bytes 1179656 | tf_op jit(solution)/shard_map/ppermute | solution.py:378
  5.9 18.0 %collective-permute-start.2 = (bf16[384,512]{1,0:T(8,128)(2,1)S(1)}, bf16[384,512]{1,0:T(8,128)(2,1)S(1)}, u32[]{:S(2)}, u32[]{:S(2)}) collective-permute-start(bf16[384,512]{1,0:T(8,128)(2,1)S(1)} %get-tuple-element.39), channel_id=1, source_target_pairs={{0,4},{8,12},{16,20},{24,28},{4,0},{12,8},{20,16},{28,24},{1,5},{9... | collective-permute-start | bytes 1179656 | tf_op jit(solution)/shard_map/ppermute | solution.py:384
  9.4 15.2 %collective-permute-start = (bf16[384,512]{1,0:T(8,128)(2,1)S(1)}, bf16[384,512]{1,0:T(8,128)(2,1)S(1)}, u32[]{:S(2)}, u32[]{:S(2)}) collective-permute-start(bf16[384,512]{1,0:T(8,128)(2,1)S(1)} %get-tuple-element.36), channel_id=1, source_target_pairs={{4,8},{12,16},{20,24},{8,4},{16,12},{24,20},{5,9},{13,17},{21,25},... | collective-permute-start | bytes 1179656 | tf_op jit(solution)/shard_map/ppermute | solution.py:384
  10.1 17.3 %collective-permute-start.6 = (bf16[384,512]{1,0:T(8,128)(2,1)S(1)}, bf16[384,512]{1,0:T(8,128)(2,1)S(1)}, u32[]{:S(2)}, u32[]{:S(2)}) collective-permute-start(bf16[384,512]{1,0:T(8,128)(2,1)S(1)} %get-tuple-element.58), channel_id=1, source_target_pairs={{0,3},{1,2},{2,1},{3,0},{4,7},{5,6},{6,5},{7,4},{8,11},{9,10},{10,... | collective-permute-start | bytes 1179656 | tf_op jit(solution)/shard_map/ppermute | solution.py:378
  13.0 14.4 %collective-permute-start.7 = (bf16[384,512]{1,0:T(8,128)(2,1)S(1)}, bf16[384,512]{1,0:T(8,128)(2,1)S(1)}, u32[]{:S(2)}, u32[]{:S(2)}) collective-permute-start(bf16[384,512]{1,0:T(8,128)(2,1)S(1)} %get-tuple-element.59), channel_id=1, source_target_pairs={{0,1},{1,0},{2,3},{3,2},{4,5},{5,4},{6,7},{7,6},{8,9},{9,8},{10,11... | collective-permute-start | bytes 1179656 | tf_op jit(solution)/shard_map/ppermute | solution.py:378
  23.9 13.6 %slice-start = ((s8[4718592]{0:T(1024)(128)(4,1)}), s8[4194304]{0:T(1024)(128)(4,1)S(1)}, s32[]{:S(2)}) async-start(s8[4718592]{0:T(1024)(128)(4,1)} %bitcast.1), calls=%async_computation | async-start | bytes 8388608
  24.7 12.9 %slice-start.1 = ((s8[4718592]{0:T(1024)(128)(4,1)}), s8[524288]{0:T(1024)(128)(4,1)S(1)}, s32[]{:S(2)}) async-start(s8[4718592]{0:T(1024)(128)(4,1)} %bitcast.1), calls=%async_computation.1 | async-start | bytes 1048576
  25.5 13.1 %collective-permute-start.3 = (bf16[384,512]{1,0:T(8,128)(2,1)S(1)}, bf16[384,512]{1,0:T(8,128)(2,1)S(1)}, u32[]{:S(2)}, u32[]{:S(2)}) collective-permute-start(bf16[384,512]{1,0:T(8,128)(2,1)S(1)} %get-tuple-element.52), channel_id=1, source_target_pairs={{0,1},{1,0},{2,3},{3,2},{4,5},{5,4},{6,7},{7,6},{8,9},{9,8},{10,11... | collective-permute-start | bytes 1179656 | tf_op jit(solution)/shard_map/ppermute | solution.py:378
  25.5 12.0 %collective-permute-start.4 = (bf16[384,512]{1,0:T(8,128)(2,1)S(1)}, bf16[384,512]{1,0:T(8,128)(2,1)S(1)}, u32[]{:S(2)}, u32[]{:S(2)}) collective-permute-start(bf16[384,512]{1,0:T(8,128)(2,1)S(1)} %get-tuple-element.54), channel_id=1, source_target_pairs={{0,2},{1,3},{2,0},{3,1},{4,6},{5,7},{6,4},{7,5},{8,10},{9,11},{10,... | collective-permute-start | bytes 1179656 | tf_op jit(solution)/shard_map/ppermute | solution.py:378
  26.1 18.9 %collective-permute-start.5 = (bf16[384,512]{1,0:T(8,128)(2,1)S(1)}, bf16[384,512]{1,0:T(8,128)(2,1)S(1)}, u32[]{:S(2)}, u32[]{:S(2)}) collective-permute-start(bf16[384,512]{1,0:T(8,128)(2,1)S(1)} %get-tuple-element.55), channel_id=1, source_target_pairs={{0,3},{1,2},{2,1},{3,0},{4,7},{5,6},{6,5},{7,4},{8,11},{9,10},{10,... | collective-permute-start | bytes 1179656 | tf_op jit(solution)/shard_map/ppermute | solution.py:378
  27.8 19.8 %collective-permute-start.8 = (bf16[384,512]{1,0:T(8,128)(2,1)S(1)}, bf16[384,512]{1,0:T(8,128)(2,1)S(1)}, u32[]{:S(2)}, u32[]{:S(2)}) collective-permute-start(bf16[384,512]{1,0:T(8,128)(2,1)S(1)} %get-tuple-element.61), channel_id=1, source_target_pairs={{0,4},{8,12},{16,20},{24,28},{4,0},{12,8},{20,16},{28,24},{1,5},{9... | collective-permute-start | bytes 1179656 | tf_op jit(solution)/shard_map/ppermute | solution.py:384
  30.3 17.3 %collective-permute-start.9 = (bf16[384,512]{1,0:T(8,128)(2,1)S(1)}, bf16[384,512]{1,0:T(8,128)(2,1)S(1)}, u32[]{:S(2)}, u32[]{:S(2)}) collective-permute-start(bf16[384,512]{1,0:T(8,128)(2,1)S(1)} %get-tuple-element.62), channel_id=1, source_target_pairs={{4,8},{12,16},{20,24},{8,4},{16,12},{24,20},{5,9},{13,17},{21,25},... | collective-permute-start | bytes 1179656 | tf_op jit(solution)/shard_map/ppermute | solution.py:384

commit v23 on v22

--- a/solution.py
+++ b/solution.py
@@ -189,7 +189,7 @@
 
 
 def end_kernel(n, near, waits, *refs):
-    halo_ref, plain_ref, rest = refs[waits], refs[waits + 1], refs[-(n + 2):]
+    halo_ref, plain_ref, rest = refs[0], refs[waits + 1], refs[-(n + 2):]
     active_refs, (slope_ref, wide) = rest[:n], rest[n:]
     ch, odd = lax.axis_index("ch"), odd_place()
     channels, length = slope_ref.shape
@@ -215,7 +215,7 @@
 
 def one_end(near, halo, plain, active, slope, wide, waited):
     n = len(active)
-    operands = [(o, True) for o in (*waited, halo, plain, *active, slope, wide)]
+    operands = [(o, True) for o in (halo, *waited, plain, *active, slope, wide)]
     results = kernel_call(
         "near_end" if near else "far_end", functools.partial(end_kernel, n, near, len(waited)), operands,
         [(a.shape, a.dtype, True) for a in (*active, slope, wide)],

time: 49.2 us -> 47.9 us (0.974)
  waiting for transfers between devices: 17 us -> 15.8 us
    ppermute x4, starting transfers between devices: 5.59 us -> 7.12 us  [swap(): return lax.ppermute(values, 'ctx', pairs + [(b, a) for a, b in pairs])]
    ppermute x6, starting transfers between devices: 5.7 us -> 4.19 us  [exchange(): lax.ppermute(piece, 'ch', [(i, i ^ k) for i in range(lax.axis_size('ch'))])]
    ppermute x4, waiting for transfers between devices: 7.64 us -> 6.43 us  [swap(): return lax.ppermute(values, 'ctx', pairs + [(b, a) for a, b in pairs])]
  transfers between devices with their start and end apart: 10 -> 10, of which waited for: 4 -> 4; matrix products, arithmetic and copies ran while one was open for 0% -> 0% of each run, Pallas kernels for 33% -> 34%
where the time goes in v23:
time: 47.9 us; the launch traced here: 47.7 us
  Pallas kernels  19.7 us (41%)
  waiting for transfers between devices  15.8 us (33%)
  starting transfers between devices  11.3 us (24%)
  between operations  0.94 us (2%)
    pallas_call x13, Pallas kernels, kernel_call(): pl.pallas_call(kernel, in_specs=[INSIDE if held else ANY for _, held in o...  19.7 us
    ppermute x6, waiting for transfers between devices, exchange(): lax.ppermute(piece, 'ch', [(i, i ^ k) for i in range(lax.axis_size('ch'))])  9.34 us
    ppermute x4, starting transfers between devices, swap(): return lax.ppermute(values, 'ctx', pairs + [(b, a) for a, b in pairs])  7.12 us
    ppermute x4, waiting for transfers between devices, swap(): return lax.ppermute(values, 'ctx', pairs + [(b, a) for a, b in pairs])  6.43 us
    ppermute x6, starting transfers between devices, exchange(): lax.ppermute(piece, 'ch', [(i, i ^ k) for i in range(lax.axis_size('ch'))])  4.19 us
  transfers between devices with their start and end apart: 10, of which 4 were waited for; matrix products, arithmetic and copies ran while one was open for 0% of the time, Pallas kernels for 34%

profile of v23, /device:TPU:0, one launch (start us, length us, event | category | flops | bytes accessed | tf_op | source)
XLA Modules:
  0.0 47.7 jit_solution(16070533473791337182)
XLA Ops:
  0.6 2.2 %upstream.3 = (bf16[384,512]{1,0:T(8,128)(2,1)S(1)}, bf16[1536,512]{1,0:T(8,128)(2,1)S(1)}, bf16[384,512]{1,0:T(8,128)(2,1)S(1)}) custom-call(bf16[1536,1536]{1,0:T(8,128)(2,1)} %pw_ref.11, bf16[1536,512]{1,0:T(8,128)(2,1)} %cot_ref.1, bf16[384,2048]{1,0:T(8,128)(2,1)} %x_ref.7), custom_call_target="tpu_custom_call" | custom-call | tf_op jit(solution)/shard_map/upstream/pallas_call | solution.py:19
  2.8 3.0 %collective-permute-start.1 = (bf16[384,512]{1,0:T(8,128)(2,1)S(1)}, bf16[384,512]{1,0:T(8,128)(2,1)S(1)}, u32[]{:S(2)}, u32[]{:S(2)}) collective-permute-start(bf16[384,512]{1,0:T(8,128)(2,1)S(1)} %get-tuple-element.38), channel_id=1, source_target_pairs={{0,4},{8,12},{16,20},{24,28},{4,0},{12,8},{20,16},{28,24},{1,5},{9... | collective-permute-start | bytes 1179656 | tf_op jit(solution)/shard_map/ppermute | solution.py:384
  5.8 1.5 %collective-permute-start.2 = (bf16[384,512]{1,0:T(8,128)(2,1)S(1)}, bf16[384,512]{1,0:T(8,128)(2,1)S(1)}, u32[]{:S(2)}, u32[]{:S(2)}) collective-permute-start(bf16[384,512]{1,0:T(8,128)(2,1)S(1)} %get-tuple-element.39), channel_id=1, source_target_pairs={{0,2},{1,3},{2,0},{3,1},{4,6},{5,7},{6,4},{7,5},{8,10},{9,11},{10,... | collective-permute-start | bytes 1179656 | tf_op jit(solution)/shard_map/ppermute | solution.py:378
  7.4 2.0 %upstream.4 = (bf16[384,512]{1,0:T(8,128)(2,1)S(1)}, bf16[384,512]{1,0:T(8,128)(2,1)S(1)}) custom-call(bf16[1536,1536]{1,0:T(8,128)(2,1)} %pw_ref.11, bf16[1536,512]{1,0:T(8,128)(2,1)S(1)} %get-tuple-element.35.cot_ref, bf16[384,2048]{1,0:T(8,128)(2,1)} %x_ref.7), custom_call_target="tpu_custom_call" | custom-call | tf_op jit(solution)/shard_map/upstream/pallas_call | solution.py:19
  9.4 0.7 %collective-permute-start = (bf16[384,512]{1,0:T(8,128)(2,1)S(1)}, bf16[384,512]{1,0:T(8,128)(2,1)S(1)}, u32[]{:S(2)}, u32[]{:S(2)}) collective-permute-start(bf16[384,512]{1,0:T(8,128)(2,1)S(1)} %get-tuple-element.36), channel_id=1, source_target_pairs={{4,8},{12,16},{20,24},{8,4},{16,12},{24,20},{5,9},{13,17},{21,25},... | collective-permute-start | bytes 1179656 | tf_op jit(solution)/shard_map/ppermute | solution.py:384
  10.1 0.1 collective-permute-start.6
  10.2 2.8 %upstream.5 = (bf16[384,512]{1,0:T(8,128)(2,1)S(1)}, bf16[384,512]{1,0:T(8,128)(2,1)S(1)}) custom-call(bf16[1536,1536]{1,0:T(8,128)(2,1)} %pw_ref.11, bf16[1536,512]{1,0:T(8,128)(2,1)S(1)} %get-tuple-element.35.cot_ref, bf16[384,2048]{1,0:T(8,128)(2,1)} %x_ref.7), custom_call_target="tpu_custom_call" | custom-call | tf_op jit(solution)/shard_map/upstream/pallas_call | solution.py:19
  13.0 0.7 %collective-permute-start.7 = (bf16[384,512]{1,0:T(8,128)(2,1)S(1)}, bf16[384,512]{1,0:T(8,128)(2,1)S(1)}, u32[]{:S(2)}, u32[]{:S(2)}) collective-permute-start(bf16[384,512]{1,0:T(8,128)(2,1)S(1)} %get-tuple-element.59), channel_id=1, source_target_pairs={{0,1},{1,0},{2,3},{3,2},{4,5},{5,4},{6,7},{7,6},{8,9},{9,8},{10,11... | collective-permute-start | bytes 1179656 | tf_op jit(solution)/shard_map/ppermute | solution.py:378
  13.7 3.3 %interior.1 = (bf16[384,512]{1,0:T(8,128)(2,1)S(1)}, bf16[384,512]{1,0:T(8,128)(2,1)S(1)}, bf16[384,512]{1,0:T(8,128)(2,1)S(1)}, bf16[384,512]{1,0:T(8,128)(2,1)...) custom-call(bf16[384,2048]{1,0:T(8,128)(2,1)} %x_ref.7, ...), custom_call_target="tpu_custom_call" | custom-call | tf_op jit(solution)/shard_map/interior/pallas_call | solution.py:19
  17.0 5.6 %collective-permute-done.1.refs_0_ = bf16[384,512]{1,0:T(8,128)(2,1)S(1)} collective-permute-done((bf16[384,512]{1,0:T(8,128)(2,1)S(1)}, bf16[384,512]{1,0:T(8,128)(2,1)S(1)}, u32[]{:S(2)}, u32[]{:S(2)}) %collective-permute-start.1) | collective-permute-done | bytes 393248 | tf_op jit(solution)/shard_map/ppermute | solution.py:384
  22.6 0.0 collective-permute-done.2.refs_1_.rest_0_
  22.7 0.8 %near_end.1 = (bf16[384,512]{1,0:T(8,128)(2,1)S(1)}, bf16[384,512]{1,0:T(8,128)(2,1)S(1)}, bf16[384,512]{1,0:T(8,128)(2,1)S(1)}, bf16[384,512]{1,0:T(8,128)(2,1)...) custom-call(bf16[384,512]{1,0:T(8,128)(2,1)S(1)} %collective-permute, ...), custom_call_target="tpu_custom_call", output_to_operand_aliasing={{0}: (3, {}), {1}: (4, {}), {2}: (5, {}), {3}: (6, {}), {4}... | custom-call | tf_op jit(solution)/shard_map/near_end/pallas_call | solution.py:19
  23.4 0.0 collective-permute-done.refs_0_
  23.4 0.0 slice-start.1
  23.4 0.8 %far_end.1 = (bf16[384,512]{1,0:T(8,128)(2,1)S(1)}, bf16[384,512]{1,0:T(8,128)(2,1)S(1)}, bf16[384,512]{1,0:T(8,128)(2,1)S(1)}, bf16[384,512]{1,0:T(8,128)(2,1)S...) custom-call(bf16[384,512]{1,0:T(8,128)(2,1)S(1)} %collective-permute, ...), custom_call_target="tpu_custom_call", output_to_operand_aliasing={{0}: (2, {}), {1}: (3, {}), {2}: (4, {}), {3}: (5, {}), {4}... | custom-call | tf_op jit(solution)/shard_map/far_end/pallas_call | solution.py:19
  24.2 0.1 collective-permute-start.3
  24.3 1.6 %collective-permute-start.4 = (bf16[384,512]{1,0:T(8,128)(2,1)S(1)}, bf16[384,512]{1,0:T(8,128)(2,1)S(1)}, u32[]{:S(2)}, u32[]{:S(2)}) collective-permute-start(bf16[384,512]{1,0:T(8,128)(2,1)S(1)} %get-tuple-element.54), channel_id=1, source_target_pairs={{0,2},{1,3},{2,0},{3,1},{4,6},{5,7},{6,4},{7,5},{8,10},{9,11},{10,... | collective-permute-start | bytes 1179656 | tf_op jit(solution)/shard_map/ppermute | solution.py:378
  25.9 0.3 collective-permute-start.5
  26.2 0.0 collective-permute-done.6.refs_0_
  26.2 0.0 collective-permute-done.7.rest_2_
  26.2 0.4 grad_conv.1
  26.5 2.6 %collective-permute-start.8 = (bf16[384,512]{1,0:T(8,128)(2,1)S(1)}, bf16[384,512]{1,0:T(8,128)(2,1)S(1)}, u32[]{:S(2)}, u32[]{:S(2)}) collective-permute-start(bf16[384,512]{1,0:T(8,128)(2,1)S(1)} %get-tuple-element.61), channel_id=1, source_target_pairs={{0,4},{8,12},{16,20},{24,28},{4,0},{12,8},{20,16},{28,24},{1,5},{9... | collective-permute-start | bytes 1179656 | tf_op jit(solution)/shard_map/ppermute | solution.py:384
  29.1 0.9 %collective-permute-start.9 = (bf16[384,512]{1,0:T(8,128)(2,1)S(1)}, bf16[384,512]{1,0:T(8,128)(2,1)S(1)}, u32[]{:S(2)}, u32[]{:S(2)}) collective-permute-start(bf16[384,512]{1,0:T(8,128)(2,1)S(1)} %get-tuple-element.62), channel_id=1, source_target_pairs={{4,8},{12,16},{20,24},{8,4},{16,12},{24,20},{5,9},{13,17},{21,25},... | collective-permute-start | bytes 1179656 | tf_op jit(solution)/shard_map/ppermute | solution.py:384
  30.0 1.7 %back_interior.1 = (bf16[384,2048]{1,0:T(8,128)(2,1)}, f32[384,1024]{1,0:T(8,128)S(1)}) custom-call(bf16[384,2048]{1,0:T(8,128)(2,1)S(1)} %get-tuple-element.63.grad_ref, bf16[3,384,96]{2,1,0:T(8,128)(2,1)S(1)} %get-tuple-element.64.turned_ref), custom_call_target="tpu_custom_call" | custom-call | tf_op jit(solution)/shard_map/back_interior/pallas_call | solution.py:19
  31.7 4.6 %collective-permute-done.4.rest_0_ = bf16[384,512]{1,0:T(8,128)(2,1)S(1)} collective-permute-done((bf16[384,512]{1,0:T(8,128)(2,1)S(1)}, bf16[384,512]{1,0:T(8,128)(2,1)S(1)}, u32[]{:S(2)}, u32[]{:S(2)}) %collective-permute-start.4) | collective-permute-done | bytes 393248 | tf_op jit(solution)/shard_map/ppermute | solution.py:378
  36.3 1.0 %early_mix.1.rest_2_ = f32[1536,512]{1,0:T(8,128)S(1)} custom-call(bf16[1536,1536]{1,0:T(8,128)(2,1)S(1)} %bitcast.2, bf16[384,512]{1,0:T(8,128)(2,1)S(1)} %collective-permute-done.4.rest_0_), custom_call_target="tpu_custom_call" | custom-call | tf_op jit(solution)/shard_map/early_mix/pallas_call | solution.py:19
  37.3 0.0 collective-permute-done.3.rest_0_
  37.3 1.8 %half_mix.1.sum_ref = f32[1536,512]{1,0:T(8,128)S(1)} custom-call(bf16[1536,1536]{1,0:T(8,128)(2,1)S(1)} %bitcast.2, bf16[384,512]{1,0:T(8,128)(2,1)S(1)} %collective-permute-done.3.rest_0_, bf16[384,512]{1,0:T(8,128)(2,1)S(1)} %get-tuple-element.53.rest_1_, f32[1536,512]{1,0:T(8,128)S(1)} %early_mix.1.rest_2_), custom_call_target="tpu_custom_call", output_to_operand_aliasing={{}: (3, {})} | custom-call | tf_op jit(solution)/shard_map/half_mix/pallas_call | solution.py:19
  39.1 4.7 %collective-permute-done.5.rest_0_ = bf16[384,512]{1,0:T(8,128)(2,1)S(1)} collective-permute-done((bf16[384,512]{1,0:T(8,128)(2,1)S(1)}, bf16[384,512]{1,0:T(8,128)(2,1)S(1)}, u32[]{:S(2)}, u32[]{:S(2)}) %collective-permute-start.5) | collective-permute-done | bytes 393248 | tf_op jit(solution)/shard_map/ppermute | solution.py:378
  43.8 1.8 %late_mix.1 = (bf16[1536,512]{1,0:T(8,128)(2,1)}, f32[8,128]{1,0:T(8,128)S(1)}) custom-call(bf16[1536,1536]{1,0:T(8,128)(2,1)S(1)} %bitcast.2, f32[1536,512]{1,0:T(8,128)S(1)} %half_mix.1.sum_ref, bf16[384,512]{1,0:T(8,128)(2,1)S(1)} %collective-permute-done.5.rest_0_), custom_call_target="tpu_custom_call" | custom-call | tf_op jit(solution)/shard_map/late_mix/pallas_call | solution.py:19
  45.6 0.8 %collective-permute-done.8.near_ref = bf16[384,512]{1,0:T(8,128)(2,1)S(1)} collective-permute-done((bf16[384,512]{1,0:T(8,128)(2,1)S(1)}, bf16[384,512]{1,0:T(8,128)(2,1)S(1)}, u32[]{:S(2)}, u32[]{:S(2)}) %collective-permute-start.8) | collective-permute-done | bytes 393248 | tf_op jit(solution)/shard_map/ppermute | solution.py:384
  46.4 1.2 %back_ends.1 = bf16[384,2048]{1,0:T(8,128)(2,1)} custom-call(bf16[384,512]{1,0:T(8,128)(2,1)S(1)} %collective-permute-done.8.near_ref, bf16[384,512]{1,0:T(8,128)(2,1)S(1)} %collective-permute-done.9.far_ref, f32[384,1024]{1,0:T(8,128)S(1)} %get-tuple-element.65.ends_ref, ...), custom_call_target="tpu_custom_call", output_to_operand_aliasing={{}: (5, {})} | custom-call | tf_op jit(solution)/shard_map/back_ends/pallas_call | solution.py:19
  (6 shorter events, 0.0 us)
Async XLA Ops:
  2.8 19.8 %collective-permute-start.1 = (bf16[384,512]{1,0:T(8,128)(2,1)S(1)}, bf16[384,512]{1,0:T(8,128)(2,1)S(1)}, u32[]{:S(2)}, u32[]{:S(2)}) collective-permute-start(bf16[384,512]{1,0:T(8,128)(2,1)S(1)} %get-tuple-element.38), channel_id=1, source_target_pairs={{0,4},{8,12},{16,20},{24,28},{4,0},{12,8},{20,16},{28,24},{1,5},{9... | collective-permute-start | bytes 1179656 | tf_op jit(solution)/shard_map/ppermute | solution.py:384
  5.8 16.8 %collective-permute-start.2 = (bf16[384,512]{1,0:T(8,128)(2,1)S(1)}, bf16[384,512]{1,0:T(8,128)(2,1)S(1)}, u32[]{:S(2)}, u32[]{:S(2)}) collective-permute-start(bf16[384,512]{1,0:T(8,128)(2,1)S(1)} %get-tuple-element.39), channel_id=1, source_target_pairs={{0,2},{1,3},{2,0},{3,1},{4,6},{5,7},{6,4},{7,5},{8,10},{9,11},{10,... | collective-permute-start | bytes 1179656 | tf_op jit(solution)/shard_map/ppermute | solution.py:378
  9.4 14.0 %collective-permute-start = (bf16[384,512]{1,0:T(8,128)(2,1)S(1)}, bf16[384,512]{1,0:T(8,128)(2,1)S(1)}, u32[]{:S(2)}, u32[]{:S(2)}) collective-permute-start(bf16[384,512]{1,0:T(8,128)(2,1)S(1)} %get-tuple-element.36), channel_id=1, source_target_pairs={{4,8},{12,16},{20,24},{8,4},{16,12},{24,20},{5,9},{13,17},{21,25},... | collective-permute-start | bytes 1179656 | tf_op jit(solution)/shard_map/ppermute | solution.py:384
  10.1 16.1 %collective-permute-start.6 = (bf16[384,512]{1,0:T(8,128)(2,1)S(1)}, bf16[384,512]{1,0:T(8,128)(2,1)S(1)}, u32[]{:S(2)}, u32[]{:S(2)}) collective-permute-start(bf16[384,512]{1,0:T(8,128)(2,1)S(1)} %get-tuple-element.58), channel_id=1, source_target_pairs={{0,3},{1,2},{2,1},{3,0},{4,7},{5,6},{6,5},{7,4},{8,11},{9,10},{10,... | collective-permute-start | bytes 1179656 | tf_op jit(solution)/shard_map/ppermute | solution.py:378
  13.0 13.2 %collective-permute-start.7 = (bf16[384,512]{1,0:T(8,128)(2,1)S(1)}, bf16[384,512]{1,0:T(8,128)(2,1)S(1)}, u32[]{:S(2)}, u32[]{:S(2)}) collective-permute-start(bf16[384,512]{1,0:T(8,128)(2,1)S(1)} %get-tuple-element.59), channel_id=1, source_target_pairs={{0,1},{1,0},{2,3},{3,2},{4,5},{5,4},{6,7},{7,6},{8,9},{9,8},{10,11... | collective-permute-start | bytes 1179656 | tf_op jit(solution)/shard_map/ppermute | solution.py:378
  22.6 13.6 %slice-start = ((s8[4718592]{0:T(1024)(128)(4,1)}), s8[4194304]{0:T(1024)(128)(4,1)S(1)}, s32[]{:S(2)}) async-start(s8[4718592]{0:T(1024)(128)(4,1)} %bitcast.1), calls=%async_computation | async-start | bytes 8388608
  23.4 12.9 %slice-start.1 = ((s8[4718592]{0:T(1024)(128)(4,1)}), s8[524288]{0:T(1024)(128)(4,1)S(1)}, s32[]{:S(2)}) async-start(s8[4718592]{0:T(1024)(128)(4,1)} %bitcast.1), calls=%async_computation.1 | async-start | bytes 1048576
  24.2 13.0 %collective-permute-start.3 = (bf16[384,512]{1,0:T(8,128)(2,1)S(1)}, bf16[384,512]{1,0:T(8,128)(2,1)S(1)}, u32[]{:S(2)}, u32[]{:S(2)}) collective-permute-start(bf16[384,512]{1,0:T(8,128)(2,1)S(1)} %get-tuple-element.52), channel_id=1, source_target_pairs={{0,1},{1,0},{2,3},{3,2},{4,5},{5,4},{6,7},{7,6},{8,9},{9,8},{10,11... | collective-permute-start | bytes 1179656 | tf_op jit(solution)/shard_map/ppermute | solution.py:378
  24.3 12.0 %collective-permute-start.4 = (bf16[384,512]{1,0:T(8,128)(2,1)S(1)}, bf16[384,512]{1,0:T(8,128)(2,1)S(1)}, u32[]{:S(2)}, u32[]{:S(2)}) collective-permute-start(bf16[384,512]{1,0:T(8,128)(2,1)S(1)} %get-tuple-element.54), channel_id=1, source_target_pairs={{0,2},{1,3},{2,0},{3,1},{4,6},{5,7},{6,4},{7,5},{8,10},{9,11},{10,... | collective-permute-start | bytes 1179656 | tf_op jit(solution)/shard_map/ppermute | solution.py:378
  25.9 17.9 %collective-permute-start.5 = (bf16[384,512]{1,0:T(8,128)(2,1)S(1)}, bf16[384,512]{1,0:T(8,128)(2,1)S(1)}, u32[]{:S(2)}, u32[]{:S(2)}) collective-permute-start(bf16[384,512]{1,0:T(8,128)(2,1)S(1)} %get-tuple-element.55), channel_id=1, source_target_pairs={{0,3},{1,2},{2,1},{3,0},{4,7},{5,6},{6,5},{7,4},{8,11},{9,10},{10,... | collective-permute-start | bytes 1179656 | tf_op jit(solution)/shard_map/ppermute | solution.py:378
  26.5 19.9 %collective-permute-start.8 = (bf16[384,512]{1,0:T(8,128)(2,1)S(1)}, bf16[384,512]{1,0:T(8,128)(2,1)S(1)}, u32[]{:S(2)}, u32[]{:S(2)}) collective-permute-start(bf16[384,512]{1,0:T(8,128)(2,1)S(1)} %get-tuple-element.61), channel_id=1, source_target_pairs={{0,4},{8,12},{16,20},{24,28},{4,0},{12,8},{20,16},{28,24},{1,5},{9... | collective-permute-start | bytes 1179656 | tf_op jit(solution)/shard_map/ppermute | solution.py:384
  29.1 17.3 %collective-permute-start.9 = (bf16[384,512]{1,0:T(8,128)(2,1)S(1)}, bf16[384,512]{1,0:T(8,128)(2,1)S(1)}, u32[]{:S(2)}, u32[]{:S(2)}) collective-permute-start(bf16[384,512]{1,0:T(8,128)(2,1)S(1)} %get-tuple-element.62), channel_id=1, source_target_pairs={{4,8},{12,16},{20,24},{8,4},{16,12},{24,20},{5,9},{13,17},{21,25},... | collective-permute-start | bytes 1179656 | tf_op jit(solution)/shard_map/ppermute | solution.py:384
